TPU v7x, 32 devices: a whole 2x2x4 slice. The times are simulated.
32 devices in a mesh: sp: 16 (over z, y, core), tp: 2 (over x).
Axes of the slice: x: 2, y: 2, z: 4, core: 2. Of those that a mesh axis runs over, the one named last changes fastest.
Arguments:
- tokens: bfloat16 [256, 128, 512], P(('sp', 'tp')), may hold values from -6 to 6
- cotangent: bfloat16 [256, 128, 512], P(('sp', 'tp')), may hold values from -12 to 12
- w_in: float32 [512, 2048], P('sp', 'tp'), may hold values from -0.25 to 0.25
- w_out: float32 [512, 2048], P('sp', 'tp'), may hold values from -0.125 to 0.125
- mixer_weights: float32 [2, 8, 2, 64, 64], replicated, may hold values from -0.75 to 0.75
- vectors: float32 [13, 512], replicated, may hold values from -0.6 to 1.6, as said below
- w_in_moment: float32 [512, 2048], P('sp', 'tp'), may hold values from -4 to 4
- w_out_moment: float32 [512, 2048], P('sp', 'tp'), may hold values from -4 to 4
- mixer_moment: float32 [2, 8, 2, 64, 64], replicated, may hold values from -4 to 4
- vectors_moment: float32 [13, 512], replicated, may hold values from -4 to 4
- w_in_average: float32 [512, 2048], P('sp', 'tp'), may hold values from -0.25 to 0.25
- w_out_average: float32 [512, 2048], P('sp', 'tp'), may hold values from -0.125 to 0.125
- mixer_average: float32 [2, 8, 2, 64, 64], replicated, may hold values from -0.75 to 0.75
- vectors_average: float32 [13, 512], replicated, may hold values from -0.6 to 1.6, as said below
Outputs:
- output: bfloat16 [256, 128, 512], P(('sp', 'tp'))
- grad_tokens: bfloat16 [256, 128, 512], P(('sp', 'tp'))
- new_w_in: float32 [512, 2048], P('sp', 'tp')
- new_w_out: float32 [512, 2048], P('sp', 'tp')
- new_mixer: float32 [2, 8, 2, 64, 64], replicated
- new_vectors: float32 [13, 512], replicated
- new_w_in_moment: float32 [512, 2048], P('sp', 'tp')
- new_w_out_moment: float32 [512, 2048], P('sp', 'tp')
- new_mixer_moment: float32 [2, 8, 2, 64, 64], replicated
- new_vectors_moment: float32 [13, 512], replicated
- new_w_in_average: float32 [512, 2048], P('sp', 'tp')
- new_w_out_average: float32 [512, 2048], P('sp', 'tp')
- new_mixer_average: float32 [2, 8, 2, 64, 64], replicated
- new_vectors_average: float32 [13, 512], replicated
- w_in_copy: bfloat16 [512, 2048], P('sp', 'tp')
- w_out_copy: bfloat16 [512, 2048], P('sp', 'tp')
Inputs may be any that keep to these rules, and one draw needn't show every extreme that they name: `vectors`: gain rows 0 and 2 lie near one, the other rows near zero. `vectors_average`: gain rows 0 and 2 lie near one, the other rows near zero.
All inputs are finite; a program needn't handle non-finite values.
Results may differ from a plain program's by a relative error of at most 0.014.
The roundings to bfloat16 on the way count: a program that leaves them out, or rounds other values in their place, can miss the bound.
Values may be sent and summed in bfloat16 or wider, within the bound.
No kernel may reach another device: no remote copies, remote signals or barrier semaphores. Data moves between devices by JAX's collectives and lax.ppermute only.
A program may use at most 128 MiB of HBM per device.

v0:
```python
import math

import jax
import jax.numpy as jnp
from jax import lax
from jax.sharding import PartitionSpec as P

FF = 2048
MODES = 32
G = 128


EPSILON = 1e-05
LEARNING_RATE = 0.05
MOMENTUM = 0.9
WEIGHT_DECAY = 0.0001
AVERAGE = 0.75


def dft_tables():
    positions = jnp.arange(G, dtype=jnp.int32)
    wave_index = jnp.arange(MODES, dtype=jnp.int32)
    norm_root = 1.0 / math.sqrt(G)
    step_angle = 2.0 * math.pi / G
    phase_w = (positions[:, None] * wave_index[None, :] % G).astype(jnp.float32) * step_angle
    factor = jnp.where(wave_index == 0, 1.0, 2.0).astype(jnp.float32)
    cos_w = jnp.cos(phase_w) * norm_root
    sin_w = jnp.sin(phase_w) * norm_root
    forward_w = jnp.stack([cos_w, -sin_w], axis=1)
    inverse_w = jnp.stack([cos_w * factor, -sin_w * factor], axis=1)
    frequency = jnp.where(wave_index < MODES // 2, wave_index, wave_index - MODES)
    phase_h = (frequency[:, None] * positions[None, :] % G).astype(jnp.float32) * step_angle
    cos_h = jnp.cos(phase_h) * norm_root
    sin_h = jnp.sin(phase_h) * norm_root
    forward_h = jnp.stack([jnp.stack([cos_h, -sin_h], -1), jnp.stack([sin_h, cos_h], -1)], -2)
    inverse_h = jnp.stack([jnp.stack([cos_h, sin_h], -1), jnp.stack([-sin_h, cos_h], -1)], -2)
    return tuple(
        [table.astype(jnp.bfloat16) for table in (forward_w, inverse_w, forward_h, inverse_h)]
    )


def norm_forward(values, gain, shift):
    center = values - jnp.mean(values, axis=-1, keepdims=True)
    inverse = lax.rsqrt(jnp.mean(center * center, axis=-1, keepdims=True) + EPSILON)
    normal = center * inverse
    return (normal * gain + shift, normal, inverse)


def norm_backward(upstream, normal, inverse, gain):
    scaled = upstream * gain
    centered = scaled - jnp.mean(scaled, axis=-1, keepdims=True)
    centered = centered - normal * jnp.mean(scaled * normal, axis=-1, keepdims=True)
    return (centered * inverse, jnp.sum(upstream * normal, axis=0), jnp.sum(upstream, axis=0))


def gelu_grad(values, upstream):
    return jax.vjp(jax.nn.gelu, values)[1](upstream)[0]


def mix_matrix(weight):
    upper_half = jnp.concatenate([weight[0], weight[1]], axis=1)
    lower_half = jnp.concatenate([-weight[1], weight[0]], axis=1)
    return jnp.concatenate([upper_half, lower_half], axis=0)


def mix_grad(grad_matrix, half_size):
    real_part = grad_matrix[:half_size, :half_size] + grad_matrix[half_size:, half_size:]
    imag_part = grad_matrix[:half_size, half_size:] - grad_matrix[half_size:, :half_size]
    return jnp.stack([real_part, imag_part])


def contract(left, right, left_axis, right_axis):
    return lax.dot_general(
        left, right, (((left_axis,), (right_axis,)), ((), ())), preferred_element_type=jnp.float32
    )


def update(weight, gradient, moment, average, decay_rate):
    step_grad = gradient + decay_rate * weight
    new_moment = MOMENTUM * moment + step_grad
    new_weight = weight - LEARNING_RATE * (step_grad + MOMENTUM * new_moment)
    new_average = AVERAGE * average + (1.0 - AVERAGE) * new_weight
    return (new_weight, new_moment, new_average)


def on_device(
    tokens,
    cotangent,
    w_in,
    w_out,
    mixer_weights,
    vectors,
    w_in_moment,
    w_out_moment,
    mixer_moment,
    vectors_moment,
    w_in_average,
    w_out_average,
    mixer_average,
    vectors_average,
):
    sp_count = lax.axis_size("sp")
    tp_count = lax.axis_size("tp")
    device_count = sp_count * tp_count
    grid_rows, grid_size, model_width = tokens.shape
    local_tokens = grid_rows * grid_size
    block_count = mixer_weights.shape[1]
    block_size = mixer_weights.shape[3]
    pair_count = block_count * MODES // device_count
    item_count = grid_rows * device_count // grid_size
    shard_units = w_in.shape[1]
    grad_scale = 1.0 / math.sqrt(local_tokens * device_count)
    forward_w, inverse_w, forward_h, inverse_h = dft_tables()
    sp_index = lax.axis_index("sp")
    tp_index = lax.axis_index("tp")
    block_index = (sp_index * tp_count + tp_index) * pair_count // MODES
    onehot = (jnp.arange(block_count, dtype=jnp.int32) == block_index).astype(jnp.float32)
    gain_one, shift_one, gain_two, shift_two, bias_out = (
        vectors[0],
        vectors[1],
        vectors[2],
        vectors[3],
        vectors[4],
    )
    bias_in = vectors[5:9].reshape(FF)
    mixer_bias = vectors[9:13].reshape(2, block_count, 2 * block_size)
    bias_mix = jnp.sum(onehot[None, :, None] * mixer_bias, axis=1)
    mix_weight = jnp.sum(onehot[None, :, None, None, None] * mixer_weights, axis=1)
    matrix_one = mix_matrix(mix_weight[0]).astype(jnp.bfloat16)
    matrix_two = mix_matrix(mix_weight[1]).astype(jnp.bfloat16)

    def to_item_order(arrived):
        shaped = arrived.reshape(tp_count, sp_count, grid_rows, pair_count, 2, block_size)
        return jnp.swapaxes(shaped, 0, 1).reshape(grid_size, item_count, pair_count, 2, block_size)

    def to_pair_order(returned):
        shaped = returned.reshape(grid_rows, tp_count, sp_count, pair_count, 2, block_size)
        return jnp.swapaxes(shaped, 1, 2).reshape(grid_rows, block_count, MODES, 2, block_size)

    flat_tokens = tokens.reshape(local_tokens, model_width).astype(jnp.float32)
    normed_one, normal_one, inverse_one = norm_forward(flat_tokens, gain_one, shift_one)
    normed_one = normed_one.astype(jnp.bfloat16).reshape(
        grid_rows, grid_size, block_count, block_size
    )
    across = jnp.einsum(
        "rwbc,wek->rbkec", normed_one, forward_w, preferred_element_type=jnp.float32
    )
    across = across.astype(jnp.bfloat16).reshape(grid_rows, block_count * MODES, 2 * block_size)
    arrived = lax.all_to_all(
        lax.all_to_all(across, "sp", split_axis=1, concat_axis=0, tiled=True),
        "tp",
        split_axis=1,
        concat_axis=0,
        tiled=True,
    )
    spectrum = to_item_order(arrived)
    modal_part = jnp.einsum(
        "mhef,hipec->mipfc", forward_h, spectrum, preferred_element_type=jnp.float32
    )
    modal_flat = modal_part.astype(jnp.bfloat16).reshape(
        MODES * item_count * pair_count, 2 * block_size
    )
    mix_inner = jnp.dot(modal_flat, matrix_one, preferred_element_type=jnp.float32) + bias_mix[0]
    active = jax.nn.gelu(mix_inner).astype(jnp.bfloat16)
    mix_outer = (
        jnp.dot(active, matrix_two, preferred_element_type=jnp.float32) + bias_mix[1]
    ).astype(jnp.bfloat16)
    mix_outer = mix_outer.reshape(MODES, item_count, pair_count, 2, block_size)
    gridded = jnp.einsum(
        "mhef,mipec->hipfc", inverse_h, mix_outer, preferred_element_type=jnp.float32
    )
    gridded = gridded.astype(jnp.bfloat16).reshape(
        grid_size * item_count, pair_count, 2 * block_size
    )
    returned = lax.all_to_all(
        lax.all_to_all(gridded, "sp", split_axis=0, concat_axis=1, tiled=True),
        "tp",
        split_axis=0,
        concat_axis=1,
        tiled=True,
    )
    spatial = jnp.einsum(
        "rbkec,wek->rwbc", to_pair_order(returned), inverse_w, preferred_element_type=jnp.float32
    )
    middle = flat_tokens + spatial.reshape(local_tokens, model_width)
    normed_two, normal_two, inverse_two = norm_forward(middle, gain_two, shift_two)
    normed_two = normed_two.astype(jnp.bfloat16)
    w_in_full, w_out_full = (
        lax.all_gather(w_in.astype(jnp.bfloat16), "sp", axis=0, tiled=True),
        lax.all_gather(w_out.astype(jnp.bfloat16), "sp", axis=0, tiled=True),
    )
    bias_half = lax.dynamic_slice_in_dim(bias_in, tp_index * shard_units, shard_units)
    rows_all = lax.all_gather(normed_two, "tp", axis=0, tiled=True)
    hidden = jnp.dot(rows_all, w_in_full, preferred_element_type=jnp.float32) + bias_half
    active_two = jax.nn.gelu(hidden).astype(jnp.bfloat16)
    row_slice = active_two
    mlp_output = lax.psum_scatter(
        contract(row_slice, w_out_full, 1, 1).astype(jnp.bfloat16),
        "tp",
        scatter_dimension=0,
        tiled=True,
    ).astype(jnp.float32)
    output = middle + mlp_output + bias_out
    flat_cotangent = cotangent.reshape(local_tokens, model_width)
    cotangent_f32 = flat_cotangent.astype(jnp.float32)
    grad_bias_out = jnp.sum(cotangent_f32, axis=0)
    cotangent_all = lax.all_gather(flat_cotangent, "tp", axis=0, tiled=True)
    grad_active = jnp.dot(cotangent_all, w_out_full, preferred_element_type=jnp.float32)
    grad_hidden = gelu_grad(hidden, grad_active).astype(jnp.bfloat16)
    grad_w_out = contract(cotangent_all, active_two, 0, 0)
    grad_w_in = contract(rows_all, grad_hidden, 0, 0)
    bias_grad_half = jnp.sum(grad_hidden.astype(jnp.float32), axis=0)
    grad_bias_in = lax.dynamic_update_slice_in_dim(
        jnp.zeros((FF,), jnp.float32), bias_grad_half, tp_index * shard_units, 0
    )
    row_slice = grad_hidden
    grad_normed = lax.psum_scatter(
        contract(row_slice, w_in_full, 1, 1).astype(jnp.bfloat16),
        "tp",
        scatter_dimension=0,
        tiled=True,
    ).astype(jnp.float32)
    grad_in_shard, grad_out_shard = (
        lax.psum_scatter(grad_w_in, "sp", scatter_dimension=0, tiled=True),
        lax.psum_scatter(grad_w_out, "sp", scatter_dimension=0, tiled=True),
    )
    grad_middle_norm, grad_gain_two, grad_shift_two = norm_backward(
        grad_normed, normal_two, inverse_two, gain_two
    )
    grad_middle = cotangent_f32 + grad_middle_norm
    grad_spatial = grad_middle.astype(jnp.bfloat16).reshape(
        grid_rows, grid_size, block_count, block_size
    )
    grad_gridded = jnp.einsum(
        "rwbc,wek->rbkec", grad_spatial, inverse_w, preferred_element_type=jnp.float32
    )
    grad_gridded = grad_gridded.astype(jnp.bfloat16).reshape(
        grid_rows, block_count * MODES, 2 * block_size
    )
    grad_arrived = lax.all_to_all(
        lax.all_to_all(grad_gridded, "sp", split_axis=1, concat_axis=0, tiled=True),
        "tp",
        split_axis=1,
        concat_axis=0,
        tiled=True,
    )
    grad_grid = to_item_order(grad_arrived)
    grad_outer = jnp.einsum(
        "mhef,hipfc->mipec", inverse_h, grad_grid, preferred_element_type=jnp.float32
    )
    grad_outer = grad_outer.astype(jnp.bfloat16).reshape(
        MODES * item_count * pair_count, 2 * block_size
    )
    grad_active_mix = contract(grad_outer, matrix_two, 1, 1)
    grad_matrix_two = contract(active, grad_outer, 0, 0)
    grad_bias_two = jnp.sum(grad_outer.astype(jnp.float32), axis=0)
    grad_inner = gelu_grad(mix_inner, grad_active_mix).astype(jnp.bfloat16)
    grad_matrix_one = contract(modal_flat, grad_inner, 0, 0)
    grad_bias_one = jnp.sum(grad_inner.astype(jnp.float32), axis=0)
    grad_modal = contract(grad_inner, matrix_one, 1, 1).astype(jnp.bfloat16)
    grad_modal = grad_modal.reshape(MODES, item_count, pair_count, 2, block_size)
    grad_spectrum = jnp.einsum(
        "mhef,mipfc->hipec", forward_h, grad_modal, preferred_element_type=jnp.float32
    )
    grad_spectrum = grad_spectrum.astype(jnp.bfloat16).reshape(
        grid_size * item_count, pair_count, 2 * block_size
    )
    grad_across = lax.all_to_all(
        lax.all_to_all(grad_spectrum, "sp", split_axis=0, concat_axis=1, tiled=True),
        "tp",
        split_axis=0,
        concat_axis=1,
        tiled=True,
    )
    grad_normed_one = jnp.einsum(
        "rbkec,wek->rwbc", to_pair_order(grad_across), forward_w, preferred_element_type=jnp.float32
    )
    grad_normed_one = grad_normed_one.reshape(local_tokens, model_width)
    grad_token_norm, grad_gain_one, grad_shift_one = norm_backward(
        grad_normed_one, normal_one, inverse_one, gain_one
    )
    grad_tokens = (
        (grad_middle + grad_token_norm)
        .astype(jnp.bfloat16)
        .reshape(grid_rows, grid_size, model_width)
    )
    mixer_local = jnp.stack(
        [mix_grad(grad_matrix_one, block_size), mix_grad(grad_matrix_two, block_size)]
    )
    mixer_local = onehot[None, :, None, None, None] * mixer_local[:, None]
    bias_local = onehot[None, :, None] * jnp.stack([grad_bias_one, grad_bias_two])[:, None]
    vector_local = jnp.concatenate(
        [
            jnp.stack(
                [grad_gain_one, grad_shift_one, grad_gain_two, grad_shift_two, grad_bias_out]
            ),
            grad_bias_in.reshape(4, model_width),
            bias_local.reshape(4, model_width),
        ],
        axis=0,
    )
    mixer_grad, vector_grad = lax.psum((mixer_local, vector_local), ("sp", "tp"))
    new_in = update(w_in, grad_in_shard * grad_scale, w_in_moment, w_in_average, WEIGHT_DECAY)
    new_out = update(w_out, grad_out_shard * grad_scale, w_out_moment, w_out_average, WEIGHT_DECAY)
    new_mix = update(
        mixer_weights, mixer_grad * grad_scale, mixer_moment, mixer_average, WEIGHT_DECAY
    )
    new_vec = update(vectors, vector_grad * grad_scale, vectors_moment, vectors_average, 0.0)
    return (
        output.astype(jnp.bfloat16).reshape(grid_rows, grid_size, model_width),
        grad_tokens,
        new_in[0],
        new_out[0],
        new_mix[0],
        new_vec[0],
        new_in[1],
        new_out[1],
        new_mix[1],
        new_vec[1],
        new_in[2],
        new_out[2],
        new_mix[2],
        new_vec[2],
        new_in[0].astype(jnp.bfloat16),
        new_out[0].astype(jnp.bfloat16),
    )


def solution(mesh):
    in_specs = (
        P(("sp", "tp"), None, None),
        P(("sp", "tp"), None, None),
        P("sp", "tp"),
        P("sp", "tp"),
        P(),
        P(),
        P("sp", "tp"),
        P("sp", "tp"),
        P(),
        P(),
        P("sp", "tp"),
        P("sp", "tp"),
        P(),
        P(),
    )
    out_specs = (
        P(("sp", "tp"), None, None),
        P(("sp", "tp"), None, None),
        P("sp", "tp"),
        P("sp", "tp"),
        P(),
        P(),
        P("sp", "tp"),
        P("sp", "tp"),
        P(),
        P(),
        P("sp", "tp"),
        P("sp", "tp"),
        P(),
        P(),
        P("sp", "tp"),
        P("sp", "tp"),
    )
    return jax.shard_map(
        on_device, mesh=mesh, in_specs=in_specs, out_specs=out_specs, check_vma=False
    )
```

profile of v0, /device:TPU:0, one launch (start us, length us, event | category | flops | bytes accessed | tf_op | source)
XLA Modules:
  0.0 662.7 jit_solution(2096115115907632398)
XLA Ops:
  16.1 3.1 reshape.620
  19.2 7.4 %all-to-all-start = ((bf16[8,256,128]{2,0,1:T(8,128)(2,1)}), bf16[8,256,128]{2,0,1:T(8,128)(2,1)}, u32[]{:S(2)}, u32[]{:S(2)}) async-start(bf16[8,256,128]{2,0,1:T(8,128)(2,1)} %reshape.620), calls=%async_computation | async-start | bytes 1048576 | tf_op jit(solution)/shard_map/all_to_all | solution.py:150
  30.1 11.1 %all-to-all-done = bf16[8,256,128]{2,0,1:T(8,128)(2,1)} async-done(((bf16[8,256,128]{2,0,1:T(8,128)(2,1)}), bf16[8,256,128]{2,0,1:T(8,128)(2,1)}, u32[]{:S(2)}, u32[]{:S(2)}) %all-to-all-start) | async-done | bytes 524320 | tf_op jit(solution)/shard_map/all_to_all | solution.py:150
  43.3 4.2 all-to-all-start.1
  48.8 7.2 %all-to-all-done.1 = bf16[128,16,128]{2,0,1:T(8,128)(2,1)} async-done(((bf16[128,16,128]{2,0,1:T(8,128)(2,1)}), bf16[128,16,128]{2,0,1:T(8,128)(2,1)}, u32[]{:S(2)}, u32[]{:S(2)}) %all-to-all-start.1) | async-done | bytes 524320 | tf_op jit(solution)/shard_map/all_to_all | solution.py:149
  58.2 3.2 reshape.568
  70.0 3.6 copy.150
  73.6 3.1 reshape.573
  76.6 4.4 all-to-all-start.2
  81.8 13.8 %all-to-all-done.2 = bf16[256,8,128]{2,1,0:T(8,128)(2,1)} async-done(((bf16[256,8,128]{2,1,0:T(8,128)(2,1)}), bf16[256,8,128]{2,1,0:T(8,128)(2,1)}, u32[]{:S(2)}, u32[]{:S(2)}) %all-to-all-start.2) | async-done | bytes 524320 | tf_op jit(solution)/shard_map/all_to_all | solution.py:176
  97.6 4.2 all-to-all-start.3
  102.5 7.9 %all-to-all-done.3 = bf16[16,128,128]{2,1,0:T(8,128)(2,1)} async-done(((bf16[16,128,128]{2,1,0:T(8,128)(2,1)}), bf16[16,128,128]{2,1,0:T(8,128)(2,1)}, u32[]{:S(2)}, u32[]{:S(2)}) %all-to-all-start.3) | async-done | bytes 524320 | tf_op jit(solution)/shard_map/all_to_all | solution.py:175
  112.2 3.2 reshape.574
  118.7 3.9 copy.205
  122.6 4.8 reshape.621
  132.1 31.1 %all-gather.5.cloned.1.call-done = bf16[2048,512]{1,0:T(8,128)(2,1)} async-done(((bf16[1024,512]{1,0:T(8,128)(2,1)}), bf16[2048,512]{1,0:T(8,128)(2,1)}) %all-gather.5.cloned.1.call-update) | async-done | bytes 2097168 | tf_op jit(solution)/shard_map/all_gather | solution.py:193
  163.3 11.0 %multiply_convert_fusion = (bf16[2048,1024]{1,0:T(8,128)(2,1)}, f32[2048,1024]{1,0:T(8,128)}) fusion(f32[1024]{0:T(1024)S(1)} %dynamic_slice.3, bf16[2048,512]{1,0:T(8,128)(2,1)} %all-gather.5.cloned.1.call-done, bf16[512,1024]{1,0:T(8,128)(2,1)} %all-gather.7.cloned.1.call-done), kind=kOutput, calls=%fused_computation.10 | convolution fusion | flops 2168455168 | bytes 15732736 | tf_op jit(solution)/shard_map/dot_general | solution.py:194
  174.2 23.7 %all-gather.11.cloned.1.call-done = bf16[2048,512]{1,0:T(8,128)(2,1)} async-done(((bf16[1024,512]{1,0:T(8,128)(2,1)}), bf16[2048,512]{1,0:T(8,128)(2,1)}) %all-gather.11.cloned.1.call-update) | async-done | bytes 2097168 | tf_op jit(solution)/shard_map/all_gather | solution.py:207
  198.0 6.6 convolution_bitcast_fusion.2
  204.6 61.7 %reduce-scatter.11.cloned.1.call-done = f32[32,1024]{1,0:T(8,128)} async-done(((f32[512,1024]{1,0:T(8,128)}), f32[32,1024]{1,0:T(8,128)}) %reduce-scatter.11.cloned.1.call-update) | async-done | bytes 131088 | tf_op jit(solution)/shard_map/reduce_scatter | solution.py:225
  268.3 37.8 %all-gather.9.cloned.1.call-done = bf16[512,1024]{1,0:T(8,128)(2,1)} async-done(((bf16[32,1024]{1,0:T(8,128)(2,1)}), bf16[512,1024]{1,0:T(8,128)(2,1)}) %all-gather.9.cloned.1.call-update) | async-done | bytes 1048592 | tf_op jit(solution)/shard_map/all_gather | solution.py:190
  306.1 10.8 %convert_reduce_fusion = (f32[1024]{0:T(1024)}, bf16[2048,1024]{1,0:T(8,128)(2,1)S(1)}) fusion(f32[2048,1024]{1,0:T(8,128)} %get-tuple-element.79, f32[1024]{0:T(1024)} %copy-done.66, bf16[2048,512]{1,0:T(8,128)(2,1)} %all-gather.11.cloned.1.call-done, bf16[512,1024]{1,0:T(8,128)(2,1)} %all-gather.9.cloned.1.call-done), kind=kOutput, calls=%fused_computation.9 | convolution fusion | flops 2195717120 | bytes 15736832 | tf_op jit(solution)/shard_map/dot_general | solution.py:208
  318.9 3.8 convolution_convert_fusion
  322.7 30.9 %reduce-scatter.7.cloned.1.call-done = bf16[1024,512]{1,0:T(8,128)(2,1)} async-done(((bf16[2048,512]{1,0:T(8,128)(2,1)}), bf16[1024,512]{1,0:T(8,128)(2,1)}) %reduce-scatter.7.cloned.1.call-update) | async-done | bytes 1048592 | tf_op jit(solution)/shard_map/reduce_scatter | solution.py:217
  353.7 4.1 fusion.14
  359.9 3.9 reshape.622
  363.8 3.0 copy.158
  366.8 2.3 fusion.24
  371.2 3.3 reshape.623
  374.5 5.7 all-to-all-start.4
  380.2 6.5 fusion.101
  386.8 7.9 %all-to-all-done.4 = bf16[8,256,128]{2,0,1:T(8,128)(2,1)} async-done(((bf16[8,256,128]{2,0,1:T(8,128)(2,1)}), bf16[8,256,128]{2,0,1:T(8,128)(2,1)}, u32[]{:S(2)}, u32[]{:S(2)}) %all-to-all-start.4) | async-done | bytes 524320 | tf_op jit(solution)/shard_map/all_to_all | solution.py:241
  396.0 10.8 %all_to_all.132 = bf16[128,16,128]{2,0,1:T(8,128)(2,1)S(1)} all-to-all(bf16[128,16,128]{2,0,1:T(8,128)(2,1)S(1)} %copy.163), channel_id=1, replica_groups=mesh['sp'=16,'tp'=2] {'tp'}, dimensions={1} | all-to-all | bytes 1048576 | tf_op jit(solution)/shard_map/all_to_all | solution.py:240
  408.0 3.2 reshape.582
  418.7 6.2 convolution_convert_fusion.1
  429.3 3.6 copy.170
  432.9 3.1 reshape.586
  436.0 4.7 all-to-all-start.6
  441.6 9.8 %reduce-scatter.9.cloned.1.call-done = f32[32,1024]{1,0:T(8,128)} async-done(((f32[512,1024]{1,0:T(8,128)}), f32[32,1024]{1,0:T(8,128)}) %reduce-scatter.9.cloned.1.call-update) | async-done | bytes 131088 | tf_op jit(solution)/shard_map/reduce_scatter | solution.py:224
  458.3 4.2 all-to-all-start.7
  462.5 125.6 %all-reduce.2.cloned.1.call-done = f32[2,8,2,64,64]{4,3,2,1,0:T(8,128)} async-done(((f32[2,8,2,64,64]{4,3,2,1,0:T(8,128)}), f32[2,8,2,64,64]{4,3,2,1,0:T(8,128)}) %all-reduce.2.cloned.1.call-update) | async-done | bytes 524304 | tf_op jit(solution)/shard_map/psum | solution.py:302
  588.2 4.4 multiply_add_fusion
  594.5 3.3 reshape.587
  599.3 2.5 multiply_reduce_fusion
  601.9 3.8 copy.216
  605.9 5.0 reshape.624
  611.1 39.3 %psum.15 = f32[13,512]{1,0:T(8,128)S(1)} all-reduce(f32[13,512]{1,0:T(8,128)S(1)} %concatenate.33), channel_id=1, replica_groups=mesh['sp'=16,'tp'=2] {'sp','tp'}, use_global_device_ids=true, to_apply=%region_23.24 | all-reduce | flops 6656 | bytes 53248 | tf_op jit(solution)/shard_map/psum | solution.py:302
  651.2 4.6 fusion.20
  (255 shorter events, 74.0 us)
Async XLA Ops:
  19.2 22.0 %all-to-all-start = ((bf16[8,256,128]{2,0,1:T(8,128)(2,1)}), bf16[8,256,128]{2,0,1:T(8,128)(2,1)}, u32[]{:S(2)}, u32[]{:S(2)}) async-start(bf16[8,256,128]{2,0,1:T(8,128)(2,1)} %reshape.620), calls=%async_computation | async-start | bytes 1048576 | tf_op jit(solution)/shard_map/all_to_all | solution.py:150
  27.3 16.0 %copy-start.57 = (f32[8]{0:T(128)}, f32[8]{0:T(128)S(1)}, u32[]{:S(2)}) copy-start(f32[8]{0:T(128)S(1)} %compare_convert_fusion) | copy-start | bytes 100
  43.3 12.8 %all-to-all-start.1 = ((bf16[128,16,128]{2,0,1:T(8,128)(2,1)}), bf16[128,16,128]{2,0,1:T(8,128)(2,1)}, u32[]{:S(2)}, u32[]{:S(2)}) async-start(bf16[128,16,128]{2,0,1:T(8,128)(2,1)} %copy.142), calls=%async_computation.1 | async-start | bytes 1048576 | tf_op jit(solution)/shard_map/all_to_all | solution.py:149
  48.1 14.6 %copy-start.36 = (bf16[32,128,1,2]{1,0,2,3:T(8,128)(2,1)}, bf16[32,128,1,2]{1,0,2,3:T(8,128)(2,1)S(1)}, u32[]{:S(2)}) copy-start(bf16[32,128,1,2]{1,0,2,3:T(8,128)(2,1)S(1)} %get-tuple-element.60) | copy-start | bytes 49156
  48.1 14.7 %copy-start.37 = (bf16[32,128,1,2]{1,0,2,3:T(8,128)(2,1)}, bf16[32,128,1,2]{1,0,2,3:T(8,128)(2,1)S(1)}, u32[]{:S(2)}) copy-start(bf16[32,128,1,2]{1,0,2,3:T(8,128)(2,1)S(1)} %get-tuple-element.63) | copy-start | bytes 49156
  76.6 19.0 %all-to-all-start.2 = ((bf16[256,8,128]{2,1,0:T(8,128)(2,1)}), bf16[256,8,128]{2,1,0:T(8,128)(2,1)}, u32[]{:S(2)}, u32[]{:S(2)}) async-start(bf16[256,8,128]{2,1,0:T(8,128)(2,1)} %reshape.573), calls=%async_computation.2 | async-start | bytes 1048576 | tf_op jit(solution)/shard_map/all_to_all | solution.py:176
  81.1 51.0 %all-gather.7.cloned.1.call-start = ((), (), s32[]{:S(2)}) async-start(), calls=%async_computation.13 | async-start | bytes 1114112 | tf_op jit(solution)/shard_map/all_gather | solution.py:189
  97.6 12.8 %all-to-all-start.3 = ((bf16[16,128,128]{2,1,0:T(8,128)(2,1)}), bf16[16,128,128]{2,1,0:T(8,128)(2,1)}, u32[]{:S(2)}, u32[]{:S(2)}) async-start(bf16[16,128,128]{2,1,0:T(8,128)(2,1)} %bitcast.311), calls=%async_computation.3 | async-start | bytes 1048576 | tf_op jit(solution)/shard_map/all_to_all | solution.py:175
  101.8 61.4 %all-gather.5.cloned.1.call-start = ((), (), s32[]{:S(2)}) async-start(), calls=%async_computation.12 | async-start | bytes 3145728 | tf_op jit(solution)/shard_map/all_gather | solution.py:193
  102.4 14.4 %copy-start.26 = (bf16[128,1,32]{0,2,1:T(8,128)(2,1)}, bf16[128,1,32]{0,2,1:T(8,128)(2,1)S(1)}, u32[]{:S(2)}) copy-start(bf16[128,1,32]{0,2,1:T(8,128)(2,1)S(1)} %get-tuple-element.89) | copy-start | bytes 24580
  102.4 14.4 %copy-start.28 = (bf16[128,1,32]{0,2,1:T(8,128)(2,1)}, bf16[128,1,32]{0,2,1:T(8,128)(2,1)S(1)}, u32[]{:S(2)}) copy-start(bf16[128,1,32]{0,2,1:T(8,128)(2,1)S(1)} %get-tuple-element.90) | copy-start | bytes 24580
  131.2 66.7 %all-gather.11.cloned.1.call-start = ((), (), s32[]{:S(2)}) async-start(), calls=%async_computation.16 | async-start | bytes 3145728 | tf_op jit(solution)/shard_map/all_gather | solution.py:207
  132.0 134.4 %reduce-scatter.11.cloned.1.call-start = ((), (), s32[]{:S(2)}) async-start(), calls=%async_computation.19 | async-start | bytes 2228224 | tf_op jit(solution)/shard_map/reduce_scatter | solution.py:225
  132.1 42.2 %copy-start.66 = (f32[1024]{0:T(1024)}, f32[1024]{0:T(1024)S(1)}, u32[]{:S(2)}) copy-start(f32[1024]{0:T(1024)S(1)} %dynamic_slice.3) | copy-start | bytes 12292
  204.6 61.8 %copy-start.16 = (f32[32,1024]{1,0:T(8,128)S(1)}, f32[32,1024]{1,0:T(8,128)}, u32[]{:S(2)}) copy-start(f32[32,1024]{1,0:T(8,128)} %param.17) | copy-start | bytes 393220
  204.6 61.8 %copy-start.17 = (f32[32,1024]{1,0:T(8,128)S(1)}, f32[32,1024]{1,0:T(8,128)}, u32[]{:S(2)}) copy-start(f32[32,1024]{1,0:T(8,128)} %param.21) | copy-start | bytes 393220
  204.6 101.5 %all-gather.9.cloned.1.call-start = ((), (), s32[]{:S(2)}) async-start(), calls=%async_computation.14 | async-start | bytes 1114112 | tf_op jit(solution)/shard_map/all_gather | solution.py:190
  268.1 85.6 %reduce-scatter.7.cloned.1.call-start = ((), (), s32[]{:S(2)}) async-start(), calls=%async_computation.17 | async-start | bytes 3145728 | tf_op jit(solution)/shard_map/reduce_scatter | solution.py:217
  306.1 12.8 %copy-start.68 = (bf16[512,1024]{1,0:T(8,128)(2,1)S(1)}, bf16[512,1024]{1,0:T(8,128)(2,1)}, u32[]{:S(2)}) copy-start(bf16[512,1024]{1,0:T(8,128)(2,1)} %all-gather.7.cloned.1.call-done) | copy-start | bytes 3145732
  322.7 31.0 %copy-start.21 = (f32[1024]{0:T(1024)S(1)}, f32[1024]{0:T(1024)}, u32[]{:S(2)}) copy-start(f32[1024]{0:T(1024)} %copy-done.20) | copy-start | bytes 12292
  322.7 31.0 %copy-start.24 = (f32[1024]{0:T(1024)S(1)}, f32[1024]{0:T(1024)}, u32[]{:S(2)}) copy-start(f32[1024]{0:T(1024)} %copy-done.23) | copy-start | bytes 12292
  322.7 31.0 %copy-start.41 = (f32[1,512]{1,0:T(1,128)S(1)}, f32[1,512]{1,0:T(1,128)}, u32[]{:S(2)}) copy-start(f32[1,512]{1,0:T(1,128)} %get-tuple-element.53) | copy-start | bytes 6148
  374.5 20.2 %all-to-all-start.4 = ((bf16[8,256,128]{2,0,1:T(8,128)(2,1)}), bf16[8,256,128]{2,0,1:T(8,128)(2,1)}, u32[]{:S(2)}, u32[]{:S(2)}) async-start(bf16[8,256,128]{2,0,1:T(8,128)(2,1)} %reshape.623), calls=%async_computation.6 | async-start | bytes 1048576 | tf_op jit(solution)/shard_map/all_to_all | solution.py:241
  380.2 71.3 %reduce-scatter.9.cloned.1.call-start = ((), (), s32[]{:S(2)}) async-start(), calls=%async_computation.18 | async-start | bytes 2228224 | tf_op jit(solution)/shard_map/reduce_scatter | solution.py:224
  386.8 201.4 %all-reduce.2.cloned.1.call-start = ((), (), s32[]{:S(2)}) async-start(), calls=%async_computation.20 | async-start | bytes 2097152 | tf_op jit(solution)/shard_map/psum | solution.py:302
  418.6 232.5 %reduce-scatter.5.cloned.1.call-start = ((), (), s32[]{:S(2)}) async-start(), calls=%async_computation.15 | async-start | bytes 3145728 | tf_op jit(solution)/shard_map/reduce_scatter | solution.py:197
  429.3 11.4 %copy-start.14 = (f32[32,1024]{1,0:T(8,128)S(1)}, f32[32,1024]{1,0:T(8,128)}, u32[]{:S(2)}) copy-start(f32[32,1024]{1,0:T(8,128)} %param.25) | copy-start | bytes 393220
  429.3 12.1 %copy-start.65 = (f32[1024]{0:T(1024)S(1)}, f32[1024]{0:T(1024)}, u32[]{:S(2)}) copy-start(f32[1024]{0:T(1024)} %get-tuple-element.81) | copy-start | bytes 12292
  429.3 22.2 %copy-start.9 = (f32[32,1024]{1,0:T(8,128)S(1)}, f32[32,1024]{1,0:T(8,128)}, u32[]{:S(2)}) copy-start(f32[32,1024]{1,0:T(8,128)} %param.16) | copy-start | bytes 393220
  432.9 21.9 %copy-start.69 = (f32[2,64]{1,0:T(2,128)S(1)}, f32[2,64]{1,0:T(2,128)}, u32[]{:S(2)}) copy-start(f32[2,64]{1,0:T(2,128)} %get-tuple-element.83) | copy-start | bytes 1540
  432.9 21.9 %copy-start.67 = (f32[128]{0:T(128)S(1)}, f32[128]{0:T(128)}, u32[]{:S(2)}) copy-start(f32[128]{0:T(128)} %get-tuple-element.85) | copy-start | bytes 1540
  432.9 21.9 %copy-start.59 = (f32[8]{0:T(128)S(1)}, f32[8]{0:T(128)}, u32[]{:S(2)}) copy-start(f32[8]{0:T(128)} %copy-done.57) | copy-start | bytes 100
  436.0 20.3 %all-to-all-start.6 = ((bf16[256,8,128]{2,1,0:T(8,128)(2,1)}), bf16[256,8,128]{2,1,0:T(8,128)(2,1)}, u32[]{:S(2)}, u32[]{:S(2)}) async-start(bf16[256,8,128]{2,1,0:T(8,128)(2,1)} %reshape.586), calls=%async_computation.8 | async-start | bytes 1048576 | tf_op jit(solution)/shard_map/all_to_all | solution.py:269
  453.1 139.5 %copy-start.7 = (f32[32,1024]{1,0:T(8,128)}, f32[32,1024]{1,0:T(8,128)S(1)}, u32[]{:S(2)}) copy-start(f32[32,1024]{1,0:T(8,128)S(1)} %get-tuple-element.30) | copy-start | bytes 393220
  458.3 134.3 %all-to-all-start.7 = ((bf16[16,128,128]{2,1,0:T(8,128)(2,1)}), bf16[16,128,128]{2,1,0:T(8,128)(2,1)}, u32[]{:S(2)}, u32[]{:S(2)}) async-start(bf16[16,128,128]{2,1,0:T(8,128)(2,1)} %bitcast.310), calls=%async_computation.9 | async-start | bytes 1048576 | tf_op jit(solution)/shard_map/all_to_all | solution.py:268
  605.8 44.6 %copy-start.19 = (f32[13,512]{1,0:T(8,128)S(1)}, f32[13,512]{1,0:T(8,128)}, u32[]{:S(2)}) copy-start(f32[13,512]{1,0:T(8,128)} %param.19) | copy-start | bytes 79876
  605.8 44.6 %copy-start.51 = (f32[13,512]{1,0:T(8,128)S(1)}, f32[13,512]{1,0:T(8,128)}, u32[]{:S(2)}) copy-start(f32[13,512]{1,0:T(8,128)} %param.27) | copy-start | bytes 79876
  605.8 44.6 %copy-start.52 = (f32[13,512]{1,0:T(8,128)S(1)}, f32[13,512]{1,0:T(8,128)}, u32[]{:S(2)}) copy-start(f32[13,512]{1,0:T(8,128)} %param.23) | copy-start | bytes 79876
  605.8 45.3 %copy-start.2 = (f32[1024,512]{1,0:T(8,128)S(1)}, f32[1024,512]{1,0:T(8,128)}, u32[]{:S(2)}) copy-start(f32[1024,512]{1,0:T(8,128)} %reshape.621) | copy-start | bytes 6291460
  605.8 45.3 %copy-start.22 = (f32[1024]{0:T(1024)S(1)}, f32[1024]{0:T(1024)}, u32[]{:S(2)}) copy-start(f32[1024]{0:T(1024)} %copy-done.20) | copy-start | bytes 12292
  605.8 45.3 %copy-start.25 = (f32[1024]{0:T(1024)S(1)}, f32[1024]{0:T(1024)}, u32[]{:S(2)}) copy-start(f32[1024]{0:T(1024)} %copy-done.23) | copy-start | bytes 12292
  605.8 45.3 %copy-start.42 = (f32[1,512]{1,0:T(1,128)S(1)}, f32[1,512]{1,0:T(1,128)}, u32[]{:S(2)}) copy-start(f32[1,512]{1,0:T(1,128)} %get-tuple-element.53) | copy-start | bytes 6148
  605.9 45.3 %copy-start.48 = (f32[1024]{0:T(1024)S(1)}, f32[1024]{0:T(1024)}, u32[]{:S(2)}) copy-start(f32[1024]{0:T(1024)} %copy-done.47) | copy-start | bytes 12292
  605.9 45.3 %copy-start.50 = (f32[1024]{0:T(1024)S(1)}, f32[1024]{0:T(1024)}, u32[]{:S(2)}) copy-start(f32[1024]{0:T(1024)} %copy-done.49) | copy-start | bytes 12292
  605.9 45.3 %copy-start.54 = (f32[1024]{0:T(1024)S(1)}, f32[1024]{0:T(1024)}, u32[]{:S(2)}) copy-start(f32[1024]{0:T(1024)} %get-tuple-element.65) | copy-start | bytes 12292
  605.9 45.3 %copy-start.55 = (f32[1024]{0:T(1024)S(1)}, f32[1024]{0:T(1024)}, u32[]{:S(2)}) copy-start(f32[1024]{0:T(1024)} %get-tuple-element.67) | copy-start | bytes 12292
  605.9 45.3 %copy-start.63 = (f32[1,512]{1,0:T(1,128)S(1)}, f32[1,512]{1,0:T(1,128)}, u32[]{:S(2)}) copy-start(f32[1,512]{1,0:T(1,128)} %get-tuple-element.51) | copy-start | bytes 6148
  605.9 45.3 %copy-start.64 = (f32[1,512]{1,0:T(1,128)S(1)}, f32[1,512]{1,0:T(1,128)}, u32[]{:S(2)}) copy-start(f32[1,512]{1,0:T(1,128)} %get-tuple-element.56) | copy-start | bytes 6148
  (39 other events, 143.7 us)
Sparse Core Ops, SparseCore 0:
  84.7 38.2 all-gather.6
  131.4 31.8 all-gather.4
  164.8 33.1 all-gather.10
  204.7 61.5 reduce-scatter.10
  269.1 36.8 all-gather.8
  322.8 30.7 reduce-scatter.6
  386.9 64.4 reduce-scatter.8
  458.0 130.1 all-reduce.1
  590.4 31.3 reduce-scatter.4
where the time goes:
time: 673 us; the launch traced here: 663 us
  waiting for transfers between devices  371 us (55%)
  local copies, waits for them, and re-layouts  91.3 us (14%)
  matrix products  63.7 us (9%)
  blocking collectives  50.2 us (7%)
  starting transfers between devices  35.9 us (5%)
  other arithmetic  35.7 us (5%)
  between operations  15.3 us (2%)
    psum x1, waiting for transfers between devices, on_device(): lax.psum((mixer_local, vector_local), ('sp', 'tp'))  126 us
    reduce_scatter x1, waiting for transfers between devices, on_device(): lax.psum_scatter(grad_w_out, 'sp', scatter_dimension=0, tiled=True)  61.7 us
    psum x1, blocking collectives, on_device(): lax.psum((mixer_local, vector_local), ('sp', 'tp'))  39.3 us
    all_gather x1, waiting for transfers between devices, on_device(): lax.all_gather(w_out.astype(jnp.bfloat16), 'sp', axis=0, tiled=True)  37.8 us
    all_gather x1, waiting for transfers between devices, on_device(): rows_all = lax.all_gather(normed_two, 'tp', axis=0, tiled=True)  31.1 us
    reduce_scatter x1, waiting for transfers between devices, on_device(): lax.psum_scatter(contract(row_slice, w_in_full, 1, 1).astype(jnp.bfloat16...  30.9 us
    dot_general x8, matrix products, contract(): lax.dot_general(left, right, (((left_axis,), (right_axis,)), ((), ())), p...  26 us
    all_gather x1, waiting for transfers between devices, on_device(): cotangent_all = lax.all_gather(flat_cotangent, 'tp', axis=0, tiled=True)  23.7 us
  transfers between devices with their start and end apart: 16, of which 13 were waited for; matrix products, arithmetic and copies ran while one was open for 16% of the time, Pallas kernels for 0%

commit v1 on v0

v1 whole, which is shorter than its diff:
```python
import functools
import math

import jax
import jax.numpy as jnp
import ml_dtypes
import numpy as np
from jax import lax
from jax.experimental import pallas as pl
from jax.experimental.pallas import tpu as pltpu
from jax.sharding import PartitionSpec as P

MODES = 32
EPSILON = 1e-05
LEARNING_RATE = 0.05
MOMENTUM = 0.9
WEIGHT_DECAY = 0.0001
AVERAGE = 0.75
GELU_SCALE = math.sqrt(2.0 / math.pi)
GELU_CUBE = 0.044715
CHUNK = 512
ROWS = 256
BF16 = jnp.bfloat16
F32 = jnp.float32
AXES = ("sp", "tp")


def dft_tables(grid):
    positions = np.arange(grid)
    wave = np.arange(MODES)
    root = np.float32(1.0 / math.sqrt(grid))
    step = np.float32(2.0 * math.pi / grid)
    phase_w = (positions[:, None] * wave[None, :] % grid).astype(np.float32) * step
    factor = np.where(wave == 0, 1.0, 2.0).astype(np.float32)
    cos_w, sin_w = np.cos(phase_w) * root, np.sin(phase_w) * root
    forward_w = np.stack([cos_w, -sin_w], axis=1)
    inverse_w = np.stack([cos_w * factor, -sin_w * factor], axis=1)
    frequency = np.where(wave < MODES // 2, wave, wave - MODES)
    phase_h = (frequency[:, None] * positions[None, :] % grid).astype(np.float32) * step
    cos_h, sin_h = np.cos(phase_h) * root, np.sin(phase_h) * root
    forward_h = np.stack([np.stack([cos_h, -sin_h], -1), np.stack([sin_h, cos_h], -1)], -2)
    return [t.astype(ml_dtypes.bfloat16) for t in (forward_w, inverse_w, forward_h)]


def expanded_tables(grid, grid_rows, items):
    forward_w, inverse_w, forward_h = [t.astype(np.float32) for t in dft_tables(grid)]
    eye_r = np.eye(grid_rows, dtype=np.float32)
    wide_f = np.einsum("wek,rs->kresw", forward_w, eye_r).reshape(-1, grid_rows * grid)
    wide_i = np.einsum("wek,rs->kresw", inverse_w, eye_r).reshape(-1, grid_rows * grid)
    eye_i = np.eye(items, dtype=np.float32)
    high = np.einsum("mhef,ij->fimhje", forward_h, eye_i).reshape(2 * items * MODES, -1)
    ones = np.einsum("mhef,ek->kfm", forward_h.astype(np.float64), forward_w.astype(np.float64).sum(0))
    ones = np.repeat(ones[:, :, None], items, axis=2).reshape(MODES, -1).astype(np.float32)
    cast = [t.astype(ml_dtypes.bfloat16) for t in (wide_f, wide_i, high)]
    return cast[0], cast[1], cast[2], ones


def dot(left, right):
    return jnp.dot(left, right, preferred_element_type=F32)


def dot_nt(left, right):
    return lax.dot_general(left, right, (((1,), (1,)), ((), ())), preferred_element_type=F32)


def dot_tn(left, right):
    return lax.dot_general(left, right, (((0,), (0,)), ((), ())), preferred_element_type=F32)


def normalize(values):
    center = values - jnp.mean(values, axis=-1, keepdims=True)
    inverse = lax.rsqrt(jnp.mean(center * center, axis=-1, keepdims=True) + EPSILON)
    return center * inverse, inverse


def norm_back(upstream, normal, inverse, gain):
    scaled = upstream * gain
    centered = scaled - jnp.mean(scaled, axis=-1, keepdims=True)
    centered = centered - normal * jnp.mean(scaled * normal, axis=-1, keepdims=True)
    return centered * inverse


def gelu_pair(values):
    square = values * values
    bent = jnp.tanh(values * (GELU_SCALE + (GELU_SCALE * GELU_CUBE) * square))
    half = 0.5 + 0.5 * bent
    slope = half + (values * half) * (1.0 - bent) * (GELU_SCALE + (3.0 * GELU_SCALE * GELU_CUBE) * square)
    return values * half, slope


def gelu_value(values):
    square = values * values
    bent = jnp.tanh(values * (GELU_SCALE + (GELU_SCALE * GELU_CUBE) * square))
    return values * (0.5 + 0.5 * bent)


def gather_lanes(ref, groups):
    count = ref.shape[0] // groups
    width = ref.shape[2]
    parts = [ref[g * count : (g + 1) * count].reshape(count * ref.shape[1], width) for g in range(groups)]
    return parts[0] if groups == 1 else jnp.concatenate(parts, axis=1)


def scatter_lanes(ref, values, groups):
    count = ref.shape[0] // groups
    width = ref.shape[2]
    for g in range(groups):
        piece = values[:, g * width : (g + 1) * width]
        ref[g * count : (g + 1) * count] = piece.reshape(count, ref.shape[1], width)


def gather_modes(ref, modes):
    rows = ref.shape[1] // modes
    parts = [
        ref[:, k * rows : (k + 1) * rows, :].reshape(ref.shape[0] * rows, ref.shape[2]) for k in range(modes)
    ]
    return parts[0] if modes == 1 else jnp.concatenate(parts, axis=1)


def scatter_modes(ref, values, modes):
    rows = ref.shape[1] // modes
    width = ref.shape[2]
    for k in range(modes):
        piece = values[:, k * width : (k + 1) * width]
        ref[:, k * rows : (k + 1) * rows, :] = piece.reshape(ref.shape[0], rows, width)


def to_mix_rows(values, modes, width):
    half = values.shape[0] // 2
    parts = []
    for k in range(modes):
        piece = values[:, k * width : (k + 1) * width]
        parts.append(jnp.concatenate([piece[:half], piece[half:]], axis=1))
    return parts[0] if modes == 1 else jnp.concatenate(parts, axis=0)


def from_mix_rows(values, modes, width):
    half = values.shape[0] // modes
    parts = []
    for k in range(modes):
        piece = values[k * half : (k + 1) * half]
        parts.append(jnp.concatenate([piece[:, :width], piece[:, width:]], axis=0))
    return parts[0] if modes == 1 else jnp.concatenate(parts, axis=1)


def enter_kernel(groups, tokens_ref, table_ref, send_ref):
    normal, _ = normalize(tokens_ref[...].astype(F32))
    spectrum = dot(table_ref[...], normal.astype(BF16)).astype(BF16)
    scatter_lanes(send_ref, spectrum, groups)


def mix_kernel(
    modes, got_ref, high_ref, back_ref, mats_ref, bias_ref, gain_ref, shift_ref, ones_ref,
    send_ref, hat_ref, modal_ref, inner_ref, active_ref,
):
    width = got_ref.shape[2]
    hat = dot(high_ref[...], gather_modes(got_ref, modes))
    hat_ref[...] = hat
    pieces = []
    for k in range(modes):
        piece = hat[:, k * width : (k + 1) * width] * gain_ref[...]
        pieces.append(piece + ones_ref[:, k : k + 1] * shift_ref[...])
    modal = pieces[0] if modes == 1 else jnp.concatenate(pieces, axis=1)
    modal = to_mix_rows(modal.astype(BF16), modes, width)
    modal_ref[...] = modal
    inner = dot(modal, mats_ref[0]) + bias_ref[0:1, :]
    inner_ref[...] = inner
    active = gelu_value(inner).astype(BF16)
    active_ref[...] = active
    outer = (dot(active, mats_ref[1]) + bias_ref[1:2, :]).astype(BF16)
    gridded = dot(back_ref[...], from_mix_rows(outer, modes, width)).astype(BF16)
    scatter_modes(send_ref, gridded, modes)


def fold(grad, width, block):
    real = grad[:width, :width] + grad[width:, width:]
    imag = grad[:width, width:] - grad[width:, :width]
    out = []
    for part in (real, imag):
        if width == block:
            out.append(part)
        else:
            lane = lax.broadcasted_iota(jnp.int32, (block, width), 1)
            out.append(jnp.where(lane < block, part[:block], part[block:]))
    return jnp.concatenate(out, axis=0)


def unmix_kernel(
    modes, block, got_ref, high_ref, back_ref, mats_ref, ones_ref, hat_ref, modal_ref, inner_ref, active_ref,
    send_ref, small_ref,
):
    width = got_ref.shape[2]
    grad_outer = dot(high_ref[...], gather_modes(got_ref, modes)).astype(BF16)
    grad_outer = to_mix_rows(grad_outer, modes, width)
    _, slope = gelu_pair(inner_ref[...])
    grad_inner = (dot_nt(grad_outer, mats_ref[1]) * slope).astype(BF16)
    grad_modal = dot_nt(grad_inner, mats_ref[0]).astype(BF16)
    grad_modal = from_mix_rows(grad_modal, modes, width)
    spectrum = dot(back_ref[...], grad_modal).astype(BF16)
    scatter_modes(send_ref, spectrum, modes)
    rows = 2 * block
    small_ref[0:rows] = fold(dot_tn(modal_ref[...], grad_inner), width, block)
    small_ref[rows : 2 * rows] = fold(dot_tn(active_ref[...], grad_outer), width, block)
    bias_one = jnp.sum(grad_inner.astype(F32), axis=0, keepdims=True)
    bias_two = jnp.sum(grad_outer.astype(F32), axis=0, keepdims=True)
    gain = jnp.zeros((1, width), F32)
    shift = jnp.zeros((1, width), F32)
    for k in range(modes):
        lanes = slice(k * width, (k + 1) * width)
        upstream = grad_modal[:, lanes].astype(F32)
        gain = gain + jnp.sum(upstream * hat_ref[:, lanes], axis=0, keepdims=True)
        shift = shift + jnp.sum(upstream * ones_ref[:, k : k + 1], axis=0, keepdims=True)
    tail = [bias_one[:, :width], bias_one[:, width:], bias_two[:, :width], bias_two[:, width:], gain, shift]
    tail.append(jnp.zeros((2, width), F32))
    small_ref[2 * rows : 2 * rows + 8] = jnp.concatenate(tail, axis=0)


def mlp_kernel(
    groups, w_index, in_index, out_index,
    got_ref, tokens_ref, cotangent_ref, weights_ref, vectors_ref, bias_ref, wide_ref, wide_t_ref,
    output_ref, middle_ref, send_ref, grad_in_ref, grad_out_ref, small_ref,
    normed, normed_t, cotangent_t, normal, spread, total, grad_total, w_in, w_out, active, grad_hidden, grad_bias,
):
    step = pl.program_id(0)
    tokens = tokens_ref.shape[0]
    blocks = w_in.shape[0] // weights_ref.shape[2]
    block_rows = weights_ref.shape[2]
    per_half = weights_ref.shape[3] // CHUNK
    row_blocks = [slice(r, r + ROWS) for r in range(0, tokens, ROWS)]

    @pl.when(step == 0)
    def _():
        spectrum = gather_lanes(got_ref, groups)
        bias_out = jnp.zeros((1, tokens_ref.shape[1]), F32)
        for rows in row_blocks:
            spatial = dot(wide_t_ref[rows, :], spectrum)
            middle = tokens_ref[rows, :].astype(F32) + spatial
            unit, inverse = normalize(middle)
            normal[rows, :] = unit
            spread[rows, :] = inverse
            scaled = (unit * vectors_ref[2:3, :] + vectors_ref[3:4, :]).astype(BF16)
            normed[rows, :] = scaled
            normed_t[:, rows] = scaled.T
            total[rows, :] = middle + vectors_ref[4:5, :]
            upstream = cotangent_ref[rows, :]
            cotangent_t[:, rows] = upstream.T
            bias_out = bias_out + jnp.sum(upstream.astype(F32), axis=0, keepdims=True)
        small_ref[2:3, :] = bias_out
        small_ref[7:8, :] = jnp.zeros_like(bias_out)

    half = step // per_half
    columns = pl.ds(pl.multiple_of((step % per_half) * CHUNK, CHUNK), CHUNK)
    for j in range(blocks):
        rows = slice(j * block_rows, (j + 1) * block_rows)
        source = w_index[half * blocks + j]
        w_in[rows, :] = weights_ref[source, 0, :, columns]
        w_out[rows, :] = weights_ref[source, 1, :, columns]
    bias = bias_ref[pl.ds(step, 1), :]
    bias_grad = jnp.zeros((1, CHUNK), F32)
    for rows in row_blocks:
        hidden = dot(normed[rows, :], w_in[...]) + bias
        value, slope = gelu_pair(hidden)
        value = value.astype(BF16)
        active[rows, :] = value
        back = (dot(cotangent_ref[rows, :], w_out[...]) * slope).astype(BF16)
        grad_hidden[rows, :] = back
        bias_grad = bias_grad + jnp.sum(back.astype(F32), axis=0, keepdims=True)
        total[rows, :] += dot_nt(value, w_out[...])
        first = dot_nt(back, w_in[...])
        grad_total[rows, :] = jnp.where(step == 0, first, grad_total[rows, :] + first)
    grad_bias[pl.ds(step, 1), :] = bias_grad
    for grad, target, index in (
        (dot(normed_t[...], grad_hidden[...]), grad_in_ref, in_index),
        (dot(cotangent_t[...], active[...]), grad_out_ref, out_index),
    ):
        grad = grad.astype(BF16)
        for j in range(blocks):
            target[index[half * blocks + j], :, columns] = grad[j * block_rows : (j + 1) * block_rows]

    @pl.when(step == pl.num_programs(0) - 1)
    def _():
        gain = jnp.zeros((1, tokens_ref.shape[1]), F32)
        shift = jnp.zeros((1, tokens_ref.shape[1]), F32)
        for rows in row_blocks:
            upstream = grad_total[rows, :]
            unit = normal[rows, :]
            gain = gain + jnp.sum(upstream * unit, axis=0, keepdims=True)
            shift = shift + jnp.sum(upstream, axis=0, keepdims=True)
            back = norm_back(upstream, unit, spread[rows, :], vectors_ref[2:3, :])
            middle = cotangent_ref[rows, :].astype(F32) + back
            middle_ref[rows, :] = middle
            normed[rows, :] = middle.astype(BF16)
            output_ref[rows, :] = total[rows, :].astype(BF16)
        small_ref[0:1, :] = gain
        small_ref[1:2, :] = shift
        small_ref[3:7, :] = grad_bias[...]
        spectrum = dot(wide_ref[...], normed[...]).astype(BF16)
        scatter_lanes(send_ref, spectrum, groups)


def leave_kernel(groups, got_ref, tokens_ref, middle_ref, vectors_ref, table_ref, out_ref):
    spectrum = gather_lanes(got_ref, groups)
    for start in range(0, tokens_ref.shape[0], ROWS):
        rows = slice(start, start + ROWS)
        upstream = dot(table_ref[rows, :], spectrum)
        unit, inverse = normalize(tokens_ref[rows, :].astype(F32))
        back = norm_back(upstream, unit, inverse, vectors_ref[0:1, :])
        out_ref[rows, :] = (middle_ref[rows, :] + back).astype(BF16)


def update(weight, gradient, moment, average, decay_rate):
    step_grad = gradient + decay_rate * weight
    new_moment = MOMENTUM * moment + step_grad
    new_weight = weight - LEARNING_RATE * (step_grad + MOMENTUM * new_moment)
    new_average = AVERAGE * average + (1.0 - AVERAGE) * new_weight
    return (new_weight, new_moment, new_average)


def call(body, outs, *args, scratch=(), vmem=32, grid=None, prefetch=0, flops=0):
    params = pltpu.CompilerParams(vmem_limit_bytes=vmem << 20)
    whole = pl.BlockSpec(memory_space=pltpu.VMEM)
    outs = [jax.ShapeDtypeStruct(s, d) for s, d in outs]
    size = sum(math.prod(a.shape) * a.dtype.itemsize for a in list(args) + outs)
    return pl.pallas_call(
        body,
        out_shape=outs,
        grid_spec=pltpu.PrefetchScalarGridSpec(
            num_scalar_prefetch=prefetch,
            grid=(1,) if grid is None else grid,
            in_specs=[whole] * (len(args) - prefetch),
            out_specs=[whole] * len(outs),
            scratch_shapes=list(scratch),
        ),
        compiler_params=params,
        cost_estimate=pl.CostEstimate(flops=flops, bytes_accessed=size, transcendentals=0),
    )(*args)


def on_device(
    tokens, cotangent, w_in, w_out, mixer_weights, vectors, w_in_moment, w_out_moment, mixer_moment, vectors_moment,
    w_in_average, w_out_average, mixer_average, vectors_average,
):
    sp_count, tp_count = lax.axis_size("sp"), lax.axis_size("tp")
    devices = sp_count * tp_count
    grid_rows, grid, width = tokens.shape
    local = grid_rows * grid
    items = grid_rows * devices // grid
    block_count, block = mixer_weights.shape[1], mixer_weights.shape[3]
    hidden = w_in.shape[1] * tp_count
    model = w_in.shape[0] * sp_count
    lanes = 2 * block if devices * 2 * block <= MODES * width else block
    groups = width // lanes
    per_group = devices // groups
    modes = MODES // per_group
    joined = lanes // block
    scale = 1.0 / math.sqrt(local * devices)
    wide_f, wide_i, high, ones = expanded_tables(grid, grid_rows, items)
    me = lax.axis_index("sp") * tp_count + lax.axis_index("tp")
    group = me // per_group
    exchange = functools.partial(lax.all_to_all, axis_name=AXES, split_axis=0, concat_axis=0, tiled=True)
    chunk = (devices, modes * grid_rows * 2, lanes)
    rows_all = tokens.reshape(local, width)
    upstream_all = cotangent.reshape(local, width)
    shard_rows, shard_columns = w_in.shape
    near = devices == 32 and per_group == 8 and shard_rows % 16 == 0

    pair = jnp.stack([w_in.astype(BF16), w_out.astype(BF16)])
    if near:
        weights = lax.all_gather(pair, AXES)
        row_block = jnp.arange(sp_count, dtype=jnp.int32)
        half = jnp.arange(tp_count, dtype=jnp.int32)
        owner = row_block[None, :] * tp_count + half[:, None]
        w_index = owner.reshape(-1)
        offset = owner ^ me
        bits = [(offset >> b) & 1 for b in range(5)]
        far = bits[4] * 2 + bits[3]
        in_index = (((bits[1] * 2 + bits[0]) * 2 + bits[2]) * 4 + far).reshape(-1)
        out_index = (((bits[1] * 2 + bits[2]) * 2 + bits[0]) * 4 + far).reshape(-1)
    else:
        weights = lax.all_gather(pair, "sp", axis=1, tiled=True)
        weights = lax.all_gather(weights, "tp")
        w_index = in_index = out_index = jnp.arange(tp_count, dtype=jnp.int32)
    w_blocks = weights.shape[2]

    own_mixer = lax.dynamic_slice_in_dim(mixer_weights, group * joined, joined, 1).astype(BF16)
    eye = jnp.eye(joined, dtype=BF16)
    real = jnp.einsum("lbio,bc->lbico", own_mixer[:, :, 0], eye).reshape(2, lanes, lanes)
    imag = jnp.einsum("lbio,bc->lbico", own_mixer[:, :, 1], eye).reshape(2, lanes, lanes)
    mats = jnp.concatenate(
        [jnp.concatenate([real, imag], axis=2), jnp.concatenate([-imag, real], axis=2)], axis=1
    )
    own_bias = lax.dynamic_slice_in_dim(
        vectors[9:13].reshape(2, block_count, 2, block), group * joined, joined, 1
    )
    own_bias = jnp.swapaxes(own_bias, 1, 2).reshape(2, 2 * lanes)
    own_gain = lax.dynamic_slice_in_dim(vectors[0:1], group * lanes, lanes, 1)
    own_shift = lax.dynamic_slice_in_dim(vectors[1:2], group * lanes, lanes, 1)
    ones = jnp.asarray(np.swapaxes(ones.reshape(per_group, modes, -1), 1, 2))
    own_ones = lax.dynamic_index_in_dim(ones, me % per_group, 0, keepdims=False)

    wide_f, wide_f_t = jnp.asarray(wide_f), jnp.asarray(wide_f.T)
    wide_i, wide_i_t = jnp.asarray(wide_i), jnp.asarray(wide_i.T)
    high, high_t = jnp.asarray(high), jnp.asarray(high.T)
    wide_flops = 2 * wide_f.shape[0] * wide_f.shape[1] * width
    (sent,) = call(
        functools.partial(enter_kernel, groups), [(chunk, BF16)], rows_all, wide_f, flops=wide_flops
    )
    got = exchange(sent)
    half_rows = items * MODES
    sent, hat, modal, inner, active = call(
        functools.partial(mix_kernel, modes),
        [
            (chunk, BF16),
            ((2 * half_rows, modes * lanes), F32),
            ((modes * half_rows, 2 * lanes), BF16),
            ((modes * half_rows, 2 * lanes), F32),
            ((modes * half_rows, 2 * lanes), BF16),
        ],
        got, high, high_t, mats, own_bias, own_gain, own_shift, own_ones,
    )
    got = exchange(sent)
    steps = hidden // CHUNK
    blocks = model // w_blocks
    grad_shape = (tp_count * blocks, w_blocks, hidden // tp_count)
    output, middle, sent, grad_in, grad_out, mlp_small = call(
        functools.partial(mlp_kernel, groups),
        [
            ((local, width), BF16),
            ((local, width), F32),
            (chunk, BF16),
            (grad_shape, BF16),
            (grad_shape, BF16),
            ((8, width), F32),
        ],
        w_index, in_index, out_index,
        got, rows_all, upstream_all, weights, vectors, vectors[5:9].reshape(steps, CHUNK), wide_i, wide_i_t,
        scratch=[
            pltpu.VMEM((local, width), BF16),
            pltpu.VMEM((width, local), BF16),
            pltpu.VMEM((width, local), BF16),
            pltpu.VMEM((local, width), F32),
            pltpu.VMEM((local, 1), F32),
            pltpu.VMEM((local, width), F32),
            pltpu.VMEM((local, width), F32),
            pltpu.VMEM((model, CHUNK), BF16),
            pltpu.VMEM((model, CHUNK), BF16),
            pltpu.VMEM((local, CHUNK), BF16),
            pltpu.VMEM((local, CHUNK), BF16),
            pltpu.VMEM((steps, CHUNK), F32),
        ],
        vmem=50, grid=(steps,), prefetch=3, flops=12 * local * width * hidden + 2 * wide_flops,
    )

    got = exchange(sent)
    small_rows = 4 * block + 8
    sent, mix_small = call(
        functools.partial(unmix_kernel, modes, block),
        [(chunk, BF16), ((small_rows, lanes), F32)],
        got, high, high_t, mats, own_ones, hat, modal, inner, active,
    )
    got = exchange(sent)
    (grad_tokens,) = call(
        functools.partial(leave_kernel, groups),
        [((local, width), BF16)],
        got, rows_all, middle, vectors, wide_f_t, flops=wide_flops,
    )

    def permute(values, mask):
        return lax.ppermute(values, AXES, [(d, d ^ mask) for d in range(devices)])

    if near:
        shard = (4, shard_rows, shard_columns)
        grad_in = grad_in.reshape((2, 2, 2) + shard)
        grad_out = grad_out.reshape((2, 2, 2) + shard)
        sums = []
        for grad, first, second in ((grad_in, 1, 4), (grad_out, 4, 1)):
            one = permute(grad[1], 2)
            two = permute((grad[0, 1].astype(F32) + one[1].astype(F32)).astype(BF16), first)
            three = grad[0, 0, 1].astype(F32) + one[0, 1].astype(F32) + two[1].astype(F32)
            three = permute(three.astype(BF16), second)
            total = grad[0, 0, 0].astype(F32) + one[0, 0].astype(F32) + two[0].astype(F32) + three.astype(F32)
            sums.append(total)
        both = jnp.stack(sums, axis=1)
        away = [permute(both[j].astype(BF16), 8 * j) for j in (1, 2, 3)]
        both = both[0] + away[0].astype(F32) + away[1].astype(F32) + away[2].astype(F32)
        grad_in, grad_out = both[0], both[1]
    else:
        grads = jnp.stack([grad_in, grad_out]).astype(F32)
        grads = lax.psum_scatter(grads, "tp", scatter_dimension=1, tiled=True)
        grads = lax.psum_scatter(grads, "sp", scatter_dimension=2, tiled=True)
        grad_in, grad_out = grads[0, 0], grads[1, 0]
    new_in = update(w_in, grad_in * scale, w_in_moment, w_in_average, WEIGHT_DECAY)
    new_out = update(w_out, grad_out * scale, w_out_moment, w_out_average, WEIGHT_DECAY)

    onehot = (jnp.arange(groups, dtype=jnp.int32) == group).astype(F32)
    mix_all, mlp_all = lax.psum((onehot[:, None, None] * mix_small[None], mlp_small), AXES)
    mixer_grad = mix_all[:, : 4 * block].reshape(groups, 2, 2, block, joined, block)
    mixer_grad = mixer_grad.transpose(1, 0, 4, 2, 3, 5).reshape(mixer_weights.shape)
    tail = mix_all[:, 4 * block :]
    bias_grad = tail[:, :4].reshape(groups, 2, 2, joined, block).transpose(1, 0, 3, 2, 4).reshape(4, width)
    vector_grad = jnp.concatenate(
        [
            tail[:, 4].reshape(1, width),
            tail[:, 5].reshape(1, width),
            mlp_all[:7],
            bias_grad,
        ],
        axis=0,
    )
    new_mix = update(mixer_weights, mixer_grad * scale, mixer_moment, mixer_average, WEIGHT_DECAY)
    new_vec = update(vectors, vector_grad * scale, vectors_moment, vectors_average, 0.0)
    shape = tokens.shape
    return (
        output.reshape(shape), grad_tokens.reshape(shape),
        new_in[0], new_out[0], new_mix[0], new_vec[0],
        new_in[1], new_out[1], new_mix[1], new_vec[1],
        new_in[2], new_out[2], new_mix[2], new_vec[2],
        new_in[0].astype(BF16), new_out[0].astype(BF16),
    )


def solution(mesh):
    rows, split, whole = P(AXES, None, None), P("sp", "tp"), P()
    state = (split, split, whole, whole)
    return jax.shard_map(
        on_device,
        mesh=mesh,
        in_specs=(rows, rows) + state * 3,
        out_specs=(rows, rows) + state * 3 + (split, split),
        check_vma=False,
    )
```

time: 673 us -> 349 us (0.52); the launches traced: 663 us -> 348 us
  waiting for transfers between devices: 371 us -> 195 us
  local copies, waits for them, and re-layouts: 91.3 us -> 15.4 us
  matrix products: 63.7 us -> 0 us
  Pallas kernels: 0 us -> 34.8 us
  other arithmetic: 35.7 us -> 18.8 us
  blocking collectives: 50.2 us -> 40.7 us
  starting transfers between devices: 35.9 us -> 28.6 us
    reduce_scatter x4 -> x0, waiting for transfers between devices: 102 us -> none  [the longest x1 61.7 us: on_device(): lax.psum_scatter(grad_w_out, 'sp', scatter_dimension=0, tiled=True)]
    all_gather x4 -> x1, waiting for transfers between devices: 92.7 us -> 19.1 us  [on_device(): weights = lax.all_gather(pair, AXES)]
    dot_general x20 -> x0, matrix products: 63.7 us -> none  [the longest x8 26 us: contract(): lax.dot_general(left, right, (((left_axis,), (right_axis,)), ((), ())), p...]
    reshape x22 -> x6, local copies, waits for them, and re-layouts: 56 us -> 0.58 us  [the longest x2 0.18 us: on_device(): tail[:, :4].reshape(groups, 2, 2, joined, block).transpose(1, 0, 3, 2, 4)]
    pallas_call x0 -> x5, Pallas kernels: none -> 34.8 us  [call(): pl.pallas_call(body, out_shape=outs, grid_spec=pltpu.PrefetchScalarGridSp...]
    all_to_all x7 -> x4, starting transfers between devices: 34.9 us -> 18.6 us  [on_device(): got = exchange(sent)]
    ppermute x0 -> x9, waiting for transfers between devices: none -> 16 us  [permute(): return lax.ppermute(values, AXES, [(d, d ^ mask) for d in range(devices)])]
    all_to_all x7 -> x4, waiting for transfers between devices: 49.2 us -> 33.6 us  [on_device(): got = exchange(sent)]
  transfers between devices with their start and end apart: 16 -> 15, of which waited for: 13 -> 9; matrix products, arithmetic and copies ran while one was open for 16% -> 7% of each run, Pallas kernels for 0% -> 1%
where the time goes in v1:
time: 349 us; the launch traced here: 348 us
  waiting for transfers between devices  195 us (56%)
  blocking collectives  40.7 us (12%)
  Pallas kernels  34.8 us (10%)
  starting transfers between devices  28.6 us (8%)
  other arithmetic  18.8 us (5%)
  local copies, waits for them, and re-layouts  15.4 us (4%)
  between operations  14.5 us (4%)
    psum x1, waiting for transfers between devices, on_device(): lax.psum((onehot[:, None, None] * mix_small[None], mlp_small), AXES)  126 us
    psum x1, blocking collectives, on_device(): lax.psum((onehot[:, None, None] * mix_small[None], mlp_small), AXES)  40.7 us
    pallas_call x5, Pallas kernels, call(): pl.pallas_call(body, out_shape=outs, grid_spec=pltpu.PrefetchScalarGridSp...  34.8 us
    all_to_all x4, waiting for transfers between devices, on_device(): got = exchange(sent)  33.6 us
    all_gather x1, waiting for transfers between devices, on_device(): weights = lax.all_gather(pair, AXES)  19.1 us
    all_to_all x4, starting transfers between devices, on_device(): got = exchange(sent)  18.6 us
    ppermute x9, waiting for transfers between devices, permute(): return lax.ppermute(values, AXES, [(d, d ^ mask) for d in range(devices)])  16 us
    ppermute x9, starting transfers between devices, permute(): return lax.ppermute(values, AXES, [(d, d ^ mask) for d in range(devices)])  9.75 us
  transfers between devices with their start and end apart: 15, of which 9 were waited for; matrix products, arithmetic and copies ran while one was open for 7% of the time, Pallas kernels for 1%

profile of v1, /device:TPU:0, one launch (start us, length us, event | category | flops | bytes accessed | tf_op | source)
XLA Modules:
  0.0 347.9 jit_solution(11224463174153181605)
XLA Ops:
  7.2 1.0 convert_bitcast_fusion
  8.9 1.2 copy-done
  10.1 1.2 copy-done.3
  11.4 1.9 shard_map.324
  13.3 7.3 %all-to-all-start = ((bf16[32,64,128]{2,1,0:T(8,128)(2,1)}), bf16[32,64,128]{2,1,0:T(8,128)(2,1)S(1)}, u32[]{:S(2)}, u32[]{:S(2)}) async-start(bf16[32,64,128]{2,1,0:T(8,128)(2,1)} %shard_map.324), calls=%async_computation | async-start | bytes 1048576 | tf_op jit(solution)/shard_map/all_to_all | solution.py:408
  20.8 1.1 dynamic-slice_convert_fusion
  22.5 0.9 dynamic-slice_bitcast_fusion.ones_ref
  23.4 14.9 %all-to-all-done.got_ref = bf16[32,64,128]{2,1,0:T(8,128)(2,1)S(1)} async-done(((bf16[32,64,128]{2,1,0:T(8,128)(2,1)}), bf16[32,64,128]{2,1,0:T(8,128)(2,1)S(1)}, u32[]{:S(2)}, u32[]{:S(2)}) %all-to-all-start) | async-done | bytes 524320 | tf_op jit(solution)/shard_map/all_to_all | solution.py:408
  38.4 1.6 shard_map.325
  40.0 3.6 %all-to-all-start.1 = ((bf16[32,64,128]{2,1,0:T(8,128)(2,1)}), bf16[32,64,128]{2,1,0:T(8,128)(2,1)S(1)}, u32[]{:S(2)}, u32[]{:S(2)}) async-start(bf16[32,64,128]{2,1,0:T(8,128)(2,1)} %get-tuple-element.29), calls=%async_computation.1 | async-start | bytes 1048576 | tf_op jit(solution)/shard_map/all_to_all | solution.py:421
  43.7 18.7 %all-to-all-done.1.got_ref = bf16[32,64,128]{2,1,0:T(8,128)(2,1)S(1)} async-done(((bf16[32,64,128]{2,1,0:T(8,128)(2,1)}), bf16[32,64,128]{2,1,0:T(8,128)(2,1)S(1)}, u32[]{:S(2)}, u32[]{:S(2)}) %all-to-all-start.1) | async-done | bytes 524320 | tf_op jit(solution)/shard_map/all_to_all | solution.py:421
  62.4 19.1 %all-gather.3.cloned.1.call-done = bf16[64,32,1024]{2,1,0:T(8,128)(2,1)} async-done(((bf16[2,32,1024]{2,1,0:T(8,128)(2,1)}), bf16[64,32,1024]{2,1,0:T(8,128)(2,1)}) %all-gather.3.cloned.1.call-update) | async-done | bytes 4194320 | tf_op jit(solution)/shard_map/all_gather | solution.py:369
  81.5 1.2 copy-done.8
  82.7 26.2 %shard_map.326 = (bf16[1024,512]{1,0:T(8,128)(2,1)}, f32[1024,512]{1,0:T(8,128)}, bf16[32,64,128]{2,1,0:T(8,128)(2,1)}, bf16[32,32,1024]{2,1,0:T(8,128)(2,1)}, b...) custom-call(s32[32]{0:T(128)S(1)} %add.176.w_index, s32[32]{0:T(128)S(1)} %get-tuple-element.71.in_index, ...), custom_call_target="tpu_custom_call" | custom-call | flops 13958643712 | bytes 16828800 | tf_op jit(solution)/shard_map/pallas_call | solution.py:324
  109.0 3.1 all-to-all-start.2
  112.1 2.4 slice.130
  114.8 1.1 slice.121
  116.1 40.7 %psum.15 = f32[8,512]{1,0:T(8,128)S(1)} all-reduce(f32[8,512]{1,0:T(8,128)S(1)} %get-tuple-element.41), channel_id=1, replica_groups=mesh['sp'=16,'tp'=2] {'sp','tp'}, use_global_device_ids=true, to_apply=%region_1.2 | all-reduce | flops 4096 | bytes 32768 | tf_op jit(solution)/shard_map/psum | solution.py:496
  156.8 1.6 shard_map.327
  158.4 4.6 %all-to-all-start.3 = ((bf16[32,64,128]{2,1,0:T(8,128)(2,1)}), bf16[32,64,128]{2,1,0:T(8,128)(2,1)}, u32[]{:S(2)}, u32[]{:S(2)}) async-start(bf16[32,64,128]{2,1,0:T(8,128)(2,1)} %get-tuple-element.36), calls=%async_computation.3 | async-start | bytes 1048576 | tf_op jit(solution)/shard_map/all_to_all | solution.py:461
  163.2 0.9 broadcast_multiply_fusion
  164.1 2.2 fusion.1
  166.3 1.7 collective-permute-start.4
  168.0 1.4 fusion.2
  169.4 1.5 collective-permute-start.1
  170.9 126.3 %all-reduce.2.cloned.1.call-done = f32[4,264,128]{2,1,0:T(8,128)} async-done(((f32[4,264,128]{2,1,0:T(8,128)}), f32[4,264,128]{2,1,0:T(8,128)}) %all-reduce.2.cloned.1.call-update) | async-done | bytes 540688 | tf_op jit(solution)/shard_map/psum | solution.py:496
  297.3 1.1 slice_multiply_fusion
  299.1 1.1 copy-done.10
  300.5 3.3 multiply_add_fusion
  303.8 1.2 fusion.3
  305.0 1.5 collective-permute-start.5
  306.6 0.8 slice_bitcast_fusion.22
  307.4 0.7 slice.178
  308.3 1.2 fusion.6
  309.6 0.9 collective-permute-start.2
  310.5 3.1 collective-permute-done.5
  313.6 1.3 fusion.5
  314.9 2.9 collective-permute-done.2
  317.8 1.3 fusion.8
  319.3 1.6 collective-permute-start.6
  320.9 1.5 collective-permute-start.8
  323.5 2.2 collective-permute-done.6
  325.7 2.9 collective-permute-done.8
  328.6 4.9 %collective-permute-done.7 = bf16[2,32,1024]{2,1,0:T(8,128)(2,1)S(1)} collective-permute-done((bf16[2,32,1024]{2,1,0:T(8,128)(2,1)S(1)}, bf16[2,32,1024]{2,1,0:T(8,128)(2,1)S(1)}, u32[]{:S(2)}, u32[]{:S(2)}) %collective-permute-start.7) | collective-permute-done | bytes 131104 | tf_op jit(solution)/shard_map/ppermute | solution.py:469
  333.6 0.8 fusion.19
  335.7 0.7 multiply_add_fusion.4
  336.4 1.2 copy-done.4
  337.6 3.5 shard_map.328
  (82 shorter events, 6.3 us)
Async XLA Ops:
  7.2 74.3 %all-gather.3.cloned.1.call-start = ((), (), s32[]{:S(2)}) async-start(), calls=%async_computation.5 | async-start | bytes 4325376 | tf_op jit(solution)/shard_map/all_gather | solution.py:369
  8.2 12.4 %copy-start.7 = (f32[13,512]{1,0:T(8,128)S(1)}, f32[13,512]{1,0:T(8,128)}, u32[]{:S(2)}) copy-start(f32[13,512]{1,0:T(8,128)} %vectors_ref.3) | copy-start | bytes 79876
  8.9 1.2 copy-start
  10.1 1.2 copy-start.3
  13.3 25.1 %copy-start.5 = (bf16[512,128]{1,0:T(8,128)(2,1)S(1)}, bf16[512,128]{1,0:T(8,128)(2,1)}, u32[]{:S(2)}) copy-start(bf16[512,128]{1,0:T(8,128)(2,1)} %constant.97.clone.back_ref) | copy-start | bytes 393220
  13.3 25.1 %copy-start.6 = (bf16[128,512]{1,0:T(8,128)(2,1)S(1)}, bf16[128,512]{1,0:T(8,128)(2,1)}, u32[]{:S(2)}) copy-start(bf16[128,512]{1,0:T(8,128)(2,1)} %constant.96.clone.high_ref) | copy-start | bytes 393220
  13.3 25.1 %all-to-all-start = ((bf16[32,64,128]{2,1,0:T(8,128)(2,1)}), bf16[32,64,128]{2,1,0:T(8,128)(2,1)S(1)}, u32[]{:S(2)}, u32[]{:S(2)}) async-start(bf16[32,64,128]{2,1,0:T(8,128)(2,1)} %shard_map.324), calls=%async_computation | async-start | bytes 1048576 | tf_op jit(solution)/shard_map/all_to_all | solution.py:408
  20.8 60.7 %copy-start.1 = (bf16[8,128,512]{2,1,0:T(8,128)(2,1)S(1)}, bf16[8,128,512]{2,1,0:T(8,128)(2,1)}, u32[]{:S(2)}) copy-start(bf16[8,128,512]{2,1,0:T(8,128)(2,1)} %param.21) | copy-start | bytes 3145732
  40.0 22.4 %all-to-all-start.1 = ((bf16[32,64,128]{2,1,0:T(8,128)(2,1)}), bf16[32,64,128]{2,1,0:T(8,128)(2,1)S(1)}, u32[]{:S(2)}, u32[]{:S(2)}) async-start(bf16[32,64,128]{2,1,0:T(8,128)(2,1)} %get-tuple-element.29), calls=%async_computation.1 | async-start | bytes 1048576 | tf_op jit(solution)/shard_map/all_to_all | solution.py:421
  81.5 1.2 copy-start.8
  109.0 47.8 %all-to-all-start.2 = ((bf16[32,64,128]{2,1,0:T(8,128)(2,1)}), bf16[32,64,128]{2,1,0:T(8,128)(2,1)S(1)}, u32[]{:S(2)}, u32[]{:S(2)}) async-start(bf16[32,64,128]{2,1,0:T(8,128)(2,1)} %get-tuple-element.31), calls=%async_computation.2 | async-start | bytes 1048576 | tf_op jit(solution)/shard_map/all_to_all | solution.py:454
  112.1 2.7 copy-start.9
  114.6 49.6 %collective-permute-start.3 = (bf16[2,2,4,32,1024]{4,3,2,1,0:T(8,128)(2,1)}, bf16[2,2,4,32,1024]{4,3,2,1,0:T(8,128)(2,1)}, u32[]{:S(2)}, u32[]{:S(2)}) collective-permute-start(bf16[2,2,4,32,1024]{4,3,2,1,0:T(8,128)(2,1)} %bitcast.28), channel_id=1, source_target_pairs={{0,2},{1,3},{2,0},{3,1},{4,6},{5,7},{6,4},{7,5},{8,10},{9,11},{10,... | collective-permute-start | bytes 3145736 | tf_op jit(solution)/shard_map/ppermute | solution.py:469
  115.9 52.1 %collective-permute-start = (bf16[2,2,4,32,1024]{4,3,2,1,0:T(8,128)(2,1)}, bf16[2,2,4,32,1024]{4,3,2,1,0:T(8,128)(2,1)}, u32[]{:S(2)}, u32[]{:S(2)}) collective-permute-start(bf16[2,2,4,32,1024]{4,3,2,1,0:T(8,128)(2,1)} %bitcast.17), channel_id=1, source_target_pairs={{0,2},{1,3},{2,0},{3,1},{4,6},{5,7},{6,4},{7,5},{8,10},{9,11},{10,... | collective-permute-start | bytes 3145736 | tf_op jit(solution)/shard_map/ppermute | solution.py:469
  158.4 178.0 %all-to-all-start.3 = ((bf16[32,64,128]{2,1,0:T(8,128)(2,1)}), bf16[32,64,128]{2,1,0:T(8,128)(2,1)}, u32[]{:S(2)}, u32[]{:S(2)}) async-start(bf16[32,64,128]{2,1,0:T(8,128)(2,1)} %get-tuple-element.36), calls=%async_computation.3 | async-start | bytes 1048576 | tf_op jit(solution)/shard_map/all_to_all | solution.py:461
  163.0 134.3 %all-reduce.2.cloned.1.call-start = ((), (), s32[]{:S(2)}) async-start(), calls=%async_computation.4 | async-start | bytes 1081344 | tf_op jit(solution)/shard_map/psum | solution.py:496
  166.3 137.5 %collective-permute-start.4 = (bf16[2,4,32,1024]{3,2,1,0:T(8,128)(2,1)}, bf16[2,4,32,1024]{3,2,1,0:T(8,128)(2,1)}, u32[]{:S(2)}, u32[]{:S(2)}) collective-permute-start(bf16[2,4,32,1024]{3,2,1,0:T(8,128)(2,1)} %fusion.1), channel_id=1, source_target_pairs={{0,4},{1,5},{2,6},{3,7},{4,0},{5,1},{6,2},{7,3},{8,12},{9,13},{10,... | collective-permute-start | bytes 1572872 | tf_op jit(solution)/shard_map/ppermute | solution.py:469
  169.4 138.9 %collective-permute-start.1 = (bf16[2,4,32,1024]{3,2,1,0:T(8,128)(2,1)S(1)}, bf16[2,4,32,1024]{3,2,1,0:T(8,128)(2,1)}, u32[]{:S(2)}, u32[]{:S(2)}) collective-permute-start(bf16[2,4,32,1024]{3,2,1,0:T(8,128)(2,1)S(1)} %fusion.2), channel_id=1, source_target_pairs={{0,1},{1,0},{2,3},{3,2},{4,5},{5,4},{6,7},{7,6},{8,9},{9,8},{10,11... | collective-permute-start | bytes 1572872 | tf_op jit(solution)/shard_map/ppermute | solution.py:469
  299.0 1.2 copy-start.10
  299.0 1.5 copy-start.11
  305.0 8.6 %collective-permute-start.5 = (bf16[4,32,1024]{2,1,0:T(8,128)(2,1)S(1)}, bf16[4,32,1024]{2,1,0:T(8,128)(2,1)S(1)}, u32[]{:S(2)}, u32[]{:S(2)}) collective-permute-start(bf16[4,32,1024]{2,1,0:T(8,128)(2,1)S(1)} %fusion.3), channel_id=1, source_target_pairs={{0,1},{1,0},{2,3},{3,2},{4,5},{5,4},{6,7},{7,6},{8,9},{9,8},{10,11... | collective-permute-start | bytes 786440 | tf_op jit(solution)/shard_map/ppermute | solution.py:469
  309.6 8.2 %collective-permute-start.2 = (bf16[4,32,1024]{2,1,0:T(8,128)(2,1)S(1)}, bf16[4,32,1024]{2,1,0:T(8,128)(2,1)S(1)}, u32[]{:S(2)}, u32[]{:S(2)}) collective-permute-start(bf16[4,32,1024]{2,1,0:T(8,128)(2,1)S(1)} %fusion.6), channel_id=1, source_target_pairs={{0,4},{1,5},{2,6},{3,7},{4,0},{5,1},{6,2},{7,3},{8,12},{9,13},{10,... | collective-permute-start | bytes 786440 | tf_op jit(solution)/shard_map/ppermute | solution.py:469
  314.9 7.9 %copy-start.20 = (f32[13,512]{1,0:T(8,128)S(1)}, f32[13,512]{1,0:T(8,128)}, u32[]{:S(2)}) copy-start(f32[13,512]{1,0:T(8,128)} %param.34) | copy-start | bytes 79876
  314.9 7.9 %copy-start.21 = (f32[13,512]{1,0:T(8,128)S(1)}, f32[13,512]{1,0:T(8,128)}, u32[]{:S(2)}) copy-start(f32[13,512]{1,0:T(8,128)} %param.30) | copy-start | bytes 79876
  319.1 14.4 %copy-start.12 = (f32[32,1024]{1,0:T(8,128)S(1)}, f32[32,1024]{1,0:T(8,128)}, u32[]{:S(2)}) copy-start(f32[32,1024]{1,0:T(8,128)} %param.24) | copy-start | bytes 393220
  319.1 14.4 %copy-start.13 = (f32[32,1024]{1,0:T(8,128)S(1)}, f32[32,1024]{1,0:T(8,128)}, u32[]{:S(2)}) copy-start(f32[32,1024]{1,0:T(8,128)} %param.23) | copy-start | bytes 393220
  319.1 14.4 %copy-start.18 = (f32[32,1024]{1,0:T(8,128)S(1)}, f32[32,1024]{1,0:T(8,128)}, u32[]{:S(2)}) copy-start(f32[32,1024]{1,0:T(8,128)} %param.28) | copy-start | bytes 393220
  319.1 14.4 %copy-start.19 = (f32[32,1024]{1,0:T(8,128)S(1)}, f32[32,1024]{1,0:T(8,128)}, u32[]{:S(2)}) copy-start(f32[32,1024]{1,0:T(8,128)} %param.27) | copy-start | bytes 393220
  319.2 15.8 %copy-start.16 = (f32[32,1024]{1,0:T(8,128)S(1)}, f32[32,1024]{1,0:T(8,128)}, u32[]{:S(2)}) copy-start(f32[32,1024]{1,0:T(8,128)} %param.32) | copy-start | bytes 393220
  319.2 16.5 %copy-start.17 = (f32[32,1024]{1,0:T(8,128)S(1)}, f32[32,1024]{1,0:T(8,128)}, u32[]{:S(2)}) copy-start(f32[32,1024]{1,0:T(8,128)} %param.31) | copy-start | bytes 393220
  319.2 17.1 %copy-start.2 = (f32[1024,512]{1,0:T(8,128)S(1)}, f32[1024,512]{1,0:T(8,128)}, u32[]{:S(2)}) copy-start(f32[1024,512]{1,0:T(8,128)} %get-tuple-element.37.middle_ref) | copy-start | bytes 6291460
  319.3 6.4 %collective-permute-start.6 = (bf16[2,32,1024]{2,1,0:T(8,128)(2,1)S(1)}, bf16[2,32,1024]{2,1,0:T(8,128)(2,1)S(1)}, u32[]{:S(2)}, u32[]{:S(2)}) collective-permute-start(bf16[2,32,1024]{2,1,0:T(8,128)(2,1)S(1)} %get-tuple-element.56), channel_id=1, source_target_pairs={{0,8},{1,9},{2,10},{3,11},{4,12},{5,13},{6,14},{7,15},{8,0},{9,1},... | collective-permute-start | bytes 393224 | tf_op jit(solution)/shard_map/ppermute | solution.py:469
  320.9 7.7 %collective-permute-start.8 = (bf16[2,32,1024]{2,1,0:T(8,128)(2,1)S(1)}, bf16[2,32,1024]{2,1,0:T(8,128)(2,1)S(1)}, u32[]{:S(2)}, u32[]{:S(2)}) collective-permute-start(bf16[2,32,1024]{2,1,0:T(8,128)(2,1)S(1)} %get-tuple-element.57), channel_id=1, source_target_pairs={{0,24},{1,25},{2,26},{3,27},{4,28},{5,29},{6,30},{7,31},{8,16},{9,... | collective-permute-start | bytes 393224 | tf_op jit(solution)/shard_map/ppermute | solution.py:469
  322.4 11.1 %collective-permute-start.7 = (bf16[2,32,1024]{2,1,0:T(8,128)(2,1)S(1)}, bf16[2,32,1024]{2,1,0:T(8,128)(2,1)S(1)}, u32[]{:S(2)}, u32[]{:S(2)}) collective-permute-start(bf16[2,32,1024]{2,1,0:T(8,128)(2,1)S(1)} %get-tuple-element.58), channel_id=1, source_target_pairs={{0,16},{1,17},{2,18},{3,19},{4,20},{5,21},{6,22},{7,23},{8,24},{9,... | collective-permute-start | bytes 393224 | tf_op jit(solution)/shard_map/ppermute | solution.py:469
  334.3 0.7 copy-start.14
  334.4 1.3 copy-start.15
  336.4 1.2 copy-start.4
Sparse Core Ops, SparseCore 0:
  11.6 69.8 all-gather.2
  169.6 127.5 all-reduce.1

commit v2 on v1

v2 whole, which is shorter than its diff:
```python
import functools
import math

import jax
import jax.numpy as jnp
import ml_dtypes
import numpy as np
from jax import lax
from jax.experimental import pallas as pl
from jax.experimental.pallas import tpu as pltpu
from jax.sharding import PartitionSpec as P

MODES = 32
EPSILON = 1e-05
LEARNING_RATE = 0.05
MOMENTUM = 0.9
WEIGHT_DECAY = 0.0001
AVERAGE = 0.75
GELU_SCALE = math.sqrt(2.0 / math.pi)
GELU_CUBE = 0.044715
CHUNK = 512
ROWS = 256
BF16 = jnp.bfloat16
F32 = jnp.float32
AXES = ("sp", "tp")
COST = 60 << 20


def dft_tables(grid):
    positions = np.arange(grid)
    wave = np.arange(MODES)
    root = np.float32(1.0 / math.sqrt(grid))
    step = np.float32(2.0 * math.pi / grid)
    phase_w = (positions[:, None] * wave[None, :] % grid).astype(np.float32) * step
    factor = np.where(wave == 0, 1.0, 2.0).astype(np.float32)
    cos_w, sin_w = np.cos(phase_w) * root, np.sin(phase_w) * root
    forward_w = np.stack([cos_w, -sin_w], axis=1)
    inverse_w = np.stack([cos_w * factor, -sin_w * factor], axis=1)
    frequency = np.where(wave < MODES // 2, wave, wave - MODES)
    phase_h = (frequency[:, None] * positions[None, :] % grid).astype(np.float32) * step
    cos_h, sin_h = np.cos(phase_h) * root, np.sin(phase_h) * root
    forward_h = np.stack([np.stack([cos_h, -sin_h], -1), np.stack([sin_h, cos_h], -1)], -2)
    return [t.astype(ml_dtypes.bfloat16) for t in (forward_w, inverse_w, forward_h)]


def expanded_tables(grid, grid_rows, items):
    forward_w, inverse_w, forward_h = [t.astype(np.float32) for t in dft_tables(grid)]
    eye_r = np.eye(grid_rows, dtype=np.float32)
    wide_f = np.einsum("wek,rs->kresw", forward_w, eye_r).reshape(-1, grid_rows * grid)
    wide_i = np.einsum("wek,rs->kresw", inverse_w, eye_r).reshape(-1, grid_rows * grid)
    eye_i = np.eye(items, dtype=np.float32)
    high = np.einsum("mhef,ij->fimhje", forward_h, eye_i).reshape(2 * items * MODES, -1)
    ones = np.einsum("mhef,ek->kfm", forward_h.astype(np.float64), forward_w.astype(np.float64).sum(0))
    ones = np.repeat(ones[:, :, None], items, axis=2).reshape(MODES, -1).astype(np.float32)
    cast = [t.astype(ml_dtypes.bfloat16) for t in (wide_f, wide_i, high)]
    return cast[0], cast[1], cast[2], ones


def dot(left, right):
    return jnp.dot(left, right, preferred_element_type=F32)


def dot_nt(left, right):
    return lax.dot_general(left, right, (((1,), (1,)), ((), ())), preferred_element_type=F32)


def dot_tn(left, right):
    return lax.dot_general(left, right, (((0,), (0,)), ((), ())), preferred_element_type=F32)


def normalize(values):
    center = values - jnp.mean(values, axis=-1, keepdims=True)
    inverse = lax.rsqrt(jnp.mean(center * center, axis=-1, keepdims=True) + EPSILON)
    return center * inverse, inverse


def norm_back(upstream, normal, inverse, gain):
    scaled = upstream * gain
    centered = scaled - jnp.mean(scaled, axis=-1, keepdims=True)
    centered = centered - normal * jnp.mean(scaled * normal, axis=-1, keepdims=True)
    return centered * inverse


def gelu_pair(values):
    square = values * values
    bent = jnp.tanh(values * (GELU_SCALE + (GELU_SCALE * GELU_CUBE) * square))
    half = 0.5 + 0.5 * bent
    slope = half + (values * half) * (1.0 - bent) * (GELU_SCALE + (3.0 * GELU_SCALE * GELU_CUBE) * square)
    return values * half, slope


def gelu_value(values):
    square = values * values
    bent = jnp.tanh(values * (GELU_SCALE + (GELU_SCALE * GELU_CUBE) * square))
    return values * (0.5 + 0.5 * bent)


def gather_lanes(ref, groups):
    count = ref.shape[0] // groups
    width = ref.shape[2]
    parts = [ref[g * count : (g + 1) * count].reshape(count * ref.shape[1], width) for g in range(groups)]
    return parts[0] if groups == 1 else jnp.concatenate(parts, axis=1)


def scatter_lanes(ref, values, groups):
    count = ref.shape[0] // groups
    width = ref.shape[2]
    for g in range(groups):
        piece = values[:, g * width : (g + 1) * width]
        ref[g * count : (g + 1) * count] = piece.reshape(count, ref.shape[1], width)


def gather_modes(ref, modes):
    rows = ref.shape[1] // modes
    parts = [
        ref[:, k * rows : (k + 1) * rows, :].reshape(ref.shape[0] * rows, ref.shape[2]) for k in range(modes)
    ]
    return parts[0] if modes == 1 else jnp.concatenate(parts, axis=1)


def scatter_modes(ref, values, modes):
    rows = ref.shape[1] // modes
    width = ref.shape[2]
    for k in range(modes):
        piece = values[:, k * width : (k + 1) * width]
        ref[:, k * rows : (k + 1) * rows, :] = piece.reshape(ref.shape[0], rows, width)


def to_mix_rows(values, modes, width):
    half = values.shape[0] // 2
    parts = []
    for k in range(modes):
        piece = values[:, k * width : (k + 1) * width]
        parts.append(jnp.concatenate([piece[:half], piece[half:]], axis=1))
    return parts[0] if modes == 1 else jnp.concatenate(parts, axis=0)


def from_mix_rows(values, modes, width):
    half = values.shape[0] // modes
    parts = []
    for k in range(modes):
        piece = values[k * half : (k + 1) * half]
        parts.append(jnp.concatenate([piece[:, :width], piece[:, width:]], axis=0))
    return parts[0] if modes == 1 else jnp.concatenate(parts, axis=1)


def enter_kernel(groups, tokens_ref, table_ref, send_ref):
    normal, _ = normalize(tokens_ref[...].astype(F32))
    spectrum = dot(table_ref[...], normal.astype(BF16)).astype(BF16)
    scatter_lanes(send_ref, spectrum, groups)


def mix_kernel(
    modes, got_ref, high_ref, back_ref, mats_ref, bias_ref, gain_ref, shift_ref, ones_ref,
    send_ref, hat_ref, modal_ref, inner_ref, active_ref,
):
    width = got_ref.shape[2]
    hat = dot(high_ref[...], gather_modes(got_ref, modes))
    hat_ref[...] = hat
    hat_ref.flush()
    pieces = []
    for k in range(modes):
        piece = hat[:, k * width : (k + 1) * width] * gain_ref[...]
        pieces.append(piece + ones_ref[:, k : k + 1] * shift_ref[...])
    modal = pieces[0] if modes == 1 else jnp.concatenate(pieces, axis=1)
    modal = to_mix_rows(modal.astype(BF16), modes, width)
    modal_ref[...] = modal
    modal_ref.flush()
    inner = dot(modal, mats_ref[0]) + bias_ref[0:1, :]
    inner_ref[...] = inner
    inner_ref.flush()
    active = gelu_value(inner).astype(BF16)
    active_ref[...] = active
    active_ref.flush()
    outer = (dot(active, mats_ref[1]) + bias_ref[1:2, :]).astype(BF16)
    gridded = dot(back_ref[...], from_mix_rows(outer, modes, width)).astype(BF16)
    scatter_modes(send_ref, gridded, modes)


def fold(grad, width, block):
    real = grad[:width, :width] + grad[width:, width:]
    imag = grad[:width, width:] - grad[width:, :width]
    out = []
    for part in (real, imag):
        if width == block:
            out.append(part)
        else:
            lane = lax.broadcasted_iota(jnp.int32, (block, width), 1)
            out.append(jnp.where(lane < block, part[:block], part[block:]))
    return jnp.concatenate(out, axis=0)


def by_block(sums, width, block):
    real, imag = sums[:, :width], sums[:, width:]
    if width == block:
        return [real, imag]
    lane = lax.broadcasted_iota(jnp.int32, real.shape, 1)
    turned_real, turned_imag = pltpu.roll(real, block, 1), pltpu.roll(imag, block, 1)
    return [jnp.where(lane < block, real, turned_imag), jnp.where(lane < block, turned_real, imag)]


def unmix_kernel(
    modes, block, got_ref, high_ref, back_ref, mats_ref, ones_ref, hat_ref, modal_ref, inner_ref, active_ref,
    mlp_ref, send_ref, small_ref,
):
    width = got_ref.shape[2]
    grad_outer = dot(high_ref[...], gather_modes(got_ref, modes)).astype(BF16)
    grad_outer = to_mix_rows(grad_outer, modes, width)
    _, slope = gelu_pair(inner_ref[...])
    grad_inner = (dot_nt(grad_outer, mats_ref[1]) * slope).astype(BF16)
    grad_modal = dot_nt(grad_inner, mats_ref[0]).astype(BF16)
    grad_modal = from_mix_rows(grad_modal, modes, width)
    spectrum = dot(back_ref[...], grad_modal).astype(BF16)
    scatter_modes(send_ref, spectrum, modes)
    rows = 2 * block
    grads = [fold(dot_tn(modal_ref[...], grad_inner), width, block)]
    grads.append(fold(dot_tn(active_ref[...], grad_outer), width, block))
    bias_one = by_block(jnp.sum(grad_inner.astype(F32), axis=0, keepdims=True), width, block)
    bias_two = by_block(jnp.sum(grad_outer.astype(F32), axis=0, keepdims=True), width, block)
    gain = jnp.zeros((1, width), F32)
    shift = jnp.zeros((1, width), F32)
    for k in range(modes):
        lanes = slice(k * width, (k + 1) * width)
        upstream = grad_modal[:, lanes].astype(F32)
        gain = gain + jnp.sum(upstream * hat_ref[:, lanes], axis=0, keepdims=True)
        shift = shift + jnp.sum(upstream * ones_ref[:, k : k + 1], axis=0, keepdims=True)
    tail = jnp.concatenate(bias_one + bias_two + [gain, shift, jnp.zeros((2, width), F32)], axis=0)
    mlp = [mlp_ref[:, q : q + width] for q in range(0, mlp_ref.shape[1], width)]
    message = jnp.concatenate(grads + [tail] + mlp, axis=0).astype(BF16)
    small_ref[0 : message.shape[0]] = message
    rest = small_ref.shape[0] - message.shape[0]
    small_ref[message.shape[0] :] = jnp.zeros((rest, width), BF16)


def add_up(*values):
    total = values[0].astype(F32)
    for value in values[1:]:
        total = total + value.astype(F32)
    return total


def first_kernel(kept_ref, one_ref, in_ref, out_ref):
    for part, ref in enumerate((in_ref, out_ref)):
        ref[...] = add_up(kept_ref[part, 1], one_ref[part, 1]).astype(BF16)


def second_kernel(kept_ref, one_ref, in_ref, out_ref, mine_ref, core_ref, y_ref, x_ref, small_ref):
    small = add_up(mine_ref[...], core_ref[...]).astype(BF16)
    small_ref[...] = small
    for part, source, ref in ((0, in_ref, y_ref), (1, out_ref, x_ref)):
        rows = 0
        for z in range(4):
            value = add_up(kept_ref[part, 0, 1, z], one_ref[part, 0, 1, z], source[1, z]).astype(BF16)
            ref[rows : rows + value.shape[0]] = value
            rows += value.shape[0]
        ref[rows:] = small


def third_kernel(kept_ref, one_ref, in_ref, out_ref, y_ref, x_ref, small_ref, other_ref, own_ref, mine_ref, *away_refs):
    size = kept_ref.shape[4]
    along_x = small_ref[...].astype(F32) + x_ref[4 * size :].astype(F32)
    along_y = y_ref[4 * size :].astype(F32) + other_ref[...].astype(F32)
    small = (along_x + along_y).astype(BF16)
    mine_ref[...] = small
    for part, source, last in ((0, in_ref, y_ref), (1, out_ref, x_ref)):
        for z in range(4):
            rows = slice(z * size, (z + 1) * size)
            total = add_up(kept_ref[part, 0, 0, z], one_ref[part, 0, 0, z], source[0, z], last[rows])
            if z == 0:
                own_ref[part] = total
            else:
                away_refs[z - 1][part * size : (part + 1) * size] = total.astype(BF16)
    for ref in away_refs:
        ref[2 * size :] = small


def step_small(
    block, scale, held, mixer_ref, moment_ref, average_ref, vectors_ref, vec_moment_ref,
    vec_average_ref, new_mixer, new_moment, new_average, new_vectors, new_vec_moment, new_vec_average, grad_ref,
):
    groups, _, width = held.shape
    joined = width // block
    rows = 2 * block
    for group in range(groups):
        for layer in range(2):
            grad = held[group, layer * rows : (layer + 1) * rows] * scale
            for part in range(2):
                for j in range(joined):
                    b = group * joined + j
                    piece = grad[part * block : (part + 1) * block, j * block : (j + 1) * block]
                    value, moment, average = update(
                        mixer_ref[layer, b, part], piece, moment_ref[layer, b, part], average_ref[layer, b, part],
                        WEIGHT_DECAY,
                    )
                    new_mixer[layer, b, part] = value
                    new_moment[layer, b, part] = moment
                    new_average[layer, b, part] = average
        tail = held[group, 2 * rows : 2 * rows + 8]
        grad_ref[0:2, group * width : (group + 1) * width] = tail[4:6]
        for layer in range(2):
            for j in range(2):
                b = group * joined + (j if joined == 2 else 0)
                per_row = vectors_ref.shape[1] // (2 * block)
                lane = (b % per_row) * 2 * block + (0 if joined == 2 else j * block)
                row = 9 + layer * 2 + b // per_row
                grad_ref[row : row + 1, lane : lane + width] = tail[2 * layer + j : 2 * layer + j + 1]
    for q in range(groups):
        part = slice(2 * rows + 8 + 8 * q, 2 * rows + 16 + 8 * q)
        total = held[0, part]
        for group in range(1, groups):
            total = total + held[group, part]
        grad_ref[2:9, q * width : (q + 1) * width] = total[0:7]
    value, moment, average = update(
        vectors_ref[...], grad_ref[0:13, :] * scale, vec_moment_ref[...], vec_average_ref[...], 0.0
    )
    new_vectors[...] = value
    new_vec_moment[...] = moment
    new_vec_average[...] = average


def step_all(block, scale, place_ref, own_ref, mine_ref, *refs):
    away_refs, weights, small = refs[:3], refs[3:9], refs[9:15]
    new_weights, new_small, (held, grad_ref) = refs[15:23], refs[23:29], refs[29:]
    size = own_ref.shape[1]
    far = place_ref[0] >> 3
    held[far] = mine_ref[...].astype(F32)
    for z, ref in enumerate(away_refs):
        held[far ^ (z + 1)] = ref[2 * size :].astype(F32)
    for part in range(2):
        rows = slice(part * size, (part + 1) * size)
        total = own_ref[part] + add_up(*[ref[rows] for ref in away_refs])
        count = weights[part].shape[0]
        for q in range(size // count):
            lanes = slice(q * 128, (q + 1) * 128)
            grad = total[q * count : (q + 1) * count] * scale
            values = update(
                weights[part][:, lanes], grad, weights[2 + part][:, lanes], weights[4 + part][:, lanes], WEIGHT_DECAY
            )
            for i, value in enumerate(values):
                new_weights[2 * i + part][:, lanes] = value
            new_weights[6 + part][:, lanes] = values[0].astype(BF16)
    step_small(block, scale, held, *small, *new_small, grad_ref)


def load_weights(near, place_ref, pieces, w_in, w_out, sems):
    copies = []
    if not near:
        copies = [(pieces[0].at[:, part], target) for part, target in enumerate((w_in, w_out))]
    else:
        me = place_ref[0]
        at = [(me >> 1) & 1, (me >> 2) & 1, me & 1, me >> 3]
        size = pieces[0].shape[3]
        for i, ref in enumerate(pieces):
            for j in range(2):
                x, y = (i >> 1 & 1, j) if i & 1 else (j, i >> 1 & 1)
                for k in range(2):
                    z = 2 * (i & 1) + k
                    row = (((at[3] ^ z) * 2 + (at[1] ^ y)) * 2 + (at[0] ^ (i >> 2))) * size
                    rows = pl.ds(pl.multiple_of(row, size), size)
                    for part, target in enumerate((w_in, w_out)):
                        copies.append((ref.at[j, k, part], target.at[at[2] ^ x, rows]))
    copies = [pltpu.make_async_copy(source, target, sems.at[i]) for i, (source, target) in enumerate(copies)]
    for copy in copies:
        copy.start()
    return copies


def mlp_kernel(
    groups, near, place_ref, got_ref, wide_t_ref, tokens_ref, cotangent_ref, vectors_ref, bias_ref, wide_ref, *refs
):
    count = 8 if near else 1
    pieces, refs = refs[:count], refs[count:]
    output_ref, middle_ref, send_ref, small_ref, *refs = refs
    grad_refs, refs = refs[:2], refs[2:]
    normed, normed_t, cotangent_t, normal, spread, upstream_ref, w_in, w_out, active, grad_hidden, sems = refs
    copies = load_weights(near, place_ref, pieces, w_in, w_out, sems)
    tokens, width = tokens_ref.shape
    halves, _, columns = w_in.shape
    gain, shift, bias_out = vectors_ref[2:3, :], vectors_ref[3:4, :], vectors_ref[4:5, :]
    row_blocks = [slice(r, r + ROWS) for r in range(0, tokens, ROWS)]
    spectrum = gather_lanes(got_ref, groups)
    bias_out_grad = jnp.zeros((1, width), F32)
    for rows in row_blocks:
        middle = tokens_ref[rows, :].astype(F32) + dot(wide_t_ref[rows, :], spectrum)
        unit, inverse = normalize(middle)
        normal[rows, :] = unit
        spread[rows, :] = inverse
        scaled = (unit * gain + shift).astype(BF16)
        normed[rows, :] = scaled
        normed_t[:, rows] = scaled.T
        middle_ref[rows, :] = middle + bias_out
        upstream = cotangent_ref[rows, :]
        cotangent_t[:, rows] = upstream.T
        bias_out_grad = bias_out_grad + jnp.sum(upstream.astype(F32), axis=0, keepdims=True)
    for copy in copies:
        copy.wait()
    gain_grad = jnp.zeros((1, width), F32)
    shift_grad = jnp.zeros((1, width), F32)
    chunks = [(h, c) for h in range(halves) for c in range(0, columns, CHUNK)]
    bias_grads = [jnp.zeros((1, CHUNK), F32) for _ in chunks]
    for rows in row_blocks:
        for i, (h, c) in enumerate(chunks):
            lanes, flat = slice(c, c + CHUNK), slice(h * columns + c, h * columns + c + CHUNK)
            hidden = dot(normed[rows, :], w_in[h, :, lanes]) + bias_ref[i : i + 1, :]
            value, slope = gelu_pair(hidden)
            active[rows, flat] = value.astype(BF16)
            back = (dot(cotangent_ref[rows, :], w_out[h, :, lanes]) * slope).astype(BF16)
            grad_hidden[rows, flat] = back
            bias_grads[i] = bias_grads[i] + jnp.sum(back.astype(F32), axis=0, keepdims=True)
        total, back = middle_ref[rows, :], None
        for h in range(halves):
            flat = slice(h * columns, (h + 1) * columns)
            total = total + dot_nt(active[rows, flat], w_out[h])
            term = dot_nt(grad_hidden[rows, flat], w_in[h])
            back = term if back is None else back + term
        output_ref[rows, :] = total.astype(BF16)
        unit = normal[rows, :]
        gain_grad = gain_grad + jnp.sum(back * unit, axis=0, keepdims=True)
        shift_grad = shift_grad + jnp.sum(back, axis=0, keepdims=True)
        middle = cotangent_ref[rows, :].astype(F32) + norm_back(back, unit, spread[rows, :], gain)
        middle_ref[rows, :] = middle
        upstream_ref[rows, :] = middle.astype(BF16)
    output_ref.flush()
    middle_ref.flush()
    small_ref[0:3, :] = jnp.concatenate([gain_grad, shift_grad, bias_out_grad], axis=0)
    small_ref[3:7, :] = jnp.concatenate(bias_grads, axis=0)
    small_ref[7:8, :] = jnp.zeros((1, width), F32)
    spectrum = dot(wide_ref[...], upstream_ref[...]).astype(BF16)
    scatter_lanes(send_ref, spectrum, groups)
    for i, (h, c) in enumerate(chunks):
        flat = slice(h * columns + c, h * columns + c + CHUNK)
        grads = [
            dot(normed_t[...], grad_hidden[:, flat]).astype(BF16), dot(cotangent_t[...], active[:, flat]).astype(BF16)
        ]
        if not near:
            for ref, grad in zip(grad_refs, grads, strict=True):
                ref[h, :, c : c + CHUNK] = grad
            continue
        me = place_ref[0]
        at = [(me >> 1) & 1, (me >> 2) & 1, me & 1, me >> 3]
        size = w_in.shape[1] // 16
        x = h ^ at[2]
        for core in range(2):
            for ref, mine in ((grad_refs[0], core), (grad_refs[1], 1 - core)):

                @pl.when(at[0] == mine)
                def _(ref=ref, core=core, c=c, x=x, grads=grads):
                    for z in range(4):
                        for y in range(2):
                            rows = slice(((z * 2 + y) * 2 + core) * size, ((z * 2 + y) * 2 + core + 1) * size)
                            for q in range(CHUNK // 128):
                                lanes = slice(q * 128, (q + 1) * 128)
                                place = slice((c // 128 + q) * size, (c // 128 + q + 1) * size)
                                ref[0, x, y ^ at[1], z ^ at[3], place, :] = grads[0][rows, lanes]
                                ref[1, y ^ at[1], x, z ^ at[3], place, :] = grads[1][rows, lanes]


def leave_kernel(groups, got_ref, tokens_ref, middle_ref, vectors_ref, table_ref, out_ref):
    spectrum = gather_lanes(got_ref, groups)
    for start in range(0, tokens_ref.shape[0], ROWS):
        rows = slice(start, start + ROWS)
        upstream = dot(table_ref[rows, :], spectrum)
        unit, inverse = normalize(tokens_ref[rows, :].astype(F32))
        back = norm_back(upstream, unit, inverse, vectors_ref[0:1, :])
        out_ref[rows, :] = (middle_ref[rows, :] + back).astype(BF16)


def update(weight, gradient, moment, average, decay_rate):
    step_grad = gradient + decay_rate * weight
    new_moment = MOMENTUM * moment + step_grad
    new_weight = weight - LEARNING_RATE * (step_grad + MOMENTUM * new_moment)
    new_average = AVERAGE * average + (1.0 - AVERAGE) * new_weight
    return (new_weight, new_moment, new_average)


class Source:
    def __init__(self, ref, copy):
        self.ref, self.copy, self.shape = ref, copy, ref.shape

    def __getitem__(self, index):
        if self.copy is not None:
            self.copy.wait()
            self.copy = None
        return self.ref[index]


class Sink:
    def __init__(self, ref, copy):
        self.ref, self.copy, self.shape, self.sent = ref, copy, ref.shape, False

    def __getitem__(self, index):
        return self.ref[index]

    def __setitem__(self, index, value):
        self.ref[index] = value

    def flush(self):
        if not self.sent:
            self.copy.start()
            self.sent = True


class Far:
    def __init__(self, *what):
        self.what = what


def call(body, outs, *args, scalars=(), raw=(), scratch=(), flops=0, carry=(), cost=None, vmem=20):
    near, far, there = [pl.BlockSpec(memory_space=m) for m in (pltpu.VMEM, pltpu.HBM, pl.ANY)]
    in_far, out_far = [isinstance(a, Far) for a in args], [isinstance(o, Far) for o in outs]
    args = [
        pltpu.with_memory_space_constraint(*((a.what[0], pltpu.HBM) if f else (a, pltpu.VMEM)))
        for a, f in zip(args, in_far, strict=True)
    ]
    raw = [pltpu.with_memory_space_constraint(a, pltpu.HBM) for a in raw]
    outs = [o.what if f else o for o, f in zip(outs, out_far, strict=True)]
    outs = [jax.ShapeDtypeStruct(s, d) for s, d in outs]
    n_scalar, n_in, n_raw, n_carry, n_out = len(scalars), len(args), len(raw), len(carry), len(outs)
    buffers = [pltpu.VMEM(a.shape, a.dtype) for a, f in zip(args + outs, in_far + out_far, strict=True) if f]

    def inner(*refs):
        refs = list(refs)

        def take(count):
            taken = refs[:count]
            del refs[:count]
            return taken

        scalar_refs, in_refs, raw_refs, _, out_refs, _ = [
            take(n) for n in (n_scalar, n_in, n_raw, n_carry, n_out, n_carry)
        ]
        space = take(len(buffers))
        sems = take(1)[0] if buffers else None
        sources, sinks, used = [], [], 0
        for ref, away in zip(in_refs, in_far, strict=True):
            if away:
                copy = pltpu.make_async_copy(ref, space[used], sems.at[used])
                copy.start()
                ref = Source(space[used], copy)
                used += 1
            sources.append(ref)
        for ref, away in zip(out_refs, out_far, strict=True):
            if away:
                ref = Sink(space[used], pltpu.make_async_copy(space[used], ref, sems.at[used]))
                used += 1
            sinks.append(ref)
        body(*scalar_refs, *sources, *raw_refs, *sinks, *refs)
        for source in sources:
            if isinstance(source, Source) and source.copy is not None:
                source.copy.wait()
        sinks = [sink for sink in sinks if isinstance(sink, Sink)]
        for sink in sinks:
            sink.flush()
        for sink in sinks:
            sink.copy.wait()

    every = list(args) + list(raw)
    size = sum(math.prod(a.shape) * a.dtype.itemsize for a in every + outs) if cost is None else cost
    sems = [pltpu.SemaphoreType.DMA((len(buffers),))] if buffers else []
    return pl.pallas_call(
        inner,
        out_shape=[(pltpu.HBM if f else pltpu.VMEM)(o.shape, o.dtype) for o, f in zip(outs, out_far, strict=True)]
        + [jax.ShapeDtypeStruct(a.shape, a.dtype) for a in carry],
        in_specs=[pl.BlockSpec(memory_space=pltpu.SMEM)] * n_scalar
        + [far if f else near for f in in_far]
        + [far] * n_raw
        + [there] * n_carry,
        out_specs=[far if f else near for f in out_far] + [there] * n_carry,
        scratch_shapes=buffers + sems + list(scratch),
        input_output_aliases={n_scalar + n_in + n_raw + i: n_out + i for i in range(n_carry)},
        compiler_params=pltpu.CompilerParams(vmem_limit_bytes=vmem << 20),
        cost_estimate=pl.CostEstimate(flops=flops, bytes_accessed=size, transcendentals=0),
    )(*scalars, *args, *raw, *carry)


def on_device(
    tokens, cotangent, w_in, w_out, mixer_weights, vectors, w_in_moment, w_out_moment, mixer_moment, vectors_moment,
    w_in_average, w_out_average, mixer_average, vectors_average,
):
    sp_count, tp_count = lax.axis_size("sp"), lax.axis_size("tp")
    devices = sp_count * tp_count
    grid_rows, grid, width = tokens.shape
    local = grid_rows * grid
    items = grid_rows * devices // grid
    block_count, block = mixer_weights.shape[1], mixer_weights.shape[3]
    hidden = w_in.shape[1] * tp_count
    model = w_in.shape[0] * sp_count
    lanes = 2 * block if devices * 2 * block <= MODES * width else block
    groups = width // lanes
    per_group = devices // groups
    modes = MODES // per_group
    joined = lanes // block
    scale = 1.0 / math.sqrt(local * devices)
    wide_f, wide_i, high, ones = expanded_tables(grid, grid_rows, items)
    me = lax.axis_index("sp") * tp_count + lax.axis_index("tp")
    group = me // per_group
    exchange = functools.partial(lax.all_to_all, axis_name=AXES, split_axis=0, concat_axis=0, tiled=True)
    chunk = (devices, modes * grid_rows * 2, lanes)
    rows_all = tokens.reshape(local, width)
    upstream_all = cotangent.reshape(local, width)
    shard_rows, shard_columns = w_in.shape
    shard_size = shard_rows * shard_columns // 128
    near = devices == 32 and per_group == 8 and shard_rows % 16 == 0

    def permute(values, mask):
        return lax.ppermute(values, AXES, [(d, d ^ mask) for d in range(devices)])

    pair = jnp.stack([w_in.astype(BF16), w_out.astype(BF16)])
    if near:
        line = [pair] + [permute(pair, 8 * z) for z in (1, 2, 3)]
        carried = [jnp.stack([v, permute(v, m)]) for v, m in ((jnp.stack(line[:2]), 1), (jnp.stack(line[2:]), 4))]
    else:
        weights = lax.all_gather(pair, "sp", axis=1, tiled=True)
        pieces, carried = [lax.all_gather(weights, "tp")], []

    own_mixer = lax.dynamic_slice_in_dim(mixer_weights, group * joined, joined, 1).astype(BF16)
    eye = jnp.eye(joined, dtype=BF16)
    real = jnp.einsum("lbio,bc->lbico", own_mixer[:, :, 0], eye).reshape(2, lanes, lanes)
    imag = jnp.einsum("lbio,bc->lbico", own_mixer[:, :, 1], eye).reshape(2, lanes, lanes)
    mats = jnp.concatenate(
        [jnp.concatenate([real, imag], axis=2), jnp.concatenate([-imag, real], axis=2)], axis=1
    )
    own_bias = lax.dynamic_slice_in_dim(
        vectors[9:13].reshape(2, block_count, 2, block), group * joined, joined, 1
    )
    own_bias = jnp.swapaxes(own_bias, 1, 2).reshape(2, 2 * lanes)
    own_gain = lax.dynamic_slice_in_dim(vectors[0:1], group * lanes, lanes, 1)
    own_shift = lax.dynamic_slice_in_dim(vectors[1:2], group * lanes, lanes, 1)
    ones = jnp.asarray(np.swapaxes(ones.reshape(per_group, modes, -1), 1, 2))
    own_ones = lax.dynamic_index_in_dim(ones, me % per_group, 0, keepdims=False)

    wide_f, wide_f_t = jnp.asarray(wide_f), jnp.asarray(wide_f.T)
    wide_i, wide_i_t = jnp.asarray(wide_i), jnp.asarray(wide_i.T)
    high, high_t = jnp.asarray(high), jnp.asarray(high.T)
    wide_flops = 2 * wide_f.shape[0] * wide_f.shape[1] * width
    (sent,) = call(
        functools.partial(enter_kernel, groups), [(chunk, BF16)], Far(rows_all), Far(wide_f), flops=wide_flops
    )
    got = exchange(sent)
    half_rows = items * MODES
    sent, hat, modal, inner, active, *carried = call(
        functools.partial(mix_kernel, modes),
        [
            (chunk, BF16),
            Far((2 * half_rows, modes * lanes), F32),
            Far((modes * half_rows, 2 * lanes), BF16),
            Far((modes * half_rows, 2 * lanes), F32),
            Far((modes * half_rows, 2 * lanes), BF16),
        ],
        got, high, high_t, mats, own_bias, own_gain, own_shift, own_ones,
        carry=carried,
    )
    if near:
        pieces = carried + [permute(carried[0], 4), permute(carried[1], 1)]
        pieces += [permute(p, 2) for p in pieces]
    got = exchange(sent)
    steps = hidden // CHUNK
    grads = [((2, 2, 2, 4, shard_size, 128), BF16)] * 2 if near else [((tp_count, model, shard_columns), BF16)] * 2
    output, middle, sent, mlp_small, *grads = call(
        functools.partial(mlp_kernel, groups, near),
        [Far((local, width), BF16), Far((local, width), F32), (chunk, BF16), ((8, width), F32)] + grads,
        got, Far(wide_i_t), Far(rows_all), Far(upstream_all), vectors, vectors[5:9].reshape(steps, CHUNK), Far(wide_i),
        scalars=[me[None]], raw=pieces,
        scratch=[
            pltpu.VMEM((local, width), BF16),
            pltpu.VMEM((width, local), BF16),
            pltpu.VMEM((width, local), BF16),
            pltpu.VMEM((local, width), F32),
            pltpu.VMEM((local, 1), F32),
            pltpu.VMEM((local, width), BF16),
            pltpu.VMEM((tp_count, model, shard_columns), BF16),
            pltpu.VMEM((tp_count, model, shard_columns), BF16),
            pltpu.VMEM((local, hidden), BF16),
            pltpu.VMEM((local, hidden), BF16),
            pltpu.SemaphoreType.DMA((64 if near else 2,)),
        ],
        flops=12 * local * width * hidden + 2 * wide_flops, vmem=44,
    )

    carried = []
    if near:
        shard = (4, shard_size, 128)
        kept, one = grads[0], permute(grads[1], 2)
        sent_in, sent_out = call(
            first_kernel, [((2,) + shard, BF16)] * 2, kept, one, cost=0,
        )
        carried = [permute(sent_in, 1), permute(sent_out, 4)]

    got = exchange(sent)
    small_rows = -(-(4 * block + 8 + 8 * groups) // 16) * 16
    sent, small = call(
        functools.partial(unmix_kernel, modes, block),
        [(chunk, BF16), ((small_rows, lanes), BF16)],
        got, Far(high), Far(high_t), Far(mats), own_ones, Far(hat), Far(modal), Far(inner), Far(active), mlp_small,
        cost=COST,
    )
    if near:
        over_y, over_x, small = call(
            second_kernel, [((4 * shard_size + small_rows, 128), BF16)] * 2 + [((small_rows, 128), BF16)],
            kept, one, *carried, small, permute(small, 2), cost=0,
        )
        from_y, from_x, from_both = permute(over_y, 4), permute(over_x, 1), permute(small, 5)
        own, mine, *away = call(
            third_kernel,
            [((2, shard_size, 128), F32), ((small_rows, 128), BF16)] + [((2 * shard_size + small_rows, 128), BF16)] * 3,
            kept, one, *carried, from_y, from_x, small, from_both, cost=0,
        )
        away = [permute(a, 8 * (z + 1)) for z, a in enumerate(away)]
    got = exchange(sent)
    (grad_tokens,) = call(
        functools.partial(leave_kernel, groups),
        [Far((local, width), BF16)],
        got, Far(rows_all), Far(middle), vectors, Far(wide_f_t), flops=wide_flops,
    )

    state = [mixer_weights, mixer_moment, mixer_average, vectors, vectors_moment, vectors_average]
    new_state = [Far(a.shape, F32) for a in state]
    scratch = [pltpu.VMEM((16, width), F32)]
    if near:
        weights = [w_in, w_out, w_in_moment, w_out_moment, w_in_average, w_out_average]
        *stepped, grad_tokens = call(
            functools.partial(step_all, block, scale),
            [Far(w_in.shape, F32)] * 6 + [Far(w_in.shape, BF16)] * 2 + new_state,
            own, mine, *away, *weights, *state,
            scalars=[me[None]], scratch=[pltpu.VMEM((groups, small_rows, lanes), F32)] + scratch, carry=[grad_tokens],
        )
        new_in, new_out = stepped[0:8:2], stepped[1:8:2]
        stepped = stepped[8:]
    else:
        grads = jnp.stack(grads).astype(F32)
        grads = lax.psum_scatter(grads, "tp", scatter_dimension=1, tiled=True)
        grads = lax.psum_scatter(grads, "sp", scatter_dimension=2, tiled=True)
        new_in = update(w_in, grads[0, 0] * scale, w_in_moment, w_in_average, WEIGHT_DECAY)
        new_out = update(w_out, grads[1, 0] * scale, w_out_moment, w_out_average, WEIGHT_DECAY)
        new_in, new_out = new_in + (new_in[0].astype(BF16),), new_out + (new_out[0].astype(BF16),)
        onehot = (jnp.arange(groups, dtype=jnp.int32) == group).astype(F32)[:, None, None]
        held = lax.psum(onehot * small.astype(F32), AXES)
        stepped = call(functools.partial(step_small, block, scale), new_state, held, *state, scratch=scratch)
    new_mix, new_vec = stepped[0:3], stepped[3:6]
    shape = tokens.shape
    return (
        output.reshape(shape), grad_tokens.reshape(shape),
        new_in[0], new_out[0], new_mix[0], new_vec[0],
        new_in[1], new_out[1], new_mix[1], new_vec[1],
        new_in[2], new_out[2], new_mix[2], new_vec[2],
        new_in[3], new_out[3],
    )


def solution(mesh):
    rows, split, whole = P(AXES, None, None), P("sp", "tp"), P()
    state = (split, split, whole, whole)
    return jax.shard_map(
        on_device,
        mesh=mesh,
        in_specs=(rows, rows) + state * 3,
        out_specs=(rows, rows) + state * 3 + (split, split),
        check_vma=False,
    )
```

time: 349 us -> 157 us (0.45)
  waiting for transfers between devices: 195 us -> 56 us
  blocking collectives: 40.7 us -> 0 us
  other arithmetic: 18.8 us -> 1.54 us
  Pallas kernels: 34.8 us -> 49.9 us
  between operations: 14.5 us -> 1.38 us
  starting transfers between devices: 28.6 us -> 41.2 us
  local copies, waits for them, and re-layouts: 15.4 us -> 5.63 us
    psum x1 -> x0, waiting for transfers between devices: 126 us -> none  [on_device(): lax.psum((onehot[:, None, None] * mix_small[None], mlp_small), AXES)]
    psum x1 -> x0, blocking collectives: 40.7 us -> none  [on_device(): lax.psum((onehot[:, None, None] * mix_small[None], mlp_small), AXES)]
    ppermute x9 -> x21, waiting for transfers between devices: 16 us -> 45.5 us  [permute(): return lax.ppermute(values, AXES, [(d, d ^ mask) for d in range(devices)])]
    all_to_all x4, waiting for transfers between devices: 33.6 us -> 10.5 us  [on_device(): got = exchange(sent)]
    all_gather x1 -> x0, waiting for transfers between devices: 19.1 us -> none  [on_device(): weights = lax.all_gather(pair, AXES)]
    pallas_call x5 -> x9, Pallas kernels: 34.8 us -> 49.9 us  [call(): pl.pallas_call(inner, out_shape=[(pltpu.HBM if f else pltpu.VMEM)(o.shape...]
    ppermute x9 -> x21, starting transfers between devices: 9.75 us -> 24.8 us  [permute(): return lax.ppermute(values, AXES, [(d, d ^ mask) for d in range(devices)])]
    convert_element_type x6 -> x0, other arithmetic: 6.84 us -> none  [the longest x2 3.59 us: on_device(): (grad[0, 1].astype(F32) + one[1].astype(F32)).astype(BF16)]
  transfers between devices with their start and end apart: 15 -> 25, of which waited for: 9 -> 12; matrix products, arithmetic and copies ran while one was open for 7% -> 2% of each run, Pallas kernels for 1% -> 12%
where the time goes in v2:
time: 157 us; the launch traced here: 156 us
  waiting for transfers between devices  56 us (36%)
  Pallas kernels  49.9 us (32%)
  starting transfers between devices  41.2 us (26%)
  local copies, waits for them, and re-layouts  5.63 us (4%)
    pallas_call x9, Pallas kernels, call(): pl.pallas_call(inner, out_shape=[(pltpu.HBM if f else pltpu.VMEM)(o.shape...  49.9 us
    ppermute x21, waiting for transfers between devices, permute(): return lax.ppermute(values, AXES, [(d, d ^ mask) for d in range(devices)])  45.5 us
    ppermute x21, starting transfers between devices, permute(): return lax.ppermute(values, AXES, [(d, d ^ mask) for d in range(devices)])  24.8 us
    all_to_all x4, starting transfers between devices, on_device(): got = exchange(sent)  16.4 us
    all_to_all x4, waiting for transfers between devices, on_device(): got = exchange(sent)  10.5 us
    unnamed x53, local copies, waits for them, and re-layouts  3.37 us
  transfers between devices with their start and end apart: 25, of which 12 were waited for; matrix products, arithmetic and copies ran while one was open for 2% of the time, Pallas kernels for 12%

profile of v2, /device:TPU:0, one launch (start us, length us, event | category | flops | bytes accessed | tf_op | source)
XLA Modules:
  0.0 155.7 jit_solution(13441300186639098433)
XLA Ops:
  0.6 1.0 convert_bitcast_fusion
  1.7 4.1 %collective-permute-start.2 = (bf16[2,32,1024]{2,1,0:T(8,128)(2,1)S(1)}, bf16[2,32,1024]{2,1,0:T(8,128)(2,1)S(1)}, u32[]{:S(2)}, u32[]{:S(2)}) collective-permute-start(bf16[2,32,1024]{2,1,0:T(8,128)(2,1)S(1)} %get-tuple-element.101), channel_id=1, source_target_pairs={{0,16},{1,17},{2,18},{3,19},{4,20},{5,21},{6,22},{7,23},{8,24},{9,... | collective-permute-start | bytes 393224 | tf_op jit(solution)/shard_map/ppermute | solution.py:606
  5.8 1.6 %collective-permute-start = (bf16[2,32,1024]{2,1,0:T(8,128)(2,1)S(1)}, bf16[2,32,1024]{2,1,0:T(8,128)(2,1)S(1)}, u32[]{:S(2)}, u32[]{:S(2)}) collective-permute-start(bf16[2,32,1024]{2,1,0:T(8,128)(2,1)S(1)} %get-tuple-element.101), channel_id=1, source_target_pairs={{0,8},{1,9},{2,10},{3,11},{4,12},{5,13},{6,14},{7,15},{8,0},{9,1},... | collective-permute-start | bytes 393224 | tf_op jit(solution)/shard_map/ppermute | solution.py:606
  7.4 3.3 %shard_map.324 = bf16[32,64,128]{2,1,0:T(8,128)(2,1)} custom-call(bf16[1024,512]{1,0:T(8,128)(2,1)} %bitcast.37, bf16[512,1024]{1,0:T(8,128)(2,1)} %constant.60.clone.refs_1_), custom_call_target="tpu_custom_call" | custom-call | flops 536870912 | bytes 2621440 | tf_op jit(solution)/shard_map/pallas_call | solution.py:560
  10.7 6.1 %all-to-all-start = ((bf16[32,64,128]{2,1,0:T(8,128)(2,1)}), bf16[32,64,128]{2,1,0:T(8,128)(2,1)S(1)}, u32[]{:S(2)}, u32[]{:S(2)}) async-start(bf16[32,64,128]{2,1,0:T(8,128)(2,1)} %shard_map.324), calls=%async_computation | async-start | bytes 1048576 | tf_op jit(solution)/shard_map/all_to_all | solution.py:639
  16.8 1.0 dynamic-slice_convert_fusion
  18.2 0.9 dynamic-slice_bitcast_fusion.refs_7_.refs_4_
  19.2 1.8 %collective-permute-start.1 = (bf16[2,2,32,1024]{3,2,1,0:T(8,128)(2,1)S(1)}, bf16[2,2,32,1024]{3,2,1,0:T(8,128)(2,1)S(1)}, u32[]{:S(2)}, u32[]{:S(2)}) collective-permute-start(bf16[2,2,32,1024]{3,2,1,0:T(8,128)(2,1)S(1)} %get-tuple-element.99), channel_id=1, source_target_pairs={{0,1},{1,0},{2,3},{3,2},{4,5},{5,4},{6,7},{7,6},{8,9},{9,8},{10,11... | collective-permute-start | bytes 786440 | tf_op jit(solution)/shard_map/ppermute | solution.py:606
  21.1 1.5 collective-permute-start.4
  23.0 7.8 %collective-permute-done.1 = bf16[2,2,32,1024]{3,2,1,0:T(8,128)(2,1)S(1)} collective-permute-done((bf16[2,2,32,1024]{3,2,1,0:T(8,128)(2,1)S(1)}, bf16[2,2,32,1024]{3,2,1,0:T(8,128)(2,1)S(1)}, u32[]{:S(2)}, u32[]{:S(2)}) %collective-permute-start.1) | collective-permute-done | bytes 262176 | tf_op jit(solution)/shard_map/ppermute | solution.py:606
  30.8 0.6 collective-permute-done.4
  31.8 2.3 %shard_map.325 = (bf16[32,64,128]{2,1,0:T(8,128)(2,1)}, f32[128,512]{1,0:T(8,128)}, bf16[256,256]{1,0:T(8,128)(2,1)}, f32[256,256]{1,0:T(8,128)}, bf16[256,256]{...) custom-call(bf16[32,64,128]{2,1,0:T(8,128)(2,1)S(1)} %all-to-all-don, ...), custom_call_target="tpu_custom_call", output_to_operand_aliasing={{5}: (8, {}), {6}: (9, {})} | custom-call | bytes 2364416 | tf_op jit(solution)/shard_map/pallas_call | solution.py:560
  34.1 1.5 collective-permute-start.5
  35.6 1.5 collective-permute-start.6
  37.1 3.4 %all-to-all-start.1 = ((bf16[32,64,128]{2,1,0:T(8,128)(2,1)}), bf16[32,64,128]{2,1,0:T(8,128)(2,1)S(1)}, u32[]{:S(2)}, u32[]{:S(2)}) async-start(bf16[32,64,128]{2,1,0:T(8,128)(2,1)} %get-tuple-element.56), calls=%async_computation.1 | async-start | bytes 1048576 | tf_op jit(solution)/shard_map/all_to_all | solution.py:656
  40.6 0.3 collective-permute-start.7
  41.1 11.1 %collective-permute-done.5.refs_10_ = bf16[2,2,2,32,1024]{4,3,2,1,0:T(8,128)(2,1)S(1)} collective-permute-done((bf16[2,2,2,32,1024]{4,3,2,1,0:T(8,128)(2,1)S(1)}, bf16[2,2,2,32,1024]{4,3,2,1,0:T(8,128)(2,1)S(1)}, u32[]{:S(2)}, u32[]{:S(2)}) %collective-permute-start.5) | collective-permute-done | bytes 524320 | tf_op jit(solution)/shard_map/ppermute | solution.py:606
  52.2 0.4 collective-permute-start.9
  52.6 1.5 collective-permute-done.6.refs_11_
  54.2 1.2 all-to-all-done.1.refs_1_
  55.4 0.8 copy-done.9
  56.2 1.0 copy-done.10
  57.3 25.2 %shard_map.326 = (bf16[1024,512]{1,0:T(8,128)(2,1)}, f32[1024,512]{1,0:T(8,128)}, bf16[32,64,128]{2,1,0:T(8,128)(2,1)S(1)}, f32[8,512]{1,0:T(8,128)S(1)}, bf16[2...) custom-call(s32[1]{0:T(128)} %bitcast.refs_0_, bf16[32,64,128]{2,1,0:T(8,128)(2,1)S(1)} %copy-done.10, ...), custom_call_target="tpu_custom_call" | custom-call | flops 13958643712 | bytes 16828416 | tf_op jit(solution)/shard_map/pallas_call | solution.py:560
  82.4 1.1 collective-permute-start.11
  83.6 3.3 %all-to-all-start.2 = ((bf16[32,64,128]{2,1,0:T(8,128)(2,1)}), bf16[32,64,128]{2,1,0:T(8,128)(2,1)S(1)}, u32[]{:S(2)}, u32[]{:S(2)}) async-start(bf16[32,64,128]{2,1,0:T(8,128)(2,1)} %copy-done.11), calls=%async_computation.2 | async-start | bytes 1048576 | tf_op jit(solution)/shard_map/all_to_all | solution.py:689
  86.8 0.8 collective-permute-done.11.refs_1_
  87.7 2.7 %shard_map.327 = (bf16[2,4,256,128]{3,2,1,0:T(8,128)(2,1)}, bf16[2,4,256,128]{3,2,1,0:T(8,128)(2,1)}) custom-call(bf16[2,2,2,4,256,128]{5,4,3,2,1,0:T(8,128)(2,1)S(1)} %get-tuple-element.60.refs_0_, bf16[2,2,2,4,256,128]{5,4,3,2,1,0:T(8,128)(2,1)} %collective-permute-done.11.refs_1_), custom_call_target="tpu_custom_call" | custom-call | tf_op jit(solution)/shard_map/pallas_call | solution.py:560
  90.4 1.1 collective-permute-start.12
  91.5 1.3 collective-permute-start.13
  92.8 9.1 %all-to-all-done.2.refs_0_ = bf16[32,64,128]{2,1,0:T(8,128)(2,1)S(1)} async-done(((bf16[32,64,128]{2,1,0:T(8,128)(2,1)}), bf16[32,64,128]{2,1,0:T(8,128)(2,1)S(1)}, u32[]{:S(2)}, u32[]{:S(2)}) %all-to-all-start.2) | async-done | bytes 524320 | tf_op jit(solution)/shard_map/all_to_all | solution.py:689
  101.9 2.8 %shard_map.328 = (bf16[32,64,128]{2,1,0:T(8,128)(2,1)S(1)}, bf16[304,128]{1,0:T(8,128)(2,1)S(1)}) custom-call(bf16[32,64,128]{2,1,0:T(8,128)(2,1)S(1)} %all-to-all-done.2.refs_0_, bf16[128,512]{1,0:T(8,128)(2,1)} %constant.64.clone.refs_1_, bf16[512,128]{1,0:T(8,128)(2,1)} %constant.65.clone.refs_2_, bf16[2,256,256]{2,1,0:T(8,128)(2,1)} %copy-done, ...), custom_call_target="tpu_custom_call" | custom-call | bytes 62914560 | tf_op jit(solution)/shard_map/pallas_call | solution.py:560
  104.7 0.8 copy-done.8
  105.5 3.6 %all-to-all-start.3 = ((bf16[32,64,128]{2,1,0:T(8,128)(2,1)}), bf16[32,64,128]{2,1,0:T(8,128)(2,1)S(1)}, u32[]{:S(2)}, u32[]{:S(2)}) async-start(bf16[32,64,128]{2,1,0:T(8,128)(2,1)} %copy-done.8), calls=%async_computation.3 | async-start | bytes 1048576 | tf_op jit(solution)/shard_map/all_to_all | solution.py:709
  109.1 0.3 collective-permute-start.14
  109.4 1.0 collective-permute-done.14.refs_5_
  110.4 1.9 %shard_map.329 = (bf16[1328,128]{1,0:T(8,128)(2,1)S(1)}, bf16[1328,128]{1,0:T(8,128)(2,1)S(1)}, bf16[304,128]{1,0:T(8,128)(2,1)S(1)}) custom-call(bf16[2,2,2,4,256,128]{5,4,3,2,1,0:T(8,128)(2,1)S(1)} %get-tuple-element.60.refs_0_, bf16[2,2,2,4,256,128]{5,4,3,2,1,0:T(8,128)(2,1)} %collective-permute-done.11.refs_1_, ...), custom_call_target="tpu_custom_call" | custom-call | tf_op jit(solution)/shard_map/pallas_call | solution.py:560
  112.3 1.8 %collective-permute-start.15 = (bf16[1328,128]{1,0:T(8,128)(2,1)S(1)}, bf16[1328,128]{1,0:T(8,128)(2,1)S(1)}, u32[]{:S(2)}, u32[]{:S(2)}) collective-permute-start(bf16[1328,128]{1,0:T(8,128)(2,1)S(1)} %get-tuple-element.71), channel_id=1, source_target_pairs={{0,4},{1,5},{2,6},{3,7},{4,0},{5,1},{6,2},{7,3},{8,12},{9,13},{10,... | collective-permute-start | bytes 1019912 | tf_op jit(solution)/shard_map/ppermute | solution.py:606
  114.2 1.5 collective-permute-start.16
  115.9 12.4 %collective-permute-done.17.refs_7_ = bf16[304,128]{1,0:T(8,128)(2,1)S(1)} collective-permute-done((bf16[304,128]{1,0:T(8,128)(2,1)S(1)}, bf16[304,128]{1,0:T(8,128)(2,1)S(1)}, u32[]{:S(2)}, u32[]{:S(2)}) %collective-permute-start.17) | collective-permute-done | bytes 77856 | tf_op jit(solution)/shard_map/ppermute | solution.py:606
  128.2 2.6 %shard_map.330 = (f32[2,256,128]{2,1,0:T(8,128)S(1)}, bf16[304,128]{1,0:T(8,128)(2,1)S(1)}, bf16[816,128]{1,0:T(8,128)(2,1)}, bf16[816,128]{1,0:T(8,128)(2,1)}, bf16[816,128]{1,0:T(8,128)(2,1)}) custom-call(bf16[2,2,2,4,256,128]{5,4,3,2,1,0:T(8,128)(2,1)S(1)} %get-tuple-element.60.refs_0_, bf16[2,2,2,4,256,128]{5,4,3,2,1,0:T(8,128)(2,1)} %collective-permute-done.11.refs_1_, ...), custom_call_target="tpu_custom_call" | custom-call | tf_op jit(solution)/shard_map/pallas_call | solution.py:560
  130.9 0.6 copy-done.19
  131.5 1.7 %collective-permute-start.18 = (bf16[816,128]{1,0:T(8,128)(2,1)}, bf16[816,128]{1,0:T(8,128)(2,1)S(1)}, u32[]{:S(2)}, u32[]{:S(2)}) collective-permute-start(bf16[816,128]{1,0:T(8,128)(2,1)} %get-tuple-element.76), channel_id=1, source_target_pairs={{0,8},{1,9},{2,10},{3,11},{4,12},{5,13},{6,14},{7,15},{8,0},{9,1},... | collective-permute-start | bytes 626696 | tf_op jit(solution)/shard_map/ppermute | solution.py:606
  133.2 2.1 %collective-permute-start.19 = (bf16[816,128]{1,0:T(8,128)(2,1)}, bf16[816,128]{1,0:T(8,128)(2,1)S(1)}, u32[]{:S(2)}, u32[]{:S(2)}) collective-permute-start(bf16[816,128]{1,0:T(8,128)(2,1)} %get-tuple-element.77), channel_id=1, source_target_pairs={{0,16},{1,17},{2,18},{3,19},{4,20},{5,21},{6,22},{7,23},{8,24},{9,... | collective-permute-start | bytes 626696 | tf_op jit(solution)/shard_map/ppermute | solution.py:606
  135.2 0.7 collective-permute-start.20
  136.0 5.1 %shard_map.331.refs_18_ = bf16[1024,512]{1,0:T(8,128)(2,1)} custom-call(bf16[32,64,128]{2,1,0:T(8,128)(2,1)S(1)} %all-to-all-done.3.refs_0_, bf16[1024,512]{1,0:T(8,128)(2,1)} %bitcast.39, f32[1024,512]{1,0:T(8,128)} %get-tuple-element.80.refs_2_, f32[13,512]{1,0:T(8,128)S(1)} %copy-done.14, bf16[1024,512]{1,0:T(8,128)(2,1)} %constant.61.clone.refs_4_), custom_call_target="tpu_custom_call" | custom-call | flops 536870912 | bytes 5793792 | tf_op jit(solution)/shard_map/pallas_call | solution.py:560
  141.1 0.8 collective-permute-done.18.refs_3_
  141.9 9.4 %collective-permute-done.19.refs_4_ = bf16[816,128]{1,0:T(8,128)(2,1)S(1)} collective-permute-done((bf16[816,128]{1,0:T(8,128)(2,1)}, bf16[816,128]{1,0:T(8,128)(2,1)S(1)}, u32[]{:S(2)}, u32[]{:S(2)}) %collective-permute-start.19) | collective-permute-done | bytes 208928 | tf_op jit(solution)/shard_map/ppermute | solution.py:606
  151.4 4.1 %shard_map.332 = (f32[32,1024]{1,0:T(8,128)}, f32[32,1024]{1,0:T(8,128)}, f32[32,1024]{1,0:T(8,128)}, f32[32,1024]{1,0:T(8,128)}, f32[32,1024]{1,0:T(8,128)}, /*...) custom-call(s32[1]{0:T(128)} %bitcast.refs_0_, ...), custom_call_target="tpu_custom_call", output_to_operand_aliasing={{14}: (18, {})} | custom-call | bytes 5976064 | tf_op jit(solution)/shard_map/pallas_call | solution.py:560
  (85 shorter events, 1.9 us)
Async XLA Ops:
  1.6 15.2 %copy-start.14 = (f32[13,512]{1,0:T(8,128)S(1)}, f32[13,512]{1,0:T(8,128)}, u32[]{:S(2)}) copy-start(f32[13,512]{1,0:T(8,128)} %refs_15_.1) | copy-start | bytes 79876
  1.7 19.4 %collective-permute-start.2 = (bf16[2,32,1024]{2,1,0:T(8,128)(2,1)S(1)}, bf16[2,32,1024]{2,1,0:T(8,128)(2,1)S(1)}, u32[]{:S(2)}, u32[]{:S(2)}) collective-permute-start(bf16[2,32,1024]{2,1,0:T(8,128)(2,1)S(1)} %get-tuple-element.101), channel_id=1, source_target_pairs={{0,16},{1,17},{2,18},{3,19},{4,20},{5,21},{6,22},{7,23},{8,24},{9,... | collective-permute-start | bytes 393224 | tf_op jit(solution)/shard_map/ppermute | solution.py:606
  5.8 13.3 %collective-permute-start = (bf16[2,32,1024]{2,1,0:T(8,128)(2,1)S(1)}, bf16[2,32,1024]{2,1,0:T(8,128)(2,1)S(1)}, u32[]{:S(2)}, u32[]{:S(2)}) collective-permute-start(bf16[2,32,1024]{2,1,0:T(8,128)(2,1)S(1)} %get-tuple-element.101), channel_id=1, source_target_pairs={{0,8},{1,9},{2,10},{3,11},{4,12},{5,13},{6,14},{7,15},{8,0},{9,1},... | collective-permute-start | bytes 393224 | tf_op jit(solution)/shard_map/ppermute | solution.py:606
  7.4 13.7 %collective-permute-start.3 = (bf16[2,32,1024]{2,1,0:T(8,128)(2,1)S(1)}, bf16[2,32,1024]{2,1,0:T(8,128)(2,1)S(1)}, u32[]{:S(2)}, u32[]{:S(2)}) collective-permute-start(bf16[2,32,1024]{2,1,0:T(8,128)(2,1)S(1)} %get-tuple-element.101), channel_id=1, source_target_pairs={{0,24},{1,25},{2,26},{3,27},{4,28},{5,29},{6,30},{7,31},{8,16},{9,... | collective-permute-start | bytes 393224 | tf_op jit(solution)/shard_map/ppermute | solution.py:606
  10.7 21.1 %all-to-all-start = ((bf16[32,64,128]{2,1,0:T(8,128)(2,1)}), bf16[32,64,128]{2,1,0:T(8,128)(2,1)S(1)}, u32[]{:S(2)}, u32[]{:S(2)}) async-start(bf16[32,64,128]{2,1,0:T(8,128)(2,1)} %shard_map.324), calls=%async_computation | async-start | bytes 1048576 | tf_op jit(solution)/shard_map/all_to_all | solution.py:639
  19.2 12.6 %copy-start.12 = (bf16[512,128]{1,0:T(8,128)(2,1)S(1)}, bf16[512,128]{1,0:T(8,128)(2,1)}, u32[]{:S(2)}) copy-start(bf16[512,128]{1,0:T(8,128)(2,1)} %constant.65.clone.refs_2_) | copy-start | bytes 393220
  19.2 12.6 %copy-start.13 = (bf16[128,512]{1,0:T(8,128)(2,1)S(1)}, bf16[128,512]{1,0:T(8,128)(2,1)}, u32[]{:S(2)}) copy-start(bf16[128,512]{1,0:T(8,128)(2,1)} %constant.64.clone.refs_1_) | copy-start | bytes 393220
  19.2 11.6 %collective-permute-start.1 = (bf16[2,2,32,1024]{3,2,1,0:T(8,128)(2,1)S(1)}, bf16[2,2,32,1024]{3,2,1,0:T(8,128)(2,1)S(1)}, u32[]{:S(2)}, u32[]{:S(2)}) collective-permute-start(bf16[2,2,32,1024]{3,2,1,0:T(8,128)(2,1)S(1)} %get-tuple-element.99), channel_id=1, source_target_pairs={{0,1},{1,0},{2,3},{3,2},{4,5},{5,4},{6,7},{7,6},{8,9},{9,8},{10,11... | collective-permute-start | bytes 786440 | tf_op jit(solution)/shard_map/ppermute | solution.py:606
  21.1 10.4 %collective-permute-start.4 = (bf16[2,2,32,1024]{3,2,1,0:T(8,128)(2,1)S(1)}, bf16[2,2,32,1024]{3,2,1,0:T(8,128)(2,1)S(1)}, u32[]{:S(2)}, u32[]{:S(2)}) collective-permute-start(bf16[2,2,32,1024]{3,2,1,0:T(8,128)(2,1)S(1)} %get-tuple-element.97), channel_id=1, source_target_pairs={{0,4},{1,5},{2,6},{3,7},{4,0},{5,1},{6,2},{7,3},{8,12},{9,13},{10,... | collective-permute-start | bytes 786440 | tf_op jit(solution)/shard_map/ppermute | solution.py:606
  23.0 11.1 %copy-start = (bf16[2,256,256]{2,1,0:T(8,128)(2,1)}, bf16[2,256,256]{2,1,0:T(8,128)(2,1)S(1)}, u32[]{:S(2)}) copy-start(bf16[2,256,256]{2,1,0:T(8,128)(2,1)S(1)} %maximum_maximum_fusion.refs_3_) | copy-start | bytes 786436
  34.1 22.1 %copy-start.1 = (bf16[2,2,2,32,1024]{4,3,2,1,0:T(8,128)(2,1)}, bf16[2,2,2,32,1024]{4,3,2,1,0:T(8,128)(2,1)S(1)}, u32[]{:S(2)}) copy-start(bf16[2,2,2,32,1024]{4,3,2,1,0:T(8,128)(2,1)S(1)} %get-tuple-element.57.refs_8_) | copy-start | bytes 1572868
  34.1 22.1 %copy-start.2 = (bf16[2,2,2,32,1024]{4,3,2,1,0:T(8,128)(2,1)}, bf16[2,2,2,32,1024]{4,3,2,1,0:T(8,128)(2,1)S(1)}, u32[]{:S(2)}) copy-start(bf16[2,2,2,32,1024]{4,3,2,1,0:T(8,128)(2,1)S(1)} %get-tuple-element.58.refs_9_) | copy-start | bytes 1572868
  34.1 18.1 %collective-permute-start.5 = (bf16[2,2,2,32,1024]{4,3,2,1,0:T(8,128)(2,1)S(1)}, bf16[2,2,2,32,1024]{4,3,2,1,0:T(8,128)(2,1)S(1)}, u32[]{:S(2)}, u32[]{:S(2)}) collective-permute-start(bf16[2,2,2,32,1024]{4,3,2,1,0:T(8,128)(2,1)S(1)} %get-tuple-element.57.refs_8_), channel_id=1, source_target_pairs={{0,4},{1,5},{2,6},{3,7},{4,0},{5,1},{6,2},{7,3},{8,12},{9,13},{10,... | collective-permute-start | bytes 1572872 | tf_op jit(solution)/shard_map/ppermute | solution.py:606
  35.6 18.5 %collective-permute-start.6 = (bf16[2,2,2,32,1024]{4,3,2,1,0:T(8,128)(2,1)S(1)}, bf16[2,2,2,32,1024]{4,3,2,1,0:T(8,128)(2,1)S(1)}, u32[]{:S(2)}, u32[]{:S(2)}) collective-permute-start(bf16[2,2,2,32,1024]{4,3,2,1,0:T(8,128)(2,1)S(1)} %get-tuple-element.58.refs_9_), channel_id=1, source_target_pairs={{0,1},{1,0},{2,3},{3,2},{4,5},{5,4},{6,7},{7,6},{8,9},{9,8},{10,11... | collective-permute-start | bytes 1572872 | tf_op jit(solution)/shard_map/ppermute | solution.py:606
  37.1 18.3 %all-to-all-start.1 = ((bf16[32,64,128]{2,1,0:T(8,128)(2,1)}), bf16[32,64,128]{2,1,0:T(8,128)(2,1)S(1)}, u32[]{:S(2)}, u32[]{:S(2)}) async-start(bf16[32,64,128]{2,1,0:T(8,128)(2,1)} %get-tuple-element.56), calls=%async_computation.1 | async-start | bytes 1048576 | tf_op jit(solution)/shard_map/all_to_all | solution.py:656
  40.6 13.6 %collective-permute-start.7 = (bf16[2,2,2,32,1024]{4,3,2,1,0:T(8,128)(2,1)S(1)}, bf16[2,2,2,32,1024]{4,3,2,1,0:T(8,128)(2,1)S(1)}, u32[]{:S(2)}, u32[]{:S(2)}) collective-permute-start(bf16[2,2,2,32,1024]{4,3,2,1,0:T(8,128)(2,1)S(1)} %get-tuple-element.57.refs_8_), channel_id=1, source_target_pairs={{0,2},{1,3},{2,0},{3,1},{4,6},{5,7},{6,4},{7,5},{8,10},{9,11},{10,... | collective-permute-start | bytes 1572872 | tf_op jit(solution)/shard_map/ppermute | solution.py:606
  40.9 13.3 %collective-permute-start.8 = (bf16[2,2,2,32,1024]{4,3,2,1,0:T(8,128)(2,1)S(1)}, bf16[2,2,2,32,1024]{4,3,2,1,0:T(8,128)(2,1)}, u32[]{:S(2)}, u32[]{:S(2)}) collective-permute-start(bf16[2,2,2,32,1024]{4,3,2,1,0:T(8,128)(2,1)S(1)} %get-tuple-element.58.refs_9_), channel_id=1, source_target_pairs={{0,2},{1,3},{2,0},{3,1},{4,6},{5,7},{6,4},{7,5},{8,10},{9,11},{10,... | collective-permute-start | bytes 1572872 | tf_op jit(solution)/shard_map/ppermute | solution.py:606
  52.2 4.0 %copy-start.23 = (bf16[2,2,2,32,1024]{4,3,2,1,0:T(8,128)(2,1)}, bf16[2,2,2,32,1024]{4,3,2,1,0:T(8,128)(2,1)S(1)}, u32[]{:S(2)}) copy-start(bf16[2,2,2,32,1024]{4,3,2,1,0:T(8,128)(2,1)S(1)} %collective-permute-done.5.refs_10_) | copy-start | bytes 1572868
  52.2 3.9 %collective-permute-start.9 = (bf16[2,2,2,32,1024]{4,3,2,1,0:T(8,128)(2,1)S(1)}, bf16[2,2,2,32,1024]{4,3,2,1,0:T(8,128)(2,1)}, u32[]{:S(2)}, u32[]{:S(2)}) collective-permute-start(bf16[2,2,2,32,1024]{4,3,2,1,0:T(8,128)(2,1)S(1)} %collective-permute-done.5.refs_10_), channel_id=1, source_target_pairs={{0,2},{1,3},{2,0},{3,1},{4,6},{5,7},{6,4},{7,5},{8,10},{9,11},{10,... | collective-permute-start | bytes 1572872 | tf_op jit(solution)/shard_map/ppermute | solution.py:606
  54.2 2.0 %copy-start.24 = (bf16[2,2,2,32,1024]{4,3,2,1,0:T(8,128)(2,1)}, bf16[2,2,2,32,1024]{4,3,2,1,0:T(8,128)(2,1)S(1)}, u32[]{:S(2)}) copy-start(bf16[2,2,2,32,1024]{4,3,2,1,0:T(8,128)(2,1)S(1)} %collective-permute-done.6.refs_11_) | copy-start | bytes 1572868
  54.2 2.0 %collective-permute-start.10 = (bf16[2,2,2,32,1024]{4,3,2,1,0:T(8,128)(2,1)S(1)}, bf16[2,2,2,32,1024]{4,3,2,1,0:T(8,128)(2,1)}, u32[]{:S(2)}, u32[]{:S(2)}) collective-permute-start(bf16[2,2,2,32,1024]{4,3,2,1,0:T(8,128)(2,1)S(1)} %collective-permute-done.6.refs_11_), channel_id=1, source_target_pairs={{0,2},{1,3},{2,0},{3,1},{4,6},{5,7},{6,4},{7,5},{8,10},{9,11},{10,... | collective-permute-start | bytes 1572872 | tf_op jit(solution)/shard_map/ppermute | solution.py:606
  54.2 2.0 %copy-start.25 = (bf16[2,2,2,32,1024]{4,3,2,1,0:T(8,128)(2,1)}, bf16[2,2,2,32,1024]{4,3,2,1,0:T(8,128)(2,1)S(1)}, u32[]{:S(2)}) copy-start(bf16[2,2,2,32,1024]{4,3,2,1,0:T(8,128)(2,1)S(1)} %collective-permute-done.7.refs_12_) | copy-start | bytes 1572868
  56.2 1.0 copy-start.10
  82.4 1.1 copy-start.11
  82.4 5.2 %collective-permute-start.11 = (bf16[2,2,2,4,256,128]{5,4,3,2,1,0:T(8,128)(2,1)}, bf16[2,2,2,4,256,128]{5,4,3,2,1,0:T(8,128)(2,1)}, u32[]{:S(2)}, u32[]{:S(2)}) collective-permute-start(bf16[2,2,2,4,256,128]{5,4,3,2,1,0:T(8,128)(2,1)} %get-tuple-element.61), channel_id=1, source_target_pairs={{0,2},{1,3},{2,0},{3,1},{4,6},{5,7},{6,4},{7,5},{8,10},{9,11},{10,... | collective-permute-start | bytes 6291464 | tf_op jit(solution)/shard_map/ppermute | solution.py:606
  83.6 18.3 %all-to-all-start.2 = ((bf16[32,64,128]{2,1,0:T(8,128)(2,1)}), bf16[32,64,128]{2,1,0:T(8,128)(2,1)S(1)}, u32[]{:S(2)}, u32[]{:S(2)}) async-start(bf16[32,64,128]{2,1,0:T(8,128)(2,1)} %copy-done.11), calls=%async_computation.2 | async-start | bytes 1048576 | tf_op jit(solution)/shard_map/all_to_all | solution.py:689
  90.4 20.1 %collective-permute-start.12 = (bf16[2,4,256,128]{3,2,1,0:T(8,128)(2,1)}, bf16[2,4,256,128]{3,2,1,0:T(8,128)(2,1)S(1)}, u32[]{:S(2)}, u32[]{:S(2)}) collective-permute-start(bf16[2,4,256,128]{3,2,1,0:T(8,128)(2,1)} %get-tuple-element.62), channel_id=1, source_target_pairs={{0,1},{1,0},{2,3},{3,2},{4,5},{5,4},{6,7},{7,6},{8,9},{9,8},{10,11... | collective-permute-start | bytes 1572872 | tf_op jit(solution)/shard_map/ppermute | solution.py:606
  91.5 19.0 %collective-permute-start.13 = (bf16[2,4,256,128]{3,2,1,0:T(8,128)(2,1)}, bf16[2,4,256,128]{3,2,1,0:T(8,128)(2,1)}, u32[]{:S(2)}, u32[]{:S(2)}) collective-permute-start(bf16[2,4,256,128]{3,2,1,0:T(8,128)(2,1)} %get-tuple-element.63), channel_id=1, source_target_pairs={{0,4},{1,5},{2,6},{3,7},{4,0},{5,1},{6,2},{7,3},{8,12},{9,13},{10,... | collective-permute-start | bytes 1572872 | tf_op jit(solution)/shard_map/ppermute | solution.py:606
  105.5 30.4 %all-to-all-start.3 = ((bf16[32,64,128]{2,1,0:T(8,128)(2,1)}), bf16[32,64,128]{2,1,0:T(8,128)(2,1)S(1)}, u32[]{:S(2)}, u32[]{:S(2)}) async-start(bf16[32,64,128]{2,1,0:T(8,128)(2,1)} %copy-done.8), calls=%async_computation.3 | async-start | bytes 1048576 | tf_op jit(solution)/shard_map/all_to_all | solution.py:709
  109.1 1.3 collective-permute-start.14
  112.3 15.9 %collective-permute-start.15 = (bf16[1328,128]{1,0:T(8,128)(2,1)S(1)}, bf16[1328,128]{1,0:T(8,128)(2,1)S(1)}, u32[]{:S(2)}, u32[]{:S(2)}) collective-permute-start(bf16[1328,128]{1,0:T(8,128)(2,1)S(1)} %get-tuple-element.71), channel_id=1, source_target_pairs={{0,4},{1,5},{2,6},{3,7},{4,0},{5,1},{6,2},{7,3},{8,12},{9,13},{10,... | collective-permute-start | bytes 1019912 | tf_op jit(solution)/shard_map/ppermute | solution.py:606
  114.2 14.1 %collective-permute-start.16 = (bf16[1328,128]{1,0:T(8,128)(2,1)S(1)}, bf16[1328,128]{1,0:T(8,128)(2,1)S(1)}, u32[]{:S(2)}, u32[]{:S(2)}) collective-permute-start(bf16[1328,128]{1,0:T(8,128)(2,1)S(1)} %get-tuple-element.72), channel_id=1, source_target_pairs={{0,1},{1,0},{2,3},{3,2},{4,5},{5,4},{6,7},{7,6},{8,9},{9,8},{10,11... | collective-permute-start | bytes 1019912 | tf_op jit(solution)/shard_map/ppermute | solution.py:606
  115.6 12.6 %collective-permute-start.17 = (bf16[304,128]{1,0:T(8,128)(2,1)S(1)}, bf16[304,128]{1,0:T(8,128)(2,1)S(1)}, u32[]{:S(2)}, u32[]{:S(2)}) collective-permute-start(bf16[304,128]{1,0:T(8,128)(2,1)S(1)} %get-tuple-element.73.refs_6_), channel_id=1, source_target_pairs={{0,5},{1,4},{2,7},{3,6},{4,1},{5,0},{6,3},{7,2},{8,13},{9,12},{10,... | collective-permute-start | bytes 233480 | tf_op jit(solution)/shard_map/ppermute | solution.py:606
  131.5 10.4 %collective-permute-start.18 = (bf16[816,128]{1,0:T(8,128)(2,1)}, bf16[816,128]{1,0:T(8,128)(2,1)S(1)}, u32[]{:S(2)}, u32[]{:S(2)}) collective-permute-start(bf16[816,128]{1,0:T(8,128)(2,1)} %get-tuple-element.76), channel_id=1, source_target_pairs={{0,8},{1,9},{2,10},{3,11},{4,12},{5,13},{6,14},{7,15},{8,0},{9,1},... | collective-permute-start | bytes 626696 | tf_op jit(solution)/shard_map/ppermute | solution.py:606
  133.2 18.2 %collective-permute-start.19 = (bf16[816,128]{1,0:T(8,128)(2,1)}, bf16[816,128]{1,0:T(8,128)(2,1)S(1)}, u32[]{:S(2)}, u32[]{:S(2)}) collective-permute-start(bf16[816,128]{1,0:T(8,128)(2,1)} %get-tuple-element.77), channel_id=1, source_target_pairs={{0,16},{1,17},{2,18},{3,19},{4,20},{5,21},{6,22},{7,23},{8,24},{9,... | collective-permute-start | bytes 626696 | tf_op jit(solution)/shard_map/ppermute | solution.py:606
  135.2 16.1 %collective-permute-start.20 = (bf16[816,128]{1,0:T(8,128)(2,1)}, bf16[816,128]{1,0:T(8,128)(2,1)S(1)}, u32[]{:S(2)}, u32[]{:S(2)}) collective-permute-start(bf16[816,128]{1,0:T(8,128)(2,1)} %get-tuple-element.78), channel_id=1, source_target_pairs={{0,24},{1,25},{2,26},{3,27},{4,28},{5,29},{6,30},{7,31},{8,16},{9,... | collective-permute-start | bytes 626696 | tf_op jit(solution)/shard_map/ppermute | solution.py:606
  135.9 15.4 %copy-start.3 = (f32[2,8,2,64,64]{4,3,2,1,0:T(8,128)S(1)}, f32[2,8,2,64,64]{4,3,2,1,0:T(8,128)}, u32[]{:S(2)}) copy-start(f32[2,8,2,64,64]{4,3,2,1,0:T(8,128)} %refs_12_.1) | copy-start | bytes 1572868
  135.9 15.4 %copy-start.4 = (f32[2,8,2,64,64]{4,3,2,1,0:T(8,128)S(1)}, f32[2,8,2,64,64]{4,3,2,1,0:T(8,128)}, u32[]{:S(2)}) copy-start(f32[2,8,2,64,64]{4,3,2,1,0:T(8,128)} %refs_13_.1) | copy-start | bytes 1572868
  135.9 15.4 %copy-start.5 = (f32[2,8,2,64,64]{4,3,2,1,0:T(8,128)S(1)}, f32[2,8,2,64,64]{4,3,2,1,0:T(8,128)}, u32[]{:S(2)}) copy-start(f32[2,8,2,64,64]{4,3,2,1,0:T(8,128)} %refs_14_.1) | copy-start | bytes 1572868
  135.9 15.4 %copy-start.6 = (f32[32,1024]{1,0:T(8,128)S(1)}, f32[32,1024]{1,0:T(8,128)}, u32[]{:S(2)}) copy-start(f32[32,1024]{1,0:T(8,128)} %refs_7_.2) | copy-start | bytes 393220
  135.9 15.4 %copy-start.7 = (f32[32,1024]{1,0:T(8,128)S(1)}, f32[32,1024]{1,0:T(8,128)}, u32[]{:S(2)}) copy-start(f32[32,1024]{1,0:T(8,128)} %refs_6_.1) | copy-start | bytes 393220
  135.9 15.4 %copy-start.15 = (f32[32,1024]{1,0:T(8,128)S(1)}, f32[32,1024]{1,0:T(8,128)}, u32[]{:S(2)}) copy-start(f32[32,1024]{1,0:T(8,128)} %refs_8_.1) | copy-start | bytes 393220
  136.0 15.4 %copy-start.16 = (f32[32,1024]{1,0:T(8,128)S(1)}, f32[32,1024]{1,0:T(8,128)}, u32[]{:S(2)}) copy-start(f32[32,1024]{1,0:T(8,128)} %refs_9_.1) | copy-start | bytes 393220
  136.0 15.4 %copy-start.17 = (f32[32,1024]{1,0:T(8,128)S(1)}, f32[32,1024]{1,0:T(8,128)}, u32[]{:S(2)}) copy-start(f32[32,1024]{1,0:T(8,128)} %refs_10_.1) | copy-start | bytes 393220
  136.0 15.4 %copy-start.18 = (f32[32,1024]{1,0:T(8,128)S(1)}, f32[32,1024]{1,0:T(8,128)}, u32[]{:S(2)}) copy-start(f32[32,1024]{1,0:T(8,128)} %refs_11_.1) | copy-start | bytes 393220
  136.0 15.4 %copy-start.20 = (bf16[304,128]{1,0:T(8,128)(2,1)S(1)}, bf16[304,128]{1,0:T(8,128)(2,1)}, u32[]{:S(2)}) copy-start(bf16[304,128]{1,0:T(8,128)(2,1)} %copy-done.19) | copy-start | bytes 233476
  136.0 15.4 %copy-start.21 = (f32[13,512]{1,0:T(8,128)S(1)}, f32[13,512]{1,0:T(8,128)}, u32[]{:S(2)}) copy-start(f32[13,512]{1,0:T(8,128)} %refs_16_.1) | copy-start | bytes 79876
  136.0 15.4 %copy-start.22 = (f32[13,512]{1,0:T(8,128)S(1)}, f32[13,512]{1,0:T(8,128)}, u32[]{:S(2)}) copy-start(f32[13,512]{1,0:T(8,128)} %refs_17_.1) | copy-start | bytes 79876
  (3 other events, 2.2 us)

commit v3 on v2

--- a/solution.py
+++ b/solution.py
@@ -200,8 +200,8 @@
 
 
 def unmix_kernel(
-    modes, block, got_ref, high_ref, back_ref, mats_ref, ones_ref, hat_ref, modal_ref, inner_ref, active_ref,
-    mlp_ref, send_ref, small_ref,
+    modes, block, place_ref, got_ref, high_ref, back_ref, mats_ref, ones_ref, hat_ref, modal_ref, inner_ref, active_ref,
+    mlp_ref, send_ref, keep_ref, give_ref,
 ):
     width = got_ref.shape[2]
     grad_outer = dot(high_ref[...], gather_modes(got_ref, modes)).astype(BF16)
@@ -212,6 +212,7 @@
     grad_modal = from_mix_rows(grad_modal, modes, width)
     spectrum = dot(back_ref[...], grad_modal).astype(BF16)
     scatter_modes(send_ref, spectrum, modes)
+    send_ref.flush()
     rows = 2 * block
     grads = [fold(dot_tn(modal_ref[...], grad_inner), width, block)]
     grads.append(fold(dot_tn(active_ref[...], grad_outer), width, block))
@@ -226,10 +227,16 @@
         shift = shift + jnp.sum(upstream * ones_ref[:, k : k + 1], axis=0, keepdims=True)
     tail = jnp.concatenate(bias_one + bias_two + [gain, shift, jnp.zeros((2, width), F32)], axis=0)
     mlp = [mlp_ref[:, q : q + width] for q in range(0, mlp_ref.shape[1], width)]
-    message = jnp.concatenate(grads + [tail] + mlp, axis=0).astype(BF16)
-    small_ref[0 : message.shape[0]] = message
-    rest = small_ref.shape[0] - message.shape[0]
-    small_ref[message.shape[0] :] = jnp.zeros((rest, width), BF16)
+    count = len(mlp) // 2
+    rows = keep_ref.shape[0] - 2 * block - 8 - 8 * count
+    rest = [jnp.zeros((rows, width), F32)] if rows else []
+    for half, parts in enumerate(([grads[0], tail] + mlp[:count], [grads[1], jnp.zeros_like(tail)] + mlp[count:])):
+        message = jnp.concatenate(parts + rest, axis=0).astype(BF16)
+        for ref, core in ((keep_ref, half), (give_ref, 1 - half)):
+
+            @pl.when(place_ref[0] == core)
+            def _(ref=ref, message=message):
+                ref[...] = message
 
 
 def add_up(*values):
@@ -241,49 +248,49 @@
 
 def first_kernel(kept_ref, one_ref, in_ref, out_ref):
     for part, ref in enumerate((in_ref, out_ref)):
-        ref[...] = add_up(kept_ref[part, 1], one_ref[part, 1]).astype(BF16)
-
-
-def second_kernel(kept_ref, one_ref, in_ref, out_ref, mine_ref, core_ref, y_ref, x_ref, small_ref):
-    small = add_up(mine_ref[...], core_ref[...]).astype(BF16)
-    small_ref[...] = small
+        ref[...] = add_up(kept_ref[part, 1], one_ref[part]).astype(BF16)
+
+
+def second_kernel(kept_ref, in_ref, out_ref, mine_ref, core_ref, one_ref, small_ref, y_ref, x_ref):
+    small_ref[...] = add_up(mine_ref[...], core_ref[...]).astype(BF16)
     for part, source, ref in ((0, in_ref, y_ref), (1, out_ref, x_ref)):
-        rows = 0
-        for z in range(4):
-            value = add_up(kept_ref[part, 0, 1, z], one_ref[part, 0, 1, z], source[1, z]).astype(BF16)
-            ref[rows : rows + value.shape[0]] = value
-            rows += value.shape[0]
-        ref[rows:] = small
-
-
-def third_kernel(kept_ref, one_ref, in_ref, out_ref, y_ref, x_ref, small_ref, other_ref, own_ref, mine_ref, *away_refs):
-    size = kept_ref.shape[4]
-    along_x = small_ref[...].astype(F32) + x_ref[4 * size :].astype(F32)
-    along_y = y_ref[4 * size :].astype(F32) + other_ref[...].astype(F32)
-    small = (along_x + along_y).astype(BF16)
-    mine_ref[...] = small
+        ref[...] = add_up(kept_ref[part, 0, 1], one_ref[part], source[1]).astype(BF16)
+
+
+def third_kernel(place_ref, kept_ref, in_ref, out_ref, y_ref, x_ref, *refs):
+    small_refs, (one_ref, line_ref, own_ref), away_refs = refs[:4], refs[4:7], refs[7:]
+    for z, ref in enumerate(small_refs):
+        line_ref[(place_ref[0] >> 3) ^ z] = ref[...]
     for part, source, last in ((0, in_ref, y_ref), (1, out_ref, x_ref)):
         for z in range(4):
-            rows = slice(z * size, (z + 1) * size)
-            total = add_up(kept_ref[part, 0, 0, z], one_ref[part, 0, 0, z], source[0, z], last[rows])
+            total = add_up(kept_ref[part, 0, 0, z], one_ref[part, z], source[0, z], last[z])
             if z == 0:
                 own_ref[part] = total
             else:
-                away_refs[z - 1][part * size : (part + 1) * size] = total.astype(BF16)
-    for ref in away_refs:
-        ref[2 * size :] = small
-
-
-def step_small(
-    block, scale, held, mixer_ref, moment_ref, average_ref, vectors_ref, vec_moment_ref,
+                away_refs[z - 1][part] = total.astype(BF16)
+
+
+def plane_kernel(mine_ref, x_ref, y_ref, other_ref, total_ref):
+    total_ref[...] = (add_up(mine_ref[...], x_ref[...]) + add_up(y_ref[...], other_ref[...])).astype(BF16)
+
+
+def step_rest(
+    block, scale, place_ref, own_ref, other_ref, mixer_ref, moment_ref, average_ref, vectors_ref, vec_moment_ref,
     vec_average_ref, new_mixer, new_moment, new_average, new_vectors, new_vec_moment, new_vec_average, grad_ref,
 ):
-    groups, _, width = held.shape
+    groups, _, width = own_ref.shape
     joined = width // block
     rows = 2 * block
+    slices = groups // 2
+    core = place_ref[0]
+
+    def held(half, group, part):
+        mine, theirs = own_ref[group, part, :], other_ref[group, part, :]
+        return jnp.where(core == half, mine, theirs).astype(F32)
+
     for group in range(groups):
         for layer in range(2):
-            grad = held[group, layer * rows : (layer + 1) * rows] * scale
+            grad = held(layer, group, slice(0, rows)) * scale
             for part in range(2):
                 for j in range(joined):
                     b = group * joined + j
@@ -295,7 +302,10 @@
                     new_mixer[layer, b, part] = value
                     new_moment[layer, b, part] = moment
                     new_average[layer, b, part] = average
-        tail = held[group, 2 * rows : 2 * rows + 8]
+    for ref in (new_mixer, new_moment, new_average):
+        ref.flush()
+    for group in range(groups):
+        tail = held(0, group, slice(rows, rows + 16))
         grad_ref[0:2, group * width : (group + 1) * width] = tail[4:6]
         for layer in range(2):
             for j in range(2):
@@ -304,12 +314,14 @@
                 lane = (b % per_row) * 2 * block + (0 if joined == 2 else j * block)
                 row = 9 + layer * 2 + b // per_row
                 grad_ref[row : row + 1, lane : lane + width] = tail[2 * layer + j : 2 * layer + j + 1]
-    for q in range(groups):
-        part = slice(2 * rows + 8 + 8 * q, 2 * rows + 16 + 8 * q)
-        total = held[0, part]
+    for half in range(2):
+        part = slice(rows, rows + 8 + 8 * slices + 8 * ((slices + 1) % 2))
+        total = held(half, 0, part)
         for group in range(1, groups):
-            total = total + held[group, part]
-        grad_ref[2:9, q * width : (q + 1) * width] = total[0:7]
+            total = total + held(half, group, part)
+        for q in range(slices):
+            lane = (half * slices + q) * width
+            grad_ref[2:9, lane : lane + width] = total[8 + 8 * q : 15 + 8 * q]
     value, moment, average = update(
         vectors_ref[...], grad_ref[0:13, :] * scale, vec_moment_ref[...], vec_average_ref[...], 0.0
     )
@@ -318,19 +330,17 @@
     new_vec_average[...] = average
 
 
-def step_all(block, scale, place_ref, own_ref, mine_ref, *refs):
-    away_refs, weights, small = refs[:3], refs[3:9], refs[9:15]
-    new_weights, new_small, (held, grad_ref) = refs[15:23], refs[23:29], refs[29:]
-    size = own_ref.shape[1]
-    far = place_ref[0] >> 3
-    held[far] = mine_ref[...].astype(F32)
-    for z, ref in enumerate(away_refs):
-        held[far ^ (z + 1)] = ref[2 * size :].astype(F32)
+def step_all(block, scale, place_ref, *refs):
+    step_weights(scale, *refs[:10], *refs[18:26])
+    step_rest(block, scale, place_ref, *refs[10:18], *refs[26:])
+
+
+def step_weights(scale, own_ref, *refs):
+    away_refs, weights, new_weights = refs[:3], refs[3:9], refs[9:17]
     for part in range(2):
-        rows = slice(part * size, (part + 1) * size)
-        total = own_ref[part] + add_up(*[ref[rows] for ref in away_refs])
+        total = add_up(own_ref[part], *[ref[part] for ref in away_refs])
         count = weights[part].shape[0]
-        for q in range(size // count):
+        for q in range(total.shape[0] // count):
             lanes = slice(q * 128, (q + 1) * 128)
             grad = total[q * count : (q + 1) * count] * scale
             values = update(
@@ -339,7 +349,8 @@
             for i, value in enumerate(values):
                 new_weights[2 * i + part][:, lanes] = value
             new_weights[6 + part][:, lanes] = values[0].astype(BF16)
-    step_small(block, scale, held, *small, *new_small, grad_ref)
+    for ref in new_weights:
+        ref.flush()
 
 
 def load_weights(near, place_ref, pieces, w_in, w_out, sems):
@@ -427,6 +438,7 @@
     small_ref[7:8, :] = jnp.zeros((1, width), F32)
     spectrum = dot(wide_ref[...], upstream_ref[...]).astype(BF16)
     scatter_lanes(send_ref, spectrum, groups)
+    send_ref.flush()
     for i, (h, c) in enumerate(chunks):
         flat = slice(h * columns + c, h * columns + c + CHUNK)
         grads = [
@@ -508,6 +520,7 @@
 def call(body, outs, *args, scalars=(), raw=(), scratch=(), flops=0, carry=(), cost=None, vmem=20):
     near, far, there = [pl.BlockSpec(memory_space=m) for m in (pltpu.VMEM, pltpu.HBM, pl.ANY)]
     in_far, out_far = [isinstance(a, Far) for a in args], [isinstance(o, Far) for o in outs]
+    index = [a.what[1:] if f else () for a, f in zip(args, in_far, strict=True)]
     args = [
         pltpu.with_memory_space_constraint(*((a.what[0], pltpu.HBM) if f else (a, pltpu.VMEM)))
         for a, f in zip(args, in_far, strict=True)
@@ -516,7 +529,11 @@
     outs = [o.what if f else o for o, f in zip(outs, out_far, strict=True)]
     outs = [jax.ShapeDtypeStruct(s, d) for s, d in outs]
     n_scalar, n_in, n_raw, n_carry, n_out = len(scalars), len(args), len(raw), len(carry), len(outs)
-    buffers = [pltpu.VMEM(a.shape, a.dtype) for a, f in zip(args + outs, in_far + out_far, strict=True) if f]
+    shapes = [np.empty(a.shape, np.bool_)[i].shape if i else a.shape for a, i in zip(args, index, strict=True)]
+    shapes += [o.shape for o in outs]
+    buffers = [
+        pltpu.VMEM(shape, a.dtype) for shape, a, f in zip(shapes, args + outs, in_far + out_far, strict=True) if f
+    ]
 
     def inner(*refs):
         refs = list(refs)
@@ -532,9 +549,9 @@
         space = take(len(buffers))
         sems = take(1)[0] if buffers else None
         sources, sinks, used = [], [], 0
-        for ref, away in zip(in_refs, in_far, strict=True):
+        for ref, away, part in zip(in_refs, in_far, index, strict=True):
             if away:
-                copy = pltpu.make_async_copy(ref, space[used], sems.at[used])
+                copy = pltpu.make_async_copy(ref.at[part] if part else ref, space[used], sems.at[used])
                 copy.start()
                 ref = Source(space[used], copy)
                 used += 1
@@ -658,8 +675,8 @@
     grads = [((2, 2, 2, 4, shard_size, 128), BF16)] * 2 if near else [((tp_count, model, shard_columns), BF16)] * 2
     output, middle, sent, mlp_small, *grads = call(
         functools.partial(mlp_kernel, groups, near),
-        [Far((local, width), BF16), Far((local, width), F32), (chunk, BF16), ((8, width), F32)] + grads,
-        got, Far(wide_i_t), Far(rows_all), Far(upstream_all), vectors, vectors[5:9].reshape(steps, CHUNK), Far(wide_i),
+        [Far((local, width), BF16), Far((local, width), F32), Far(chunk, BF16), ((8, width), F32)] + grads,
+        Far(got), Far(wide_i_t), Far(rows_all), Far(upstream_all), vectors, vectors[5:9].reshape(steps, CHUNK), Far(wide_i),
         scalars=[me[None]], raw=pieces,
         scratch=[
             pltpu.VMEM((local, width), BF16),
@@ -682,47 +699,55 @@
         shard = (4, shard_size, 128)
         kept, one = grads[0], permute(grads[1], 2)
         sent_in, sent_out = call(
-            first_kernel, [((2,) + shard, BF16)] * 2, kept, one, cost=0,
+            first_kernel, [((2,) + shard, BF16)] * 2, kept, Far(one, slice(None), 1), cost=0
         )
         carried = [permute(sent_in, 1), permute(sent_out, 4)]
 
     got = exchange(sent)
-    small_rows = -(-(4 * block + 8 + 8 * groups) // 16) * 16
-    sent, small = call(
+    small_rows = -(-(2 * block + 8 + 8 * (groups // 2)) // 16) * 16
+    place = ((me >> 1) & 1 if near else jnp.int32(0))[None]
+    sent, small, given = call(
         functools.partial(unmix_kernel, modes, block),
-        [(chunk, BF16), ((small_rows, lanes), BF16)],
+        [Far(chunk, BF16), ((small_rows, lanes), BF16), ((small_rows, lanes), BF16)],
         got, Far(high), Far(high_t), Far(mats), own_ones, Far(hat), Far(modal), Far(inner), Far(active), mlp_small,
-        cost=COST,
+        scalars=[place], cost=COST, vmem=20 if near else 48,
     )
     if near:
-        over_y, over_x, small = call(
-            second_kernel, [((4 * shard_size + small_rows, 128), BF16)] * 2 + [((small_rows, 128), BF16)],
-            kept, one, *carried, small, permute(small, 2), cost=0,
+        both = slice(None)
+        small, over_y, over_x = call(
+            second_kernel, [((small_rows, lanes), BF16)] + [(shard, BF16)] * 2,
+            kept, *carried, small, permute(given, 2), Far(one, both, 0, 1), cost=0,
         )
-        from_y, from_x, from_both = permute(over_y, 4), permute(over_x, 1), permute(small, 5)
-        own, mine, *away = call(
+        line, own, *away = call(
             third_kernel,
-            [((2, shard_size, 128), F32), ((small_rows, 128), BF16)] + [((2 * shard_size + small_rows, 128), BF16)] * 3,
-            kept, one, *carried, from_y, from_x, small, from_both, cost=0,
+            [((4, small_rows, lanes), BF16), ((2, shard_size, 128), F32)] + [((2, shard_size, 128), BF16)] * 3,
+            kept, *carried, permute(over_y, 4), permute(over_x, 1),
+            small, *[permute(small, 8 * z) for z in (1, 2, 3)], Far(one, both, 0, 0),
+            scalars=[me[None]], cost=0,
         )
         away = [permute(a, 8 * (z + 1)) for z, a in enumerate(away)]
     got = exchange(sent)
     (grad_tokens,) = call(
         functools.partial(leave_kernel, groups),
         [Far((local, width), BF16)],
-        got, Far(rows_all), Far(middle), vectors, Far(wide_f_t), flops=wide_flops,
-    )
+        got, Far(rows_all), Far(middle), vectors, Far(wide_f_t), cost=COST,
+    )
+
+    if near:
+        line, *away, grad_tokens = call(
+            plane_kernel, [(line.shape, BF16)], line, *[permute(line, m) for m in (1, 4, 5)], cost=0, carry=[*away, grad_tokens]
+        )
+        other = permute(line, 2)
 
     state = [mixer_weights, mixer_moment, mixer_average, vectors, vectors_moment, vectors_average]
     new_state = [Far(a.shape, F32) for a in state]
-    scratch = [pltpu.VMEM((16, width), F32)]
     if near:
         weights = [w_in, w_out, w_in_moment, w_out_moment, w_in_average, w_out_average]
         *stepped, grad_tokens = call(
             functools.partial(step_all, block, scale),
             [Far(w_in.shape, F32)] * 6 + [Far(w_in.shape, BF16)] * 2 + new_state,
-            own, mine, *away, *weights, *state,
-            scalars=[me[None]], scratch=[pltpu.VMEM((groups, small_rows, lanes), F32)] + scratch, carry=[grad_tokens],
+            own, *away, *weights, line, other, *state,
+            scalars=[place], scratch=[pltpu.VMEM((16, width), F32)], carry=[grad_tokens], cost=0,
         )
         new_in, new_out = stepped[0:8:2], stepped[1:8:2]
         stepped = stepped[8:]
@@ -734,8 +759,11 @@
         new_out = update(w_out, grads[1, 0] * scale, w_out_moment, w_out_average, WEIGHT_DECAY)
         new_in, new_out = new_in + (new_in[0].astype(BF16),), new_out + (new_out[0].astype(BF16),)
         onehot = (jnp.arange(groups, dtype=jnp.int32) == group).astype(F32)[:, None, None]
-        held = lax.psum(onehot * small.astype(F32), AXES)
-        stepped = call(functools.partial(step_small, block, scale), new_state, held, *state, scratch=scratch)
+        line, other = lax.psum((onehot * small.astype(F32), onehot * given.astype(F32)), AXES)
+        stepped = call(
+            functools.partial(step_rest, block, scale), new_state, line, other, *state,
+            scalars=[place], scratch=[pltpu.VMEM((16, width), F32)],
+        )
     new_mix, new_vec = stepped[0:3], stepped[3:6]
     shape = tokens.shape
     return (

time: 157 us -> 150 us (0.955)
  waiting for transfers between devices: 56 us -> 44.9 us
  starting transfers between devices: 41.2 us -> 47.1 us
  local copies, waits for them, and re-layouts: 5.63 us -> 2.78 us
  Pallas kernels: 49.9 us -> 51.5 us
    ppermute x21 -> x27, waiting for transfers between devices: 45.5 us -> 34.3 us  [permute(): return lax.ppermute(values, AXES, [(d, d ^ mask) for d in range(devices)])]
    ppermute x21 -> x27, starting transfers between devices: 24.8 us -> 31.9 us  [permute(): return lax.ppermute(values, AXES, [(d, d ^ mask) for d in range(devices)])]
    unnamed x53 -> x43, local copies, waits for them, and re-layouts: 3.37 us -> 0.53 us
    pallas_call x9 -> x10, Pallas kernels: 49.9 us -> 51.5 us  [call(): pl.pallas_call(inner, out_shape=[(pltpu.HBM if f else pltpu.VMEM)(o.shape...]
  transfers between devices with their start and end apart: 25 -> 31, of which waited for: 12 -> 13; matrix products, arithmetic and copies ran while one was open for 2% -> 2% of each run, Pallas kernels for 12% -> 13%
where the time goes in v3:
time: 150 us; the launch traced here: 149 us
  Pallas kernels  51.5 us (34%)
  starting transfers between devices  47.1 us (31%)
  waiting for transfers between devices  44.9 us (30%)
  local copies, waits for them, and re-layouts  2.78 us (2%)
  other arithmetic  1.54 us (1%)
    pallas_call x10, Pallas kernels, call(): pl.pallas_call(inner, out_shape=[(pltpu.HBM if f else pltpu.VMEM)(o.shape...  51.5 us
    ppermute x27, waiting for transfers between devices, permute(): return lax.ppermute(values, AXES, [(d, d ^ mask) for d in range(devices)])  34.3 us
    ppermute x27, starting transfers between devices, permute(): return lax.ppermute(values, AXES, [(d, d ^ mask) for d in range(devices)])  31.9 us
    all_to_all x4, starting transfers between devices, on_device(): got = exchange(sent)  15.2 us
    all_to_all x4, waiting for transfers between devices, on_device(): got = exchange(sent)  10.7 us
  transfers between devices with their start and end apart: 31, of which 13 were waited for; matrix products, arithmetic and copies ran while one was open for 2% of the time, Pallas kernels for 13%

profile of v3, /device:TPU:0, one launch (start us, length us, event | category | flops | bytes accessed | tf_op | source)
XLA Modules:
  0.0 149.2 jit_solution(1917123701100605487)
XLA Ops:
  0.6 1.0 convert_bitcast_fusion
  1.7 4.1 %collective-permute-start.2 = (bf16[2,32,1024]{2,1,0:T(8,128)(2,1)S(1)}, bf16[2,32,1024]{2,1,0:T(8,128)(2,1)S(1)}, u32[]{:S(2)}, u32[]{:S(2)}) collective-permute-start(bf16[2,32,1024]{2,1,0:T(8,128)(2,1)S(1)} %get-tuple-element.113), channel_id=1, source_target_pairs={{0,16},{1,17},{2,18},{3,19},{4,20},{5,21},{6,22},{7,23},{8,24},{9,... | collective-permute-start | bytes 393224 | tf_op jit(solution)/shard_map/ppermute | solution.py:623
  5.8 1.3 collective-permute-start.3
  7.3 3.3 %shard_map.324 = bf16[32,64,128]{2,1,0:T(8,128)(2,1)} custom-call(bf16[1024,512]{1,0:T(8,128)(2,1)} %bitcast.39, bf16[512,1024]{1,0:T(8,128)(2,1)} %constant.61.clone.refs_1_), custom_call_target="tpu_custom_call" | custom-call | flops 536870912 | bytes 2621440 | tf_op jit(solution)/shard_map/pallas_call | solution.py:577
  10.7 5.2 %all-to-all-start = ((bf16[32,64,128]{2,1,0:T(8,128)(2,1)}), bf16[32,64,128]{2,1,0:T(8,128)(2,1)S(1)}, u32[]{:S(2)}, u32[]{:S(2)}) async-start(bf16[32,64,128]{2,1,0:T(8,128)(2,1)} %shard_map.324), calls=%async_computation | async-start | bytes 1048576 | tf_op jit(solution)/shard_map/all_to_all | solution.py:656
  15.9 1.0 dynamic-slice_convert_fusion
  17.3 0.9 dynamic-slice_bitcast_fusion.refs_7_.refs_5_
  18.3 1.8 %collective-permute-start.4 = (bf16[2,2,32,1024]{3,2,1,0:T(8,128)(2,1)S(1)}, bf16[2,2,32,1024]{3,2,1,0:T(8,128)(2,1)S(1)}, u32[]{:S(2)}, u32[]{:S(2)}) collective-permute-start(bf16[2,2,32,1024]{3,2,1,0:T(8,128)(2,1)S(1)} %get-tuple-element.109), channel_id=1, source_target_pairs={{0,4},{1,5},{2,6},{3,7},{4,0},{5,1},{6,2},{7,3},{8,12},{9,13},{10,... | collective-permute-start | bytes 786440 | tf_op jit(solution)/shard_map/ppermute | solution.py:623
  20.2 1.5 %collective-permute-start.1 = (bf16[2,2,32,1024]{3,2,1,0:T(8,128)(2,1)S(1)}, bf16[2,2,32,1024]{3,2,1,0:T(8,128)(2,1)S(1)}, u32[]{:S(2)}, u32[]{:S(2)}) collective-permute-start(bf16[2,2,32,1024]{3,2,1,0:T(8,128)(2,1)S(1)} %get-tuple-element.111), channel_id=1, source_target_pairs={{0,1},{1,0},{2,3},{3,2},{4,5},{5,4},{6,7},{7,6},{8,9},{9,8},{10,11... | collective-permute-start | bytes 786440 | tf_op jit(solution)/shard_map/ppermute | solution.py:623
  22.1 8.2 %collective-permute-done.4 = bf16[2,2,32,1024]{3,2,1,0:T(8,128)(2,1)S(1)} collective-permute-done((bf16[2,2,32,1024]{3,2,1,0:T(8,128)(2,1)S(1)}, bf16[2,2,32,1024]{3,2,1,0:T(8,128)(2,1)S(1)}, u32[]{:S(2)}, u32[]{:S(2)}) %collective-permute-start.4) | collective-permute-done | bytes 262176 | tf_op jit(solution)/shard_map/ppermute | solution.py:623
  30.9 2.3 %shard_map.325 = (bf16[32,64,128]{2,1,0:T(8,128)(2,1)}, f32[128,512]{1,0:T(8,128)}, bf16[256,256]{1,0:T(8,128)(2,1)}, f32[256,256]{1,0:T(8,128)}, bf16[256,256]{...) custom-call(bf16[32,64,128]{2,1,0:T(8,128)(2,1)S(1)} %all-to-all-don, ...), custom_call_target="tpu_custom_call", output_to_operand_aliasing={{5}: (8, {}), {6}: (9, {})} | custom-call | bytes 2364416 | tf_op jit(solution)/shard_map/pallas_call | solution.py:577
  33.2 1.9 %collective-permute-start.6 = (bf16[2,2,2,32,1024]{4,3,2,1,0:T(8,128)(2,1)S(1)}, bf16[2,2,2,32,1024]{4,3,2,1,0:T(8,128)(2,1)S(1)}, u32[]{:S(2)}, u32[]{:S(2)}) collective-permute-start(bf16[2,2,2,32,1024]{4,3,2,1,0:T(8,128)(2,1)S(1)} %get-tuple-element.64.refs_9_), channel_id=1, source_target_pairs={{0,1},{1,0},{2,3},{3,2},{4,5},{5,4},{6,7},{7,6},{8,9},{9,8},{10,11... | collective-permute-start | bytes 1572872 | tf_op jit(solution)/shard_map/ppermute | solution.py:623
  35.0 1.2 collective-permute-start.5
  36.2 3.4 %all-to-all-start.1 = ((bf16[32,64,128]{2,1,0:T(8,128)(2,1)}), bf16[32,64,128]{2,1,0:T(8,128)(2,1)S(1)}, u32[]{:S(2)}, u32[]{:S(2)}) async-start(bf16[32,64,128]{2,1,0:T(8,128)(2,1)} %get-tuple-element.62), calls=%async_computation.1 | async-start | bytes 1048576 | tf_op jit(solution)/shard_map/all_to_all | solution.py:673
  40.2 11.2 %collective-permute-done.6.refs_11_ = bf16[2,2,2,32,1024]{4,3,2,1,0:T(8,128)(2,1)S(1)} collective-permute-done((bf16[2,2,2,32,1024]{4,3,2,1,0:T(8,128)(2,1)S(1)}, bf16[2,2,2,32,1024]{4,3,2,1,0:T(8,128)(2,1)S(1)}, u32[]{:S(2)}, u32[]{:S(2)}) %collective-permute-start.6) | collective-permute-done | bytes 524320 | tf_op jit(solution)/shard_map/ppermute | solution.py:623
  51.8 1.0 collective-permute-done.5.refs_10_
  52.8 1.6 %all-to-all-done.1.refs_1_ = bf16[32,64,128]{2,1,0:T(8,128)(2,1)S(1)} async-done(((bf16[32,64,128]{2,1,0:T(8,128)(2,1)}), bf16[32,64,128]{2,1,0:T(8,128)(2,1)S(1)}, u32[]{:S(2)}, u32[]{:S(2)}) %all-to-all-start.1) | async-done | bytes 524320 | tf_op jit(solution)/shard_map/all_to_all | solution.py:673
  54.8 0.4 copy-done.17
  55.3 25.3 %shard_map.326 = (bf16[1024,512]{1,0:T(8,128)(2,1)}, f32[1024,512]{1,0:T(8,128)}, bf16[32,64,128]{2,1,0:T(8,128)(2,1)}, f32[8,512]{1,0:T(8,128)S(1)}, bf16[2,2,2...) custom-call(s32[1]{0:T(128)} %bitcast.refs_0_, bf16[32,64,128]{2,1,0:T(8,128)(2,1)} %copy-done.17, ...), custom_call_target="tpu_custom_call" | custom-call | flops 13958643712 | bytes 16828416 | tf_op jit(solution)/shard_map/pallas_call | solution.py:577
  80.6 1.1 collective-permute-start.11
  81.7 2.7 %all-to-all-start.2 = ((bf16[32,64,128]{2,1,0:T(8,128)(2,1)}), bf16[32,64,128]{2,1,0:T(8,128)(2,1)S(1)}, u32[]{:S(2)}, u32[]{:S(2)}) async-start(bf16[32,64,128]{2,1,0:T(8,128)(2,1)} %get-tuple-element.70), calls=%async_computation.2 | async-start | bytes 1048576 | tf_op jit(solution)/shard_map/all_to_all | solution.py:706
  84.4 1.4 collective-permute-done.11.refs_1_.refs_5_.refs_10_
  85.8 2.3 %shard_map.327 = (bf16[2,4,256,128]{3,2,1,0:T(8,128)(2,1)}, bf16[2,4,256,128]{3,2,1,0:T(8,128)(2,1)}) custom-call(bf16[2,2,2,4,256,128]{5,4,3,2,1,0:T(8,128)(2,1)S(1)} %get-tuple-element.66.refs_0_.refs_1_, bf16[2,2,2,4,256,128]{5,4,3,2,1,0:T(8,128)(2,1)} %collective-permute-done.11.refs_1_.refs_5_.refs_10_), custom_call_target="tpu_custom_call" | custom-call | tf_op jit(solution)/shard_map/pallas_call | solution.py:577
  88.2 1.2 collective-permute-start.12
  89.3 1.2 collective-permute-start.13
  90.5 8.9 %all-to-all-done.2.refs_1_ = bf16[32,64,128]{2,1,0:T(8,128)(2,1)S(1)} async-done(((bf16[32,64,128]{2,1,0:T(8,128)(2,1)}), bf16[32,64,128]{2,1,0:T(8,128)(2,1)S(1)}, u32[]{:S(2)}, u32[]{:S(2)}) %all-to-all-start.2) | async-done | bytes 524320 | tf_op jit(solution)/shard_map/all_to_all | solution.py:706
  99.4 3.0 %shard_map.328 = (bf16[32,64,128]{2,1,0:T(8,128)(2,1)}, bf16[160,128]{1,0:T(8,128)(2,1)S(1)}, bf16[160,128]{1,0:T(8,128)(2,1)S(1)}) custom-call(s32[1]{0:T(128)} %bitcast.22.refs_0_, bf16[32,64,128]{2,1,0:T(8,128)(2,1)S(1)} %all-to-all-done.2.refs_1_, bf16[128,512]{1,0:T(8,128)(2,1)} %constant.65.clone.refs_1_.refs_2_, ...), custom_call_target="tpu_custom_call" | custom-call | bytes 62914560 | tf_op jit(solution)/shard_map/pallas_call | solution.py:577
  102.4 3.9 %all-to-all-start.3 = ((bf16[32,64,128]{2,1,0:T(8,128)(2,1)}), bf16[32,64,128]{2,1,0:T(8,128)(2,1)S(1)}, u32[]{:S(2)}, u32[]{:S(2)}) async-start(bf16[32,64,128]{2,1,0:T(8,128)(2,1)} %get-tuple-element.86), calls=%async_computation.3 | async-start | bytes 1048576 | tf_op jit(solution)/shard_map/all_to_all | solution.py:729
  106.3 1.2 collective-permute-done.14.refs_4_
  107.5 2.3 %shard_map.329 = (bf16[160,128]{1,0:T(8,128)(2,1)S(1)}, bf16[4,256,128]{2,1,0:T(8,128)(2,1)S(1)}, bf16[4,256,128]{2,1,0:T(8,128)(2,1)S(1)}) custom-call(bf16[2,2,2,4,256,128]{5,4,3,2,1,0:T(8,128)(2,1)S(1)} %get-tuple-element.66.refs_0_.refs_1_, bf16[2,4,256,128]{3,2,1,0:T(8,128)(2,1)S(1)} %collective-permute-done.12.refs_1_.refs_2_, ...), custom_call_target="tpu_custom_call" | custom-call | tf_op jit(solution)/shard_map/pallas_call | solution.py:577
  109.8 1.6 %collective-permute-start.15 = (bf16[4,256,128]{2,1,0:T(8,128)(2,1)S(1)}, bf16[4,256,128]{2,1,0:T(8,128)(2,1)S(1)}, u32[]{:S(2)}, u32[]{:S(2)}) collective-permute-start(bf16[4,256,128]{2,1,0:T(8,128)(2,1)S(1)} %get-tuple-element.78), channel_id=1, source_target_pairs={{0,4},{1,5},{2,6},{3,7},{4,0},{5,1},{6,2},{7,3},{8,12},{9,13},{10,... | collective-permute-start | bytes 786440 | tf_op jit(solution)/shard_map/ppermute | solution.py:623
  111.4 1.5 collective-permute-start.16
  112.9 1.5 collective-permute-start.17
  114.3 2.5 %collective-permute-start.18 = (bf16[160,128]{1,0:T(8,128)(2,1)S(1)}, bf16[160,128]{1,0:T(8,128)(2,1)S(1)}, u32[]{:S(2)}, u32[]{:S(2)}) collective-permute-start(bf16[160,128]{1,0:T(8,128)(2,1)S(1)} %get-tuple-element.80.refs_6_), channel_id=1, source_target_pairs={{0,16},{1,17},{2,18},{3,19},{4,20},{5,21},{6,22},{7,23},{8,24},{9,... | collective-permute-start | bytes 122888 | tf_op jit(solution)/shard_map/ppermute | solution.py:623
  116.8 0.5 collective-permute-start.19
  117.3 6.8 %collective-permute-done.18.refs_8_ = bf16[160,128]{1,0:T(8,128)(2,1)S(1)} collective-permute-done((bf16[160,128]{1,0:T(8,128)(2,1)S(1)}, bf16[160,128]{1,0:T(8,128)(2,1)S(1)}, u32[]{:S(2)}, u32[]{:S(2)}) %collective-permute-start.18) | collective-permute-done | bytes 40992 | tf_op jit(solution)/shard_map/ppermute | solution.py:623
  124.1 2.9 %shard_map.330 = (bf16[4,160,128]{2,1,0:T(8,128)(2,1)}, f32[2,256,128]{2,1,0:T(8,128)S(1)}, bf16[2,256,128]{2,1,0:T(8,128)(2,1)S(1)}, bf16[2,256,128]{2,1,0:T(8,128)(2,1)}, bf16[2,256,128]{2,1,0:T(8,128)(2,1)}) custom-call(s32[1]{0:T(128)} %bitcast.refs_0_, bf16[2,2,2,4,256,128]{5,4,3,2,1,0:T(8,128)(2,1)S(1)} %get-tuple-element.66.refs_0_.refs_1_, ...), custom_call_target="tpu_custom_call" | custom-call | tf_op jit(solution)/shard_map/pallas_call | solution.py:577
  127.0 1.1 collective-permute-start.23
  128.1 1.5 collective-permute-start.20
  129.5 1.5 collective-permute-start.21
  131.0 0.5 collective-permute-start.22
  131.5 0.7 collective-permute-start.24
  132.2 2.7 %collective-permute-start.25 = (bf16[2,256,128]{2,1,0:T(8,128)(2,1)}, bf16[2,256,128]{2,1,0:T(8,128)(2,1)S(1)}, u32[]{:S(2)}, u32[]{:S(2)}) collective-permute-start(bf16[2,256,128]{2,1,0:T(8,128)(2,1)} %get-tuple-element.85), channel_id=1, source_target_pairs={{0,24},{1,25},{2,26},{3,27},{4,28},{5,29},{6,30},{7,31},{8,16},{9,... | collective-permute-start | bytes 393224 | tf_op jit(solution)/shard_map/ppermute | solution.py:623
  135.0 5.1 %shard_map.331.refs_7_ = bf16[1024,512]{1,0:T(8,128)(2,1)} custom-call(bf16[32,64,128]{2,1,0:T(8,128)(2,1)S(1)} %all-to-all-done.3.refs_0_, bf16[1024,512]{1,0:T(8,128)(2,1)} %bitcast.41, f32[1024,512]{1,0:T(8,128)} %get-tuple-element.87.refs_2_, f32[13,512]{1,0:T(8,128)S(1)} %copy-done.10, bf16[1024,512]{1,0:T(8,128)(2,1)} %constant.62.clone.refs_4_), custom_call_target="tpu_custom_call" | custom-call | bytes 62914560 | tf_op jit(solution)/shard_map/pallas_call | solution.py:577
  140.1 2.3 %collective-permute-done.24.refs_5_ = bf16[2,256,128]{2,1,0:T(8,128)(2,1)S(1)} collective-permute-done((bf16[2,256,128]{2,1,0:T(8,128)(2,1)}, bf16[2,256,128]{2,1,0:T(8,128)(2,1)S(1)}, u32[]{:S(2)}, u32[]{:S(2)}) %collective-permute-start.24) | collective-permute-done | bytes 131104 | tf_op jit(solution)/shard_map/ppermute | solution.py:623
  142.4 1.0 shard_map.332
  143.5 1.4 collective-permute-done.26.refs_12_
  145.0 4.1 %shard_map.333 = (f32[32,1024]{1,0:T(8,128)}, f32[32,1024]{1,0:T(8,128)}, f32[32,1024]{1,0:T(8,128)}, f32[32,1024]{1,0:T(8,128)}, f32[32,1024]{1,0:T(8,128)}, /*...) custom-call(s32[1]{0:T(128)} %bitcast.22.refs_0_, ...), custom_call_target="tpu_custom_call", output_to_operand_aliasing={{14}: (19, {})} | custom-call | tf_op jit(solution)/shard_map/pallas_call | solution.py:577
  (88 shorter events, 3.2 us)
Async XLA Ops:
  1.7 16.5 %collective-permute-start.2 = (bf16[2,32,1024]{2,1,0:T(8,128)(2,1)S(1)}, bf16[2,32,1024]{2,1,0:T(8,128)(2,1)S(1)}, u32[]{:S(2)}, u32[]{:S(2)}) collective-permute-start(bf16[2,32,1024]{2,1,0:T(8,128)(2,1)S(1)} %get-tuple-element.113), channel_id=1, source_target_pairs={{0,16},{1,17},{2,18},{3,19},{4,20},{5,21},{6,22},{7,23},{8,24},{9,... | collective-permute-start | bytes 393224 | tf_op jit(solution)/shard_map/ppermute | solution.py:623
  5.8 12.5 %collective-permute-start.3 = (bf16[2,32,1024]{2,1,0:T(8,128)(2,1)S(1)}, bf16[2,32,1024]{2,1,0:T(8,128)(2,1)S(1)}, u32[]{:S(2)}, u32[]{:S(2)}) collective-permute-start(bf16[2,32,1024]{2,1,0:T(8,128)(2,1)S(1)} %get-tuple-element.113), channel_id=1, source_target_pairs={{0,24},{1,25},{2,26},{3,27},{4,28},{5,29},{6,30},{7,31},{8,16},{9,... | collective-permute-start | bytes 393224 | tf_op jit(solution)/shard_map/ppermute | solution.py:623
  7.1 13.0 %collective-permute-start = (bf16[2,32,1024]{2,1,0:T(8,128)(2,1)S(1)}, bf16[2,32,1024]{2,1,0:T(8,128)(2,1)S(1)}, u32[]{:S(2)}, u32[]{:S(2)}) collective-permute-start(bf16[2,32,1024]{2,1,0:T(8,128)(2,1)S(1)} %get-tuple-element.113), channel_id=1, source_target_pairs={{0,8},{1,9},{2,10},{3,11},{4,12},{5,13},{6,14},{7,15},{8,0},{9,1},... | collective-permute-start | bytes 393224 | tf_op jit(solution)/shard_map/ppermute | solution.py:623
  7.3 9.6 %copy-start.10 = (f32[13,512]{1,0:T(8,128)S(1)}, f32[13,512]{1,0:T(8,128)}, u32[]{:S(2)}) copy-start(f32[13,512]{1,0:T(8,128)} %refs_16_.1) | copy-start | bytes 79876
  10.7 20.2 %all-to-all-start = ((bf16[32,64,128]{2,1,0:T(8,128)(2,1)}), bf16[32,64,128]{2,1,0:T(8,128)(2,1)S(1)}, u32[]{:S(2)}, u32[]{:S(2)}) async-start(bf16[32,64,128]{2,1,0:T(8,128)(2,1)} %shard_map.324), calls=%async_computation | async-start | bytes 1048576 | tf_op jit(solution)/shard_map/all_to_all | solution.py:656
  18.3 12.6 %copy-start.8 = (bf16[128,512]{1,0:T(8,128)(2,1)S(1)}, bf16[128,512]{1,0:T(8,128)(2,1)}, u32[]{:S(2)}) copy-start(bf16[128,512]{1,0:T(8,128)(2,1)} %constant.65.clone.refs_1_.refs_2_) | copy-start | bytes 393220
  18.3 12.6 %copy-start.9 = (bf16[512,128]{1,0:T(8,128)(2,1)S(1)}, bf16[512,128]{1,0:T(8,128)(2,1)}, u32[]{:S(2)}) copy-start(bf16[512,128]{1,0:T(8,128)(2,1)} %constant.66.clone.refs_2_.refs_3_) | copy-start | bytes 393220
  18.3 12.0 %collective-permute-start.4 = (bf16[2,2,32,1024]{3,2,1,0:T(8,128)(2,1)S(1)}, bf16[2,2,32,1024]{3,2,1,0:T(8,128)(2,1)S(1)}, u32[]{:S(2)}, u32[]{:S(2)}) collective-permute-start(bf16[2,2,32,1024]{3,2,1,0:T(8,128)(2,1)S(1)} %get-tuple-element.109), channel_id=1, source_target_pairs={{0,4},{1,5},{2,6},{3,7},{4,0},{5,1},{6,2},{7,3},{8,12},{9,13},{10,... | collective-permute-start | bytes 786440 | tf_op jit(solution)/shard_map/ppermute | solution.py:623
  20.2 10.5 %collective-permute-start.1 = (bf16[2,2,32,1024]{3,2,1,0:T(8,128)(2,1)S(1)}, bf16[2,2,32,1024]{3,2,1,0:T(8,128)(2,1)S(1)}, u32[]{:S(2)}, u32[]{:S(2)}) collective-permute-start(bf16[2,2,32,1024]{3,2,1,0:T(8,128)(2,1)S(1)} %get-tuple-element.111), channel_id=1, source_target_pairs={{0,1},{1,0},{2,3},{3,2},{4,5},{5,4},{6,7},{7,6},{8,9},{9,8},{10,11... | collective-permute-start | bytes 786440 | tf_op jit(solution)/shard_map/ppermute | solution.py:623
  22.1 11.0 %copy-start = (bf16[2,256,256]{2,1,0:T(8,128)(2,1)}, bf16[2,256,256]{2,1,0:T(8,128)(2,1)S(1)}, u32[]{:S(2)}) copy-start(bf16[2,256,256]{2,1,0:T(8,128)(2,1)S(1)} %maximum_maximum_fusion.refs_3_.refs_4_) | copy-start | bytes 786436
  33.2 22.1 %copy-start.1 = (bf16[2,2,2,32,1024]{4,3,2,1,0:T(8,128)(2,1)}, bf16[2,2,2,32,1024]{4,3,2,1,0:T(8,128)(2,1)S(1)}, u32[]{:S(2)}) copy-start(bf16[2,2,2,32,1024]{4,3,2,1,0:T(8,128)(2,1)S(1)} %get-tuple-element.64.refs_9_) | copy-start | bytes 1572868
  33.2 22.1 %copy-start.2 = (bf16[2,2,2,32,1024]{4,3,2,1,0:T(8,128)(2,1)}, bf16[2,2,2,32,1024]{4,3,2,1,0:T(8,128)(2,1)S(1)}, u32[]{:S(2)}) copy-start(bf16[2,2,2,32,1024]{4,3,2,1,0:T(8,128)(2,1)S(1)} %get-tuple-element.63.refs_8_) | copy-start | bytes 1572868
  33.2 18.3 %collective-permute-start.6 = (bf16[2,2,2,32,1024]{4,3,2,1,0:T(8,128)(2,1)S(1)}, bf16[2,2,2,32,1024]{4,3,2,1,0:T(8,128)(2,1)S(1)}, u32[]{:S(2)}, u32[]{:S(2)}) collective-permute-start(bf16[2,2,2,32,1024]{4,3,2,1,0:T(8,128)(2,1)S(1)} %get-tuple-element.64.refs_9_), channel_id=1, source_target_pairs={{0,1},{1,0},{2,3},{3,2},{4,5},{5,4},{6,7},{7,6},{8,9},{9,8},{10,11... | collective-permute-start | bytes 1572872 | tf_op jit(solution)/shard_map/ppermute | solution.py:623
  35.0 17.7 %collective-permute-start.5 = (bf16[2,2,2,32,1024]{4,3,2,1,0:T(8,128)(2,1)S(1)}, bf16[2,2,2,32,1024]{4,3,2,1,0:T(8,128)(2,1)S(1)}, u32[]{:S(2)}, u32[]{:S(2)}) collective-permute-start(bf16[2,2,2,32,1024]{4,3,2,1,0:T(8,128)(2,1)S(1)} %get-tuple-element.63.refs_8_), channel_id=1, source_target_pairs={{0,4},{1,5},{2,6},{3,7},{4,0},{5,1},{6,2},{7,3},{8,12},{9,13},{10,... | collective-permute-start | bytes 1572872 | tf_op jit(solution)/shard_map/ppermute | solution.py:623
  36.2 18.3 %all-to-all-start.1 = ((bf16[32,64,128]{2,1,0:T(8,128)(2,1)}), bf16[32,64,128]{2,1,0:T(8,128)(2,1)S(1)}, u32[]{:S(2)}, u32[]{:S(2)}) async-start(bf16[32,64,128]{2,1,0:T(8,128)(2,1)} %get-tuple-element.62), calls=%async_computation.1 | async-start | bytes 1048576 | tf_op jit(solution)/shard_map/all_to_all | solution.py:673
  39.6 13.1 %collective-permute-start.7 = (bf16[2,2,2,32,1024]{4,3,2,1,0:T(8,128)(2,1)S(1)}, bf16[2,2,2,32,1024]{4,3,2,1,0:T(8,128)(2,1)S(1)}, u32[]{:S(2)}, u32[]{:S(2)}) collective-permute-start(bf16[2,2,2,32,1024]{4,3,2,1,0:T(8,128)(2,1)S(1)} %get-tuple-element.63.refs_8_), channel_id=1, source_target_pairs={{0,2},{1,3},{2,0},{3,1},{4,6},{5,7},{6,4},{7,5},{8,10},{9,11},{10,... | collective-permute-start | bytes 1572872 | tf_op jit(solution)/shard_map/ppermute | solution.py:623
  40.0 12.8 %collective-permute-start.8 = (bf16[2,2,2,32,1024]{4,3,2,1,0:T(8,128)(2,1)S(1)}, bf16[2,2,2,32,1024]{4,3,2,1,0:T(8,128)(2,1)}, u32[]{:S(2)}, u32[]{:S(2)}) collective-permute-start(bf16[2,2,2,32,1024]{4,3,2,1,0:T(8,128)(2,1)S(1)} %get-tuple-element.64.refs_9_), channel_id=1, source_target_pairs={{0,2},{1,3},{2,0},{3,1},{4,6},{5,7},{6,4},{7,5},{8,10},{9,11},{10,... | collective-permute-start | bytes 1572872 | tf_op jit(solution)/shard_map/ppermute | solution.py:623
  51.5 3.0 %collective-permute-start.10 = (bf16[2,2,2,32,1024]{4,3,2,1,0:T(8,128)(2,1)S(1)}, bf16[2,2,2,32,1024]{4,3,2,1,0:T(8,128)(2,1)}, u32[]{:S(2)}, u32[]{:S(2)}) collective-permute-start(bf16[2,2,2,32,1024]{4,3,2,1,0:T(8,128)(2,1)S(1)} %collective-permute-done.6.refs_11_), channel_id=1, source_target_pairs={{0,2},{1,3},{2,0},{3,1},{4,6},{5,7},{6,4},{7,5},{8,10},{9,11},{10,... | collective-permute-start | bytes 1572872 | tf_op jit(solution)/shard_map/ppermute | solution.py:623
  52.8 2.0 %collective-permute-start.9 = (bf16[2,2,2,32,1024]{4,3,2,1,0:T(8,128)(2,1)S(1)}, bf16[2,2,2,32,1024]{4,3,2,1,0:T(8,128)(2,1)}, u32[]{:S(2)}, u32[]{:S(2)}) collective-permute-start(bf16[2,2,2,32,1024]{4,3,2,1,0:T(8,128)(2,1)S(1)} %collective-permute-done.5.refs_10_), channel_id=1, source_target_pairs={{0,2},{1,3},{2,0},{3,1},{4,6},{5,7},{6,4},{7,5},{8,10},{9,11},{10,... | collective-permute-start | bytes 1572872 | tf_op jit(solution)/shard_map/ppermute | solution.py:623
  80.6 5.2 %collective-permute-start.11 = (bf16[2,2,2,4,256,128]{5,4,3,2,1,0:T(8,128)(2,1)}, bf16[2,2,2,4,256,128]{5,4,3,2,1,0:T(8,128)(2,1)}, u32[]{:S(2)}, u32[]{:S(2)}) collective-permute-start(bf16[2,2,2,4,256,128]{5,4,3,2,1,0:T(8,128)(2,1)} %get-tuple-element.67), channel_id=1, source_target_pairs={{0,2},{1,3},{2,0},{3,1},{4,6},{5,7},{6,4},{7,5},{8,10},{9,11},{10,... | collective-permute-start | bytes 6291464 | tf_op jit(solution)/shard_map/ppermute | solution.py:623
  81.7 17.7 %all-to-all-start.2 = ((bf16[32,64,128]{2,1,0:T(8,128)(2,1)}), bf16[32,64,128]{2,1,0:T(8,128)(2,1)S(1)}, u32[]{:S(2)}, u32[]{:S(2)}) async-start(bf16[32,64,128]{2,1,0:T(8,128)(2,1)} %get-tuple-element.70), calls=%async_computation.2 | async-start | bytes 1048576 | tf_op jit(solution)/shard_map/all_to_all | solution.py:706
  88.2 19.4 %collective-permute-start.12 = (bf16[2,4,256,128]{3,2,1,0:T(8,128)(2,1)}, bf16[2,4,256,128]{3,2,1,0:T(8,128)(2,1)S(1)}, u32[]{:S(2)}, u32[]{:S(2)}) collective-permute-start(bf16[2,4,256,128]{3,2,1,0:T(8,128)(2,1)} %get-tuple-element.68), channel_id=1, source_target_pairs={{0,1},{1,0},{2,3},{3,2},{4,5},{5,4},{6,7},{7,6},{8,9},{9,8},{10,11... | collective-permute-start | bytes 1572872 | tf_op jit(solution)/shard_map/ppermute | solution.py:623
  89.3 18.2 %collective-permute-start.13 = (bf16[2,4,256,128]{3,2,1,0:T(8,128)(2,1)}, bf16[2,4,256,128]{3,2,1,0:T(8,128)(2,1)}, u32[]{:S(2)}, u32[]{:S(2)}) collective-permute-start(bf16[2,4,256,128]{3,2,1,0:T(8,128)(2,1)} %get-tuple-element.69), channel_id=1, source_target_pairs={{0,4},{1,5},{2,6},{3,7},{4,0},{5,1},{6,2},{7,3},{8,12},{9,13},{10,... | collective-permute-start | bytes 1572872 | tf_op jit(solution)/shard_map/ppermute | solution.py:623
  102.4 32.6 %all-to-all-start.3 = ((bf16[32,64,128]{2,1,0:T(8,128)(2,1)}), bf16[32,64,128]{2,1,0:T(8,128)(2,1)S(1)}, u32[]{:S(2)}, u32[]{:S(2)}) async-start(bf16[32,64,128]{2,1,0:T(8,128)(2,1)} %get-tuple-element.86), calls=%async_computation.3 | async-start | bytes 1048576 | tf_op jit(solution)/shard_map/all_to_all | solution.py:729
  106.3 1.3 collective-permute-start.14
  109.8 14.2 %collective-permute-start.15 = (bf16[4,256,128]{2,1,0:T(8,128)(2,1)S(1)}, bf16[4,256,128]{2,1,0:T(8,128)(2,1)S(1)}, u32[]{:S(2)}, u32[]{:S(2)}) collective-permute-start(bf16[4,256,128]{2,1,0:T(8,128)(2,1)S(1)} %get-tuple-element.78), channel_id=1, source_target_pairs={{0,4},{1,5},{2,6},{3,7},{4,0},{5,1},{6,2},{7,3},{8,12},{9,13},{10,... | collective-permute-start | bytes 786440 | tf_op jit(solution)/shard_map/ppermute | solution.py:623
  111.4 12.7 %collective-permute-start.16 = (bf16[4,256,128]{2,1,0:T(8,128)(2,1)S(1)}, bf16[4,256,128]{2,1,0:T(8,128)(2,1)S(1)}, u32[]{:S(2)}, u32[]{:S(2)}) collective-permute-start(bf16[4,256,128]{2,1,0:T(8,128)(2,1)S(1)} %get-tuple-element.79), channel_id=1, source_target_pairs={{0,1},{1,0},{2,3},{3,2},{4,5},{5,4},{6,7},{7,6},{8,9},{9,8},{10,11... | collective-permute-start | bytes 786440 | tf_op jit(solution)/shard_map/ppermute | solution.py:623
  112.9 4.4 %collective-permute-start.17 = (bf16[160,128]{1,0:T(8,128)(2,1)S(1)}, bf16[160,128]{1,0:T(8,128)(2,1)S(1)}, u32[]{:S(2)}, u32[]{:S(2)}) collective-permute-start(bf16[160,128]{1,0:T(8,128)(2,1)S(1)} %get-tuple-element.80.refs_6_), channel_id=1, source_target_pairs={{0,8},{1,9},{2,10},{3,11},{4,12},{5,13},{6,14},{7,15},{8,0},{9,1},... | collective-permute-start | bytes 122888 | tf_op jit(solution)/shard_map/ppermute | solution.py:623
  114.3 9.7 %collective-permute-start.18 = (bf16[160,128]{1,0:T(8,128)(2,1)S(1)}, bf16[160,128]{1,0:T(8,128)(2,1)S(1)}, u32[]{:S(2)}, u32[]{:S(2)}) collective-permute-start(bf16[160,128]{1,0:T(8,128)(2,1)S(1)} %get-tuple-element.80.refs_6_), channel_id=1, source_target_pairs={{0,16},{1,17},{2,18},{3,19},{4,20},{5,21},{6,22},{7,23},{8,24},{9,... | collective-permute-start | bytes 122888 | tf_op jit(solution)/shard_map/ppermute | solution.py:623
  116.8 7.3 %collective-permute-start.19 = (bf16[160,128]{1,0:T(8,128)(2,1)S(1)}, bf16[160,128]{1,0:T(8,128)(2,1)S(1)}, u32[]{:S(2)}, u32[]{:S(2)}) collective-permute-start(bf16[160,128]{1,0:T(8,128)(2,1)S(1)} %get-tuple-element.80.refs_6_), channel_id=1, source_target_pairs={{0,24},{1,25},{2,26},{3,27},{4,28},{5,29},{6,30},{7,31},{8,16},{9,... | collective-permute-start | bytes 122888 | tf_op jit(solution)/shard_map/ppermute | solution.py:623
  127.0 5.2 %collective-permute-start.23 = (bf16[2,256,128]{2,1,0:T(8,128)(2,1)S(1)}, bf16[2,256,128]{2,1,0:T(8,128)(2,1)S(1)}, u32[]{:S(2)}, u32[]{:S(2)}) collective-permute-start(bf16[2,256,128]{2,1,0:T(8,128)(2,1)S(1)} %get-tuple-element.83), channel_id=1, source_target_pairs={{0,8},{1,9},{2,10},{3,11},{4,12},{5,13},{6,14},{7,15},{8,0},{9,1},... | collective-permute-start | bytes 393224 | tf_op jit(solution)/shard_map/ppermute | solution.py:623
  128.1 14.3 %collective-permute-start.20 = (bf16[4,160,128]{2,1,0:T(8,128)(2,1)}, bf16[4,160,128]{2,1,0:T(8,128)(2,1)S(1)}, u32[]{:S(2)}, u32[]{:S(2)}) collective-permute-start(bf16[4,160,128]{2,1,0:T(8,128)(2,1)} %get-tuple-element.82.refs_0_), channel_id=1, source_target_pairs={{0,1},{1,0},{2,3},{3,2},{4,5},{5,4},{6,7},{7,6},{8,9},{9,8},{10,11... | collective-permute-start | bytes 491528 | tf_op jit(solution)/shard_map/ppermute | solution.py:623
  129.5 12.9 %collective-permute-start.21 = (bf16[4,160,128]{2,1,0:T(8,128)(2,1)}, bf16[4,160,128]{2,1,0:T(8,128)(2,1)S(1)}, u32[]{:S(2)}, u32[]{:S(2)}) collective-permute-start(bf16[4,160,128]{2,1,0:T(8,128)(2,1)} %get-tuple-element.82.refs_0_), channel_id=1, source_target_pairs={{0,4},{1,5},{2,6},{3,7},{4,0},{5,1},{6,2},{7,3},{8,12},{9,13},{10,... | collective-permute-start | bytes 491528 | tf_op jit(solution)/shard_map/ppermute | solution.py:623
  131.0 11.4 %collective-permute-start.22 = (bf16[4,160,128]{2,1,0:T(8,128)(2,1)}, bf16[4,160,128]{2,1,0:T(8,128)(2,1)S(1)}, u32[]{:S(2)}, u32[]{:S(2)}) collective-permute-start(bf16[4,160,128]{2,1,0:T(8,128)(2,1)} %get-tuple-element.82.refs_0_), channel_id=1, source_target_pairs={{0,5},{1,4},{2,7},{3,6},{4,1},{5,0},{6,3},{7,2},{8,13},{9,12},{10,... | collective-permute-start | bytes 491528 | tf_op jit(solution)/shard_map/ppermute | solution.py:623
  131.5 10.8 %collective-permute-start.24 = (bf16[2,256,128]{2,1,0:T(8,128)(2,1)}, bf16[2,256,128]{2,1,0:T(8,128)(2,1)S(1)}, u32[]{:S(2)}, u32[]{:S(2)}) collective-permute-start(bf16[2,256,128]{2,1,0:T(8,128)(2,1)} %get-tuple-element.84), channel_id=1, source_target_pairs={{0,16},{1,17},{2,18},{3,19},{4,20},{5,21},{6,22},{7,23},{8,24},{9,... | collective-permute-start | bytes 393224 | tf_op jit(solution)/shard_map/ppermute | solution.py:623
  132.2 10.2 %collective-permute-start.25 = (bf16[2,256,128]{2,1,0:T(8,128)(2,1)}, bf16[2,256,128]{2,1,0:T(8,128)(2,1)S(1)}, u32[]{:S(2)}, u32[]{:S(2)}) collective-permute-start(bf16[2,256,128]{2,1,0:T(8,128)(2,1)} %get-tuple-element.85), channel_id=1, source_target_pairs={{0,24},{1,25},{2,26},{3,27},{4,28},{5,29},{6,30},{7,31},{8,16},{9,... | collective-permute-start | bytes 393224 | tf_op jit(solution)/shard_map/ppermute | solution.py:623
  134.9 9.9 %copy-start.5 = (f32[2,8,2,64,64]{4,3,2,1,0:T(8,128)S(1)}, f32[2,8,2,64,64]{4,3,2,1,0:T(8,128)}, u32[]{:S(2)}) copy-start(f32[2,8,2,64,64]{4,3,2,1,0:T(8,128)} %refs_15_.1) | copy-start | bytes 1572868
  134.9 9.9 %copy-start.6 = (f32[32,1024]{1,0:T(8,128)S(1)}, f32[32,1024]{1,0:T(8,128)}, u32[]{:S(2)}) copy-start(f32[32,1024]{1,0:T(8,128)} %refs_6_.1) | copy-start | bytes 393220
  134.9 9.9 %copy-start.7 = (f32[32,1024]{1,0:T(8,128)S(1)}, f32[32,1024]{1,0:T(8,128)}, u32[]{:S(2)}) copy-start(f32[32,1024]{1,0:T(8,128)} %refs_5_.3) | copy-start | bytes 393220
  135.0 9.9 %copy-start.11 = (f32[32,1024]{1,0:T(8,128)S(1)}, f32[32,1024]{1,0:T(8,128)}, u32[]{:S(2)}) copy-start(f32[32,1024]{1,0:T(8,128)} %refs_7_.2) | copy-start | bytes 393220
  135.0 9.9 %copy-start.12 = (f32[32,1024]{1,0:T(8,128)S(1)}, f32[32,1024]{1,0:T(8,128)}, u32[]{:S(2)}) copy-start(f32[32,1024]{1,0:T(8,128)} %refs_8_.1) | copy-start | bytes 393220
  135.0 9.9 %copy-start.13 = (f32[32,1024]{1,0:T(8,128)S(1)}, f32[32,1024]{1,0:T(8,128)}, u32[]{:S(2)}) copy-start(f32[32,1024]{1,0:T(8,128)} %refs_9_.1) | copy-start | bytes 393220
  135.0 9.9 %copy-start.14 = (f32[32,1024]{1,0:T(8,128)S(1)}, f32[32,1024]{1,0:T(8,128)}, u32[]{:S(2)}) copy-start(f32[32,1024]{1,0:T(8,128)} %refs_10_.1) | copy-start | bytes 393220
  135.0 9.9 %copy-start.15 = (f32[13,512]{1,0:T(8,128)S(1)}, f32[13,512]{1,0:T(8,128)}, u32[]{:S(2)}) copy-start(f32[13,512]{1,0:T(8,128)} %refs_17_.1) | copy-start | bytes 79876
  135.0 9.9 %copy-start.16 = (f32[13,512]{1,0:T(8,128)S(1)}, f32[13,512]{1,0:T(8,128)}, u32[]{:S(2)}) copy-start(f32[13,512]{1,0:T(8,128)} %refs_18_.1) | copy-start | bytes 79876
  140.1 4.9 %copy-start.3 = (f32[2,8,2,64,64]{4,3,2,1,0:T(8,128)S(1)}, f32[2,8,2,64,64]{4,3,2,1,0:T(8,128)}, u32[]{:S(2)}) copy-start(f32[2,8,2,64,64]{4,3,2,1,0:T(8,128)} %refs_13_.1) | copy-start | bytes 1572868
  140.1 4.9 %copy-start.4 = (f32[2,8,2,64,64]{4,3,2,1,0:T(8,128)S(1)}, f32[2,8,2,64,64]{4,3,2,1,0:T(8,128)}, u32[]{:S(2)}) copy-start(f32[2,8,2,64,64]{4,3,2,1,0:T(8,128)} %refs_14_.1) | copy-start | bytes 1572868
  143.4 1.5 collective-permute-start.26
  (4 other events, 8.3 us)

commit v4 on v3

--- a/solution.py
+++ b/solution.py
@@ -20,10 +20,12 @@
 GELU_CUBE = 0.044715
 CHUNK = 512
 ROWS = 256
+SPAN = 4
 BF16 = jnp.bfloat16
 F32 = jnp.float32
 AXES = ("sp", "tp")
 COST = 60 << 20
+OUT_BLOCKS = 4
 
 
 def dft_tables(grid):
@@ -43,11 +45,11 @@
     return [t.astype(ml_dtypes.bfloat16) for t in (forward_w, inverse_w, forward_h)]
 
 
-def expanded_tables(grid, grid_rows, items):
+def expanded_tables(grid, items):
     forward_w, inverse_w, forward_h = [t.astype(np.float32) for t in dft_tables(grid)]
-    eye_r = np.eye(grid_rows, dtype=np.float32)
-    wide_f = np.einsum("wek,rs->kresw", forward_w, eye_r).reshape(-1, grid_rows * grid)
-    wide_i = np.einsum("wek,rs->kresw", inverse_w, eye_r).reshape(-1, grid_rows * grid)
+    eye_r = np.eye(SPAN, dtype=np.float32)
+    wide_f = np.einsum("wek,rs->kresw", forward_w, eye_r).reshape(-1, SPAN * grid)
+    wide_i = np.einsum("wek,rs->kresw", inverse_w, eye_r).reshape(-1, SPAN * grid)
     eye_i = np.eye(items, dtype=np.float32)
     high = np.einsum("mhef,ij->fimhje", forward_h, eye_i).reshape(2 * items * MODES, -1)
     ones = np.einsum("mhef,ek->kfm", forward_h.astype(np.float64), forward_w.astype(np.float64).sum(0))
@@ -93,6 +95,21 @@
     square = values * values
     bent = jnp.tanh(values * (GELU_SCALE + (GELU_SCALE * GELU_CUBE) * square))
     return values * (0.5 + 0.5 * bent)
+
+
+def along_w(table_ref, values, rows):
+    table = table_ref[...]
+    span = table.shape[1]
+    parts = [dot(table, values[r : r + span]).reshape(MODES, -1, values.shape[1]) for r in range(0, rows, span)]
+    return jnp.concatenate(parts, axis=1).reshape(-1, values.shape[1]).astype(BF16)
+
+
+def spans(spectrum):
+    whole = spectrum.astype(F32).reshape(MODES, -1, spectrum.shape[1])
+    size = 2 * SPAN
+    return [
+        whole[:, r : r + size].reshape(MODES * size, -1).astype(BF16) for r in range(0, whole.shape[1], size)
+    ]
 
 
 def gather_lanes(ref, groups):
@@ -146,8 +163,7 @@
 
 def enter_kernel(groups, tokens_ref, table_ref, send_ref):
     normal, _ = normalize(tokens_ref[...].astype(F32))
-    spectrum = dot(table_ref[...], normal.astype(BF16)).astype(BF16)
-    scatter_lanes(send_ref, spectrum, groups)
+    scatter_lanes(send_ref, along_w(table_ref, normal.astype(BF16), normal.shape[0]), groups)
 
 
 def mix_kernel(
@@ -254,7 +270,7 @@
 def second_kernel(kept_ref, in_ref, out_ref, mine_ref, core_ref, one_ref, small_ref, y_ref, x_ref):
     small_ref[...] = add_up(mine_ref[...], core_ref[...]).astype(BF16)
     for part, source, ref in ((0, in_ref, y_ref), (1, out_ref, x_ref)):
-        ref[...] = add_up(kept_ref[part, 0, 1], one_ref[part], source[1]).astype(BF16)
+        ref[...] = add_up(kept_ref[part, 0, 1], one_ref[part], source[...]).astype(BF16)
 
 
 def third_kernel(place_ref, kept_ref, in_ref, out_ref, y_ref, x_ref, *refs):
@@ -263,7 +279,7 @@
         line_ref[(place_ref[0] >> 3) ^ z] = ref[...]
     for part, source, last in ((0, in_ref, y_ref), (1, out_ref, x_ref)):
         for z in range(4):
-            total = add_up(kept_ref[part, 0, 0, z], one_ref[part, z], source[0, z], last[z])
+            total = add_up(kept_ref[part, 0, 0, z], one_ref[part, z], source[z], last[z])
             if z == 0:
                 own_ref[part] = total
             else:
@@ -331,8 +347,8 @@
 
 
 def step_all(block, scale, place_ref, *refs):
+    step_rest(block, scale, place_ref, *refs[10:18], *refs[26:])
     step_weights(scale, *refs[:10], *refs[18:26])
-    step_rest(block, scale, place_ref, *refs[10:18], *refs[26:])
 
 
 def step_weights(scale, own_ref, *refs):
@@ -353,10 +369,10 @@
         ref.flush()
 
 
-def load_weights(near, place_ref, pieces, w_in, w_out, sems):
+def load_weights(near, place_ref, pieces, targets, sems):
     copies = []
     if not near:
-        copies = [(pieces[0].at[:, part], target) for part, target in enumerate((w_in, w_out))]
+        copies = [(pieces[0].at[:, part], target) for part, target in targets]
     else:
         me = place_ref[0]
         at = [(me >> 1) & 1, (me >> 2) & 1, me & 1, me >> 3]
@@ -368,7 +384,7 @@
                     z = 2 * (i & 1) + k
                     row = (((at[3] ^ z) * 2 + (at[1] ^ y)) * 2 + (at[0] ^ (i >> 2))) * size
                     rows = pl.ds(pl.multiple_of(row, size), size)
-                    for part, target in enumerate((w_in, w_out)):
+                    for part, target in targets:
                         copies.append((ref.at[j, k, part], target.at[at[2] ^ x, rows]))
     copies = [pltpu.make_async_copy(source, target, sems.at[i]) for i, (source, target) in enumerate(copies)]
     for copy in copies:
@@ -376,33 +392,49 @@
     return copies
 
 
+def place_rows(ref, values, columns, orders):
+    if not orders:
+        ref[:, columns] = values
+        return
+    size = values.shape[0] // len(orders)
+    for block, order in enumerate(orders):
+        ref[pl.ds(pl.multiple_of(order * size, size), size), columns] = values[block * size : (block + 1) * size]
+
+
 def mlp_kernel(
     groups, near, place_ref, got_ref, wide_t_ref, tokens_ref, cotangent_ref, vectors_ref, bias_ref, wide_ref, *refs
 ):
     count = 8 if near else 1
     pieces, refs = refs[:count], refs[count:]
-    output_ref, middle_ref, send_ref, small_ref, *refs = refs
+    active, total_ref, middle_ref, send_ref, small_ref, *refs = refs
     grad_refs, refs = refs[:2], refs[2:]
-    normed, normed_t, cotangent_t, normal, spread, upstream_ref, w_in, w_out, active, grad_hidden, sems = refs
-    copies = load_weights(near, place_ref, pieces, w_in, w_out, sems)
+    normed, normed_t, cotangent_t, normal, spread, w_in, w_out, grad_hidden, sems = refs
+    copies = load_weights(near, place_ref, pieces, [(0, w_in), (1, w_out)], sems)
+    me = place_ref[0]
+    orders = [((z ^ (me >> 3)) + 4 * (y ^ ((me >> 2) & 1)) + 8 * (c ^ ((me >> 1) & 1))) for z in range(4) for y in range(2) for c in range(2)]
+    orders = orders if near else []
     tokens, width = tokens_ref.shape
     halves, _, columns = w_in.shape
     gain, shift, bias_out = vectors_ref[2:3, :], vectors_ref[3:4, :], vectors_ref[4:5, :]
     row_blocks = [slice(r, r + ROWS) for r in range(0, tokens, ROWS)]
-    spectrum = gather_lanes(got_ref, groups)
+    spectra = spans(gather_lanes(got_ref, groups))
+    span = wide_t_ref.shape[0]
     bias_out_grad = jnp.zeros((1, width), F32)
     for rows in row_blocks:
-        middle = tokens_ref[rows, :].astype(F32) + dot(wide_t_ref[rows, :], spectrum)
+        first = rows.start % span
+        spatial = dot(wide_t_ref[first : first + ROWS, :], spectra[rows.start // span])
+        middle = tokens_ref[rows, :].astype(F32) + spatial
         unit, inverse = normalize(middle)
         normal[rows, :] = unit
         spread[rows, :] = inverse
         scaled = (unit * gain + shift).astype(BF16)
         normed[rows, :] = scaled
-        normed_t[:, rows] = scaled.T
-        middle_ref[rows, :] = middle + bias_out
+        place_rows(normed_t, scaled.T, rows, orders)
+        total_ref[rows, :] = middle + bias_out
         upstream = cotangent_ref[rows, :]
-        cotangent_t[:, rows] = upstream.T
+        place_rows(cotangent_t, upstream.T, rows, orders)
         bias_out_grad = bias_out_grad + jnp.sum(upstream.astype(F32), axis=0, keepdims=True)
+    total_ref.flush()
     for copy in copies:
         copy.wait()
     gain_grad = jnp.zeros((1, width), F32)
@@ -418,26 +450,20 @@
             back = (dot(cotangent_ref[rows, :], w_out[h, :, lanes]) * slope).astype(BF16)
             grad_hidden[rows, flat] = back
             bias_grads[i] = bias_grads[i] + jnp.sum(back.astype(F32), axis=0, keepdims=True)
-        total, back = middle_ref[rows, :], None
-        for h in range(halves):
-            flat = slice(h * columns, (h + 1) * columns)
-            total = total + dot_nt(active[rows, flat], w_out[h])
-            term = dot_nt(grad_hidden[rows, flat], w_in[h])
-            back = term if back is None else back + term
-        output_ref[rows, :] = total.astype(BF16)
+        back = dot_nt(grad_hidden[rows, :columns], w_in[0])
+        for h in range(1, halves):
+            back = back + dot_nt(grad_hidden[rows, h * columns : (h + 1) * columns], w_in[h])
         unit = normal[rows, :]
         gain_grad = gain_grad + jnp.sum(back * unit, axis=0, keepdims=True)
         shift_grad = shift_grad + jnp.sum(back, axis=0, keepdims=True)
         middle = cotangent_ref[rows, :].astype(F32) + norm_back(back, unit, spread[rows, :], gain)
-        middle_ref[rows, :] = middle
-        upstream_ref[rows, :] = middle.astype(BF16)
-    output_ref.flush()
+        middle_ref[rows, :] = middle.astype(BF16)
+    active.flush()
     middle_ref.flush()
     small_ref[0:3, :] = jnp.concatenate([gain_grad, shift_grad, bias_out_grad], axis=0)
     small_ref[3:7, :] = jnp.concatenate(bias_grads, axis=0)
     small_ref[7:8, :] = jnp.zeros((1, width), F32)
-    spectrum = dot(wide_ref[...], upstream_ref[...]).astype(BF16)
-    scatter_lanes(send_ref, spectrum, groups)
+    scatter_lanes(send_ref, along_w(wide_ref, middle_ref, tokens), groups)
     send_ref.flush()
     for i, (h, c) in enumerate(chunks):
         flat = slice(h * columns + c, h * columns + c + CHUNK)
@@ -448,33 +474,45 @@
             for ref, grad in zip(grad_refs, grads, strict=True):
                 ref[h, :, c : c + CHUNK] = grad
             continue
-        me = place_ref[0]
-        at = [(me >> 1) & 1, (me >> 2) & 1, me & 1, me >> 3]
         size = w_in.shape[1] // 16
-        x = h ^ at[2]
-        for core in range(2):
-            for ref, mine in ((grad_refs[0], core), (grad_refs[1], 1 - core)):
-
-                @pl.when(at[0] == mine)
-                def _(ref=ref, core=core, c=c, x=x, grads=grads):
-                    for z in range(4):
-                        for y in range(2):
-                            rows = slice(((z * 2 + y) * 2 + core) * size, ((z * 2 + y) * 2 + core + 1) * size)
-                            for q in range(CHUNK // 128):
-                                lanes = slice(q * 128, (q + 1) * 128)
-                                place = slice((c // 128 + q) * size, (c // 128 + q + 1) * size)
-                                ref[0, x, y ^ at[1], z ^ at[3], place, :] = grads[0][rows, lanes]
-                                ref[1, y ^ at[1], x, z ^ at[3], place, :] = grads[1][rows, lanes]
+        x = h ^ (me & 1)
+        for core, ref in enumerate(grad_refs):
+            for y in range(2):
+                for z in range(4):
+                    block = core * 8 + y * 4 + z
+                    rows = slice(block * size, (block + 1) * size)
+                    for q in range(CHUNK // 128):
+                        lanes = slice(q * 128, (q + 1) * 128)
+                        place = slice((c // 128 + q) * size, (c // 128 + q + 1) * size)
+                        ref[0, x, y, z, place, :] = grads[0][rows, lanes]
+                        ref[1, y, x, z, place, :] = grads[1][rows, lanes]
+
+
+def output_kernel(near, place_ref, *refs):
+    count = 8 if near else 1
+    totals, actives, pieces = refs[:OUT_BLOCKS], refs[OUT_BLOCKS : 2 * OUT_BLOCKS], refs[2 * OUT_BLOCKS :][:count]
+    outputs, w_out, sems = refs[2 * OUT_BLOCKS + count], *refs[2 * OUT_BLOCKS + count + 1 :]
+    for copy in load_weights(near, place_ref, pieces, [(1, w_out)], sems):
+        copy.wait()
+    halves, _, columns = w_out.shape
+    size = totals[0].shape[0]
+    for i, (total, active) in enumerate(zip(totals, actives, strict=True)):
+        value = total[...]
+        for h in range(halves):
+            value = value + dot_nt(active[:, h * columns : (h + 1) * columns], w_out[h])
+        outputs[i * size : (i + 1) * size, :] = value.astype(BF16)
 
 
 def leave_kernel(groups, got_ref, tokens_ref, middle_ref, vectors_ref, table_ref, out_ref):
-    spectrum = gather_lanes(got_ref, groups)
+    spectra = spans(gather_lanes(got_ref, groups))
+    span = table_ref.shape[0]
     for start in range(0, tokens_ref.shape[0], ROWS):
         rows = slice(start, start + ROWS)
-        upstream = dot(table_ref[rows, :], spectrum)
+        first = start % span
+        upstream = dot(table_ref[first : first + ROWS, :], spectra[start // span])
         unit, inverse = normalize(tokens_ref[rows, :].astype(F32))
         back = norm_back(upstream, unit, inverse, vectors_ref[0:1, :])
-        out_ref[rows, :] = (middle_ref[rows, :] + back).astype(BF16)
+        out_ref[rows, :] = (middle_ref[rows, :].astype(F32) + back).astype(BF16)
 
 
 def update(weight, gradient, moment, average, decay_rate):
@@ -608,7 +646,7 @@
     modes = MODES // per_group
     joined = lanes // block
     scale = 1.0 / math.sqrt(local * devices)
-    wide_f, wide_i, high, ones = expanded_tables(grid, grid_rows, items)
+    wide_f, wide_i, high, ones = expanded_tables(grid, items)
     me = lax.axis_index("sp") * tp_count + lax.axis_index("tp")
     group = me // per_group
     exchange = functools.partial(lax.all_to_all, axis_name=AXES, split_axis=0, concat_axis=0, tiled=True)
@@ -649,7 +687,7 @@
     wide_f, wide_f_t = jnp.asarray(wide_f), jnp.asarray(wide_f.T)
     wide_i, wide_i_t = jnp.asarray(wide_i), jnp.asarray(wide_i.T)
     high, high_t = jnp.asarray(high), jnp.asarray(high.T)
-    wide_flops = 2 * wide_f.shape[0] * wide_f.shape[1] * width
+    wide_flops = 2 * MODES * 2 * local * width * SPAN
     (sent,) = call(
         functools.partial(enter_kernel, groups), [(chunk, BF16)], Far(rows_all), Far(wide_f), flops=wide_flops
     )
@@ -673,9 +711,13 @@
     got = exchange(sent)
     steps = hidden // CHUNK
     grads = [((2, 2, 2, 4, shard_size, 128), BF16)] * 2 if near else [((tp_count, model, shard_columns), BF16)] * 2
-    output, middle, sent, mlp_small, *grads = call(
+    gelus, total, middle, sent, mlp_small, *grads = call(
         functools.partial(mlp_kernel, groups, near),
-        [Far((local, width), BF16), Far((local, width), F32), Far(chunk, BF16), ((8, width), F32)] + grads,
+        [
+            Far((local, hidden), BF16), Far((local, width), F32), Far((local, width), BF16), Far(chunk, BF16),
+            ((8, width), F32),
+        ]
+        + grads,
         Far(got), Far(wide_i_t), Far(rows_all), Far(upstream_all), vectors, vectors[5:9].reshape(steps, CHUNK), Far(wide_i),
         scalars=[me[None]], raw=pieces,
         scratch=[
@@ -684,10 +726,8 @@
             pltpu.VMEM((width, local), BF16),
             pltpu.VMEM((local, width), F32),
             pltpu.VMEM((local, 1), F32),
-            pltpu.VMEM((local, width), BF16),
             pltpu.VMEM((tp_count, model, shard_columns), BF16),
             pltpu.VMEM((tp_count, model, shard_columns), BF16),
-            pltpu.VMEM((local, hidden), BF16),
             pltpu.VMEM((local, hidden), BF16),
             pltpu.SemaphoreType.DMA((64 if near else 2,)),
         ],
@@ -703,25 +743,37 @@
         )
         carried = [permute(sent_in, 1), permute(sent_out, 4)]
 
+    step = local // OUT_BLOCKS
+    parts = [slice(r, r + step) for r in range(0, local, step)]
+    (output,) = call(
+        functools.partial(output_kernel, near), [Far((local, width), BF16)],
+        *[Far(total, rows) for rows in parts], *[Far(gelus, rows) for rows in parts],
+        scalars=[me[None]], raw=pieces, cost=COST, vmem=24,
+        scratch=[
+            pltpu.VMEM((tp_count, model, shard_columns), BF16),
+            pltpu.SemaphoreType.DMA((32 if near else 1,)),
+        ],
+    )
+
     got = exchange(sent)
     small_rows = -(-(2 * block + 8 + 8 * (groups // 2)) // 16) * 16
     place = ((me >> 1) & 1 if near else jnp.int32(0))[None]
-    sent, small, given = call(
+    sent, small, given, output = call(
         functools.partial(unmix_kernel, modes, block),
         [Far(chunk, BF16), ((small_rows, lanes), BF16), ((small_rows, lanes), BF16)],
         got, Far(high), Far(high_t), Far(mats), own_ones, Far(hat), Far(modal), Far(inner), Far(active), mlp_small,
-        scalars=[place], cost=COST, vmem=20 if near else 48,
+        scalars=[place], cost=COST, vmem=20 if near else 48, carry=[output],
     )
     if near:
         both = slice(None)
         small, over_y, over_x = call(
             second_kernel, [((small_rows, lanes), BF16)] + [(shard, BF16)] * 2,
-            kept, *carried, small, permute(given, 2), Far(one, both, 0, 1), cost=0,
+            kept, *[Far(a, 1) for a in carried], small, permute(given, 2), Far(one, both, 0, 1), cost=0,
         )
         line, own, *away = call(
             third_kernel,
             [((4, small_rows, lanes), BF16), ((2, shard_size, 128), F32)] + [((2, shard_size, 128), BF16)] * 3,
-            kept, *carried, permute(over_y, 4), permute(over_x, 1),
+            kept, *[Far(a, 0) for a in carried], permute(over_y, 4), permute(over_x, 1),
             small, *[permute(small, 8 * z) for z in (1, 2, 3)], Far(one, both, 0, 0),
             scalars=[me[None]], cost=0,
         )

time: 150 us -> 145 us (0.967)
  waiting for transfers between devices: 44.9 us -> 37.7 us
    all_to_all x4, waiting for transfers between devices: 10.7 us -> 4.17 us  [on_device(): got = exchange(sent)]
    pallas_call x10 -> x11, Pallas kernels: 51.5 us -> 51.9 us  [call(): pl.pallas_call(inner, out_shape=[(pltpu.HBM if f else pltpu.VMEM)(o.shape...]
  transfers between devices with their start and end apart: 31 -> 31, of which waited for: 13 -> 12; matrix products, arithmetic and copies ran while one was open for 2% -> 3% of each run, Pallas kernels for 13% -> 17%
where the time goes in v4:
time: 145 us; the launch traced here: 144 us
  Pallas kernels  51.9 us (36%)
  starting transfers between devices  48.3 us (33%)
  waiting for transfers between devices  37.7 us (26%)
  other arithmetic  2.49 us (2%)
  local copies, waits for them, and re-layouts  2.36 us (2%)
    pallas_call x11, Pallas kernels, call(): pl.pallas_call(inner, out_shape=[(pltpu.HBM if f else pltpu.VMEM)(o.shape...  51.9 us
    ppermute x27, waiting for transfers between devices, permute(): return lax.ppermute(values, AXES, [(d, d ^ mask) for d in range(devices)])  33.5 us
    ppermute x27, starting transfers between devices, permute(): return lax.ppermute(values, AXES, [(d, d ^ mask) for d in range(devices)])  31.8 us
    all_to_all x4, starting transfers between devices, on_device(): got = exchange(sent)  16.5 us
    all_to_all x4, waiting for transfers between devices, on_device(): got = exchange(sent)  4.17 us
  transfers between devices with their start and end apart: 31, of which 12 were waited for; matrix products, arithmetic and copies ran while one was open for 3% of the time, Pallas kernels for 17%

profile of v4, /device:TPU:0, one launch (start us, length us, event | category | flops | bytes accessed | tf_op | source)
XLA Modules:
  0.0 144.2 jit_solution(8299254938329532908)
XLA Ops:
  0.7 1.0 convert_bitcast_fusion
  1.7 4.1 %collective-permute-start.2 = (bf16[2,32,1024]{2,1,0:T(8,128)(2,1)S(1)}, bf16[2,32,1024]{2,1,0:T(8,128)(2,1)S(1)}, u32[]{:S(2)}, u32[]{:S(2)}) collective-permute-start(bf16[2,32,1024]{2,1,0:T(8,128)(2,1)S(1)} %get-tuple-element.117), channel_id=1, source_target_pairs={{0,16},{1,17},{2,18},{3,19},{4,20},{5,21},{6,22},{7,23},{8,24},{9,... | collective-permute-start | bytes 393224 | tf_op jit(solution)/shard_map/ppermute | solution.py:661
  5.8 1.3 collective-permute-start.3
  7.4 3.0 %shard_map.324 = bf16[32,64,128]{2,1,0:T(8,128)(2,1)} custom-call(bf16[1024,512]{1,0:T(8,128)(2,1)} %bitcast.40, bf16[256,512]{1,0:T(8,128)(2,1)} %constant.61.clone.refs_1_), custom_call_target="tpu_custom_call" | custom-call | flops 268435456 | bytes 1835008 | tf_op jit(solution)/shard_map/pallas_call | solution.py:615
  10.4 5.2 %all-to-all-start = ((bf16[32,64,128]{2,1,0:T(8,128)(2,1)}), bf16[32,64,128]{2,1,0:T(8,128)(2,1)S(1)}, u32[]{:S(2)}, u32[]{:S(2)}) async-start(bf16[32,64,128]{2,1,0:T(8,128)(2,1)} %shard_map.324), calls=%async_computation | async-start | bytes 1048576 | tf_op jit(solution)/shard_map/all_to_all | solution.py:694
  15.6 1.0 dynamic-slice_convert_fusion
  17.0 0.9 dynamic-slice_bitcast_fusion.refs_7_.refs_5_
  18.0 1.8 %collective-permute-start.4 = (bf16[2,2,32,1024]{3,2,1,0:T(8,128)(2,1)S(1)}, bf16[2,2,32,1024]{3,2,1,0:T(8,128)(2,1)S(1)}, u32[]{:S(2)}, u32[]{:S(2)}) collective-permute-start(bf16[2,2,32,1024]{3,2,1,0:T(8,128)(2,1)S(1)} %get-tuple-element.113), channel_id=1, source_target_pairs={{0,4},{1,5},{2,6},{3,7},{4,0},{5,1},{6,2},{7,3},{8,12},{9,13},{10,... | collective-permute-start | bytes 786440 | tf_op jit(solution)/shard_map/ppermute | solution.py:661
  19.9 1.5 %collective-permute-start.1 = (bf16[2,2,32,1024]{3,2,1,0:T(8,128)(2,1)S(1)}, bf16[2,2,32,1024]{3,2,1,0:T(8,128)(2,1)}, u32[]{:S(2)}, u32[]{:S(2)}) collective-permute-start(bf16[2,2,32,1024]{3,2,1,0:T(8,128)(2,1)S(1)} %get-tuple-element.115), channel_id=1, source_target_pairs={{0,1},{1,0},{2,3},{3,2},{4,5},{5,4},{6,7},{7,6},{8,9},{9,8},{10,11... | collective-permute-start | bytes 786440 | tf_op jit(solution)/shard_map/ppermute | solution.py:661
  21.8 8.2 %collective-permute-done.4 = bf16[2,2,32,1024]{3,2,1,0:T(8,128)(2,1)S(1)} collective-permute-done((bf16[2,2,32,1024]{3,2,1,0:T(8,128)(2,1)S(1)}, bf16[2,2,32,1024]{3,2,1,0:T(8,128)(2,1)S(1)}, u32[]{:S(2)}, u32[]{:S(2)}) %collective-permute-start.4) | collective-permute-done | bytes 262176 | tf_op jit(solution)/shard_map/ppermute | solution.py:661
  30.1 0.4 collective-permute-done.1
  30.5 1.0 pad_maximum_fusion.refs_8_
  31.5 2.3 %shard_map.325 = (bf16[32,64,128]{2,1,0:T(8,128)(2,1)}, f32[128,512]{1,0:T(8,128)}, bf16[256,256]{1,0:T(8,128)(2,1)}, f32[256,256]{1,0:T(8,128)}, bf16[256,256]{...) custom-call(bf16[32,64,128]{2,1,0:T(8,128)(2,1)S(1)} %all-to-all-don, ...), custom_call_target="tpu_custom_call", output_to_operand_aliasing={{5}: (8, {}), {6}: (9, {})} | custom-call | bytes 2364416 | tf_op jit(solution)/shard_map/pallas_call | solution.py:615
  33.9 1.2 collective-permute-start.6
  35.0 1.1 collective-permute-start.5
  36.1 4.3 %all-to-all-start.1 = ((bf16[32,64,128]{2,1,0:T(8,128)(2,1)}), bf16[32,64,128]{2,1,0:T(8,128)(2,1)}, u32[]{:S(2)}, u32[]{:S(2)}) async-start(bf16[32,64,128]{2,1,0:T(8,128)(2,1)} %get-tuple-element.64), calls=%async_computation.1 | async-start | bytes 1048576 | tf_op jit(solution)/shard_map/all_to_all | solution.py:711
  41.1 11.0 %collective-permute-done.6.refs_11_.refs_12_ = bf16[2,2,2,32,1024]{4,3,2,1,0:T(8,128)(2,1)S(1)} collective-permute-done((bf16[2,2,2,32,1024]{4,3,2,1,0:T(8,128)(2,1)S(1)}, bf16[2,2,2,32,1024]{4,3,2,1,0:T(8,128)(2,1)S(1)}, u32[]{:S(2)}, u32[]{:S(2)}) %collective-permute-start.6) | collective-permute-done | bytes 524320 | tf_op jit(solution)/shard_map/ppermute | solution.py:661
  52.6 2.7 %all-to-all-done.1.refs_1_ = bf16[32,64,128]{2,1,0:T(8,128)(2,1)} async-done(((bf16[32,64,128]{2,1,0:T(8,128)(2,1)}), bf16[32,64,128]{2,1,0:T(8,128)(2,1)}, u32[]{:S(2)}, u32[]{:S(2)}) %all-to-all-start.1) | async-done | bytes 524320 | tf_op jit(solution)/shard_map/all_to_all | solution.py:711
  55.3 21.4 %shard_map.326 = (bf16[1024,2048]{1,0:T(8,128)(2,1)}, f32[1024,512]{1,0:T(8,128)}, bf16[1024,512]{1,0:T(8,128)(2,1)}, bf16[32,64,128]{2,1,0:T(8,128)(2,1)}, f32[...) custom-call(s32[1]{0:T(128)} %bitcast.1.refs_0_, ...), custom_call_target="tpu_custom_call" | custom-call | flops 13421772800 | bytes 19449856 | tf_op jit(solution)/shard_map/pallas_call | solution.py:615
  76.7 1.1 collective-permute-start.11
  77.8 3.3 %all-to-all-start.2 = ((bf16[32,64,128]{2,1,0:T(8,128)(2,1)}), bf16[32,64,128]{2,1,0:T(8,128)(2,1)S(1)}, u32[]{:S(2)}, u32[]{:S(2)}) async-start(bf16[32,64,128]{2,1,0:T(8,128)(2,1)} %get-tuple-element.67), calls=%async_computation.2 | async-start | bytes 1048576 | tf_op jit(solution)/shard_map/all_to_all | solution.py:758
  81.2 0.8 collective-permute-done.11.refs_1_.refs_5_.refs_10_
  82.0 2.3 %shard_map.329 = (bf16[2,4,256,128]{3,2,1,0:T(8,128)(2,1)}, bf16[2,4,256,128]{3,2,1,0:T(8,128)(2,1)}) custom-call(bf16[2,2,2,4,256,128]{5,4,3,2,1,0:T(8,128)(2,1)S(1)} %get-tuple-element.76.refs_0_.refs_1_, bf16[2,2,2,4,256,128]{5,4,3,2,1,0:T(8,128)(2,1)} %collective-permute-done.11.refs_1_.refs_5_.refs_10_), custom_call_target="tpu_custom_call" | custom-call | tf_op jit(solution)/shard_map/pallas_call | solution.py:615
  84.3 1.2 collective-permute-start.12
  85.5 1.4 collective-permute-start.13
  86.8 7.8 %shard_map.327.refs_11_ = bf16[1024,512]{1,0:T(8,128)(2,1)} custom-call(s32[1]{0:T(128)} %bitcast.1.refs_0_, f32[1024,512]{1,0:T(8,128)} %get-tuple-element.73.refs_1_.refs_2_.refs_3_.refs_4_, f32[1024,512]{1,0:T(8,128)} %get-tuple-element.73.refs_1_.refs_2_.refs_3_.refs_4_, f32[1024,512]{1,0:T(8,128)} %get-tuple-element.73.refs_1_.refs_2_.refs_3_.refs_4_, ...), custom_call_target="tpu_custom_call" | custom-call | bytes 62914560 | tf_op jit(solution)/shard_map/pallas_call | solution.py:615
  94.7 1.5 %all-to-all-done.2.refs_1_ = bf16[32,64,128]{2,1,0:T(8,128)(2,1)S(1)} async-done(((bf16[32,64,128]{2,1,0:T(8,128)(2,1)}), bf16[32,64,128]{2,1,0:T(8,128)(2,1)S(1)}, u32[]{:S(2)}, u32[]{:S(2)}) %all-to-all-start.2) | async-done | bytes 524320 | tf_op jit(solution)/shard_map/all_to_all | solution.py:758
  96.2 3.0 %shard_map.328 = (bf16[32,64,128]{2,1,0:T(8,128)(2,1)}, bf16[160,128]{1,0:T(8,128)(2,1)S(1)}, bf16[160,128]{1,0:T(8,128)(2,1)S(1)}, bf16[1024,512]{1,0:T(8,128)(2,1)}) custom-call(s32[1]{0:T(128)} %bitcast.refs_0_, bf16[32,64,128]{2,1,0:T(8,128)(2,1)S(1)} %all-to-all-done.2.refs_1_, ...), custom_call_target="tpu_custom_call", output_to_operand_aliasing={{3}: (11, {})} | custom-call | bytes 62914560 | tf_op jit(solution)/shard_map/pallas_call | solution.py:615
  99.2 3.6 %all-to-all-start.3 = ((bf16[32,64,128]{2,1,0:T(8,128)(2,1)}), bf16[32,64,128]{2,1,0:T(8,128)(2,1)S(1)}, u32[]{:S(2)}, u32[]{:S(2)}) async-start(bf16[32,64,128]{2,1,0:T(8,128)(2,1)} %get-tuple-element.90), calls=%async_computation.3 | async-start | bytes 1048576 | tf_op jit(solution)/shard_map/all_to_all | solution.py:781
  103.1 1.0 collective-permute-done.14.refs_4_
  104.1 1.5 %shard_map.330 = (bf16[160,128]{1,0:T(8,128)(2,1)S(1)}, bf16[4,256,128]{2,1,0:T(8,128)(2,1)S(1)}, bf16[4,256,128]{2,1,0:T(8,128)(2,1)S(1)}) custom-call(bf16[2,2,2,4,256,128]{5,4,3,2,1,0:T(8,128)(2,1)S(1)} %get-tuple-element.76.refs_0_.refs_1_, bf16[2,4,256,128]{3,2,1,0:T(8,128)(2,1)} %collective-permute-done.12.refs_1_.refs_2_, ...), custom_call_target="tpu_custom_call" | custom-call | tf_op jit(solution)/shard_map/pallas_call | solution.py:615
  105.6 1.8 %collective-permute-start.15 = (bf16[4,256,128]{2,1,0:T(8,128)(2,1)S(1)}, bf16[4,256,128]{2,1,0:T(8,128)(2,1)S(1)}, u32[]{:S(2)}, u32[]{:S(2)}) collective-permute-start(bf16[4,256,128]{2,1,0:T(8,128)(2,1)S(1)} %get-tuple-element.82), channel_id=1, source_target_pairs={{0,4},{1,5},{2,6},{3,7},{4,0},{5,1},{6,2},{7,3},{8,12},{9,13},{10,... | collective-permute-start | bytes 786440 | tf_op jit(solution)/shard_map/ppermute | solution.py:661
  107.4 1.5 %collective-permute-start.16 = (bf16[4,256,128]{2,1,0:T(8,128)(2,1)S(1)}, bf16[4,256,128]{2,1,0:T(8,128)(2,1)S(1)}, u32[]{:S(2)}, u32[]{:S(2)}) collective-permute-start(bf16[4,256,128]{2,1,0:T(8,128)(2,1)S(1)} %get-tuple-element.83), channel_id=1, source_target_pairs={{0,1},{1,0},{2,3},{3,2},{4,5},{5,4},{6,7},{7,6},{8,9},{9,8},{10,11... | collective-permute-start | bytes 786440 | tf_op jit(solution)/shard_map/ppermute | solution.py:661
  108.9 1.5 %collective-permute-start.17 = (bf16[160,128]{1,0:T(8,128)(2,1)S(1)}, bf16[160,128]{1,0:T(8,128)(2,1)S(1)}, u32[]{:S(2)}, u32[]{:S(2)}) collective-permute-start(bf16[160,128]{1,0:T(8,128)(2,1)S(1)} %get-tuple-element.84.refs_6_), channel_id=1, source_target_pairs={{0,8},{1,9},{2,10},{3,11},{4,12},{5,13},{6,14},{7,15},{8,0},{9,1},... | collective-permute-start | bytes 122888 | tf_op jit(solution)/shard_map/ppermute | solution.py:661
  110.3 2.5 %collective-permute-start.18 = (bf16[160,128]{1,0:T(8,128)(2,1)S(1)}, bf16[160,128]{1,0:T(8,128)(2,1)S(1)}, u32[]{:S(2)}, u32[]{:S(2)}) collective-permute-start(bf16[160,128]{1,0:T(8,128)(2,1)S(1)} %get-tuple-element.84.refs_6_), channel_id=1, source_target_pairs={{0,16},{1,17},{2,18},{3,19},{4,20},{5,21},{6,22},{7,23},{8,24},{9,... | collective-permute-start | bytes 122888 | tf_op jit(solution)/shard_map/ppermute | solution.py:661
  112.8 0.5 collective-permute-start.19
  113.4 7.4 %collective-permute-done.18.refs_8_ = bf16[160,128]{1,0:T(8,128)(2,1)S(1)} collective-permute-done((bf16[160,128]{1,0:T(8,128)(2,1)S(1)}, bf16[160,128]{1,0:T(8,128)(2,1)S(1)}, u32[]{:S(2)}, u32[]{:S(2)}) %collective-permute-start.18) | collective-permute-done | bytes 40992 | tf_op jit(solution)/shard_map/ppermute | solution.py:661
  120.9 2.1 %shard_map.331 = (bf16[4,160,128]{2,1,0:T(8,128)(2,1)S(1)}, f32[2,256,128]{2,1,0:T(8,128)S(1)}, bf16[2,256,128]{2,1,0:T(8,128)(2,1)S(1)}, bf16[2,256,128]{2,1,0:T(8,128)(2,1)}, bf16[2,256,128]{2,1,0:T(8,128)(2,1)}) custom-call(s32[1]{0:T(128)} %bitcast.1.refs_0_, bf16[2,2,2,4,256,128]{5,4,3,2,1,0:T(8,128)(2,1)S(1)} %get-tuple-element.76.refs_0_.refs_1_, ...), custom_call_target="tpu_custom_call" | custom-call | tf_op jit(solution)/shard_map/pallas_call | solution.py:615
  123.0 1.1 collective-permute-start.23
  124.1 1.5 %collective-permute-start.20 = (bf16[4,160,128]{2,1,0:T(8,128)(2,1)S(1)}, bf16[4,160,128]{2,1,0:T(8,128)(2,1)S(1)}, u32[]{:S(2)}, u32[]{:S(2)}) collective-permute-start(bf16[4,160,128]{2,1,0:T(8,128)(2,1)S(1)} %get-tuple-element.86.refs_0_), channel_id=1, source_target_pairs={{0,1},{1,0},{2,3},{3,2},{4,5},{5,4},{6,7},{7,6},{8,9},{9,8},{10,11... | collective-permute-start | bytes 491528 | tf_op jit(solution)/shard_map/ppermute | solution.py:661
  125.5 1.5 %collective-permute-start.21 = (bf16[4,160,128]{2,1,0:T(8,128)(2,1)S(1)}, bf16[4,160,128]{2,1,0:T(8,128)(2,1)S(1)}, u32[]{:S(2)}, u32[]{:S(2)}) collective-permute-start(bf16[4,160,128]{2,1,0:T(8,128)(2,1)S(1)} %get-tuple-element.86.refs_0_), channel_id=1, source_target_pairs={{0,4},{1,5},{2,6},{3,7},{4,0},{5,1},{6,2},{7,3},{8,12},{9,13},{10,... | collective-permute-start | bytes 491528 | tf_op jit(solution)/shard_map/ppermute | solution.py:661
  127.0 0.5 collective-permute-start.22
  127.6 0.7 collective-permute-start.24
  128.2 2.7 %collective-permute-start.25 = (bf16[2,256,128]{2,1,0:T(8,128)(2,1)}, bf16[2,256,128]{2,1,0:T(8,128)(2,1)S(1)}, u32[]{:S(2)}, u32[]{:S(2)}) collective-permute-start(bf16[2,256,128]{2,1,0:T(8,128)(2,1)} %get-tuple-element.89), channel_id=1, source_target_pairs={{0,24},{1,25},{2,26},{3,27},{4,28},{5,29},{6,30},{7,31},{8,16},{9,... | collective-permute-start | bytes 393224 | tf_op jit(solution)/shard_map/ppermute | solution.py:661
  131.1 4.5 %shard_map.332.refs_7_ = bf16[1024,512]{1,0:T(8,128)(2,1)} custom-call(bf16[32,64,128]{2,1,0:T(8,128)(2,1)S(1)} %all-to-all-done.3.refs_0_, bf16[1024,512]{1,0:T(8,128)(2,1)} %bitcast.42, bf16[1024,512]{1,0:T(8,128)(2,1)} %get-tuple-element.91.refs_2_, f32[13,512]{1,0:T(8,128)S(1)} %copy-done.10, bf16[512,256]{1,0:T(8,128)(2,1)} %constant.62.clone.refs_4_), custom_call_target="tpu_custom_call" | custom-call | bytes 62914560 | tf_op jit(solution)/shard_map/pallas_call | solution.py:615
  135.6 2.8 %collective-permute-done.24.refs_5_ = bf16[2,256,128]{2,1,0:T(8,128)(2,1)S(1)} collective-permute-done((bf16[2,256,128]{2,1,0:T(8,128)(2,1)}, bf16[2,256,128]{2,1,0:T(8,128)(2,1)S(1)}, u32[]{:S(2)}, u32[]{:S(2)}) %collective-permute-start.24) | collective-permute-done | bytes 131104 | tf_op jit(solution)/shard_map/ppermute | solution.py:661
  138.6 1.4 collective-permute-done.26.refs_12_
  140.1 3.9 %shard_map.334 = (f32[32,1024]{1,0:T(8,128)}, f32[32,1024]{1,0:T(8,128)}, f32[32,1024]{1,0:T(8,128)}, f32[32,1024]{1,0:T(8,128)}, f32[32,1024]{1,0:T(8,128)}, /*...) custom-call(s32[1]{0:T(128)} %bitcast.refs_0_, ...), custom_call_target="tpu_custom_call", output_to_operand_aliasing={{14}: (19, {})} | custom-call | tf_op jit(solution)/shard_map/pallas_call | solution.py:615
  (89 shorter events, 3.1 us)
Async XLA Ops:
  0.6 16.0 %copy-start.10 = (f32[13,512]{1,0:T(8,128)S(1)}, f32[13,512]{1,0:T(8,128)}, u32[]{:S(2)}) copy-start(f32[13,512]{1,0:T(8,128)} %refs_16_.1) | copy-start | bytes 79876
  1.7 16.3 %collective-permute-start.2 = (bf16[2,32,1024]{2,1,0:T(8,128)(2,1)S(1)}, bf16[2,32,1024]{2,1,0:T(8,128)(2,1)S(1)}, u32[]{:S(2)}, u32[]{:S(2)}) collective-permute-start(bf16[2,32,1024]{2,1,0:T(8,128)(2,1)S(1)} %get-tuple-element.117), channel_id=1, source_target_pairs={{0,16},{1,17},{2,18},{3,19},{4,20},{5,21},{6,22},{7,23},{8,24},{9,... | collective-permute-start | bytes 393224 | tf_op jit(solution)/shard_map/ppermute | solution.py:661
  5.8 12.2 %collective-permute-start.3 = (bf16[2,32,1024]{2,1,0:T(8,128)(2,1)S(1)}, bf16[2,32,1024]{2,1,0:T(8,128)(2,1)S(1)}, u32[]{:S(2)}, u32[]{:S(2)}) collective-permute-start(bf16[2,32,1024]{2,1,0:T(8,128)(2,1)S(1)} %get-tuple-element.117), channel_id=1, source_target_pairs={{0,24},{1,25},{2,26},{3,27},{4,28},{5,29},{6,30},{7,31},{8,16},{9,... | collective-permute-start | bytes 393224 | tf_op jit(solution)/shard_map/ppermute | solution.py:661
  7.1 12.7 %collective-permute-start = (bf16[2,32,1024]{2,1,0:T(8,128)(2,1)S(1)}, bf16[2,32,1024]{2,1,0:T(8,128)(2,1)S(1)}, u32[]{:S(2)}, u32[]{:S(2)}) collective-permute-start(bf16[2,32,1024]{2,1,0:T(8,128)(2,1)S(1)} %get-tuple-element.117), channel_id=1, source_target_pairs={{0,8},{1,9},{2,10},{3,11},{4,12},{5,13},{6,14},{7,15},{8,0},{9,1},... | collective-permute-start | bytes 393224 | tf_op jit(solution)/shard_map/ppermute | solution.py:661
  10.4 21.1 %all-to-all-start = ((bf16[32,64,128]{2,1,0:T(8,128)(2,1)}), bf16[32,64,128]{2,1,0:T(8,128)(2,1)S(1)}, u32[]{:S(2)}, u32[]{:S(2)}) async-start(bf16[32,64,128]{2,1,0:T(8,128)(2,1)} %shard_map.324), calls=%async_computation | async-start | bytes 1048576 | tf_op jit(solution)/shard_map/all_to_all | solution.py:694
  18.0 13.5 %copy-start.8 = (bf16[128,512]{1,0:T(8,128)(2,1)S(1)}, bf16[128,512]{1,0:T(8,128)(2,1)}, u32[]{:S(2)}) copy-start(bf16[128,512]{1,0:T(8,128)(2,1)} %constant.65.clone.refs_1_.refs_2_) | copy-start | bytes 393220
  18.0 13.5 %copy-start.9 = (bf16[512,128]{1,0:T(8,128)(2,1)S(1)}, bf16[512,128]{1,0:T(8,128)(2,1)}, u32[]{:S(2)}) copy-start(bf16[512,128]{1,0:T(8,128)(2,1)} %constant.66.clone.refs_2_.refs_3_) | copy-start | bytes 393220
  18.0 12.0 %collective-permute-start.4 = (bf16[2,2,32,1024]{3,2,1,0:T(8,128)(2,1)S(1)}, bf16[2,2,32,1024]{3,2,1,0:T(8,128)(2,1)S(1)}, u32[]{:S(2)}, u32[]{:S(2)}) collective-permute-start(bf16[2,2,32,1024]{3,2,1,0:T(8,128)(2,1)S(1)} %get-tuple-element.113), channel_id=1, source_target_pairs={{0,4},{1,5},{2,6},{3,7},{4,0},{5,1},{6,2},{7,3},{8,12},{9,13},{10,... | collective-permute-start | bytes 786440 | tf_op jit(solution)/shard_map/ppermute | solution.py:661
  19.9 10.6 %collective-permute-start.1 = (bf16[2,2,32,1024]{3,2,1,0:T(8,128)(2,1)S(1)}, bf16[2,2,32,1024]{3,2,1,0:T(8,128)(2,1)}, u32[]{:S(2)}, u32[]{:S(2)}) collective-permute-start(bf16[2,2,32,1024]{3,2,1,0:T(8,128)(2,1)S(1)} %get-tuple-element.115), channel_id=1, source_target_pairs={{0,1},{1,0},{2,3},{3,2},{4,5},{5,4},{6,7},{7,6},{8,9},{9,8},{10,11... | collective-permute-start | bytes 786440 | tf_op jit(solution)/shard_map/ppermute | solution.py:661
  21.8 12.0 %copy-start.2 = (bf16[2,256,256]{2,1,0:T(8,128)(2,1)}, bf16[2,256,256]{2,1,0:T(8,128)(2,1)S(1)}, u32[]{:S(2)}) copy-start(bf16[2,256,256]{2,1,0:T(8,128)(2,1)S(1)} %maximum_maximum_fusion.refs_3_.refs_4_) | copy-start | bytes 786436
  33.8 21.5 %copy-start = (bf16[2,2,2,32,1024]{4,3,2,1,0:T(8,128)(2,1)}, bf16[2,2,2,32,1024]{4,3,2,1,0:T(8,128)(2,1)S(1)}, u32[]{:S(2)}) copy-start(bf16[2,2,2,32,1024]{4,3,2,1,0:T(8,128)(2,1)S(1)} %get-tuple-element.66.refs_9_.refs_10_) | copy-start | bytes 1572868
  33.9 21.5 %copy-start.1 = (bf16[2,2,2,32,1024]{4,3,2,1,0:T(8,128)(2,1)}, bf16[2,2,2,32,1024]{4,3,2,1,0:T(8,128)(2,1)S(1)}, u32[]{:S(2)}) copy-start(bf16[2,2,2,32,1024]{4,3,2,1,0:T(8,128)(2,1)S(1)} %get-tuple-element.65.refs_8_.refs_9_) | copy-start | bytes 1572868
  33.9 18.2 %collective-permute-start.6 = (bf16[2,2,2,32,1024]{4,3,2,1,0:T(8,128)(2,1)S(1)}, bf16[2,2,2,32,1024]{4,3,2,1,0:T(8,128)(2,1)S(1)}, u32[]{:S(2)}, u32[]{:S(2)}) collective-permute-start(bf16[2,2,2,32,1024]{4,3,2,1,0:T(8,128)(2,1)S(1)} %get-tuple-element.66.refs_9_.refs_10_), channel_id=1, source_target_pairs={{0,1},{1,0},{2,3},{3,2},{4,5},{5,4},{6,7},{7,6},{8,9},{9,8},{10,11... | collective-permute-start | bytes 1572872 | tf_op jit(solution)/shard_map/ppermute | solution.py:661
  35.0 17.3 %collective-permute-start.5 = (bf16[2,2,2,32,1024]{4,3,2,1,0:T(8,128)(2,1)S(1)}, bf16[2,2,2,32,1024]{4,3,2,1,0:T(8,128)(2,1)S(1)}, u32[]{:S(2)}, u32[]{:S(2)}) collective-permute-start(bf16[2,2,2,32,1024]{4,3,2,1,0:T(8,128)(2,1)S(1)} %get-tuple-element.65.refs_8_.refs_9_), channel_id=1, source_target_pairs={{0,4},{1,5},{2,6},{3,7},{4,0},{5,1},{6,2},{7,3},{8,12},{9,13},{10,... | collective-permute-start | bytes 1572872 | tf_op jit(solution)/shard_map/ppermute | solution.py:661
  36.1 19.1 %all-to-all-start.1 = ((bf16[32,64,128]{2,1,0:T(8,128)(2,1)}), bf16[32,64,128]{2,1,0:T(8,128)(2,1)}, u32[]{:S(2)}, u32[]{:S(2)}) async-start(bf16[32,64,128]{2,1,0:T(8,128)(2,1)} %get-tuple-element.64), calls=%async_computation.1 | async-start | bytes 1048576 | tf_op jit(solution)/shard_map/all_to_all | solution.py:711
  40.5 12.1 %collective-permute-start.7 = (bf16[2,2,2,32,1024]{4,3,2,1,0:T(8,128)(2,1)S(1)}, bf16[2,2,2,32,1024]{4,3,2,1,0:T(8,128)(2,1)S(1)}, u32[]{:S(2)}, u32[]{:S(2)}) collective-permute-start(bf16[2,2,2,32,1024]{4,3,2,1,0:T(8,128)(2,1)S(1)} %get-tuple-element.65.refs_8_.refs_9_), channel_id=1, source_target_pairs={{0,2},{1,3},{2,0},{3,1},{4,6},{5,7},{6,4},{7,5},{8,10},{9,11},{10,... | collective-permute-start | bytes 1572872 | tf_op jit(solution)/shard_map/ppermute | solution.py:661
  40.7 11.9 %collective-permute-start.8 = (bf16[2,2,2,32,1024]{4,3,2,1,0:T(8,128)(2,1)S(1)}, bf16[2,2,2,32,1024]{4,3,2,1,0:T(8,128)(2,1)S(1)}, u32[]{:S(2)}, u32[]{:S(2)}) collective-permute-start(bf16[2,2,2,32,1024]{4,3,2,1,0:T(8,128)(2,1)S(1)} %get-tuple-element.66.refs_9_.refs_10_), channel_id=1, source_target_pairs={{0,2},{1,3},{2,0},{3,1},{4,6},{5,7},{6,4},{7,5},{8,10},{9,11},{10,... | collective-permute-start | bytes 1572872 | tf_op jit(solution)/shard_map/ppermute | solution.py:661
  52.1 3.2 %collective-permute-start.10 = (bf16[2,2,2,32,1024]{4,3,2,1,0:T(8,128)(2,1)S(1)}, bf16[2,2,2,32,1024]{4,3,2,1,0:T(8,128)(2,1)}, u32[]{:S(2)}, u32[]{:S(2)}) collective-permute-start(bf16[2,2,2,32,1024]{4,3,2,1,0:T(8,128)(2,1)S(1)} %collective-permute-done.6.refs_11_.refs_12_), channel_id=1, source_target_pairs={{0,2},{1,3},{2,0},{3,1},{4,6},{5,7},{6,4},{7,5},{8,10},{9,11},{10,... | collective-permute-start | bytes 1572872 | tf_op jit(solution)/shard_map/ppermute | solution.py:661
  52.4 2.9 %collective-permute-start.9 = (bf16[2,2,2,32,1024]{4,3,2,1,0:T(8,128)(2,1)S(1)}, bf16[2,2,2,32,1024]{4,3,2,1,0:T(8,128)(2,1)}, u32[]{:S(2)}, u32[]{:S(2)}) collective-permute-start(bf16[2,2,2,32,1024]{4,3,2,1,0:T(8,128)(2,1)S(1)} %collective-permute-done.5.refs_10_.refs_11_), channel_id=1, source_target_pairs={{0,2},{1,3},{2,0},{3,1},{4,6},{5,7},{6,4},{7,5},{8,10},{9,11},{10,... | collective-permute-start | bytes 1572872 | tf_op jit(solution)/shard_map/ppermute | solution.py:661
  76.7 5.3 %collective-permute-start.11 = (bf16[2,2,2,4,256,128]{5,4,3,2,1,0:T(8,128)(2,1)}, bf16[2,2,2,4,256,128]{5,4,3,2,1,0:T(8,128)(2,1)}, u32[]{:S(2)}, u32[]{:S(2)}) collective-permute-start(bf16[2,2,2,4,256,128]{5,4,3,2,1,0:T(8,128)(2,1)} %get-tuple-element.77), channel_id=1, source_target_pairs={{0,2},{1,3},{2,0},{3,1},{4,6},{5,7},{6,4},{7,5},{8,10},{9,11},{10,... | collective-permute-start | bytes 6291464 | tf_op jit(solution)/shard_map/ppermute | solution.py:661
  77.8 18.3 %all-to-all-start.2 = ((bf16[32,64,128]{2,1,0:T(8,128)(2,1)}), bf16[32,64,128]{2,1,0:T(8,128)(2,1)S(1)}, u32[]{:S(2)}, u32[]{:S(2)}) async-start(bf16[32,64,128]{2,1,0:T(8,128)(2,1)} %get-tuple-element.67), calls=%async_computation.2 | async-start | bytes 1048576 | tf_op jit(solution)/shard_map/all_to_all | solution.py:758
  84.3 19.8 %collective-permute-start.12 = (bf16[2,4,256,128]{3,2,1,0:T(8,128)(2,1)}, bf16[2,4,256,128]{3,2,1,0:T(8,128)(2,1)}, u32[]{:S(2)}, u32[]{:S(2)}) collective-permute-start(bf16[2,4,256,128]{3,2,1,0:T(8,128)(2,1)} %get-tuple-element.78), channel_id=1, source_target_pairs={{0,1},{1,0},{2,3},{3,2},{4,5},{5,4},{6,7},{7,6},{8,9},{9,8},{10,11... | collective-permute-start | bytes 1572872 | tf_op jit(solution)/shard_map/ppermute | solution.py:661
  85.5 18.6 %collective-permute-start.13 = (bf16[2,4,256,128]{3,2,1,0:T(8,128)(2,1)}, bf16[2,4,256,128]{3,2,1,0:T(8,128)(2,1)}, u32[]{:S(2)}, u32[]{:S(2)}) collective-permute-start(bf16[2,4,256,128]{3,2,1,0:T(8,128)(2,1)} %get-tuple-element.79), channel_id=1, source_target_pairs={{0,4},{1,5},{2,6},{3,7},{4,0},{5,1},{6,2},{7,3},{8,12},{9,13},{10,... | collective-permute-start | bytes 1572872 | tf_op jit(solution)/shard_map/ppermute | solution.py:661
  99.2 31.8 %all-to-all-start.3 = ((bf16[32,64,128]{2,1,0:T(8,128)(2,1)}), bf16[32,64,128]{2,1,0:T(8,128)(2,1)S(1)}, u32[]{:S(2)}, u32[]{:S(2)}) async-start(bf16[32,64,128]{2,1,0:T(8,128)(2,1)} %get-tuple-element.90), calls=%async_computation.3 | async-start | bytes 1048576 | tf_op jit(solution)/shard_map/all_to_all | solution.py:781
  102.8 1.3 collective-permute-start.14
  105.6 15.3 %collective-permute-start.15 = (bf16[4,256,128]{2,1,0:T(8,128)(2,1)S(1)}, bf16[4,256,128]{2,1,0:T(8,128)(2,1)S(1)}, u32[]{:S(2)}, u32[]{:S(2)}) collective-permute-start(bf16[4,256,128]{2,1,0:T(8,128)(2,1)S(1)} %get-tuple-element.82), channel_id=1, source_target_pairs={{0,4},{1,5},{2,6},{3,7},{4,0},{5,1},{6,2},{7,3},{8,12},{9,13},{10,... | collective-permute-start | bytes 786440 | tf_op jit(solution)/shard_map/ppermute | solution.py:661
  107.4 13.5 %collective-permute-start.16 = (bf16[4,256,128]{2,1,0:T(8,128)(2,1)S(1)}, bf16[4,256,128]{2,1,0:T(8,128)(2,1)S(1)}, u32[]{:S(2)}, u32[]{:S(2)}) collective-permute-start(bf16[4,256,128]{2,1,0:T(8,128)(2,1)S(1)} %get-tuple-element.83), channel_id=1, source_target_pairs={{0,1},{1,0},{2,3},{3,2},{4,5},{5,4},{6,7},{7,6},{8,9},{9,8},{10,11... | collective-permute-start | bytes 786440 | tf_op jit(solution)/shard_map/ppermute | solution.py:661
  108.9 4.6 %collective-permute-start.17 = (bf16[160,128]{1,0:T(8,128)(2,1)S(1)}, bf16[160,128]{1,0:T(8,128)(2,1)S(1)}, u32[]{:S(2)}, u32[]{:S(2)}) collective-permute-start(bf16[160,128]{1,0:T(8,128)(2,1)S(1)} %get-tuple-element.84.refs_6_), channel_id=1, source_target_pairs={{0,8},{1,9},{2,10},{3,11},{4,12},{5,13},{6,14},{7,15},{8,0},{9,1},... | collective-permute-start | bytes 122888 | tf_op jit(solution)/shard_map/ppermute | solution.py:661
  110.3 10.5 %collective-permute-start.18 = (bf16[160,128]{1,0:T(8,128)(2,1)S(1)}, bf16[160,128]{1,0:T(8,128)(2,1)S(1)}, u32[]{:S(2)}, u32[]{:S(2)}) collective-permute-start(bf16[160,128]{1,0:T(8,128)(2,1)S(1)} %get-tuple-element.84.refs_6_), channel_id=1, source_target_pairs={{0,16},{1,17},{2,18},{3,19},{4,20},{5,21},{6,22},{7,23},{8,24},{9,... | collective-permute-start | bytes 122888 | tf_op jit(solution)/shard_map/ppermute | solution.py:661
  112.8 8.1 %collective-permute-start.19 = (bf16[160,128]{1,0:T(8,128)(2,1)S(1)}, bf16[160,128]{1,0:T(8,128)(2,1)S(1)}, u32[]{:S(2)}, u32[]{:S(2)}) collective-permute-start(bf16[160,128]{1,0:T(8,128)(2,1)S(1)} %get-tuple-element.84.refs_6_), channel_id=1, source_target_pairs={{0,24},{1,25},{2,26},{3,27},{4,28},{5,29},{6,30},{7,31},{8,16},{9,... | collective-permute-start | bytes 122888 | tf_op jit(solution)/shard_map/ppermute | solution.py:661
  123.0 5.2 %collective-permute-start.23 = (bf16[2,256,128]{2,1,0:T(8,128)(2,1)S(1)}, bf16[2,256,128]{2,1,0:T(8,128)(2,1)S(1)}, u32[]{:S(2)}, u32[]{:S(2)}) collective-permute-start(bf16[2,256,128]{2,1,0:T(8,128)(2,1)S(1)} %get-tuple-element.87), channel_id=1, source_target_pairs={{0,8},{1,9},{2,10},{3,11},{4,12},{5,13},{6,14},{7,15},{8,0},{9,1},... | collective-permute-start | bytes 393224 | tf_op jit(solution)/shard_map/ppermute | solution.py:661
  124.1 14.3 %collective-permute-start.20 = (bf16[4,160,128]{2,1,0:T(8,128)(2,1)S(1)}, bf16[4,160,128]{2,1,0:T(8,128)(2,1)S(1)}, u32[]{:S(2)}, u32[]{:S(2)}) collective-permute-start(bf16[4,160,128]{2,1,0:T(8,128)(2,1)S(1)} %get-tuple-element.86.refs_0_), channel_id=1, source_target_pairs={{0,1},{1,0},{2,3},{3,2},{4,5},{5,4},{6,7},{7,6},{8,9},{9,8},{10,11... | collective-permute-start | bytes 491528 | tf_op jit(solution)/shard_map/ppermute | solution.py:661
  125.5 12.9 %collective-permute-start.21 = (bf16[4,160,128]{2,1,0:T(8,128)(2,1)S(1)}, bf16[4,160,128]{2,1,0:T(8,128)(2,1)S(1)}, u32[]{:S(2)}, u32[]{:S(2)}) collective-permute-start(bf16[4,160,128]{2,1,0:T(8,128)(2,1)S(1)} %get-tuple-element.86.refs_0_), channel_id=1, source_target_pairs={{0,4},{1,5},{2,6},{3,7},{4,0},{5,1},{6,2},{7,3},{8,12},{9,13},{10,... | collective-permute-start | bytes 491528 | tf_op jit(solution)/shard_map/ppermute | solution.py:661
  127.0 11.4 %collective-permute-start.22 = (bf16[4,160,128]{2,1,0:T(8,128)(2,1)S(1)}, bf16[4,160,128]{2,1,0:T(8,128)(2,1)S(1)}, u32[]{:S(2)}, u32[]{:S(2)}) collective-permute-start(bf16[4,160,128]{2,1,0:T(8,128)(2,1)S(1)} %get-tuple-element.86.refs_0_), channel_id=1, source_target_pairs={{0,5},{1,4},{2,7},{3,6},{4,1},{5,0},{6,3},{7,2},{8,13},{9,12},{10,... | collective-permute-start | bytes 491528 | tf_op jit(solution)/shard_map/ppermute | solution.py:661
  127.6 10.8 %collective-permute-start.24 = (bf16[2,256,128]{2,1,0:T(8,128)(2,1)}, bf16[2,256,128]{2,1,0:T(8,128)(2,1)S(1)}, u32[]{:S(2)}, u32[]{:S(2)}) collective-permute-start(bf16[2,256,128]{2,1,0:T(8,128)(2,1)} %get-tuple-element.88), channel_id=1, source_target_pairs={{0,16},{1,17},{2,18},{3,19},{4,20},{5,21},{6,22},{7,23},{8,24},{9,... | collective-permute-start | bytes 393224 | tf_op jit(solution)/shard_map/ppermute | solution.py:661
  128.2 10.2 %collective-permute-start.25 = (bf16[2,256,128]{2,1,0:T(8,128)(2,1)}, bf16[2,256,128]{2,1,0:T(8,128)(2,1)S(1)}, u32[]{:S(2)}, u32[]{:S(2)}) collective-permute-start(bf16[2,256,128]{2,1,0:T(8,128)(2,1)} %get-tuple-element.89), channel_id=1, source_target_pairs={{0,24},{1,25},{2,26},{3,27},{4,28},{5,29},{6,30},{7,31},{8,16},{9,... | collective-permute-start | bytes 393224 | tf_op jit(solution)/shard_map/ppermute | solution.py:661
  131.0 9.0 %copy-start.3 = (f32[2,8,2,64,64]{4,3,2,1,0:T(8,128)S(1)}, f32[2,8,2,64,64]{4,3,2,1,0:T(8,128)}, u32[]{:S(2)}) copy-start(f32[2,8,2,64,64]{4,3,2,1,0:T(8,128)} %refs_13_.1) | copy-start | bytes 1572868
  131.0 9.0 %copy-start.4 = (f32[2,8,2,64,64]{4,3,2,1,0:T(8,128)S(1)}, f32[2,8,2,64,64]{4,3,2,1,0:T(8,128)}, u32[]{:S(2)}) copy-start(f32[2,8,2,64,64]{4,3,2,1,0:T(8,128)} %refs_14_.1) | copy-start | bytes 1572868
  131.0 9.0 %copy-start.5 = (f32[2,8,2,64,64]{4,3,2,1,0:T(8,128)S(1)}, f32[2,8,2,64,64]{4,3,2,1,0:T(8,128)}, u32[]{:S(2)}) copy-start(f32[2,8,2,64,64]{4,3,2,1,0:T(8,128)} %refs_15_.1) | copy-start | bytes 1572868
  131.0 9.0 %copy-start.6 = (f32[32,1024]{1,0:T(8,128)S(1)}, f32[32,1024]{1,0:T(8,128)}, u32[]{:S(2)}) copy-start(f32[32,1024]{1,0:T(8,128)} %refs_6_.1) | copy-start | bytes 393220
  131.0 9.0 %copy-start.7 = (f32[32,1024]{1,0:T(8,128)S(1)}, f32[32,1024]{1,0:T(8,128)}, u32[]{:S(2)}) copy-start(f32[32,1024]{1,0:T(8,128)} %refs_5_.3) | copy-start | bytes 393220
  131.0 9.0 %copy-start.11 = (f32[32,1024]{1,0:T(8,128)S(1)}, f32[32,1024]{1,0:T(8,128)}, u32[]{:S(2)}) copy-start(f32[32,1024]{1,0:T(8,128)} %refs_7_.2) | copy-start | bytes 393220
  131.0 9.0 %copy-start.12 = (f32[32,1024]{1,0:T(8,128)S(1)}, f32[32,1024]{1,0:T(8,128)}, u32[]{:S(2)}) copy-start(f32[32,1024]{1,0:T(8,128)} %refs_8_.1) | copy-start | bytes 393220
  131.0 9.0 %copy-start.13 = (f32[32,1024]{1,0:T(8,128)S(1)}, f32[32,1024]{1,0:T(8,128)}, u32[]{:S(2)}) copy-start(f32[32,1024]{1,0:T(8,128)} %refs_9_.1) | copy-start | bytes 393220
  131.0 9.0 %copy-start.14 = (f32[32,1024]{1,0:T(8,128)S(1)}, f32[32,1024]{1,0:T(8,128)}, u32[]{:S(2)}) copy-start(f32[32,1024]{1,0:T(8,128)} %refs_10_.1) | copy-start | bytes 393220
  131.0 9.0 %copy-start.15 = (f32[13,512]{1,0:T(8,128)S(1)}, f32[13,512]{1,0:T(8,128)}, u32[]{:S(2)}) copy-start(f32[13,512]{1,0:T(8,128)} %refs_17_.1) | copy-start | bytes 79876
  131.1 9.0 %copy-start.16 = (f32[13,512]{1,0:T(8,128)S(1)}, f32[13,512]{1,0:T(8,128)}, u32[]{:S(2)}) copy-start(f32[13,512]{1,0:T(8,128)} %refs_18_.1) | copy-start | bytes 79876
  138.5 1.5 %collective-permute-start.26 = (bf16[4,160,128]{2,1,0:T(8,128)(2,1)S(1)}, bf16[4,160,128]{2,1,0:T(8,128)(2,1)S(1)}, u32[]{:S(2)}, u32[]{:S(2)}) collective-permute-start(bf16[4,160,128]{2,1,0:T(8,128)(2,1)S(1)} %get-tuple-element.95.refs_11_), channel_id=1, source_target_pairs={{0,2},{1,3},{2,0},{3,1},{4,6},{5,7},{6,4},{7,5},{8,10},{9,11},{10,... | collective-permute-start | bytes 491528 | tf_op jit(solution)/shard_map/ppermute | solution.py:661
  (4 other events, 11.5 us)

commit v5 on v4

--- a/solution.py
+++ b/solution.py
@@ -369,10 +369,12 @@
         ref.flush()
 
 
-def load_weights(near, place_ref, pieces, targets, sems):
+def load_weights(near, place_ref, pieces, part, target, sems):
     copies = []
+    part = () if part is None else (part,)
+    every = (slice(None),) * (1 - len(part))
     if not near:
-        copies = [(pieces[0].at[:, part], target) for part, target in targets]
+        copies = [(pieces[0].at[(slice(None), *part)], target)]
     else:
         me = place_ref[0]
         at = [(me >> 1) & 1, (me >> 2) & 1, me & 1, me >> 3]
@@ -384,8 +386,7 @@
                     z = 2 * (i & 1) + k
                     row = (((at[3] ^ z) * 2 + (at[1] ^ y)) * 2 + (at[0] ^ (i >> 2))) * size
                     rows = pl.ds(pl.multiple_of(row, size), size)
-                    for part, target in targets:
-                        copies.append((ref.at[j, k, part], target.at[at[2] ^ x, rows]))
+                    copies.append((ref.at[(j, k, *part)], target.at[(at[2] ^ x, *every, rows)]))
     copies = [pltpu.make_async_copy(source, target, sems.at[i]) for i, (source, target) in enumerate(copies)]
     for copy in copies:
         copy.start()
@@ -408,8 +409,11 @@
     pieces, refs = refs[:count], refs[count:]
     active, total_ref, middle_ref, send_ref, small_ref, *refs = refs
     grad_refs, refs = refs[:2], refs[2:]
-    normed, normed_t, cotangent_t, normal, spread, w_in, w_out, grad_hidden, sems = refs
-    copies = load_weights(near, place_ref, pieces, [(0, w_in), (1, w_out)], sems)
+    normed, normed_t, cotangent_t, normal, spread, weights, grad_hidden, sems = refs
+    copies = load_weights(near, place_ref, pieces, None, weights, sems)
+    cotangent_ref.start()
+    wide_ref.start()
+    w_in, w_out = weights.at[:, 0], weights.at[:, 1]
     me = place_ref[0]
     orders = [((z ^ (me >> 3)) + 4 * (y ^ ((me >> 2) & 1)) + 8 * (c ^ ((me >> 1) & 1))) for z in range(4) for y in range(2) for c in range(2)]
     orders = orders if near else []
@@ -445,7 +449,7 @@
         for i, (h, c) in enumerate(chunks):
             lanes, flat = slice(c, c + CHUNK), slice(h * columns + c, h * columns + c + CHUNK)
             hidden = dot(normed[rows, :], w_in[h, :, lanes]) + bias_ref[i : i + 1, :]
-            value, slope = gelu_pair(hidden)
+            value, slope = gelu_pair(hidden.astype(BF16))
             active[rows, flat] = value.astype(BF16)
             back = (dot(cotangent_ref[rows, :], w_out[h, :, lanes]) * slope).astype(BF16)
             grad_hidden[rows, flat] = back
@@ -492,7 +496,7 @@
     count = 8 if near else 1
     totals, actives, pieces = refs[:OUT_BLOCKS], refs[OUT_BLOCKS : 2 * OUT_BLOCKS], refs[2 * OUT_BLOCKS :][:count]
     outputs, w_out, sems = refs[2 * OUT_BLOCKS + count], *refs[2 * OUT_BLOCKS + count + 1 :]
-    for copy in load_weights(near, place_ref, pieces, [(1, w_out)], sems):
+    for copy in load_weights(near, place_ref, pieces, 1, w_out, sems):
         copy.wait()
     halves, _, columns = w_out.shape
     size = totals[0].shape[0]
@@ -525,10 +529,16 @@
 
 class Source:
     def __init__(self, ref, copy):
-        self.ref, self.copy, self.shape = ref, copy, ref.shape
+        self.ref, self.copy, self.shape, self.started = ref, copy, ref.shape, False
+
+    def start(self):
+        if not self.started:
+            self.copy.start()
+            self.started = True
 
     def __getitem__(self, index):
         if self.copy is not None:
+            self.start()
             self.copy.wait()
             self.copy = None
         return self.ref[index]
@@ -555,9 +565,14 @@
         self.what = what
 
 
+class Late(Far):
+    pass
+
+
 def call(body, outs, *args, scalars=(), raw=(), scratch=(), flops=0, carry=(), cost=None, vmem=20):
     near, far, there = [pl.BlockSpec(memory_space=m) for m in (pltpu.VMEM, pltpu.HBM, pl.ANY)]
     in_far, out_far = [isinstance(a, Far) for a in args], [isinstance(o, Far) for o in outs]
+    in_late = [isinstance(a, Late) for a in args]
     index = [a.what[1:] if f else () for a, f in zip(args, in_far, strict=True)]
     args = [
         pltpu.with_memory_space_constraint(*((a.what[0], pltpu.HBM) if f else (a, pltpu.VMEM)))
@@ -587,11 +602,12 @@
         space = take(len(buffers))
         sems = take(1)[0] if buffers else None
         sources, sinks, used = [], [], 0
-        for ref, away, part in zip(in_refs, in_far, index, strict=True):
+        for ref, away, part, late in zip(in_refs, in_far, index, in_late, strict=True):
             if away:
                 copy = pltpu.make_async_copy(ref.at[part] if part else ref, space[used], sems.at[used])
-                copy.start()
                 ref = Source(space[used], copy)
+                if not late:
+                    ref.start()
                 used += 1
             sources.append(ref)
         for ref, away in zip(out_refs, out_far, strict=True):
@@ -718,7 +734,7 @@
             ((8, width), F32),
         ]
         + grads,
-        Far(got), Far(wide_i_t), Far(rows_all), Far(upstream_all), vectors, vectors[5:9].reshape(steps, CHUNK), Far(wide_i),
+        Far(got), Far(wide_i_t), Far(rows_all), Late(upstream_all), vectors, vectors[5:9].reshape(steps, CHUNK), Late(wide_i),
         scalars=[me[None]], raw=pieces,
         scratch=[
             pltpu.VMEM((local, width), BF16),
@@ -726,10 +742,9 @@
             pltpu.VMEM((width, local), BF16),
             pltpu.VMEM((local, width), F32),
             pltpu.VMEM((local, 1), F32),
-            pltpu.VMEM((tp_count, model, shard_columns), BF16),
-            pltpu.VMEM((tp_count, model, shard_columns), BF16),
+            pltpu.VMEM((tp_count, 2, model, shard_columns), BF16),
             pltpu.VMEM((local, hidden), BF16),
-            pltpu.SemaphoreType.DMA((64 if near else 2,)),
+            pltpu.SemaphoreType.DMA((32 if near else 1,)),
         ],
         flops=12 * local * width * hidden + 2 * wide_flops, vmem=44,
     )

time: 145 us -> 143 us (0.986)
  Pallas kernels: 51.9 us -> 49.8 us
    pallas_call x11, Pallas kernels: 51.9 us -> 49.8 us  [call(): pl.pallas_call(inner, out_shape=[(pltpu.HBM if f else pltpu.VMEM)(o.shape...]
where the time goes in v5:
time: 143 us; the launch traced here: 142 us
  Pallas kernels  49.8 us (35%)
  starting transfers between devices  48.3 us (34%)
  waiting for transfers between devices  37.7 us (26%)
  other arithmetic  2.49 us (2%)
  local copies, waits for them, and re-layouts  2.36 us (2%)
  between operations  1.44 us (1%)
    pallas_call x11, Pallas kernels, call(): pl.pallas_call(inner, out_shape=[(pltpu.HBM if f else pltpu.VMEM)(o.shape...  49.8 us
    ppermute x27, waiting for transfers between devices, permute(): return lax.ppermute(values, AXES, [(d, d ^ mask) for d in range(devices)])  33.6 us
    ppermute x27, starting transfers between devices, permute(): return lax.ppermute(values, AXES, [(d, d ^ mask) for d in range(devices)])  31.8 us
    all_to_all x4, starting transfers between devices, on_device(): got = exchange(sent)  16.5 us
    all_to_all x4, waiting for transfers between devices, on_device(): got = exchange(sent)  4.17 us
  transfers between devices with their start and end apart: 31, of which 12 were waited for; matrix products, arithmetic and copies ran while one was open for 3% of the time, Pallas kernels for 17%

profile of v5, /device:TPU:0, one launch (start us, length us, event | category | flops | bytes accessed | tf_op | source)
XLA Modules:
  0.0 142.1 jit_solution(8050649883889701000)
XLA Ops:
  0.7 1.0 convert_bitcast_fusion
  1.7 4.1 %collective-permute-start.2 = (bf16[2,32,1024]{2,1,0:T(8,128)(2,1)S(1)}, bf16[2,32,1024]{2,1,0:T(8,128)(2,1)S(1)}, u32[]{:S(2)}, u32[]{:S(2)}) collective-permute-start(bf16[2,32,1024]{2,1,0:T(8,128)(2,1)S(1)} %get-tuple-element.117), channel_id=1, source_target_pairs={{0,16},{1,17},{2,18},{3,19},{4,20},{5,21},{6,22},{7,23},{8,24},{9,... | collective-permute-start | bytes 393224 | tf_op jit(solution)/shard_map/ppermute | solution.py:677
  5.8 1.3 collective-permute-start.3
  7.4 3.0 %shard_map.324 = bf16[32,64,128]{2,1,0:T(8,128)(2,1)} custom-call(bf16[1024,512]{1,0:T(8,128)(2,1)} %bitcast.40, bf16[256,512]{1,0:T(8,128)(2,1)} %constant.61.clone.refs_1_), custom_call_target="tpu_custom_call" | custom-call | flops 268435456 | bytes 1835008 | tf_op jit(solution)/shard_map/pallas_call | solution.py:631
  10.4 5.2 %all-to-all-start = ((bf16[32,64,128]{2,1,0:T(8,128)(2,1)}), bf16[32,64,128]{2,1,0:T(8,128)(2,1)S(1)}, u32[]{:S(2)}, u32[]{:S(2)}) async-start(bf16[32,64,128]{2,1,0:T(8,128)(2,1)} %shard_map.324), calls=%async_computation | async-start | bytes 1048576 | tf_op jit(solution)/shard_map/all_to_all | solution.py:710
  15.6 1.0 dynamic-slice_convert_fusion
  17.0 0.9 dynamic-slice_bitcast_fusion.refs_7_.refs_5_
  18.0 1.8 %collective-permute-start.4 = (bf16[2,2,32,1024]{3,2,1,0:T(8,128)(2,1)S(1)}, bf16[2,2,32,1024]{3,2,1,0:T(8,128)(2,1)S(1)}, u32[]{:S(2)}, u32[]{:S(2)}) collective-permute-start(bf16[2,2,32,1024]{3,2,1,0:T(8,128)(2,1)S(1)} %get-tuple-element.113), channel_id=1, source_target_pairs={{0,4},{1,5},{2,6},{3,7},{4,0},{5,1},{6,2},{7,3},{8,12},{9,13},{10,... | collective-permute-start | bytes 786440 | tf_op jit(solution)/shard_map/ppermute | solution.py:677
  19.9 1.5 %collective-permute-start.1 = (bf16[2,2,32,1024]{3,2,1,0:T(8,128)(2,1)S(1)}, bf16[2,2,32,1024]{3,2,1,0:T(8,128)(2,1)}, u32[]{:S(2)}, u32[]{:S(2)}) collective-permute-start(bf16[2,2,32,1024]{3,2,1,0:T(8,128)(2,1)S(1)} %get-tuple-element.115), channel_id=1, source_target_pairs={{0,1},{1,0},{2,3},{3,2},{4,5},{5,4},{6,7},{7,6},{8,9},{9,8},{10,11... | collective-permute-start | bytes 786440 | tf_op jit(solution)/shard_map/ppermute | solution.py:677
  21.8 8.2 %collective-permute-done.4 = bf16[2,2,32,1024]{3,2,1,0:T(8,128)(2,1)S(1)} collective-permute-done((bf16[2,2,32,1024]{3,2,1,0:T(8,128)(2,1)S(1)}, bf16[2,2,32,1024]{3,2,1,0:T(8,128)(2,1)S(1)}, u32[]{:S(2)}, u32[]{:S(2)}) %collective-permute-start.4) | collective-permute-done | bytes 262176 | tf_op jit(solution)/shard_map/ppermute | solution.py:677
  30.1 0.4 collective-permute-done.1
  30.5 1.0 pad_maximum_fusion.refs_8_
  31.5 2.3 %shard_map.325 = (bf16[32,64,128]{2,1,0:T(8,128)(2,1)}, f32[128,512]{1,0:T(8,128)}, bf16[256,256]{1,0:T(8,128)(2,1)}, f32[256,256]{1,0:T(8,128)}, bf16[256,256]{...) custom-call(bf16[32,64,128]{2,1,0:T(8,128)(2,1)S(1)} %all-to-all-don, ...), custom_call_target="tpu_custom_call", output_to_operand_aliasing={{5}: (8, {}), {6}: (9, {})} | custom-call | bytes 2364416 | tf_op jit(solution)/shard_map/pallas_call | solution.py:631
  33.9 1.2 collective-permute-start.6
  35.0 1.1 collective-permute-start.5
  36.1 4.3 %all-to-all-start.1 = ((bf16[32,64,128]{2,1,0:T(8,128)(2,1)}), bf16[32,64,128]{2,1,0:T(8,128)(2,1)}, u32[]{:S(2)}, u32[]{:S(2)}) async-start(bf16[32,64,128]{2,1,0:T(8,128)(2,1)} %get-tuple-element.64), calls=%async_computation.1 | async-start | bytes 1048576 | tf_op jit(solution)/shard_map/all_to_all | solution.py:727
  41.1 11.0 %collective-permute-done.6.refs_11_.refs_12_ = bf16[2,2,2,32,1024]{4,3,2,1,0:T(8,128)(2,1)S(1)} collective-permute-done((bf16[2,2,2,32,1024]{4,3,2,1,0:T(8,128)(2,1)S(1)}, bf16[2,2,2,32,1024]{4,3,2,1,0:T(8,128)(2,1)S(1)}, u32[]{:S(2)}, u32[]{:S(2)}) %collective-permute-start.6) | collective-permute-done | bytes 524320 | tf_op jit(solution)/shard_map/ppermute | solution.py:677
  52.6 2.7 %all-to-all-done.1.refs_1_ = bf16[32,64,128]{2,1,0:T(8,128)(2,1)} async-done(((bf16[32,64,128]{2,1,0:T(8,128)(2,1)}), bf16[32,64,128]{2,1,0:T(8,128)(2,1)}, u32[]{:S(2)}, u32[]{:S(2)}) %all-to-all-start.1) | async-done | bytes 524320 | tf_op jit(solution)/shard_map/all_to_all | solution.py:727
  55.3 19.3 %shard_map.326 = (bf16[1024,2048]{1,0:T(8,128)(2,1)}, f32[1024,512]{1,0:T(8,128)}, bf16[1024,512]{1,0:T(8,128)(2,1)}, bf16[32,64,128]{2,1,0:T(8,128)(2,1)}, f32[...) custom-call(s32[1]{0:T(128)} %bitcast.1.refs_0_, ...), custom_call_target="tpu_custom_call" | custom-call | flops 13421772800 | bytes 19449856 | tf_op jit(solution)/shard_map/pallas_call | solution.py:631
  74.6 1.1 collective-permute-start.11
  75.8 3.3 %all-to-all-start.2 = ((bf16[32,64,128]{2,1,0:T(8,128)(2,1)}), bf16[32,64,128]{2,1,0:T(8,128)(2,1)S(1)}, u32[]{:S(2)}, u32[]{:S(2)}) async-start(bf16[32,64,128]{2,1,0:T(8,128)(2,1)} %get-tuple-element.67), calls=%async_computation.2 | async-start | bytes 1048576 | tf_op jit(solution)/shard_map/all_to_all | solution.py:773
  79.1 0.8 collective-permute-done.11.refs_1_.refs_5_.refs_10_
  79.9 2.3 %shard_map.329 = (bf16[2,4,256,128]{3,2,1,0:T(8,128)(2,1)}, bf16[2,4,256,128]{3,2,1,0:T(8,128)(2,1)}) custom-call(bf16[2,2,2,4,256,128]{5,4,3,2,1,0:T(8,128)(2,1)S(1)} %get-tuple-element.76.refs_0_.refs_1_, bf16[2,2,2,4,256,128]{5,4,3,2,1,0:T(8,128)(2,1)} %collective-permute-done.11.refs_1_.refs_5_.refs_10_), custom_call_target="tpu_custom_call" | custom-call | tf_op jit(solution)/shard_map/pallas_call | solution.py:631
  82.3 1.2 collective-permute-start.12
  83.4 1.4 collective-permute-start.13
  84.8 7.8 %shard_map.327.refs_11_ = bf16[1024,512]{1,0:T(8,128)(2,1)} custom-call(s32[1]{0:T(128)} %bitcast.1.refs_0_, f32[1024,512]{1,0:T(8,128)} %get-tuple-element.73.refs_1_.refs_2_.refs_3_.refs_4_, f32[1024,512]{1,0:T(8,128)} %get-tuple-element.73.refs_1_.refs_2_.refs_3_.refs_4_, f32[1024,512]{1,0:T(8,128)} %get-tuple-element.73.refs_1_.refs_2_.refs_3_.refs_4_, ...), custom_call_target="tpu_custom_call" | custom-call | bytes 62914560 | tf_op jit(solution)/shard_map/pallas_call | solution.py:631
  92.6 1.5 %all-to-all-done.2.refs_1_ = bf16[32,64,128]{2,1,0:T(8,128)(2,1)S(1)} async-done(((bf16[32,64,128]{2,1,0:T(8,128)(2,1)}), bf16[32,64,128]{2,1,0:T(8,128)(2,1)S(1)}, u32[]{:S(2)}, u32[]{:S(2)}) %all-to-all-start.2) | async-done | bytes 524320 | tf_op jit(solution)/shard_map/all_to_all | solution.py:773
  94.1 3.0 %shard_map.328 = (bf16[32,64,128]{2,1,0:T(8,128)(2,1)}, bf16[160,128]{1,0:T(8,128)(2,1)S(1)}, bf16[160,128]{1,0:T(8,128)(2,1)S(1)}, bf16[1024,512]{1,0:T(8,128)(2,1)}) custom-call(s32[1]{0:T(128)} %bitcast.refs_0_, bf16[32,64,128]{2,1,0:T(8,128)(2,1)S(1)} %all-to-all-done.2.refs_1_, ...), custom_call_target="tpu_custom_call", output_to_operand_aliasing={{3}: (11, {})} | custom-call | bytes 62914560 | tf_op jit(solution)/shard_map/pallas_call | solution.py:631
  97.1 3.6 %all-to-all-start.3 = ((bf16[32,64,128]{2,1,0:T(8,128)(2,1)}), bf16[32,64,128]{2,1,0:T(8,128)(2,1)S(1)}, u32[]{:S(2)}, u32[]{:S(2)}) async-start(bf16[32,64,128]{2,1,0:T(8,128)(2,1)} %get-tuple-element.90), calls=%async_computation.3 | async-start | bytes 1048576 | tf_op jit(solution)/shard_map/all_to_all | solution.py:796
  101.1 1.0 collective-permute-done.14.refs_4_
  102.0 1.5 %shard_map.330 = (bf16[160,128]{1,0:T(8,128)(2,1)S(1)}, bf16[4,256,128]{2,1,0:T(8,128)(2,1)S(1)}, bf16[4,256,128]{2,1,0:T(8,128)(2,1)S(1)}) custom-call(bf16[2,2,2,4,256,128]{5,4,3,2,1,0:T(8,128)(2,1)S(1)} %get-tuple-element.76.refs_0_.refs_1_, bf16[2,4,256,128]{3,2,1,0:T(8,128)(2,1)} %collective-permute-done.12.refs_1_.refs_2_, ...), custom_call_target="tpu_custom_call" | custom-call | tf_op jit(solution)/shard_map/pallas_call | solution.py:631
  103.5 1.8 %collective-permute-start.15 = (bf16[4,256,128]{2,1,0:T(8,128)(2,1)S(1)}, bf16[4,256,128]{2,1,0:T(8,128)(2,1)S(1)}, u32[]{:S(2)}, u32[]{:S(2)}) collective-permute-start(bf16[4,256,128]{2,1,0:T(8,128)(2,1)S(1)} %get-tuple-element.82), channel_id=1, source_target_pairs={{0,4},{1,5},{2,6},{3,7},{4,0},{5,1},{6,2},{7,3},{8,12},{9,13},{10,... | collective-permute-start | bytes 786440 | tf_op jit(solution)/shard_map/ppermute | solution.py:677
  105.3 1.5 %collective-permute-start.16 = (bf16[4,256,128]{2,1,0:T(8,128)(2,1)S(1)}, bf16[4,256,128]{2,1,0:T(8,128)(2,1)S(1)}, u32[]{:S(2)}, u32[]{:S(2)}) collective-permute-start(bf16[4,256,128]{2,1,0:T(8,128)(2,1)S(1)} %get-tuple-element.83), channel_id=1, source_target_pairs={{0,1},{1,0},{2,3},{3,2},{4,5},{5,4},{6,7},{7,6},{8,9},{9,8},{10,11... | collective-permute-start | bytes 786440 | tf_op jit(solution)/shard_map/ppermute | solution.py:677
  106.8 1.5 %collective-permute-start.17 = (bf16[160,128]{1,0:T(8,128)(2,1)S(1)}, bf16[160,128]{1,0:T(8,128)(2,1)S(1)}, u32[]{:S(2)}, u32[]{:S(2)}) collective-permute-start(bf16[160,128]{1,0:T(8,128)(2,1)S(1)} %get-tuple-element.84.refs_6_), channel_id=1, source_target_pairs={{0,8},{1,9},{2,10},{3,11},{4,12},{5,13},{6,14},{7,15},{8,0},{9,1},... | collective-permute-start | bytes 122888 | tf_op jit(solution)/shard_map/ppermute | solution.py:677
  108.3 2.5 %collective-permute-start.18 = (bf16[160,128]{1,0:T(8,128)(2,1)S(1)}, bf16[160,128]{1,0:T(8,128)(2,1)S(1)}, u32[]{:S(2)}, u32[]{:S(2)}) collective-permute-start(bf16[160,128]{1,0:T(8,128)(2,1)S(1)} %get-tuple-element.84.refs_6_), channel_id=1, source_target_pairs={{0,16},{1,17},{2,18},{3,19},{4,20},{5,21},{6,22},{7,23},{8,24},{9,... | collective-permute-start | bytes 122888 | tf_op jit(solution)/shard_map/ppermute | solution.py:677
  110.7 0.5 collective-permute-start.19
  111.4 7.4 %collective-permute-done.18.refs_8_ = bf16[160,128]{1,0:T(8,128)(2,1)S(1)} collective-permute-done((bf16[160,128]{1,0:T(8,128)(2,1)S(1)}, bf16[160,128]{1,0:T(8,128)(2,1)S(1)}, u32[]{:S(2)}, u32[]{:S(2)}) %collective-permute-start.18) | collective-permute-done | bytes 40992 | tf_op jit(solution)/shard_map/ppermute | solution.py:677
  118.8 2.1 %shard_map.331 = (bf16[4,160,128]{2,1,0:T(8,128)(2,1)S(1)}, f32[2,256,128]{2,1,0:T(8,128)S(1)}, bf16[2,256,128]{2,1,0:T(8,128)(2,1)S(1)}, bf16[2,256,128]{2,1,0:T(8,128)(2,1)}, bf16[2,256,128]{2,1,0:T(8,128)(2,1)}) custom-call(s32[1]{0:T(128)} %bitcast.1.refs_0_, bf16[2,2,2,4,256,128]{5,4,3,2,1,0:T(8,128)(2,1)S(1)} %get-tuple-element.76.refs_0_.refs_1_, ...), custom_call_target="tpu_custom_call" | custom-call | tf_op jit(solution)/shard_map/pallas_call | solution.py:631
  121.0 1.1 collective-permute-start.23
  122.0 1.5 %collective-permute-start.20 = (bf16[4,160,128]{2,1,0:T(8,128)(2,1)S(1)}, bf16[4,160,128]{2,1,0:T(8,128)(2,1)S(1)}, u32[]{:S(2)}, u32[]{:S(2)}) collective-permute-start(bf16[4,160,128]{2,1,0:T(8,128)(2,1)S(1)} %get-tuple-element.86.refs_0_), channel_id=1, source_target_pairs={{0,1},{1,0},{2,3},{3,2},{4,5},{5,4},{6,7},{7,6},{8,9},{9,8},{10,11... | collective-permute-start | bytes 491528 | tf_op jit(solution)/shard_map/ppermute | solution.py:677
  123.5 1.5 %collective-permute-start.21 = (bf16[4,160,128]{2,1,0:T(8,128)(2,1)S(1)}, bf16[4,160,128]{2,1,0:T(8,128)(2,1)S(1)}, u32[]{:S(2)}, u32[]{:S(2)}) collective-permute-start(bf16[4,160,128]{2,1,0:T(8,128)(2,1)S(1)} %get-tuple-element.86.refs_0_), channel_id=1, source_target_pairs={{0,4},{1,5},{2,6},{3,7},{4,0},{5,1},{6,2},{7,3},{8,12},{9,13},{10,... | collective-permute-start | bytes 491528 | tf_op jit(solution)/shard_map/ppermute | solution.py:677
  125.0 0.5 collective-permute-start.22
  125.5 0.7 collective-permute-start.24
  126.2 2.7 %collective-permute-start.25 = (bf16[2,256,128]{2,1,0:T(8,128)(2,1)}, bf16[2,256,128]{2,1,0:T(8,128)(2,1)S(1)}, u32[]{:S(2)}, u32[]{:S(2)}) collective-permute-start(bf16[2,256,128]{2,1,0:T(8,128)(2,1)} %get-tuple-element.89), channel_id=1, source_target_pairs={{0,24},{1,25},{2,26},{3,27},{4,28},{5,29},{6,30},{7,31},{8,16},{9,... | collective-permute-start | bytes 393224 | tf_op jit(solution)/shard_map/ppermute | solution.py:677
  129.0 4.5 %shard_map.332.refs_7_ = bf16[1024,512]{1,0:T(8,128)(2,1)} custom-call(bf16[32,64,128]{2,1,0:T(8,128)(2,1)S(1)} %all-to-all-done.3.refs_0_, bf16[1024,512]{1,0:T(8,128)(2,1)} %bitcast.42, bf16[1024,512]{1,0:T(8,128)(2,1)} %get-tuple-element.91.refs_2_, f32[13,512]{1,0:T(8,128)S(1)} %copy-done.10, bf16[512,256]{1,0:T(8,128)(2,1)} %constant.62.clone.refs_4_), custom_call_target="tpu_custom_call" | custom-call | bytes 62914560 | tf_op jit(solution)/shard_map/pallas_call | solution.py:631
  133.5 2.8 %collective-permute-done.24.refs_5_ = bf16[2,256,128]{2,1,0:T(8,128)(2,1)S(1)} collective-permute-done((bf16[2,256,128]{2,1,0:T(8,128)(2,1)}, bf16[2,256,128]{2,1,0:T(8,128)(2,1)S(1)}, u32[]{:S(2)}, u32[]{:S(2)}) %collective-permute-start.24) | collective-permute-done | bytes 131104 | tf_op jit(solution)/shard_map/ppermute | solution.py:677
  136.5 1.4 collective-permute-done.26.refs_12_
  138.0 3.9 %shard_map.334 = (f32[32,1024]{1,0:T(8,128)}, f32[32,1024]{1,0:T(8,128)}, f32[32,1024]{1,0:T(8,128)}, f32[32,1024]{1,0:T(8,128)}, f32[32,1024]{1,0:T(8,128)}, /*...) custom-call(s32[1]{0:T(128)} %bitcast.refs_0_, ...), custom_call_target="tpu_custom_call", output_to_operand_aliasing={{14}: (19, {})} | custom-call | tf_op jit(solution)/shard_map/pallas_call | solution.py:631
  (89 shorter events, 3.1 us)
Async XLA Ops:
  0.6 16.0 %copy-start.10 = (f32[13,512]{1,0:T(8,128)S(1)}, f32[13,512]{1,0:T(8,128)}, u32[]{:S(2)}) copy-start(f32[13,512]{1,0:T(8,128)} %refs_16_.1) | copy-start | bytes 79876
  1.7 16.3 %collective-permute-start.2 = (bf16[2,32,1024]{2,1,0:T(8,128)(2,1)S(1)}, bf16[2,32,1024]{2,1,0:T(8,128)(2,1)S(1)}, u32[]{:S(2)}, u32[]{:S(2)}) collective-permute-start(bf16[2,32,1024]{2,1,0:T(8,128)(2,1)S(1)} %get-tuple-element.117), channel_id=1, source_target_pairs={{0,16},{1,17},{2,18},{3,19},{4,20},{5,21},{6,22},{7,23},{8,24},{9,... | collective-permute-start | bytes 393224 | tf_op jit(solution)/shard_map/ppermute | solution.py:677
  5.8 12.2 %collective-permute-start.3 = (bf16[2,32,1024]{2,1,0:T(8,128)(2,1)S(1)}, bf16[2,32,1024]{2,1,0:T(8,128)(2,1)S(1)}, u32[]{:S(2)}, u32[]{:S(2)}) collective-permute-start(bf16[2,32,1024]{2,1,0:T(8,128)(2,1)S(1)} %get-tuple-element.117), channel_id=1, source_target_pairs={{0,24},{1,25},{2,26},{3,27},{4,28},{5,29},{6,30},{7,31},{8,16},{9,... | collective-permute-start | bytes 393224 | tf_op jit(solution)/shard_map/ppermute | solution.py:677
  7.1 12.7 %collective-permute-start = (bf16[2,32,1024]{2,1,0:T(8,128)(2,1)S(1)}, bf16[2,32,1024]{2,1,0:T(8,128)(2,1)S(1)}, u32[]{:S(2)}, u32[]{:S(2)}) collective-permute-start(bf16[2,32,1024]{2,1,0:T(8,128)(2,1)S(1)} %get-tuple-element.117), channel_id=1, source_target_pairs={{0,8},{1,9},{2,10},{3,11},{4,12},{5,13},{6,14},{7,15},{8,0},{9,1},... | collective-permute-start | bytes 393224 | tf_op jit(solution)/shard_map/ppermute | solution.py:677
  10.4 21.1 %all-to-all-start = ((bf16[32,64,128]{2,1,0:T(8,128)(2,1)}), bf16[32,64,128]{2,1,0:T(8,128)(2,1)S(1)}, u32[]{:S(2)}, u32[]{:S(2)}) async-start(bf16[32,64,128]{2,1,0:T(8,128)(2,1)} %shard_map.324), calls=%async_computation | async-start | bytes 1048576 | tf_op jit(solution)/shard_map/all_to_all | solution.py:710
  18.0 13.5 %copy-start.8 = (bf16[128,512]{1,0:T(8,128)(2,1)S(1)}, bf16[128,512]{1,0:T(8,128)(2,1)}, u32[]{:S(2)}) copy-start(bf16[128,512]{1,0:T(8,128)(2,1)} %constant.65.clone.refs_1_.refs_2_) | copy-start | bytes 393220
  18.0 13.5 %copy-start.9 = (bf16[512,128]{1,0:T(8,128)(2,1)S(1)}, bf16[512,128]{1,0:T(8,128)(2,1)}, u32[]{:S(2)}) copy-start(bf16[512,128]{1,0:T(8,128)(2,1)} %constant.66.clone.refs_2_.refs_3_) | copy-start | bytes 393220
  18.0 12.0 %collective-permute-start.4 = (bf16[2,2,32,1024]{3,2,1,0:T(8,128)(2,1)S(1)}, bf16[2,2,32,1024]{3,2,1,0:T(8,128)(2,1)S(1)}, u32[]{:S(2)}, u32[]{:S(2)}) collective-permute-start(bf16[2,2,32,1024]{3,2,1,0:T(8,128)(2,1)S(1)} %get-tuple-element.113), channel_id=1, source_target_pairs={{0,4},{1,5},{2,6},{3,7},{4,0},{5,1},{6,2},{7,3},{8,12},{9,13},{10,... | collective-permute-start | bytes 786440 | tf_op jit(solution)/shard_map/ppermute | solution.py:677
  19.9 10.6 %collective-permute-start.1 = (bf16[2,2,32,1024]{3,2,1,0:T(8,128)(2,1)S(1)}, bf16[2,2,32,1024]{3,2,1,0:T(8,128)(2,1)}, u32[]{:S(2)}, u32[]{:S(2)}) collective-permute-start(bf16[2,2,32,1024]{3,2,1,0:T(8,128)(2,1)S(1)} %get-tuple-element.115), channel_id=1, source_target_pairs={{0,1},{1,0},{2,3},{3,2},{4,5},{5,4},{6,7},{7,6},{8,9},{9,8},{10,11... | collective-permute-start | bytes 786440 | tf_op jit(solution)/shard_map/ppermute | solution.py:677
  21.8 12.0 %copy-start.2 = (bf16[2,256,256]{2,1,0:T(8,128)(2,1)}, bf16[2,256,256]{2,1,0:T(8,128)(2,1)S(1)}, u32[]{:S(2)}) copy-start(bf16[2,256,256]{2,1,0:T(8,128)(2,1)S(1)} %maximum_maximum_fusion.refs_3_.refs_4_) | copy-start | bytes 786436
  33.8 21.5 %copy-start = (bf16[2,2,2,32,1024]{4,3,2,1,0:T(8,128)(2,1)}, bf16[2,2,2,32,1024]{4,3,2,1,0:T(8,128)(2,1)S(1)}, u32[]{:S(2)}) copy-start(bf16[2,2,2,32,1024]{4,3,2,1,0:T(8,128)(2,1)S(1)} %get-tuple-element.66.refs_9_.refs_10_) | copy-start | bytes 1572868
  33.9 21.5 %copy-start.1 = (bf16[2,2,2,32,1024]{4,3,2,1,0:T(8,128)(2,1)}, bf16[2,2,2,32,1024]{4,3,2,1,0:T(8,128)(2,1)S(1)}, u32[]{:S(2)}) copy-start(bf16[2,2,2,32,1024]{4,3,2,1,0:T(8,128)(2,1)S(1)} %get-tuple-element.65.refs_8_.refs_9_) | copy-start | bytes 1572868
  33.9 18.2 %collective-permute-start.6 = (bf16[2,2,2,32,1024]{4,3,2,1,0:T(8,128)(2,1)S(1)}, bf16[2,2,2,32,1024]{4,3,2,1,0:T(8,128)(2,1)S(1)}, u32[]{:S(2)}, u32[]{:S(2)}) collective-permute-start(bf16[2,2,2,32,1024]{4,3,2,1,0:T(8,128)(2,1)S(1)} %get-tuple-element.66.refs_9_.refs_10_), channel_id=1, source_target_pairs={{0,1},{1,0},{2,3},{3,2},{4,5},{5,4},{6,7},{7,6},{8,9},{9,8},{10,11... | collective-permute-start | bytes 1572872 | tf_op jit(solution)/shard_map/ppermute | solution.py:677
  35.0 17.3 %collective-permute-start.5 = (bf16[2,2,2,32,1024]{4,3,2,1,0:T(8,128)(2,1)S(1)}, bf16[2,2,2,32,1024]{4,3,2,1,0:T(8,128)(2,1)S(1)}, u32[]{:S(2)}, u32[]{:S(2)}) collective-permute-start(bf16[2,2,2,32,1024]{4,3,2,1,0:T(8,128)(2,1)S(1)} %get-tuple-element.65.refs_8_.refs_9_), channel_id=1, source_target_pairs={{0,4},{1,5},{2,6},{3,7},{4,0},{5,1},{6,2},{7,3},{8,12},{9,13},{10,... | collective-permute-start | bytes 1572872 | tf_op jit(solution)/shard_map/ppermute | solution.py:677
  36.1 19.1 %all-to-all-start.1 = ((bf16[32,64,128]{2,1,0:T(8,128)(2,1)}), bf16[32,64,128]{2,1,0:T(8,128)(2,1)}, u32[]{:S(2)}, u32[]{:S(2)}) async-start(bf16[32,64,128]{2,1,0:T(8,128)(2,1)} %get-tuple-element.64), calls=%async_computation.1 | async-start | bytes 1048576 | tf_op jit(solution)/shard_map/all_to_all | solution.py:727
  40.5 12.1 %collective-permute-start.7 = (bf16[2,2,2,32,1024]{4,3,2,1,0:T(8,128)(2,1)S(1)}, bf16[2,2,2,32,1024]{4,3,2,1,0:T(8,128)(2,1)S(1)}, u32[]{:S(2)}, u32[]{:S(2)}) collective-permute-start(bf16[2,2,2,32,1024]{4,3,2,1,0:T(8,128)(2,1)S(1)} %get-tuple-element.65.refs_8_.refs_9_), channel_id=1, source_target_pairs={{0,2},{1,3},{2,0},{3,1},{4,6},{5,7},{6,4},{7,5},{8,10},{9,11},{10,... | collective-permute-start | bytes 1572872 | tf_op jit(solution)/shard_map/ppermute | solution.py:677
  40.7 11.9 %collective-permute-start.8 = (bf16[2,2,2,32,1024]{4,3,2,1,0:T(8,128)(2,1)S(1)}, bf16[2,2,2,32,1024]{4,3,2,1,0:T(8,128)(2,1)S(1)}, u32[]{:S(2)}, u32[]{:S(2)}) collective-permute-start(bf16[2,2,2,32,1024]{4,3,2,1,0:T(8,128)(2,1)S(1)} %get-tuple-element.66.refs_9_.refs_10_), channel_id=1, source_target_pairs={{0,2},{1,3},{2,0},{3,1},{4,6},{5,7},{6,4},{7,5},{8,10},{9,11},{10,... | collective-permute-start | bytes 1572872 | tf_op jit(solution)/shard_map/ppermute | solution.py:677
  52.1 3.2 %collective-permute-start.10 = (bf16[2,2,2,32,1024]{4,3,2,1,0:T(8,128)(2,1)S(1)}, bf16[2,2,2,32,1024]{4,3,2,1,0:T(8,128)(2,1)}, u32[]{:S(2)}, u32[]{:S(2)}) collective-permute-start(bf16[2,2,2,32,1024]{4,3,2,1,0:T(8,128)(2,1)S(1)} %collective-permute-done.6.refs_11_.refs_12_), channel_id=1, source_target_pairs={{0,2},{1,3},{2,0},{3,1},{4,6},{5,7},{6,4},{7,5},{8,10},{9,11},{10,... | collective-permute-start | bytes 1572872 | tf_op jit(solution)/shard_map/ppermute | solution.py:677
  52.4 2.9 %collective-permute-start.9 = (bf16[2,2,2,32,1024]{4,3,2,1,0:T(8,128)(2,1)S(1)}, bf16[2,2,2,32,1024]{4,3,2,1,0:T(8,128)(2,1)}, u32[]{:S(2)}, u32[]{:S(2)}) collective-permute-start(bf16[2,2,2,32,1024]{4,3,2,1,0:T(8,128)(2,1)S(1)} %collective-permute-done.5.refs_10_.refs_11_), channel_id=1, source_target_pairs={{0,2},{1,3},{2,0},{3,1},{4,6},{5,7},{6,4},{7,5},{8,10},{9,11},{10,... | collective-permute-start | bytes 1572872 | tf_op jit(solution)/shard_map/ppermute | solution.py:677
  74.6 5.3 %collective-permute-start.11 = (bf16[2,2,2,4,256,128]{5,4,3,2,1,0:T(8,128)(2,1)}, bf16[2,2,2,4,256,128]{5,4,3,2,1,0:T(8,128)(2,1)}, u32[]{:S(2)}, u32[]{:S(2)}) collective-permute-start(bf16[2,2,2,4,256,128]{5,4,3,2,1,0:T(8,128)(2,1)} %get-tuple-element.77), channel_id=1, source_target_pairs={{0,2},{1,3},{2,0},{3,1},{4,6},{5,7},{6,4},{7,5},{8,10},{9,11},{10,... | collective-permute-start | bytes 6291464 | tf_op jit(solution)/shard_map/ppermute | solution.py:677
  75.8 18.3 %all-to-all-start.2 = ((bf16[32,64,128]{2,1,0:T(8,128)(2,1)}), bf16[32,64,128]{2,1,0:T(8,128)(2,1)S(1)}, u32[]{:S(2)}, u32[]{:S(2)}) async-start(bf16[32,64,128]{2,1,0:T(8,128)(2,1)} %get-tuple-element.67), calls=%async_computation.2 | async-start | bytes 1048576 | tf_op jit(solution)/shard_map/all_to_all | solution.py:773
  82.3 19.8 %collective-permute-start.12 = (bf16[2,4,256,128]{3,2,1,0:T(8,128)(2,1)}, bf16[2,4,256,128]{3,2,1,0:T(8,128)(2,1)}, u32[]{:S(2)}, u32[]{:S(2)}) collective-permute-start(bf16[2,4,256,128]{3,2,1,0:T(8,128)(2,1)} %get-tuple-element.78), channel_id=1, source_target_pairs={{0,1},{1,0},{2,3},{3,2},{4,5},{5,4},{6,7},{7,6},{8,9},{9,8},{10,11... | collective-permute-start | bytes 1572872 | tf_op jit(solution)/shard_map/ppermute | solution.py:677
  83.4 18.6 %collective-permute-start.13 = (bf16[2,4,256,128]{3,2,1,0:T(8,128)(2,1)}, bf16[2,4,256,128]{3,2,1,0:T(8,128)(2,1)}, u32[]{:S(2)}, u32[]{:S(2)}) collective-permute-start(bf16[2,4,256,128]{3,2,1,0:T(8,128)(2,1)} %get-tuple-element.79), channel_id=1, source_target_pairs={{0,4},{1,5},{2,6},{3,7},{4,0},{5,1},{6,2},{7,3},{8,12},{9,13},{10,... | collective-permute-start | bytes 1572872 | tf_op jit(solution)/shard_map/ppermute | solution.py:677
  97.1 31.8 %all-to-all-start.3 = ((bf16[32,64,128]{2,1,0:T(8,128)(2,1)}), bf16[32,64,128]{2,1,0:T(8,128)(2,1)S(1)}, u32[]{:S(2)}, u32[]{:S(2)}) async-start(bf16[32,64,128]{2,1,0:T(8,128)(2,1)} %get-tuple-element.90), calls=%async_computation.3 | async-start | bytes 1048576 | tf_op jit(solution)/shard_map/all_to_all | solution.py:796
  100.7 1.3 collective-permute-start.14
  103.5 15.3 %collective-permute-start.15 = (bf16[4,256,128]{2,1,0:T(8,128)(2,1)S(1)}, bf16[4,256,128]{2,1,0:T(8,128)(2,1)S(1)}, u32[]{:S(2)}, u32[]{:S(2)}) collective-permute-start(bf16[4,256,128]{2,1,0:T(8,128)(2,1)S(1)} %get-tuple-element.82), channel_id=1, source_target_pairs={{0,4},{1,5},{2,6},{3,7},{4,0},{5,1},{6,2},{7,3},{8,12},{9,13},{10,... | collective-permute-start | bytes 786440 | tf_op jit(solution)/shard_map/ppermute | solution.py:677
  105.3 13.5 %collective-permute-start.16 = (bf16[4,256,128]{2,1,0:T(8,128)(2,1)S(1)}, bf16[4,256,128]{2,1,0:T(8,128)(2,1)S(1)}, u32[]{:S(2)}, u32[]{:S(2)}) collective-permute-start(bf16[4,256,128]{2,1,0:T(8,128)(2,1)S(1)} %get-tuple-element.83), channel_id=1, source_target_pairs={{0,1},{1,0},{2,3},{3,2},{4,5},{5,4},{6,7},{7,6},{8,9},{9,8},{10,11... | collective-permute-start | bytes 786440 | tf_op jit(solution)/shard_map/ppermute | solution.py:677
  106.8 4.6 %collective-permute-start.17 = (bf16[160,128]{1,0:T(8,128)(2,1)S(1)}, bf16[160,128]{1,0:T(8,128)(2,1)S(1)}, u32[]{:S(2)}, u32[]{:S(2)}) collective-permute-start(bf16[160,128]{1,0:T(8,128)(2,1)S(1)} %get-tuple-element.84.refs_6_), channel_id=1, source_target_pairs={{0,8},{1,9},{2,10},{3,11},{4,12},{5,13},{6,14},{7,15},{8,0},{9,1},... | collective-permute-start | bytes 122888 | tf_op jit(solution)/shard_map/ppermute | solution.py:677
  108.3 10.5 %collective-permute-start.18 = (bf16[160,128]{1,0:T(8,128)(2,1)S(1)}, bf16[160,128]{1,0:T(8,128)(2,1)S(1)}, u32[]{:S(2)}, u32[]{:S(2)}) collective-permute-start(bf16[160,128]{1,0:T(8,128)(2,1)S(1)} %get-tuple-element.84.refs_6_), channel_id=1, source_target_pairs={{0,16},{1,17},{2,18},{3,19},{4,20},{5,21},{6,22},{7,23},{8,24},{9,... | collective-permute-start | bytes 122888 | tf_op jit(solution)/shard_map/ppermute | solution.py:677
  110.7 8.1 %collective-permute-start.19 = (bf16[160,128]{1,0:T(8,128)(2,1)S(1)}, bf16[160,128]{1,0:T(8,128)(2,1)S(1)}, u32[]{:S(2)}, u32[]{:S(2)}) collective-permute-start(bf16[160,128]{1,0:T(8,128)(2,1)S(1)} %get-tuple-element.84.refs_6_), channel_id=1, source_target_pairs={{0,24},{1,25},{2,26},{3,27},{4,28},{5,29},{6,30},{7,31},{8,16},{9,... | collective-permute-start | bytes 122888 | tf_op jit(solution)/shard_map/ppermute | solution.py:677
  121.0 5.2 %collective-permute-start.23 = (bf16[2,256,128]{2,1,0:T(8,128)(2,1)S(1)}, bf16[2,256,128]{2,1,0:T(8,128)(2,1)S(1)}, u32[]{:S(2)}, u32[]{:S(2)}) collective-permute-start(bf16[2,256,128]{2,1,0:T(8,128)(2,1)S(1)} %get-tuple-element.87), channel_id=1, source_target_pairs={{0,8},{1,9},{2,10},{3,11},{4,12},{5,13},{6,14},{7,15},{8,0},{9,1},... | collective-permute-start | bytes 393224 | tf_op jit(solution)/shard_map/ppermute | solution.py:677
  122.0 14.3 %collective-permute-start.20 = (bf16[4,160,128]{2,1,0:T(8,128)(2,1)S(1)}, bf16[4,160,128]{2,1,0:T(8,128)(2,1)S(1)}, u32[]{:S(2)}, u32[]{:S(2)}) collective-permute-start(bf16[4,160,128]{2,1,0:T(8,128)(2,1)S(1)} %get-tuple-element.86.refs_0_), channel_id=1, source_target_pairs={{0,1},{1,0},{2,3},{3,2},{4,5},{5,4},{6,7},{7,6},{8,9},{9,8},{10,11... | collective-permute-start | bytes 491528 | tf_op jit(solution)/shard_map/ppermute | solution.py:677
  123.5 12.9 %collective-permute-start.21 = (bf16[4,160,128]{2,1,0:T(8,128)(2,1)S(1)}, bf16[4,160,128]{2,1,0:T(8,128)(2,1)S(1)}, u32[]{:S(2)}, u32[]{:S(2)}) collective-permute-start(bf16[4,160,128]{2,1,0:T(8,128)(2,1)S(1)} %get-tuple-element.86.refs_0_), channel_id=1, source_target_pairs={{0,4},{1,5},{2,6},{3,7},{4,0},{5,1},{6,2},{7,3},{8,12},{9,13},{10,... | collective-permute-start | bytes 491528 | tf_op jit(solution)/shard_map/ppermute | solution.py:677
  125.0 11.4 %collective-permute-start.22 = (bf16[4,160,128]{2,1,0:T(8,128)(2,1)S(1)}, bf16[4,160,128]{2,1,0:T(8,128)(2,1)S(1)}, u32[]{:S(2)}, u32[]{:S(2)}) collective-permute-start(bf16[4,160,128]{2,1,0:T(8,128)(2,1)S(1)} %get-tuple-element.86.refs_0_), channel_id=1, source_target_pairs={{0,5},{1,4},{2,7},{3,6},{4,1},{5,0},{6,3},{7,2},{8,13},{9,12},{10,... | collective-permute-start | bytes 491528 | tf_op jit(solution)/shard_map/ppermute | solution.py:677
  125.5 10.8 %collective-permute-start.24 = (bf16[2,256,128]{2,1,0:T(8,128)(2,1)}, bf16[2,256,128]{2,1,0:T(8,128)(2,1)S(1)}, u32[]{:S(2)}, u32[]{:S(2)}) collective-permute-start(bf16[2,256,128]{2,1,0:T(8,128)(2,1)} %get-tuple-element.88), channel_id=1, source_target_pairs={{0,16},{1,17},{2,18},{3,19},{4,20},{5,21},{6,22},{7,23},{8,24},{9,... | collective-permute-start | bytes 393224 | tf_op jit(solution)/shard_map/ppermute | solution.py:677
  126.2 10.2 %collective-permute-start.25 = (bf16[2,256,128]{2,1,0:T(8,128)(2,1)}, bf16[2,256,128]{2,1,0:T(8,128)(2,1)S(1)}, u32[]{:S(2)}, u32[]{:S(2)}) collective-permute-start(bf16[2,256,128]{2,1,0:T(8,128)(2,1)} %get-tuple-element.89), channel_id=1, source_target_pairs={{0,24},{1,25},{2,26},{3,27},{4,28},{5,29},{6,30},{7,31},{8,16},{9,... | collective-permute-start | bytes 393224 | tf_op jit(solution)/shard_map/ppermute | solution.py:677
  128.9 9.0 %copy-start.3 = (f32[2,8,2,64,64]{4,3,2,1,0:T(8,128)S(1)}, f32[2,8,2,64,64]{4,3,2,1,0:T(8,128)}, u32[]{:S(2)}) copy-start(f32[2,8,2,64,64]{4,3,2,1,0:T(8,128)} %refs_13_.1) | copy-start | bytes 1572868
  128.9 9.0 %copy-start.4 = (f32[2,8,2,64,64]{4,3,2,1,0:T(8,128)S(1)}, f32[2,8,2,64,64]{4,3,2,1,0:T(8,128)}, u32[]{:S(2)}) copy-start(f32[2,8,2,64,64]{4,3,2,1,0:T(8,128)} %refs_14_.1) | copy-start | bytes 1572868
  128.9 9.0 %copy-start.5 = (f32[2,8,2,64,64]{4,3,2,1,0:T(8,128)S(1)}, f32[2,8,2,64,64]{4,3,2,1,0:T(8,128)}, u32[]{:S(2)}) copy-start(f32[2,8,2,64,64]{4,3,2,1,0:T(8,128)} %refs_15_.1) | copy-start | bytes 1572868
  128.9 9.0 %copy-start.6 = (f32[32,1024]{1,0:T(8,128)S(1)}, f32[32,1024]{1,0:T(8,128)}, u32[]{:S(2)}) copy-start(f32[32,1024]{1,0:T(8,128)} %refs_6_.1) | copy-start | bytes 393220
  128.9 9.0 %copy-start.7 = (f32[32,1024]{1,0:T(8,128)S(1)}, f32[32,1024]{1,0:T(8,128)}, u32[]{:S(2)}) copy-start(f32[32,1024]{1,0:T(8,128)} %refs_5_.3) | copy-start | bytes 393220
  128.9 9.0 %copy-start.11 = (f32[32,1024]{1,0:T(8,128)S(1)}, f32[32,1024]{1,0:T(8,128)}, u32[]{:S(2)}) copy-start(f32[32,1024]{1,0:T(8,128)} %refs_7_.2) | copy-start | bytes 393220
  129.0 9.0 %copy-start.12 = (f32[32,1024]{1,0:T(8,128)S(1)}, f32[32,1024]{1,0:T(8,128)}, u32[]{:S(2)}) copy-start(f32[32,1024]{1,0:T(8,128)} %refs_8_.1) | copy-start | bytes 393220
  129.0 9.0 %copy-start.13 = (f32[32,1024]{1,0:T(8,128)S(1)}, f32[32,1024]{1,0:T(8,128)}, u32[]{:S(2)}) copy-start(f32[32,1024]{1,0:T(8,128)} %refs_9_.1) | copy-start | bytes 393220
  129.0 9.0 %copy-start.14 = (f32[32,1024]{1,0:T(8,128)S(1)}, f32[32,1024]{1,0:T(8,128)}, u32[]{:S(2)}) copy-start(f32[32,1024]{1,0:T(8,128)} %refs_10_.1) | copy-start | bytes 393220
  129.0 9.0 %copy-start.15 = (f32[13,512]{1,0:T(8,128)S(1)}, f32[13,512]{1,0:T(8,128)}, u32[]{:S(2)}) copy-start(f32[13,512]{1,0:T(8,128)} %refs_17_.1) | copy-start | bytes 79876
  129.0 9.0 %copy-start.16 = (f32[13,512]{1,0:T(8,128)S(1)}, f32[13,512]{1,0:T(8,128)}, u32[]{:S(2)}) copy-start(f32[13,512]{1,0:T(8,128)} %refs_18_.1) | copy-start | bytes 79876
  136.5 1.5 %collective-permute-start.26 = (bf16[4,160,128]{2,1,0:T(8,128)(2,1)S(1)}, bf16[4,160,128]{2,1,0:T(8,128)(2,1)S(1)}, u32[]{:S(2)}, u32[]{:S(2)}) collective-permute-start(bf16[4,160,128]{2,1,0:T(8,128)(2,1)S(1)} %get-tuple-element.95.refs_11_), channel_id=1, source_target_pairs={{0,2},{1,3},{2,0},{3,1},{4,6},{5,7},{6,4},{7,5},{8,10},{9,11},{10,... | collective-permute-start | bytes 491528 | tf_op jit(solution)/shard_map/ppermute | solution.py:677
  (4 other events, 11.5 us)

commit v6 on v5

--- a/solution.py
+++ b/solution.py
@@ -369,7 +369,7 @@
         ref.flush()
 
 
-def load_weights(near, place_ref, pieces, part, target, sems):
+def load_weights(near, place_ref, pieces, part, target, sem):
     copies = []
     part = () if part is None else (part,)
     every = (slice(None),) * (1 - len(part))
@@ -387,10 +387,9 @@
                     row = (((at[3] ^ z) * 2 + (at[1] ^ y)) * 2 + (at[0] ^ (i >> 2))) * size
                     rows = pl.ds(pl.multiple_of(row, size), size)
                     copies.append((ref.at[(j, k, *part)], target.at[(at[2] ^ x, *every, rows)]))
-    copies = [pltpu.make_async_copy(source, target, sems.at[i]) for i, (source, target) in enumerate(copies)]
-    for copy in copies:
-        copy.start()
-    return copies
+    for source, place in copies:
+        pltpu.make_async_copy(source, place, sem).start(priority=1)
+    return pltpu.make_async_copy(target, target, sem)
 
 
 def place_rows(ref, values, columns, orders):
@@ -409,8 +408,8 @@
     pieces, refs = refs[:count], refs[count:]
     active, total_ref, middle_ref, send_ref, small_ref, *refs = refs
     grad_refs, refs = refs[:2], refs[2:]
-    normed, normed_t, cotangent_t, normal, spread, weights, grad_hidden, sems = refs
-    copies = load_weights(near, place_ref, pieces, None, weights, sems)
+    normed, normed_t, cotangent_t, normal, spread, weights, grad_hidden, sem = refs
+    arrival = load_weights(near, place_ref, pieces, None, weights, sem)
     cotangent_ref.start()
     wide_ref.start()
     w_in, w_out = weights.at[:, 0], weights.at[:, 1]
@@ -439,8 +438,7 @@
         place_rows(cotangent_t, upstream.T, rows, orders)
         bias_out_grad = bias_out_grad + jnp.sum(upstream.astype(F32), axis=0, keepdims=True)
     total_ref.flush()
-    for copy in copies:
-        copy.wait()
+    arrival.wait()
     gain_grad = jnp.zeros((1, width), F32)
     shift_grad = jnp.zeros((1, width), F32)
     chunks = [(h, c) for h in range(halves) for c in range(0, columns, CHUNK)]
@@ -495,9 +493,8 @@
 def output_kernel(near, place_ref, *refs):
     count = 8 if near else 1
     totals, actives, pieces = refs[:OUT_BLOCKS], refs[OUT_BLOCKS : 2 * OUT_BLOCKS], refs[2 * OUT_BLOCKS :][:count]
-    outputs, w_out, sems = refs[2 * OUT_BLOCKS + count], *refs[2 * OUT_BLOCKS + count + 1 :]
-    for copy in load_weights(near, place_ref, pieces, 1, w_out, sems):
-        copy.wait()
+    outputs, w_out, sem = refs[2 * OUT_BLOCKS + count], *refs[2 * OUT_BLOCKS + count + 1 :]
+    load_weights(near, place_ref, pieces, 1, w_out, sem).wait()
     halves, _, columns = w_out.shape
     size = totals[0].shape[0]
     for i, (total, active) in enumerate(zip(totals, actives, strict=True)):
@@ -744,7 +741,7 @@
             pltpu.VMEM((local, 1), F32),
             pltpu.VMEM((tp_count, 2, model, shard_columns), BF16),
             pltpu.VMEM((local, hidden), BF16),
-            pltpu.SemaphoreType.DMA((32 if near else 1,)),
+            pltpu.SemaphoreType.DMA,
         ],
         flops=12 * local * width * hidden + 2 * wide_flops, vmem=44,
     )
@@ -766,7 +763,7 @@
         scalars=[me[None]], raw=pieces, cost=COST, vmem=24,
         scratch=[
             pltpu.VMEM((tp_count, model, shard_columns), BF16),
-            pltpu.SemaphoreType.DMA((32 if near else 1,)),
+            pltpu.SemaphoreType.DMA,
         ],
     )
 

time: 143 us -> 142 us (level)
  Pallas kernels: 49.8 us -> 48.2 us
    pallas_call x11, Pallas kernels: 49.8 us -> 48.2 us  [call(): pl.pallas_call(inner, out_shape=[(pltpu.HBM if f else pltpu.VMEM)(o.shape...]
where the time goes in v6:
time: 142 us; the launch traced here: 141 us
  starting transfers between devices  48.2 us (34%)
  Pallas kernels  48.2 us (34%)
  waiting for transfers between devices  38 us (27%)
  other arithmetic  2.49 us (2%)
  local copies, waits for them, and re-layouts  2.36 us (2%)
  between operations  1.44 us (1%)
    pallas_call x11, Pallas kernels, call(): pl.pallas_call(inner, out_shape=[(pltpu.HBM if f else pltpu.VMEM)(o.shape...  48.2 us
    ppermute x27, waiting for transfers between devices, permute(): return lax.ppermute(values, AXES, [(d, d ^ mask) for d in range(devices)])  33.5 us
    ppermute x27, starting transfers between devices, permute(): return lax.ppermute(values, AXES, [(d, d ^ mask) for d in range(devices)])  31.8 us
    all_to_all x4, starting transfers between devices, on_device(): got = exchange(sent)  16.5 us
    all_to_all x4, waiting for transfers between devices, on_device(): got = exchange(sent)  4.42 us
  transfers between devices with their start and end apart: 31, of which 12 were waited for; matrix products, arithmetic and copies ran while one was open for 3% of the time, Pallas kernels for 17%

profile of v6, /device:TPU:0, one launch (start us, length us, event | category | flops | bytes accessed | tf_op | source)
XLA Modules:
  0.0 140.7 jit_solution(17055994828830430992)
XLA Ops:
  0.7 1.0 convert_bitcast_fusion
  1.7 4.1 %collective-permute-start.2 = (bf16[2,32,1024]{2,1,0:T(8,128)(2,1)S(1)}, bf16[2,32,1024]{2,1,0:T(8,128)(2,1)S(1)}, u32[]{:S(2)}, u32[]{:S(2)}) collective-permute-start(bf16[2,32,1024]{2,1,0:T(8,128)(2,1)S(1)} %get-tuple-element.117), channel_id=1, source_target_pairs={{0,16},{1,17},{2,18},{3,19},{4,20},{5,21},{6,22},{7,23},{8,24},{9,... | collective-permute-start | bytes 393224 | tf_op jit(solution)/shard_map/ppermute | solution.py:674
  5.8 1.3 collective-permute-start.3
  7.4 3.0 %shard_map.324 = bf16[32,64,128]{2,1,0:T(8,128)(2,1)} custom-call(bf16[1024,512]{1,0:T(8,128)(2,1)} %bitcast.40, bf16[256,512]{1,0:T(8,128)(2,1)} %constant.61.clone.refs_1_), custom_call_target="tpu_custom_call" | custom-call | flops 268435456 | bytes 1835008 | tf_op jit(solution)/shard_map/pallas_call | solution.py:628
  10.4 5.2 %all-to-all-start = ((bf16[32,64,128]{2,1,0:T(8,128)(2,1)}), bf16[32,64,128]{2,1,0:T(8,128)(2,1)S(1)}, u32[]{:S(2)}, u32[]{:S(2)}) async-start(bf16[32,64,128]{2,1,0:T(8,128)(2,1)} %shard_map.324), calls=%async_computation | async-start | bytes 1048576 | tf_op jit(solution)/shard_map/all_to_all | solution.py:707
  15.6 1.0 dynamic-slice_convert_fusion
  17.0 0.9 dynamic-slice_bitcast_fusion.refs_7_.refs_5_
  18.0 1.8 %collective-permute-start.4 = (bf16[2,2,32,1024]{3,2,1,0:T(8,128)(2,1)S(1)}, bf16[2,2,32,1024]{3,2,1,0:T(8,128)(2,1)S(1)}, u32[]{:S(2)}, u32[]{:S(2)}) collective-permute-start(bf16[2,2,32,1024]{3,2,1,0:T(8,128)(2,1)S(1)} %get-tuple-element.113), channel_id=1, source_target_pairs={{0,4},{1,5},{2,6},{3,7},{4,0},{5,1},{6,2},{7,3},{8,12},{9,13},{10,... | collective-permute-start | bytes 786440 | tf_op jit(solution)/shard_map/ppermute | solution.py:674
  19.9 1.5 %collective-permute-start.1 = (bf16[2,2,32,1024]{3,2,1,0:T(8,128)(2,1)S(1)}, bf16[2,2,32,1024]{3,2,1,0:T(8,128)(2,1)}, u32[]{:S(2)}, u32[]{:S(2)}) collective-permute-start(bf16[2,2,32,1024]{3,2,1,0:T(8,128)(2,1)S(1)} %get-tuple-element.115), channel_id=1, source_target_pairs={{0,1},{1,0},{2,3},{3,2},{4,5},{5,4},{6,7},{7,6},{8,9},{9,8},{10,11... | collective-permute-start | bytes 786440 | tf_op jit(solution)/shard_map/ppermute | solution.py:674
  21.8 8.2 %collective-permute-done.4 = bf16[2,2,32,1024]{3,2,1,0:T(8,128)(2,1)S(1)} collective-permute-done((bf16[2,2,32,1024]{3,2,1,0:T(8,128)(2,1)S(1)}, bf16[2,2,32,1024]{3,2,1,0:T(8,128)(2,1)S(1)}, u32[]{:S(2)}, u32[]{:S(2)}) %collective-permute-start.4) | collective-permute-done | bytes 262176 | tf_op jit(solution)/shard_map/ppermute | solution.py:674
  30.1 0.4 collective-permute-done.1
  30.5 1.0 pad_maximum_fusion.refs_8_
  31.5 2.3 %shard_map.325 = (bf16[32,64,128]{2,1,0:T(8,128)(2,1)}, f32[128,512]{1,0:T(8,128)}, bf16[256,256]{1,0:T(8,128)(2,1)}, f32[256,256]{1,0:T(8,128)}, bf16[256,256]{...) custom-call(bf16[32,64,128]{2,1,0:T(8,128)(2,1)S(1)} %all-to-all-don, ...), custom_call_target="tpu_custom_call", output_to_operand_aliasing={{5}: (8, {}), {6}: (9, {})} | custom-call | bytes 2364416 | tf_op jit(solution)/shard_map/pallas_call | solution.py:628
  33.9 1.2 collective-permute-start.6
  35.0 1.1 collective-permute-start.5
  36.1 4.3 %all-to-all-start.1 = ((bf16[32,64,128]{2,1,0:T(8,128)(2,1)}), bf16[32,64,128]{2,1,0:T(8,128)(2,1)}, u32[]{:S(2)}, u32[]{:S(2)}) async-start(bf16[32,64,128]{2,1,0:T(8,128)(2,1)} %get-tuple-element.64), calls=%async_computation.1 | async-start | bytes 1048576 | tf_op jit(solution)/shard_map/all_to_all | solution.py:724
  41.1 11.0 %collective-permute-done.6.refs_11_.refs_12_ = bf16[2,2,2,32,1024]{4,3,2,1,0:T(8,128)(2,1)S(1)} collective-permute-done((bf16[2,2,2,32,1024]{4,3,2,1,0:T(8,128)(2,1)S(1)}, bf16[2,2,2,32,1024]{4,3,2,1,0:T(8,128)(2,1)S(1)}, u32[]{:S(2)}, u32[]{:S(2)}) %collective-permute-start.6) | collective-permute-done | bytes 524320 | tf_op jit(solution)/shard_map/ppermute | solution.py:674
  52.6 2.7 %all-to-all-done.1.refs_1_ = bf16[32,64,128]{2,1,0:T(8,128)(2,1)} async-done(((bf16[32,64,128]{2,1,0:T(8,128)(2,1)}), bf16[32,64,128]{2,1,0:T(8,128)(2,1)}, u32[]{:S(2)}, u32[]{:S(2)}) %all-to-all-start.1) | async-done | bytes 524320 | tf_op jit(solution)/shard_map/all_to_all | solution.py:724
  55.3 17.9 %shard_map.326 = (bf16[1024,2048]{1,0:T(8,128)(2,1)}, f32[1024,512]{1,0:T(8,128)}, bf16[1024,512]{1,0:T(8,128)(2,1)}, bf16[32,64,128]{2,1,0:T(8,128)(2,1)}, f32[...) custom-call(s32[1]{0:T(128)} %bitcast.1.refs_0_, ...), custom_call_target="tpu_custom_call" | custom-call | flops 13421772800 | bytes 19449856 | tf_op jit(solution)/shard_map/pallas_call | solution.py:628
  73.2 1.1 collective-permute-start.11
  74.3 3.3 %all-to-all-start.2 = ((bf16[32,64,128]{2,1,0:T(8,128)(2,1)}), bf16[32,64,128]{2,1,0:T(8,128)(2,1)S(1)}, u32[]{:S(2)}, u32[]{:S(2)}) async-start(bf16[32,64,128]{2,1,0:T(8,128)(2,1)} %get-tuple-element.67), calls=%async_computation.2 | async-start | bytes 1048576 | tf_op jit(solution)/shard_map/all_to_all | solution.py:770
  77.7 0.8 collective-permute-done.11.refs_1_.refs_5_.refs_10_
  78.5 2.3 %shard_map.329 = (bf16[2,4,256,128]{3,2,1,0:T(8,128)(2,1)}, bf16[2,4,256,128]{3,2,1,0:T(8,128)(2,1)}) custom-call(bf16[2,2,2,4,256,128]{5,4,3,2,1,0:T(8,128)(2,1)S(1)} %get-tuple-element.76.refs_0_.refs_1_, bf16[2,2,2,4,256,128]{5,4,3,2,1,0:T(8,128)(2,1)} %collective-permute-done.11.refs_1_.refs_5_.refs_10_), custom_call_target="tpu_custom_call" | custom-call | tf_op jit(solution)/shard_map/pallas_call | solution.py:628
  80.8 1.2 collective-permute-start.12
  82.0 1.4 collective-permute-start.13
  83.3 7.6 %shard_map.327.refs_11_ = bf16[1024,512]{1,0:T(8,128)(2,1)} custom-call(s32[1]{0:T(128)} %bitcast.1.refs_0_, f32[1024,512]{1,0:T(8,128)} %get-tuple-element.73.refs_1_.refs_2_.refs_3_.refs_4_, f32[1024,512]{1,0:T(8,128)} %get-tuple-element.73.refs_1_.refs_2_.refs_3_.refs_4_, f32[1024,512]{1,0:T(8,128)} %get-tuple-element.73.refs_1_.refs_2_.refs_3_.refs_4_, ...), custom_call_target="tpu_custom_call" | custom-call | bytes 62914560 | tf_op jit(solution)/shard_map/pallas_call | solution.py:628
  90.9 1.8 %all-to-all-done.2.refs_1_ = bf16[32,64,128]{2,1,0:T(8,128)(2,1)S(1)} async-done(((bf16[32,64,128]{2,1,0:T(8,128)(2,1)}), bf16[32,64,128]{2,1,0:T(8,128)(2,1)S(1)}, u32[]{:S(2)}, u32[]{:S(2)}) %all-to-all-start.2) | async-done | bytes 524320 | tf_op jit(solution)/shard_map/all_to_all | solution.py:770
  92.7 3.0 %shard_map.328 = (bf16[32,64,128]{2,1,0:T(8,128)(2,1)}, bf16[160,128]{1,0:T(8,128)(2,1)S(1)}, bf16[160,128]{1,0:T(8,128)(2,1)S(1)}, bf16[1024,512]{1,0:T(8,128)(2,1)}) custom-call(s32[1]{0:T(128)} %bitcast.refs_0_, bf16[32,64,128]{2,1,0:T(8,128)(2,1)S(1)} %all-to-all-done.2.refs_1_, ...), custom_call_target="tpu_custom_call", output_to_operand_aliasing={{3}: (11, {})} | custom-call | bytes 62914560 | tf_op jit(solution)/shard_map/pallas_call | solution.py:628
  95.6 3.6 %all-to-all-start.3 = ((bf16[32,64,128]{2,1,0:T(8,128)(2,1)}), bf16[32,64,128]{2,1,0:T(8,128)(2,1)S(1)}, u32[]{:S(2)}, u32[]{:S(2)}) async-start(bf16[32,64,128]{2,1,0:T(8,128)(2,1)} %get-tuple-element.90), calls=%async_computation.3 | async-start | bytes 1048576 | tf_op jit(solution)/shard_map/all_to_all | solution.py:793
  99.6 1.0 collective-permute-done.14.refs_4_
  100.6 1.5 %shard_map.330 = (bf16[160,128]{1,0:T(8,128)(2,1)S(1)}, bf16[4,256,128]{2,1,0:T(8,128)(2,1)S(1)}, bf16[4,256,128]{2,1,0:T(8,128)(2,1)S(1)}) custom-call(bf16[2,2,2,4,256,128]{5,4,3,2,1,0:T(8,128)(2,1)S(1)} %get-tuple-element.76.refs_0_.refs_1_, bf16[2,4,256,128]{3,2,1,0:T(8,128)(2,1)} %collective-permute-done.12.refs_1_.refs_2_, ...), custom_call_target="tpu_custom_call" | custom-call | tf_op jit(solution)/shard_map/pallas_call | solution.py:628
  102.0 1.8 %collective-permute-start.15 = (bf16[4,256,128]{2,1,0:T(8,128)(2,1)S(1)}, bf16[4,256,128]{2,1,0:T(8,128)(2,1)S(1)}, u32[]{:S(2)}, u32[]{:S(2)}) collective-permute-start(bf16[4,256,128]{2,1,0:T(8,128)(2,1)S(1)} %get-tuple-element.82), channel_id=1, source_target_pairs={{0,4},{1,5},{2,6},{3,7},{4,0},{5,1},{6,2},{7,3},{8,12},{9,13},{10,... | collective-permute-start | bytes 786440 | tf_op jit(solution)/shard_map/ppermute | solution.py:674
  103.9 1.5 %collective-permute-start.16 = (bf16[4,256,128]{2,1,0:T(8,128)(2,1)S(1)}, bf16[4,256,128]{2,1,0:T(8,128)(2,1)S(1)}, u32[]{:S(2)}, u32[]{:S(2)}) collective-permute-start(bf16[4,256,128]{2,1,0:T(8,128)(2,1)S(1)} %get-tuple-element.83), channel_id=1, source_target_pairs={{0,1},{1,0},{2,3},{3,2},{4,5},{5,4},{6,7},{7,6},{8,9},{9,8},{10,11... | collective-permute-start | bytes 786440 | tf_op jit(solution)/shard_map/ppermute | solution.py:674
  105.3 1.5 %collective-permute-start.17 = (bf16[160,128]{1,0:T(8,128)(2,1)S(1)}, bf16[160,128]{1,0:T(8,128)(2,1)S(1)}, u32[]{:S(2)}, u32[]{:S(2)}) collective-permute-start(bf16[160,128]{1,0:T(8,128)(2,1)S(1)} %get-tuple-element.84.refs_6_), channel_id=1, source_target_pairs={{0,8},{1,9},{2,10},{3,11},{4,12},{5,13},{6,14},{7,15},{8,0},{9,1},... | collective-permute-start | bytes 122888 | tf_op jit(solution)/shard_map/ppermute | solution.py:674
  106.8 2.5 %collective-permute-start.18 = (bf16[160,128]{1,0:T(8,128)(2,1)S(1)}, bf16[160,128]{1,0:T(8,128)(2,1)S(1)}, u32[]{:S(2)}, u32[]{:S(2)}) collective-permute-start(bf16[160,128]{1,0:T(8,128)(2,1)S(1)} %get-tuple-element.84.refs_6_), channel_id=1, source_target_pairs={{0,16},{1,17},{2,18},{3,19},{4,20},{5,21},{6,22},{7,23},{8,24},{9,... | collective-permute-start | bytes 122888 | tf_op jit(solution)/shard_map/ppermute | solution.py:674
  109.3 0.5 collective-permute-start.19
  109.9 7.4 %collective-permute-done.18.refs_8_ = bf16[160,128]{1,0:T(8,128)(2,1)S(1)} collective-permute-done((bf16[160,128]{1,0:T(8,128)(2,1)S(1)}, bf16[160,128]{1,0:T(8,128)(2,1)S(1)}, u32[]{:S(2)}, u32[]{:S(2)}) %collective-permute-start.18) | collective-permute-done | bytes 40992 | tf_op jit(solution)/shard_map/ppermute | solution.py:674
  117.4 2.1 %shard_map.331 = (bf16[4,160,128]{2,1,0:T(8,128)(2,1)S(1)}, f32[2,256,128]{2,1,0:T(8,128)S(1)}, bf16[2,256,128]{2,1,0:T(8,128)(2,1)S(1)}, bf16[2,256,128]{2,1,0:T(8,128)(2,1)}, bf16[2,256,128]{2,1,0:T(8,128)(2,1)}) custom-call(s32[1]{0:T(128)} %bitcast.1.refs_0_, bf16[2,2,2,4,256,128]{5,4,3,2,1,0:T(8,128)(2,1)S(1)} %get-tuple-element.76.refs_0_.refs_1_, ...), custom_call_target="tpu_custom_call" | custom-call | tf_op jit(solution)/shard_map/pallas_call | solution.py:628
  119.5 1.1 collective-permute-start.23
  120.5 1.5 %collective-permute-start.20 = (bf16[4,160,128]{2,1,0:T(8,128)(2,1)S(1)}, bf16[4,160,128]{2,1,0:T(8,128)(2,1)S(1)}, u32[]{:S(2)}, u32[]{:S(2)}) collective-permute-start(bf16[4,160,128]{2,1,0:T(8,128)(2,1)S(1)} %get-tuple-element.86.refs_0_), channel_id=1, source_target_pairs={{0,1},{1,0},{2,3},{3,2},{4,5},{5,4},{6,7},{7,6},{8,9},{9,8},{10,11... | collective-permute-start | bytes 491528 | tf_op jit(solution)/shard_map/ppermute | solution.py:674
  122.0 1.5 %collective-permute-start.21 = (bf16[4,160,128]{2,1,0:T(8,128)(2,1)S(1)}, bf16[4,160,128]{2,1,0:T(8,128)(2,1)S(1)}, u32[]{:S(2)}, u32[]{:S(2)}) collective-permute-start(bf16[4,160,128]{2,1,0:T(8,128)(2,1)S(1)} %get-tuple-element.86.refs_0_), channel_id=1, source_target_pairs={{0,4},{1,5},{2,6},{3,7},{4,0},{5,1},{6,2},{7,3},{8,12},{9,13},{10,... | collective-permute-start | bytes 491528 | tf_op jit(solution)/shard_map/ppermute | solution.py:674
  123.5 0.5 collective-permute-start.22
  124.0 0.7 collective-permute-start.24
  124.7 2.7 %collective-permute-start.25 = (bf16[2,256,128]{2,1,0:T(8,128)(2,1)}, bf16[2,256,128]{2,1,0:T(8,128)(2,1)S(1)}, u32[]{:S(2)}, u32[]{:S(2)}) collective-permute-start(bf16[2,256,128]{2,1,0:T(8,128)(2,1)} %get-tuple-element.89), channel_id=1, source_target_pairs={{0,24},{1,25},{2,26},{3,27},{4,28},{5,29},{6,30},{7,31},{8,16},{9,... | collective-permute-start | bytes 393224 | tf_op jit(solution)/shard_map/ppermute | solution.py:674
  127.5 4.5 %shard_map.332.refs_7_ = bf16[1024,512]{1,0:T(8,128)(2,1)} custom-call(bf16[32,64,128]{2,1,0:T(8,128)(2,1)S(1)} %all-to-all-done.3.refs_0_, bf16[1024,512]{1,0:T(8,128)(2,1)} %bitcast.42, bf16[1024,512]{1,0:T(8,128)(2,1)} %get-tuple-element.91.refs_2_, f32[13,512]{1,0:T(8,128)S(1)} %copy-done.10, bf16[512,256]{1,0:T(8,128)(2,1)} %constant.62.clone.refs_4_), custom_call_target="tpu_custom_call" | custom-call | bytes 62914560 | tf_op jit(solution)/shard_map/pallas_call | solution.py:628
  132.1 2.8 %collective-permute-done.24.refs_5_ = bf16[2,256,128]{2,1,0:T(8,128)(2,1)S(1)} collective-permute-done((bf16[2,256,128]{2,1,0:T(8,128)(2,1)}, bf16[2,256,128]{2,1,0:T(8,128)(2,1)S(1)}, u32[]{:S(2)}, u32[]{:S(2)}) %collective-permute-start.24) | collective-permute-done | bytes 131104 | tf_op jit(solution)/shard_map/ppermute | solution.py:674
  135.1 1.4 collective-permute-done.26.refs_12_
  136.6 3.9 %shard_map.334 = (f32[32,1024]{1,0:T(8,128)}, f32[32,1024]{1,0:T(8,128)}, f32[32,1024]{1,0:T(8,128)}, f32[32,1024]{1,0:T(8,128)}, f32[32,1024]{1,0:T(8,128)}, /*...) custom-call(s32[1]{0:T(128)} %bitcast.refs_0_, ...), custom_call_target="tpu_custom_call", output_to_operand_aliasing={{14}: (19, {})} | custom-call | tf_op jit(solution)/shard_map/pallas_call | solution.py:628
  (89 shorter events, 3.1 us)
Async XLA Ops:
  0.6 16.0 %copy-start.10 = (f32[13,512]{1,0:T(8,128)S(1)}, f32[13,512]{1,0:T(8,128)}, u32[]{:S(2)}) copy-start(f32[13,512]{1,0:T(8,128)} %refs_16_.1) | copy-start | bytes 79876
  1.7 16.3 %collective-permute-start.2 = (bf16[2,32,1024]{2,1,0:T(8,128)(2,1)S(1)}, bf16[2,32,1024]{2,1,0:T(8,128)(2,1)S(1)}, u32[]{:S(2)}, u32[]{:S(2)}) collective-permute-start(bf16[2,32,1024]{2,1,0:T(8,128)(2,1)S(1)} %get-tuple-element.117), channel_id=1, source_target_pairs={{0,16},{1,17},{2,18},{3,19},{4,20},{5,21},{6,22},{7,23},{8,24},{9,... | collective-permute-start | bytes 393224 | tf_op jit(solution)/shard_map/ppermute | solution.py:674
  5.8 12.2 %collective-permute-start.3 = (bf16[2,32,1024]{2,1,0:T(8,128)(2,1)S(1)}, bf16[2,32,1024]{2,1,0:T(8,128)(2,1)S(1)}, u32[]{:S(2)}, u32[]{:S(2)}) collective-permute-start(bf16[2,32,1024]{2,1,0:T(8,128)(2,1)S(1)} %get-tuple-element.117), channel_id=1, source_target_pairs={{0,24},{1,25},{2,26},{3,27},{4,28},{5,29},{6,30},{7,31},{8,16},{9,... | collective-permute-start | bytes 393224 | tf_op jit(solution)/shard_map/ppermute | solution.py:674
  7.1 12.7 %collective-permute-start = (bf16[2,32,1024]{2,1,0:T(8,128)(2,1)S(1)}, bf16[2,32,1024]{2,1,0:T(8,128)(2,1)S(1)}, u32[]{:S(2)}, u32[]{:S(2)}) collective-permute-start(bf16[2,32,1024]{2,1,0:T(8,128)(2,1)S(1)} %get-tuple-element.117), channel_id=1, source_target_pairs={{0,8},{1,9},{2,10},{3,11},{4,12},{5,13},{6,14},{7,15},{8,0},{9,1},... | collective-permute-start | bytes 393224 | tf_op jit(solution)/shard_map/ppermute | solution.py:674
  10.4 21.1 %all-to-all-start = ((bf16[32,64,128]{2,1,0:T(8,128)(2,1)}), bf16[32,64,128]{2,1,0:T(8,128)(2,1)S(1)}, u32[]{:S(2)}, u32[]{:S(2)}) async-start(bf16[32,64,128]{2,1,0:T(8,128)(2,1)} %shard_map.324), calls=%async_computation | async-start | bytes 1048576 | tf_op jit(solution)/shard_map/all_to_all | solution.py:707
  18.0 13.5 %copy-start.8 = (bf16[128,512]{1,0:T(8,128)(2,1)S(1)}, bf16[128,512]{1,0:T(8,128)(2,1)}, u32[]{:S(2)}) copy-start(bf16[128,512]{1,0:T(8,128)(2,1)} %constant.65.clone.refs_1_.refs_2_) | copy-start | bytes 393220
  18.0 13.5 %copy-start.9 = (bf16[512,128]{1,0:T(8,128)(2,1)S(1)}, bf16[512,128]{1,0:T(8,128)(2,1)}, u32[]{:S(2)}) copy-start(bf16[512,128]{1,0:T(8,128)(2,1)} %constant.66.clone.refs_2_.refs_3_) | copy-start | bytes 393220
  18.0 12.0 %collective-permute-start.4 = (bf16[2,2,32,1024]{3,2,1,0:T(8,128)(2,1)S(1)}, bf16[2,2,32,1024]{3,2,1,0:T(8,128)(2,1)S(1)}, u32[]{:S(2)}, u32[]{:S(2)}) collective-permute-start(bf16[2,2,32,1024]{3,2,1,0:T(8,128)(2,1)S(1)} %get-tuple-element.113), channel_id=1, source_target_pairs={{0,4},{1,5},{2,6},{3,7},{4,0},{5,1},{6,2},{7,3},{8,12},{9,13},{10,... | collective-permute-start | bytes 786440 | tf_op jit(solution)/shard_map/ppermute | solution.py:674
  19.9 10.6 %collective-permute-start.1 = (bf16[2,2,32,1024]{3,2,1,0:T(8,128)(2,1)S(1)}, bf16[2,2,32,1024]{3,2,1,0:T(8,128)(2,1)}, u32[]{:S(2)}, u32[]{:S(2)}) collective-permute-start(bf16[2,2,32,1024]{3,2,1,0:T(8,128)(2,1)S(1)} %get-tuple-element.115), channel_id=1, source_target_pairs={{0,1},{1,0},{2,3},{3,2},{4,5},{5,4},{6,7},{7,6},{8,9},{9,8},{10,11... | collective-permute-start | bytes 786440 | tf_op jit(solution)/shard_map/ppermute | solution.py:674
  21.8 12.0 %copy-start.2 = (bf16[2,256,256]{2,1,0:T(8,128)(2,1)}, bf16[2,256,256]{2,1,0:T(8,128)(2,1)S(1)}, u32[]{:S(2)}) copy-start(bf16[2,256,256]{2,1,0:T(8,128)(2,1)S(1)} %maximum_maximum_fusion.refs_3_.refs_4_) | copy-start | bytes 786436
  33.8 21.5 %copy-start = (bf16[2,2,2,32,1024]{4,3,2,1,0:T(8,128)(2,1)}, bf16[2,2,2,32,1024]{4,3,2,1,0:T(8,128)(2,1)S(1)}, u32[]{:S(2)}) copy-start(bf16[2,2,2,32,1024]{4,3,2,1,0:T(8,128)(2,1)S(1)} %get-tuple-element.66.refs_9_.refs_10_) | copy-start | bytes 1572868
  33.9 21.5 %copy-start.1 = (bf16[2,2,2,32,1024]{4,3,2,1,0:T(8,128)(2,1)}, bf16[2,2,2,32,1024]{4,3,2,1,0:T(8,128)(2,1)S(1)}, u32[]{:S(2)}) copy-start(bf16[2,2,2,32,1024]{4,3,2,1,0:T(8,128)(2,1)S(1)} %get-tuple-element.65.refs_8_.refs_9_) | copy-start | bytes 1572868
  33.9 18.2 %collective-permute-start.6 = (bf16[2,2,2,32,1024]{4,3,2,1,0:T(8,128)(2,1)S(1)}, bf16[2,2,2,32,1024]{4,3,2,1,0:T(8,128)(2,1)S(1)}, u32[]{:S(2)}, u32[]{:S(2)}) collective-permute-start(bf16[2,2,2,32,1024]{4,3,2,1,0:T(8,128)(2,1)S(1)} %get-tuple-element.66.refs_9_.refs_10_), channel_id=1, source_target_pairs={{0,1},{1,0},{2,3},{3,2},{4,5},{5,4},{6,7},{7,6},{8,9},{9,8},{10,11... | collective-permute-start | bytes 1572872 | tf_op jit(solution)/shard_map/ppermute | solution.py:674
  35.0 17.3 %collective-permute-start.5 = (bf16[2,2,2,32,1024]{4,3,2,1,0:T(8,128)(2,1)S(1)}, bf16[2,2,2,32,1024]{4,3,2,1,0:T(8,128)(2,1)S(1)}, u32[]{:S(2)}, u32[]{:S(2)}) collective-permute-start(bf16[2,2,2,32,1024]{4,3,2,1,0:T(8,128)(2,1)S(1)} %get-tuple-element.65.refs_8_.refs_9_), channel_id=1, source_target_pairs={{0,4},{1,5},{2,6},{3,7},{4,0},{5,1},{6,2},{7,3},{8,12},{9,13},{10,... | collective-permute-start | bytes 1572872 | tf_op jit(solution)/shard_map/ppermute | solution.py:674
  36.1 19.1 %all-to-all-start.1 = ((bf16[32,64,128]{2,1,0:T(8,128)(2,1)}), bf16[32,64,128]{2,1,0:T(8,128)(2,1)}, u32[]{:S(2)}, u32[]{:S(2)}) async-start(bf16[32,64,128]{2,1,0:T(8,128)(2,1)} %get-tuple-element.64), calls=%async_computation.1 | async-start | bytes 1048576 | tf_op jit(solution)/shard_map/all_to_all | solution.py:724
  40.5 12.1 %collective-permute-start.7 = (bf16[2,2,2,32,1024]{4,3,2,1,0:T(8,128)(2,1)S(1)}, bf16[2,2,2,32,1024]{4,3,2,1,0:T(8,128)(2,1)S(1)}, u32[]{:S(2)}, u32[]{:S(2)}) collective-permute-start(bf16[2,2,2,32,1024]{4,3,2,1,0:T(8,128)(2,1)S(1)} %get-tuple-element.65.refs_8_.refs_9_), channel_id=1, source_target_pairs={{0,2},{1,3},{2,0},{3,1},{4,6},{5,7},{6,4},{7,5},{8,10},{9,11},{10,... | collective-permute-start | bytes 1572872 | tf_op jit(solution)/shard_map/ppermute | solution.py:674
  40.7 11.9 %collective-permute-start.8 = (bf16[2,2,2,32,1024]{4,3,2,1,0:T(8,128)(2,1)S(1)}, bf16[2,2,2,32,1024]{4,3,2,1,0:T(8,128)(2,1)S(1)}, u32[]{:S(2)}, u32[]{:S(2)}) collective-permute-start(bf16[2,2,2,32,1024]{4,3,2,1,0:T(8,128)(2,1)S(1)} %get-tuple-element.66.refs_9_.refs_10_), channel_id=1, source_target_pairs={{0,2},{1,3},{2,0},{3,1},{4,6},{5,7},{6,4},{7,5},{8,10},{9,11},{10,... | collective-permute-start | bytes 1572872 | tf_op jit(solution)/shard_map/ppermute | solution.py:674
  52.1 3.2 %collective-permute-start.10 = (bf16[2,2,2,32,1024]{4,3,2,1,0:T(8,128)(2,1)S(1)}, bf16[2,2,2,32,1024]{4,3,2,1,0:T(8,128)(2,1)}, u32[]{:S(2)}, u32[]{:S(2)}) collective-permute-start(bf16[2,2,2,32,1024]{4,3,2,1,0:T(8,128)(2,1)S(1)} %collective-permute-done.6.refs_11_.refs_12_), channel_id=1, source_target_pairs={{0,2},{1,3},{2,0},{3,1},{4,6},{5,7},{6,4},{7,5},{8,10},{9,11},{10,... | collective-permute-start | bytes 1572872 | tf_op jit(solution)/shard_map/ppermute | solution.py:674
  52.4 2.9 %collective-permute-start.9 = (bf16[2,2,2,32,1024]{4,3,2,1,0:T(8,128)(2,1)S(1)}, bf16[2,2,2,32,1024]{4,3,2,1,0:T(8,128)(2,1)}, u32[]{:S(2)}, u32[]{:S(2)}) collective-permute-start(bf16[2,2,2,32,1024]{4,3,2,1,0:T(8,128)(2,1)S(1)} %collective-permute-done.5.refs_10_.refs_11_), channel_id=1, source_target_pairs={{0,2},{1,3},{2,0},{3,1},{4,6},{5,7},{6,4},{7,5},{8,10},{9,11},{10,... | collective-permute-start | bytes 1572872 | tf_op jit(solution)/shard_map/ppermute | solution.py:674
  73.2 5.3 %collective-permute-start.11 = (bf16[2,2,2,4,256,128]{5,4,3,2,1,0:T(8,128)(2,1)}, bf16[2,2,2,4,256,128]{5,4,3,2,1,0:T(8,128)(2,1)}, u32[]{:S(2)}, u32[]{:S(2)}) collective-permute-start(bf16[2,2,2,4,256,128]{5,4,3,2,1,0:T(8,128)(2,1)} %get-tuple-element.77), channel_id=1, source_target_pairs={{0,2},{1,3},{2,0},{3,1},{4,6},{5,7},{6,4},{7,5},{8,10},{9,11},{10,... | collective-permute-start | bytes 6291464 | tf_op jit(solution)/shard_map/ppermute | solution.py:674
  74.3 18.3 %all-to-all-start.2 = ((bf16[32,64,128]{2,1,0:T(8,128)(2,1)}), bf16[32,64,128]{2,1,0:T(8,128)(2,1)S(1)}, u32[]{:S(2)}, u32[]{:S(2)}) async-start(bf16[32,64,128]{2,1,0:T(8,128)(2,1)} %get-tuple-element.67), calls=%async_computation.2 | async-start | bytes 1048576 | tf_op jit(solution)/shard_map/all_to_all | solution.py:770
  80.8 19.8 %collective-permute-start.12 = (bf16[2,4,256,128]{3,2,1,0:T(8,128)(2,1)}, bf16[2,4,256,128]{3,2,1,0:T(8,128)(2,1)}, u32[]{:S(2)}, u32[]{:S(2)}) collective-permute-start(bf16[2,4,256,128]{3,2,1,0:T(8,128)(2,1)} %get-tuple-element.78), channel_id=1, source_target_pairs={{0,1},{1,0},{2,3},{3,2},{4,5},{5,4},{6,7},{7,6},{8,9},{9,8},{10,11... | collective-permute-start | bytes 1572872 | tf_op jit(solution)/shard_map/ppermute | solution.py:674
  82.0 18.6 %collective-permute-start.13 = (bf16[2,4,256,128]{3,2,1,0:T(8,128)(2,1)}, bf16[2,4,256,128]{3,2,1,0:T(8,128)(2,1)}, u32[]{:S(2)}, u32[]{:S(2)}) collective-permute-start(bf16[2,4,256,128]{3,2,1,0:T(8,128)(2,1)} %get-tuple-element.79), channel_id=1, source_target_pairs={{0,4},{1,5},{2,6},{3,7},{4,0},{5,1},{6,2},{7,3},{8,12},{9,13},{10,... | collective-permute-start | bytes 1572872 | tf_op jit(solution)/shard_map/ppermute | solution.py:674
  95.6 31.8 %all-to-all-start.3 = ((bf16[32,64,128]{2,1,0:T(8,128)(2,1)}), bf16[32,64,128]{2,1,0:T(8,128)(2,1)S(1)}, u32[]{:S(2)}, u32[]{:S(2)}) async-start(bf16[32,64,128]{2,1,0:T(8,128)(2,1)} %get-tuple-element.90), calls=%async_computation.3 | async-start | bytes 1048576 | tf_op jit(solution)/shard_map/all_to_all | solution.py:793
  99.3 1.3 collective-permute-start.14
  102.0 15.3 %collective-permute-start.15 = (bf16[4,256,128]{2,1,0:T(8,128)(2,1)S(1)}, bf16[4,256,128]{2,1,0:T(8,128)(2,1)S(1)}, u32[]{:S(2)}, u32[]{:S(2)}) collective-permute-start(bf16[4,256,128]{2,1,0:T(8,128)(2,1)S(1)} %get-tuple-element.82), channel_id=1, source_target_pairs={{0,4},{1,5},{2,6},{3,7},{4,0},{5,1},{6,2},{7,3},{8,12},{9,13},{10,... | collective-permute-start | bytes 786440 | tf_op jit(solution)/shard_map/ppermute | solution.py:674
  103.9 13.5 %collective-permute-start.16 = (bf16[4,256,128]{2,1,0:T(8,128)(2,1)S(1)}, bf16[4,256,128]{2,1,0:T(8,128)(2,1)S(1)}, u32[]{:S(2)}, u32[]{:S(2)}) collective-permute-start(bf16[4,256,128]{2,1,0:T(8,128)(2,1)S(1)} %get-tuple-element.83), channel_id=1, source_target_pairs={{0,1},{1,0},{2,3},{3,2},{4,5},{5,4},{6,7},{7,6},{8,9},{9,8},{10,11... | collective-permute-start | bytes 786440 | tf_op jit(solution)/shard_map/ppermute | solution.py:674
  105.3 4.6 %collective-permute-start.17 = (bf16[160,128]{1,0:T(8,128)(2,1)S(1)}, bf16[160,128]{1,0:T(8,128)(2,1)S(1)}, u32[]{:S(2)}, u32[]{:S(2)}) collective-permute-start(bf16[160,128]{1,0:T(8,128)(2,1)S(1)} %get-tuple-element.84.refs_6_), channel_id=1, source_target_pairs={{0,8},{1,9},{2,10},{3,11},{4,12},{5,13},{6,14},{7,15},{8,0},{9,1},... | collective-permute-start | bytes 122888 | tf_op jit(solution)/shard_map/ppermute | solution.py:674
  106.8 10.5 %collective-permute-start.18 = (bf16[160,128]{1,0:T(8,128)(2,1)S(1)}, bf16[160,128]{1,0:T(8,128)(2,1)S(1)}, u32[]{:S(2)}, u32[]{:S(2)}) collective-permute-start(bf16[160,128]{1,0:T(8,128)(2,1)S(1)} %get-tuple-element.84.refs_6_), channel_id=1, source_target_pairs={{0,16},{1,17},{2,18},{3,19},{4,20},{5,21},{6,22},{7,23},{8,24},{9,... | collective-permute-start | bytes 122888 | tf_op jit(solution)/shard_map/ppermute | solution.py:674
  109.3 8.1 %collective-permute-start.19 = (bf16[160,128]{1,0:T(8,128)(2,1)S(1)}, bf16[160,128]{1,0:T(8,128)(2,1)S(1)}, u32[]{:S(2)}, u32[]{:S(2)}) collective-permute-start(bf16[160,128]{1,0:T(8,128)(2,1)S(1)} %get-tuple-element.84.refs_6_), channel_id=1, source_target_pairs={{0,24},{1,25},{2,26},{3,27},{4,28},{5,29},{6,30},{7,31},{8,16},{9,... | collective-permute-start | bytes 122888 | tf_op jit(solution)/shard_map/ppermute | solution.py:674
  119.5 5.2 %collective-permute-start.23 = (bf16[2,256,128]{2,1,0:T(8,128)(2,1)S(1)}, bf16[2,256,128]{2,1,0:T(8,128)(2,1)S(1)}, u32[]{:S(2)}, u32[]{:S(2)}) collective-permute-start(bf16[2,256,128]{2,1,0:T(8,128)(2,1)S(1)} %get-tuple-element.87), channel_id=1, source_target_pairs={{0,8},{1,9},{2,10},{3,11},{4,12},{5,13},{6,14},{7,15},{8,0},{9,1},... | collective-permute-start | bytes 393224 | tf_op jit(solution)/shard_map/ppermute | solution.py:674
  120.5 14.3 %collective-permute-start.20 = (bf16[4,160,128]{2,1,0:T(8,128)(2,1)S(1)}, bf16[4,160,128]{2,1,0:T(8,128)(2,1)S(1)}, u32[]{:S(2)}, u32[]{:S(2)}) collective-permute-start(bf16[4,160,128]{2,1,0:T(8,128)(2,1)S(1)} %get-tuple-element.86.refs_0_), channel_id=1, source_target_pairs={{0,1},{1,0},{2,3},{3,2},{4,5},{5,4},{6,7},{7,6},{8,9},{9,8},{10,11... | collective-permute-start | bytes 491528 | tf_op jit(solution)/shard_map/ppermute | solution.py:674
  122.0 12.9 %collective-permute-start.21 = (bf16[4,160,128]{2,1,0:T(8,128)(2,1)S(1)}, bf16[4,160,128]{2,1,0:T(8,128)(2,1)S(1)}, u32[]{:S(2)}, u32[]{:S(2)}) collective-permute-start(bf16[4,160,128]{2,1,0:T(8,128)(2,1)S(1)} %get-tuple-element.86.refs_0_), channel_id=1, source_target_pairs={{0,4},{1,5},{2,6},{3,7},{4,0},{5,1},{6,2},{7,3},{8,12},{9,13},{10,... | collective-permute-start | bytes 491528 | tf_op jit(solution)/shard_map/ppermute | solution.py:674
  123.5 11.4 %collective-permute-start.22 = (bf16[4,160,128]{2,1,0:T(8,128)(2,1)S(1)}, bf16[4,160,128]{2,1,0:T(8,128)(2,1)S(1)}, u32[]{:S(2)}, u32[]{:S(2)}) collective-permute-start(bf16[4,160,128]{2,1,0:T(8,128)(2,1)S(1)} %get-tuple-element.86.refs_0_), channel_id=1, source_target_pairs={{0,5},{1,4},{2,7},{3,6},{4,1},{5,0},{6,3},{7,2},{8,13},{9,12},{10,... | collective-permute-start | bytes 491528 | tf_op jit(solution)/shard_map/ppermute | solution.py:674
  124.0 10.8 %collective-permute-start.24 = (bf16[2,256,128]{2,1,0:T(8,128)(2,1)}, bf16[2,256,128]{2,1,0:T(8,128)(2,1)S(1)}, u32[]{:S(2)}, u32[]{:S(2)}) collective-permute-start(bf16[2,256,128]{2,1,0:T(8,128)(2,1)} %get-tuple-element.88), channel_id=1, source_target_pairs={{0,16},{1,17},{2,18},{3,19},{4,20},{5,21},{6,22},{7,23},{8,24},{9,... | collective-permute-start | bytes 393224 | tf_op jit(solution)/shard_map/ppermute | solution.py:674
  124.7 10.2 %collective-permute-start.25 = (bf16[2,256,128]{2,1,0:T(8,128)(2,1)}, bf16[2,256,128]{2,1,0:T(8,128)(2,1)S(1)}, u32[]{:S(2)}, u32[]{:S(2)}) collective-permute-start(bf16[2,256,128]{2,1,0:T(8,128)(2,1)} %get-tuple-element.89), channel_id=1, source_target_pairs={{0,24},{1,25},{2,26},{3,27},{4,28},{5,29},{6,30},{7,31},{8,16},{9,... | collective-permute-start | bytes 393224 | tf_op jit(solution)/shard_map/ppermute | solution.py:674
  127.4 9.0 %copy-start.3 = (f32[2,8,2,64,64]{4,3,2,1,0:T(8,128)S(1)}, f32[2,8,2,64,64]{4,3,2,1,0:T(8,128)}, u32[]{:S(2)}) copy-start(f32[2,8,2,64,64]{4,3,2,1,0:T(8,128)} %refs_13_.1) | copy-start | bytes 1572868
  127.4 9.0 %copy-start.4 = (f32[2,8,2,64,64]{4,3,2,1,0:T(8,128)S(1)}, f32[2,8,2,64,64]{4,3,2,1,0:T(8,128)}, u32[]{:S(2)}) copy-start(f32[2,8,2,64,64]{4,3,2,1,0:T(8,128)} %refs_14_.1) | copy-start | bytes 1572868
  127.4 9.0 %copy-start.5 = (f32[2,8,2,64,64]{4,3,2,1,0:T(8,128)S(1)}, f32[2,8,2,64,64]{4,3,2,1,0:T(8,128)}, u32[]{:S(2)}) copy-start(f32[2,8,2,64,64]{4,3,2,1,0:T(8,128)} %refs_15_.1) | copy-start | bytes 1572868
  127.5 9.0 %copy-start.6 = (f32[32,1024]{1,0:T(8,128)S(1)}, f32[32,1024]{1,0:T(8,128)}, u32[]{:S(2)}) copy-start(f32[32,1024]{1,0:T(8,128)} %refs_6_.1) | copy-start | bytes 393220
  127.5 9.0 %copy-start.7 = (f32[32,1024]{1,0:T(8,128)S(1)}, f32[32,1024]{1,0:T(8,128)}, u32[]{:S(2)}) copy-start(f32[32,1024]{1,0:T(8,128)} %refs_5_.3) | copy-start | bytes 393220
  127.5 9.0 %copy-start.11 = (f32[32,1024]{1,0:T(8,128)S(1)}, f32[32,1024]{1,0:T(8,128)}, u32[]{:S(2)}) copy-start(f32[32,1024]{1,0:T(8,128)} %refs_7_.2) | copy-start | bytes 393220
  127.5 9.0 %copy-start.12 = (f32[32,1024]{1,0:T(8,128)S(1)}, f32[32,1024]{1,0:T(8,128)}, u32[]{:S(2)}) copy-start(f32[32,1024]{1,0:T(8,128)} %refs_8_.1) | copy-start | bytes 393220
  127.5 9.0 %copy-start.13 = (f32[32,1024]{1,0:T(8,128)S(1)}, f32[32,1024]{1,0:T(8,128)}, u32[]{:S(2)}) copy-start(f32[32,1024]{1,0:T(8,128)} %refs_9_.1) | copy-start | bytes 393220
  127.5 9.0 %copy-start.14 = (f32[32,1024]{1,0:T(8,128)S(1)}, f32[32,1024]{1,0:T(8,128)}, u32[]{:S(2)}) copy-start(f32[32,1024]{1,0:T(8,128)} %refs_10_.1) | copy-start | bytes 393220
  127.5 9.0 %copy-start.15 = (f32[13,512]{1,0:T(8,128)S(1)}, f32[13,512]{1,0:T(8,128)}, u32[]{:S(2)}) copy-start(f32[13,512]{1,0:T(8,128)} %refs_17_.1) | copy-start | bytes 79876
  127.5 9.0 %copy-start.16 = (f32[13,512]{1,0:T(8,128)S(1)}, f32[13,512]{1,0:T(8,128)}, u32[]{:S(2)}) copy-start(f32[13,512]{1,0:T(8,128)} %refs_18_.1) | copy-start | bytes 79876
  135.0 1.5 %collective-permute-start.26 = (bf16[4,160,128]{2,1,0:T(8,128)(2,1)S(1)}, bf16[4,160,128]{2,1,0:T(8,128)(2,1)S(1)}, u32[]{:S(2)}, u32[]{:S(2)}) collective-permute-start(bf16[4,160,128]{2,1,0:T(8,128)(2,1)S(1)} %get-tuple-element.95.refs_11_), channel_id=1, source_target_pairs={{0,2},{1,3},{2,0},{3,1},{4,6},{5,7},{6,4},{7,5},{8,10},{9,11},{10,... | collective-permute-start | bytes 491528 | tf_op jit(solution)/shard_map/ppermute | solution.py:674
  (4 other events, 11.5 us)

commit v7 on v6

--- a/solution.py
+++ b/solution.py
@@ -449,7 +449,7 @@
             hidden = dot(normed[rows, :], w_in[h, :, lanes]) + bias_ref[i : i + 1, :]
             value, slope = gelu_pair(hidden.astype(BF16))
             active[rows, flat] = value.astype(BF16)
-            back = (dot(cotangent_ref[rows, :], w_out[h, :, lanes]) * slope).astype(BF16)
+            back = dot(cotangent_ref[rows, :], w_out[h, :, lanes]).astype(BF16) * slope
             grad_hidden[rows, flat] = back
             bias_grads[i] = bias_grads[i] + jnp.sum(back.astype(F32), axis=0, keepdims=True)
         back = dot_nt(grad_hidden[rows, :columns], w_in[0])
@@ -492,8 +492,11 @@
 
 def output_kernel(near, place_ref, *refs):
     count = 8 if near else 1
-    totals, actives, pieces = refs[:OUT_BLOCKS], refs[OUT_BLOCKS : 2 * OUT_BLOCKS], refs[2 * OUT_BLOCKS :][:count]
-    outputs, w_out, sem = refs[2 * OUT_BLOCKS + count], *refs[2 * OUT_BLOCKS + count + 1 :]
+    totals, actives, refs = refs[:OUT_BLOCKS], refs[OUT_BLOCKS : 2 * OUT_BLOCKS], refs[2 * OUT_BLOCKS :]
+    ahead = (len(refs) - count - 3) // 2
+    sources, pieces, outputs, sinks, (w_out, sem) = (
+        refs[:ahead], refs[ahead : ahead + count], refs[ahead + count], refs[ahead + count + 1 : -2], refs[-2:]
+    )
     load_weights(near, place_ref, pieces, 1, w_out, sem).wait()
     halves, _, columns = w_out.shape
     size = totals[0].shape[0]
@@ -502,6 +505,9 @@
         for h in range(halves):
             value = value + dot_nt(active[:, h * columns : (h + 1) * columns], w_out[h])
         outputs[i * size : (i + 1) * size, :] = value.astype(BF16)
+    outputs.flush()
+    for source, sink in zip(sources, sinks, strict=True):
+        sink[...] = source[...]
 
 
 def leave_kernel(groups, got_ref, tokens_ref, middle_ref, vectors_ref, table_ref, out_ref):
@@ -757,9 +763,12 @@
 
     step = local // OUT_BLOCKS
     parts = [slice(r, r + step) for r in range(0, local, step)]
-    (output,) = call(
-        functools.partial(output_kernel, near), [Far((local, width), BF16)],
-        *[Far(total, rows) for rows in parts], *[Far(gelus, rows) for rows in parts],
+    kept_forward = [high, high_t, mats, hat, modal, inner, active]
+    ahead = kept_forward[:3] if near else []
+    output, *ahead = call(
+        functools.partial(output_kernel, near),
+        [Far((local, width), BF16)] + [(a.shape, a.dtype) for a in ahead],
+        *[Far(total, rows) for rows in parts], *[Far(gelus, rows) for rows in parts], *[Far(a) for a in ahead],
         scalars=[me[None]], raw=pieces, cost=COST, vmem=24,
         scratch=[
             pltpu.VMEM((tp_count, model, shard_columns), BF16),
@@ -767,13 +776,14 @@
         ],
     )
 
+    kept_forward = ahead + [Far(a) for a in kept_forward[len(ahead) :]]
     got = exchange(sent)
     small_rows = -(-(2 * block + 8 + 8 * (groups // 2)) // 16) * 16
     place = ((me >> 1) & 1 if near else jnp.int32(0))[None]
     sent, small, given, output = call(
         functools.partial(unmix_kernel, modes, block),
         [Far(chunk, BF16), ((small_rows, lanes), BF16), ((small_rows, lanes), BF16)],
-        got, Far(high), Far(high_t), Far(mats), own_ones, Far(hat), Far(modal), Far(inner), Far(active), mlp_small,
+        got, *kept_forward[:3], own_ones, *kept_forward[3:], mlp_small,
         scalars=[place], cost=COST, vmem=20 if near else 48, carry=[output],
     )
     if near:

time: 142 us -> 141 us (level)
  no operation moved by 1% of the time
where the time goes in v7:
time: 141 us; the launch traced here: 140 us
  starting transfers between devices  48.2 us (34%)
  Pallas kernels  47.6 us (34%)
  waiting for transfers between devices  37.8 us (27%)
  other arithmetic  2.49 us (2%)
  local copies, waits for them, and re-layouts  2.36 us (2%)
  between operations  1.44 us (1%)
    pallas_call x11, Pallas kernels, call(): pl.pallas_call(inner, out_shape=[(pltpu.HBM if f else pltpu.VMEM)(o.shape...  47.6 us
    ppermute x27, waiting for transfers between devices, permute(): return lax.ppermute(values, AXES, [(d, d ^ mask) for d in range(devices)])  33.6 us
    ppermute x27, starting transfers between devices, permute(): return lax.ppermute(values, AXES, [(d, d ^ mask) for d in range(devices)])  31.8 us
    all_to_all x4, starting transfers between devices, on_device(): got = exchange(sent)  16.4 us
    all_to_all x4, waiting for transfers between devices, on_device(): got = exchange(sent)  4.24 us
  transfers between devices with their start and end apart: 31, of which 12 were waited for; matrix products, arithmetic and copies ran while one was open for 3% of the time, Pallas kernels for 17%

profile of v7, /device:TPU:0, one launch (start us, length us, event | category | flops | bytes accessed | tf_op | source)
XLA Modules:
  0.0 139.9 jit_solution(5544872143504035021)
XLA Ops:
  0.7 1.0 convert_bitcast_fusion
  1.7 4.1 %collective-permute-start.2 = (bf16[2,32,1024]{2,1,0:T(8,128)(2,1)S(1)}, bf16[2,32,1024]{2,1,0:T(8,128)(2,1)S(1)}, u32[]{:S(2)}, u32[]{:S(2)}) collective-permute-start(bf16[2,32,1024]{2,1,0:T(8,128)(2,1)S(1)} %get-tuple-element.125), channel_id=1, source_target_pairs={{0,16},{1,17},{2,18},{3,19},{4,20},{5,21},{6,22},{7,23},{8,24},{9,... | collective-permute-start | bytes 393224 | tf_op jit(solution)/shard_map/ppermute | solution.py:680
  5.8 1.3 collective-permute-start.3
  7.4 3.0 %shard_map.324 = bf16[32,64,128]{2,1,0:T(8,128)(2,1)} custom-call(bf16[1024,512]{1,0:T(8,128)(2,1)} %bitcast.39, bf16[256,512]{1,0:T(8,128)(2,1)} %constant.61.clone.refs_1_), custom_call_target="tpu_custom_call" | custom-call | flops 268435456 | bytes 1835008 | tf_op jit(solution)/shard_map/pallas_call | solution.py:634
  10.4 5.2 %all-to-all-start = ((bf16[32,64,128]{2,1,0:T(8,128)(2,1)}), bf16[32,64,128]{2,1,0:T(8,128)(2,1)S(1)}, u32[]{:S(2)}, u32[]{:S(2)}) async-start(bf16[32,64,128]{2,1,0:T(8,128)(2,1)} %shard_map.324), calls=%async_computation | async-start | bytes 1048576 | tf_op jit(solution)/shard_map/all_to_all | solution.py:713
  15.6 1.0 dynamic-slice_convert_fusion
  17.0 0.9 dynamic-slice_bitcast_fusion.refs_7_.refs_5_
  18.0 1.8 %collective-permute-start.4 = (bf16[2,2,32,1024]{3,2,1,0:T(8,128)(2,1)S(1)}, bf16[2,2,32,1024]{3,2,1,0:T(8,128)(2,1)S(1)}, u32[]{:S(2)}, u32[]{:S(2)}) collective-permute-start(bf16[2,2,32,1024]{3,2,1,0:T(8,128)(2,1)S(1)} %get-tuple-element.121), channel_id=1, source_target_pairs={{0,4},{1,5},{2,6},{3,7},{4,0},{5,1},{6,2},{7,3},{8,12},{9,13},{10,... | collective-permute-start | bytes 786440 | tf_op jit(solution)/shard_map/ppermute | solution.py:680
  19.9 1.5 %collective-permute-start.1 = (bf16[2,2,32,1024]{3,2,1,0:T(8,128)(2,1)S(1)}, bf16[2,2,32,1024]{3,2,1,0:T(8,128)(2,1)}, u32[]{:S(2)}, u32[]{:S(2)}) collective-permute-start(bf16[2,2,32,1024]{3,2,1,0:T(8,128)(2,1)S(1)} %get-tuple-element.123), channel_id=1, source_target_pairs={{0,1},{1,0},{2,3},{3,2},{4,5},{5,4},{6,7},{7,6},{8,9},{9,8},{10,11... | collective-permute-start | bytes 786440 | tf_op jit(solution)/shard_map/ppermute | solution.py:680
  21.8 8.2 %collective-permute-done.4 = bf16[2,2,32,1024]{3,2,1,0:T(8,128)(2,1)S(1)} collective-permute-done((bf16[2,2,32,1024]{3,2,1,0:T(8,128)(2,1)S(1)}, bf16[2,2,32,1024]{3,2,1,0:T(8,128)(2,1)S(1)}, u32[]{:S(2)}, u32[]{:S(2)}) %collective-permute-start.4) | collective-permute-done | bytes 262176 | tf_op jit(solution)/shard_map/ppermute | solution.py:680
  30.1 0.4 collective-permute-done.1
  30.5 1.0 pad_maximum_fusion.refs_8_
  31.5 2.3 %shard_map.325 = (bf16[32,64,128]{2,1,0:T(8,128)(2,1)}, f32[128,512]{1,0:T(8,128)}, bf16[256,256]{1,0:T(8,128)(2,1)}, f32[256,256]{1,0:T(8,128)}, bf16[256,256]{...) custom-call(bf16[32,64,128]{2,1,0:T(8,128)(2,1)S(1)} %all-to-all-don, ...), custom_call_target="tpu_custom_call", output_to_operand_aliasing={{5}: (8, {}), {6}: (9, {})} | custom-call | bytes 2364416 | tf_op jit(solution)/shard_map/pallas_call | solution.py:634
  33.9 1.2 collective-permute-start.6
  35.0 1.1 collective-permute-start.5
  36.1 4.3 %all-to-all-start.1 = ((bf16[32,64,128]{2,1,0:T(8,128)(2,1)}), bf16[32,64,128]{2,1,0:T(8,128)(2,1)}, u32[]{:S(2)}, u32[]{:S(2)}) async-start(bf16[32,64,128]{2,1,0:T(8,128)(2,1)} %get-tuple-element.68), calls=%async_computation.1 | async-start | bytes 1048576 | tf_op jit(solution)/shard_map/all_to_all | solution.py:730
  41.1 11.0 %collective-permute-done.6.refs_11_.refs_15_ = bf16[2,2,2,32,1024]{4,3,2,1,0:T(8,128)(2,1)S(1)} collective-permute-done((bf16[2,2,2,32,1024]{4,3,2,1,0:T(8,128)(2,1)S(1)}, bf16[2,2,2,32,1024]{4,3,2,1,0:T(8,128)(2,1)S(1)}, u32[]{:S(2)}, u32[]{:S(2)}) %collective-permute-start.6) | collective-permute-done | bytes 524320 | tf_op jit(solution)/shard_map/ppermute | solution.py:680
  52.6 2.7 %all-to-all-done.1.refs_1_ = bf16[32,64,128]{2,1,0:T(8,128)(2,1)} async-done(((bf16[32,64,128]{2,1,0:T(8,128)(2,1)}), bf16[32,64,128]{2,1,0:T(8,128)(2,1)}, u32[]{:S(2)}, u32[]{:S(2)}) %all-to-all-start.1) | async-done | bytes 524320 | tf_op jit(solution)/shard_map/all_to_all | solution.py:730
  55.3 17.5 %shard_map.326 = (bf16[1024,2048]{1,0:T(8,128)(2,1)}, f32[1024,512]{1,0:T(8,128)}, bf16[1024,512]{1,0:T(8,128)(2,1)}, bf16[32,64,128]{2,1,0:T(8,128)(2,1)}, f32[...) custom-call(s32[1]{0:T(128)} %bitcast.1.refs_0_, ...), custom_call_target="tpu_custom_call" | custom-call | flops 13421772800 | bytes 19449856 | tf_op jit(solution)/shard_map/pallas_call | solution.py:634
  72.8 1.1 collective-permute-start.11
  74.0 3.3 %all-to-all-start.2 = ((bf16[32,64,128]{2,1,0:T(8,128)(2,1)}), bf16[32,64,128]{2,1,0:T(8,128)(2,1)S(1)}, u32[]{:S(2)}, u32[]{:S(2)}) async-start(bf16[32,64,128]{2,1,0:T(8,128)(2,1)} %get-tuple-element.71), calls=%async_computation.2 | async-start | bytes 1048576 | tf_op jit(solution)/shard_map/all_to_all | solution.py:780
  77.3 0.8 collective-permute-done.11.refs_1_.refs_5_.refs_10_
  78.1 2.3 %shard_map.329 = (bf16[2,4,256,128]{3,2,1,0:T(8,128)(2,1)}, bf16[2,4,256,128]{3,2,1,0:T(8,128)(2,1)}) custom-call(bf16[2,2,2,4,256,128]{5,4,3,2,1,0:T(8,128)(2,1)S(1)} %get-tuple-element.84.refs_0_.refs_1_, bf16[2,2,2,4,256,128]{5,4,3,2,1,0:T(8,128)(2,1)} %collective-permute-done.11.refs_1_.refs_5_.refs_10_), custom_call_target="tpu_custom_call" | custom-call | tf_op jit(solution)/shard_map/pallas_call | solution.py:634
  80.5 1.2 collective-permute-start.12
  81.6 1.3 collective-permute-start.13
  82.9 7.8 %shard_map.327 = (bf16[1024,512]{1,0:T(8,128)(2,1)}, bf16[128,512]{1,0:T(8,128)(2,1)S(1)}, bf16[512,128]{1,0:T(8,128)(2,1)S(1)}, bf16[2,256,256]{2,1,0:T(8,128)(2,1)S(1)}) custom-call(s32[1]{0:T(128)} %bitcast.1.refs_0_, f32[1024,512]{1,0:T(8,128)} %get-tuple-element.72.refs_1_.refs_2_.refs_3_.refs_4_, ...), custom_call_target="tpu_custom_call" | custom-call | bytes 62914560 | tf_op jit(solution)/shard_map/pallas_call | solution.py:634
  90.7 1.6 %all-to-all-done.2.refs_1_ = bf16[32,64,128]{2,1,0:T(8,128)(2,1)S(1)} async-done(((bf16[32,64,128]{2,1,0:T(8,128)(2,1)}), bf16[32,64,128]{2,1,0:T(8,128)(2,1)S(1)}, u32[]{:S(2)}, u32[]{:S(2)}) %all-to-all-start.2) | async-done | bytes 524320 | tf_op jit(solution)/shard_map/all_to_all | solution.py:780
  92.3 2.6 %shard_map.328 = (bf16[32,64,128]{2,1,0:T(8,128)(2,1)}, bf16[160,128]{1,0:T(8,128)(2,1)S(1)}, bf16[160,128]{1,0:T(8,128)(2,1)S(1)}, bf16[1024,512]{1,0:T(8,128)(2,1)}) custom-call(s32[1]{0:T(128)} %bitcast.refs_0_, bf16[32,64,128]{2,1,0:T(8,128)(2,1)S(1)} %all-to-all-done.2.refs_1_, ...), custom_call_target="tpu_custom_call", output_to_operand_aliasing={{3}: (11, {})} | custom-call | bytes 62914560 | tf_op jit(solution)/shard_map/pallas_call | solution.py:634
  94.9 3.6 %all-to-all-start.3 = ((bf16[32,64,128]{2,1,0:T(8,128)(2,1)}), bf16[32,64,128]{2,1,0:T(8,128)(2,1)S(1)}, u32[]{:S(2)}, u32[]{:S(2)}) async-start(bf16[32,64,128]{2,1,0:T(8,128)(2,1)} %get-tuple-element.98), calls=%async_computation.3 | async-start | bytes 1048576 | tf_op jit(solution)/shard_map/all_to_all | solution.py:803
  98.8 1.0 collective-permute-done.14.refs_4_
  99.8 1.5 %shard_map.330 = (bf16[160,128]{1,0:T(8,128)(2,1)S(1)}, bf16[4,256,128]{2,1,0:T(8,128)(2,1)S(1)}, bf16[4,256,128]{2,1,0:T(8,128)(2,1)S(1)}) custom-call(bf16[2,2,2,4,256,128]{5,4,3,2,1,0:T(8,128)(2,1)S(1)} %get-tuple-element.84.refs_0_.refs_1_, bf16[2,4,256,128]{3,2,1,0:T(8,128)(2,1)} %collective-permute-done.12.refs_1_.refs_2_, ...), custom_call_target="tpu_custom_call" | custom-call | tf_op jit(solution)/shard_map/pallas_call | solution.py:634
  101.3 1.8 %collective-permute-start.15 = (bf16[4,256,128]{2,1,0:T(8,128)(2,1)S(1)}, bf16[4,256,128]{2,1,0:T(8,128)(2,1)S(1)}, u32[]{:S(2)}, u32[]{:S(2)}) collective-permute-start(bf16[4,256,128]{2,1,0:T(8,128)(2,1)S(1)} %get-tuple-element.90), channel_id=1, source_target_pairs={{0,4},{1,5},{2,6},{3,7},{4,0},{5,1},{6,2},{7,3},{8,12},{9,13},{10,... | collective-permute-start | bytes 786440 | tf_op jit(solution)/shard_map/ppermute | solution.py:680
  103.1 1.5 %collective-permute-start.16 = (bf16[4,256,128]{2,1,0:T(8,128)(2,1)S(1)}, bf16[4,256,128]{2,1,0:T(8,128)(2,1)S(1)}, u32[]{:S(2)}, u32[]{:S(2)}) collective-permute-start(bf16[4,256,128]{2,1,0:T(8,128)(2,1)S(1)} %get-tuple-element.91), channel_id=1, source_target_pairs={{0,1},{1,0},{2,3},{3,2},{4,5},{5,4},{6,7},{7,6},{8,9},{9,8},{10,11... | collective-permute-start | bytes 786440 | tf_op jit(solution)/shard_map/ppermute | solution.py:680
  104.6 1.5 %collective-permute-start.17 = (bf16[160,128]{1,0:T(8,128)(2,1)S(1)}, bf16[160,128]{1,0:T(8,128)(2,1)S(1)}, u32[]{:S(2)}, u32[]{:S(2)}) collective-permute-start(bf16[160,128]{1,0:T(8,128)(2,1)S(1)} %get-tuple-element.92.refs_6_), channel_id=1, source_target_pairs={{0,8},{1,9},{2,10},{3,11},{4,12},{5,13},{6,14},{7,15},{8,0},{9,1},... | collective-permute-start | bytes 122888 | tf_op jit(solution)/shard_map/ppermute | solution.py:680
  106.1 2.5 %collective-permute-start.18 = (bf16[160,128]{1,0:T(8,128)(2,1)S(1)}, bf16[160,128]{1,0:T(8,128)(2,1)S(1)}, u32[]{:S(2)}, u32[]{:S(2)}) collective-permute-start(bf16[160,128]{1,0:T(8,128)(2,1)S(1)} %get-tuple-element.92.refs_6_), channel_id=1, source_target_pairs={{0,16},{1,17},{2,18},{3,19},{4,20},{5,21},{6,22},{7,23},{8,24},{9,... | collective-permute-start | bytes 122888 | tf_op jit(solution)/shard_map/ppermute | solution.py:680
  108.5 0.5 collective-permute-start.19
  109.2 7.4 %collective-permute-done.18.refs_8_ = bf16[160,128]{1,0:T(8,128)(2,1)S(1)} collective-permute-done((bf16[160,128]{1,0:T(8,128)(2,1)S(1)}, bf16[160,128]{1,0:T(8,128)(2,1)S(1)}, u32[]{:S(2)}, u32[]{:S(2)}) %collective-permute-start.18) | collective-permute-done | bytes 40992 | tf_op jit(solution)/shard_map/ppermute | solution.py:680
  116.6 2.1 %shard_map.331 = (bf16[4,160,128]{2,1,0:T(8,128)(2,1)S(1)}, f32[2,256,128]{2,1,0:T(8,128)S(1)}, bf16[2,256,128]{2,1,0:T(8,128)(2,1)S(1)}, bf16[2,256,128]{2,1,0:T(8,128)(2,1)}, bf16[2,256,128]{2,1,0:T(8,128)(2,1)}) custom-call(s32[1]{0:T(128)} %bitcast.1.refs_0_, bf16[2,2,2,4,256,128]{5,4,3,2,1,0:T(8,128)(2,1)S(1)} %get-tuple-element.84.refs_0_.refs_1_, ...), custom_call_target="tpu_custom_call" | custom-call | tf_op jit(solution)/shard_map/pallas_call | solution.py:634
  118.7 1.1 collective-permute-start.23
  119.8 1.5 %collective-permute-start.20 = (bf16[4,160,128]{2,1,0:T(8,128)(2,1)S(1)}, bf16[4,160,128]{2,1,0:T(8,128)(2,1)S(1)}, u32[]{:S(2)}, u32[]{:S(2)}) collective-permute-start(bf16[4,160,128]{2,1,0:T(8,128)(2,1)S(1)} %get-tuple-element.94.refs_0_), channel_id=1, source_target_pairs={{0,1},{1,0},{2,3},{3,2},{4,5},{5,4},{6,7},{7,6},{8,9},{9,8},{10,11... | collective-permute-start | bytes 491528 | tf_op jit(solution)/shard_map/ppermute | solution.py:680
  121.3 1.5 %collective-permute-start.21 = (bf16[4,160,128]{2,1,0:T(8,128)(2,1)S(1)}, bf16[4,160,128]{2,1,0:T(8,128)(2,1)S(1)}, u32[]{:S(2)}, u32[]{:S(2)}) collective-permute-start(bf16[4,160,128]{2,1,0:T(8,128)(2,1)S(1)} %get-tuple-element.94.refs_0_), channel_id=1, source_target_pairs={{0,4},{1,5},{2,6},{3,7},{4,0},{5,1},{6,2},{7,3},{8,12},{9,13},{10,... | collective-permute-start | bytes 491528 | tf_op jit(solution)/shard_map/ppermute | solution.py:680
  122.8 0.5 collective-permute-start.22
  123.3 0.7 collective-permute-start.24
  123.9 2.7 %collective-permute-start.25 = (bf16[2,256,128]{2,1,0:T(8,128)(2,1)}, bf16[2,256,128]{2,1,0:T(8,128)(2,1)S(1)}, u32[]{:S(2)}, u32[]{:S(2)}) collective-permute-start(bf16[2,256,128]{2,1,0:T(8,128)(2,1)} %get-tuple-element.97), channel_id=1, source_target_pairs={{0,24},{1,25},{2,26},{3,27},{4,28},{5,29},{6,30},{7,31},{8,16},{9,... | collective-permute-start | bytes 393224 | tf_op jit(solution)/shard_map/ppermute | solution.py:680
  126.8 4.5 %shard_map.332.refs_7_ = bf16[1024,512]{1,0:T(8,128)(2,1)} custom-call(bf16[32,64,128]{2,1,0:T(8,128)(2,1)S(1)} %all-to-all-done.3.refs_0_, bf16[1024,512]{1,0:T(8,128)(2,1)} %bitcast.41, bf16[1024,512]{1,0:T(8,128)(2,1)} %get-tuple-element.99.refs_2_, f32[13,512]{1,0:T(8,128)S(1)} %copy-done.10, bf16[512,256]{1,0:T(8,128)(2,1)} %constant.62.clone.refs_4_), custom_call_target="tpu_custom_call" | custom-call | bytes 62914560 | tf_op jit(solution)/shard_map/pallas_call | solution.py:634
  131.3 2.8 %collective-permute-done.24.refs_5_ = bf16[2,256,128]{2,1,0:T(8,128)(2,1)S(1)} collective-permute-done((bf16[2,256,128]{2,1,0:T(8,128)(2,1)}, bf16[2,256,128]{2,1,0:T(8,128)(2,1)S(1)}, u32[]{:S(2)}, u32[]{:S(2)}) %collective-permute-start.24) | collective-permute-done | bytes 131104 | tf_op jit(solution)/shard_map/ppermute | solution.py:680
  134.3 1.4 collective-permute-done.26.refs_12_
  135.8 3.9 %shard_map.334 = (f32[32,1024]{1,0:T(8,128)}, f32[32,1024]{1,0:T(8,128)}, f32[32,1024]{1,0:T(8,128)}, f32[32,1024]{1,0:T(8,128)}, f32[32,1024]{1,0:T(8,128)}, /*...) custom-call(s32[1]{0:T(128)} %bitcast.refs_0_, ...), custom_call_target="tpu_custom_call", output_to_operand_aliasing={{14}: (19, {})} | custom-call | tf_op jit(solution)/shard_map/pallas_call | solution.py:634
  (89 shorter events, 3.1 us)
Async XLA Ops:
  0.6 16.0 %copy-start.10 = (f32[13,512]{1,0:T(8,128)S(1)}, f32[13,512]{1,0:T(8,128)}, u32[]{:S(2)}) copy-start(f32[13,512]{1,0:T(8,128)} %refs_16_.1) | copy-start | bytes 79876
  1.7 16.3 %collective-permute-start.2 = (bf16[2,32,1024]{2,1,0:T(8,128)(2,1)S(1)}, bf16[2,32,1024]{2,1,0:T(8,128)(2,1)S(1)}, u32[]{:S(2)}, u32[]{:S(2)}) collective-permute-start(bf16[2,32,1024]{2,1,0:T(8,128)(2,1)S(1)} %get-tuple-element.125), channel_id=1, source_target_pairs={{0,16},{1,17},{2,18},{3,19},{4,20},{5,21},{6,22},{7,23},{8,24},{9,... | collective-permute-start | bytes 393224 | tf_op jit(solution)/shard_map/ppermute | solution.py:680
  5.8 12.2 %collective-permute-start.3 = (bf16[2,32,1024]{2,1,0:T(8,128)(2,1)S(1)}, bf16[2,32,1024]{2,1,0:T(8,128)(2,1)S(1)}, u32[]{:S(2)}, u32[]{:S(2)}) collective-permute-start(bf16[2,32,1024]{2,1,0:T(8,128)(2,1)S(1)} %get-tuple-element.125), channel_id=1, source_target_pairs={{0,24},{1,25},{2,26},{3,27},{4,28},{5,29},{6,30},{7,31},{8,16},{9,... | collective-permute-start | bytes 393224 | tf_op jit(solution)/shard_map/ppermute | solution.py:680
  7.1 12.7 %collective-permute-start = (bf16[2,32,1024]{2,1,0:T(8,128)(2,1)S(1)}, bf16[2,32,1024]{2,1,0:T(8,128)(2,1)S(1)}, u32[]{:S(2)}, u32[]{:S(2)}) collective-permute-start(bf16[2,32,1024]{2,1,0:T(8,128)(2,1)S(1)} %get-tuple-element.125), channel_id=1, source_target_pairs={{0,8},{1,9},{2,10},{3,11},{4,12},{5,13},{6,14},{7,15},{8,0},{9,1},... | collective-permute-start | bytes 393224 | tf_op jit(solution)/shard_map/ppermute | solution.py:680
  10.4 21.1 %all-to-all-start = ((bf16[32,64,128]{2,1,0:T(8,128)(2,1)}), bf16[32,64,128]{2,1,0:T(8,128)(2,1)S(1)}, u32[]{:S(2)}, u32[]{:S(2)}) async-start(bf16[32,64,128]{2,1,0:T(8,128)(2,1)} %shard_map.324), calls=%async_computation | async-start | bytes 1048576 | tf_op jit(solution)/shard_map/all_to_all | solution.py:713
  18.0 13.5 %copy-start.6 = (bf16[128,512]{1,0:T(8,128)(2,1)S(1)}, bf16[128,512]{1,0:T(8,128)(2,1)}, u32[]{:S(2)}) copy-start(bf16[128,512]{1,0:T(8,128)(2,1)} %constant.65.clone.refs_1_.refs_9_) | copy-start | bytes 393220
  18.0 13.5 %copy-start.7 = (bf16[512,128]{1,0:T(8,128)(2,1)S(1)}, bf16[512,128]{1,0:T(8,128)(2,1)}, u32[]{:S(2)}) copy-start(bf16[512,128]{1,0:T(8,128)(2,1)} %constant.66.clone.refs_2_.refs_10_) | copy-start | bytes 393220
  18.0 12.0 %collective-permute-start.4 = (bf16[2,2,32,1024]{3,2,1,0:T(8,128)(2,1)S(1)}, bf16[2,2,32,1024]{3,2,1,0:T(8,128)(2,1)S(1)}, u32[]{:S(2)}, u32[]{:S(2)}) collective-permute-start(bf16[2,2,32,1024]{3,2,1,0:T(8,128)(2,1)S(1)} %get-tuple-element.121), channel_id=1, source_target_pairs={{0,4},{1,5},{2,6},{3,7},{4,0},{5,1},{6,2},{7,3},{8,12},{9,13},{10,... | collective-permute-start | bytes 786440 | tf_op jit(solution)/shard_map/ppermute | solution.py:680
  19.9 10.6 %collective-permute-start.1 = (bf16[2,2,32,1024]{3,2,1,0:T(8,128)(2,1)S(1)}, bf16[2,2,32,1024]{3,2,1,0:T(8,128)(2,1)}, u32[]{:S(2)}, u32[]{:S(2)}) collective-permute-start(bf16[2,2,32,1024]{3,2,1,0:T(8,128)(2,1)S(1)} %get-tuple-element.123), channel_id=1, source_target_pairs={{0,1},{1,0},{2,3},{3,2},{4,5},{5,4},{6,7},{7,6},{8,9},{9,8},{10,11... | collective-permute-start | bytes 786440 | tf_op jit(solution)/shard_map/ppermute | solution.py:680
  21.8 12.0 %copy-start.2 = (bf16[2,256,256]{2,1,0:T(8,128)(2,1)}, bf16[2,256,256]{2,1,0:T(8,128)(2,1)S(1)}, u32[]{:S(2)}) copy-start(bf16[2,256,256]{2,1,0:T(8,128)(2,1)S(1)} %maximum_maximum_fusion.refs_3_.refs_11_) | copy-start | bytes 786436
  33.8 21.5 %copy-start = (bf16[2,2,2,32,1024]{4,3,2,1,0:T(8,128)(2,1)}, bf16[2,2,2,32,1024]{4,3,2,1,0:T(8,128)(2,1)S(1)}, u32[]{:S(2)}) copy-start(bf16[2,2,2,32,1024]{4,3,2,1,0:T(8,128)(2,1)S(1)} %get-tuple-element.70.refs_9_.refs_13_) | copy-start | bytes 1572868
  33.9 21.5 %copy-start.1 = (bf16[2,2,2,32,1024]{4,3,2,1,0:T(8,128)(2,1)}, bf16[2,2,2,32,1024]{4,3,2,1,0:T(8,128)(2,1)S(1)}, u32[]{:S(2)}) copy-start(bf16[2,2,2,32,1024]{4,3,2,1,0:T(8,128)(2,1)S(1)} %get-tuple-element.69.refs_8_.refs_12_) | copy-start | bytes 1572868
  33.9 18.2 %collective-permute-start.6 = (bf16[2,2,2,32,1024]{4,3,2,1,0:T(8,128)(2,1)S(1)}, bf16[2,2,2,32,1024]{4,3,2,1,0:T(8,128)(2,1)S(1)}, u32[]{:S(2)}, u32[]{:S(2)}) collective-permute-start(bf16[2,2,2,32,1024]{4,3,2,1,0:T(8,128)(2,1)S(1)} %get-tuple-element.70.refs_9_.refs_13_), channel_id=1, source_target_pairs={{0,1},{1,0},{2,3},{3,2},{4,5},{5,4},{6,7},{7,6},{8,9},{9,8},{10,11... | collective-permute-start | bytes 1572872 | tf_op jit(solution)/shard_map/ppermute | solution.py:680
  35.0 17.3 %collective-permute-start.5 = (bf16[2,2,2,32,1024]{4,3,2,1,0:T(8,128)(2,1)S(1)}, bf16[2,2,2,32,1024]{4,3,2,1,0:T(8,128)(2,1)S(1)}, u32[]{:S(2)}, u32[]{:S(2)}) collective-permute-start(bf16[2,2,2,32,1024]{4,3,2,1,0:T(8,128)(2,1)S(1)} %get-tuple-element.69.refs_8_.refs_12_), channel_id=1, source_target_pairs={{0,4},{1,5},{2,6},{3,7},{4,0},{5,1},{6,2},{7,3},{8,12},{9,13},{10,... | collective-permute-start | bytes 1572872 | tf_op jit(solution)/shard_map/ppermute | solution.py:680
  36.1 19.1 %all-to-all-start.1 = ((bf16[32,64,128]{2,1,0:T(8,128)(2,1)}), bf16[32,64,128]{2,1,0:T(8,128)(2,1)}, u32[]{:S(2)}, u32[]{:S(2)}) async-start(bf16[32,64,128]{2,1,0:T(8,128)(2,1)} %get-tuple-element.68), calls=%async_computation.1 | async-start | bytes 1048576 | tf_op jit(solution)/shard_map/all_to_all | solution.py:730
  40.5 12.1 %collective-permute-start.7 = (bf16[2,2,2,32,1024]{4,3,2,1,0:T(8,128)(2,1)S(1)}, bf16[2,2,2,32,1024]{4,3,2,1,0:T(8,128)(2,1)S(1)}, u32[]{:S(2)}, u32[]{:S(2)}) collective-permute-start(bf16[2,2,2,32,1024]{4,3,2,1,0:T(8,128)(2,1)S(1)} %get-tuple-element.69.refs_8_.refs_12_), channel_id=1, source_target_pairs={{0,2},{1,3},{2,0},{3,1},{4,6},{5,7},{6,4},{7,5},{8,10},{9,11},{10,... | collective-permute-start | bytes 1572872 | tf_op jit(solution)/shard_map/ppermute | solution.py:680
  40.7 11.9 %collective-permute-start.8 = (bf16[2,2,2,32,1024]{4,3,2,1,0:T(8,128)(2,1)S(1)}, bf16[2,2,2,32,1024]{4,3,2,1,0:T(8,128)(2,1)S(1)}, u32[]{:S(2)}, u32[]{:S(2)}) collective-permute-start(bf16[2,2,2,32,1024]{4,3,2,1,0:T(8,128)(2,1)S(1)} %get-tuple-element.70.refs_9_.refs_13_), channel_id=1, source_target_pairs={{0,2},{1,3},{2,0},{3,1},{4,6},{5,7},{6,4},{7,5},{8,10},{9,11},{10,... | collective-permute-start | bytes 1572872 | tf_op jit(solution)/shard_map/ppermute | solution.py:680
  52.1 3.2 %collective-permute-start.10 = (bf16[2,2,2,32,1024]{4,3,2,1,0:T(8,128)(2,1)S(1)}, bf16[2,2,2,32,1024]{4,3,2,1,0:T(8,128)(2,1)}, u32[]{:S(2)}, u32[]{:S(2)}) collective-permute-start(bf16[2,2,2,32,1024]{4,3,2,1,0:T(8,128)(2,1)S(1)} %collective-permute-done.6.refs_11_.refs_15_), channel_id=1, source_target_pairs={{0,2},{1,3},{2,0},{3,1},{4,6},{5,7},{6,4},{7,5},{8,10},{9,11},{10,... | collective-permute-start | bytes 1572872 | tf_op jit(solution)/shard_map/ppermute | solution.py:680
  52.4 2.9 %collective-permute-start.9 = (bf16[2,2,2,32,1024]{4,3,2,1,0:T(8,128)(2,1)S(1)}, bf16[2,2,2,32,1024]{4,3,2,1,0:T(8,128)(2,1)}, u32[]{:S(2)}, u32[]{:S(2)}) collective-permute-start(bf16[2,2,2,32,1024]{4,3,2,1,0:T(8,128)(2,1)S(1)} %collective-permute-done.5.refs_10_.refs_14_), channel_id=1, source_target_pairs={{0,2},{1,3},{2,0},{3,1},{4,6},{5,7},{6,4},{7,5},{8,10},{9,11},{10,... | collective-permute-start | bytes 1572872 | tf_op jit(solution)/shard_map/ppermute | solution.py:680
  72.8 5.3 %collective-permute-start.11 = (bf16[2,2,2,4,256,128]{5,4,3,2,1,0:T(8,128)(2,1)}, bf16[2,2,2,4,256,128]{5,4,3,2,1,0:T(8,128)(2,1)}, u32[]{:S(2)}, u32[]{:S(2)}) collective-permute-start(bf16[2,2,2,4,256,128]{5,4,3,2,1,0:T(8,128)(2,1)} %get-tuple-element.85), channel_id=1, source_target_pairs={{0,2},{1,3},{2,0},{3,1},{4,6},{5,7},{6,4},{7,5},{8,10},{9,11},{10,... | collective-permute-start | bytes 6291464 | tf_op jit(solution)/shard_map/ppermute | solution.py:680
  74.0 18.3 %all-to-all-start.2 = ((bf16[32,64,128]{2,1,0:T(8,128)(2,1)}), bf16[32,64,128]{2,1,0:T(8,128)(2,1)S(1)}, u32[]{:S(2)}, u32[]{:S(2)}) async-start(bf16[32,64,128]{2,1,0:T(8,128)(2,1)} %get-tuple-element.71), calls=%async_computation.2 | async-start | bytes 1048576 | tf_op jit(solution)/shard_map/all_to_all | solution.py:780
  80.5 19.4 %collective-permute-start.12 = (bf16[2,4,256,128]{3,2,1,0:T(8,128)(2,1)}, bf16[2,4,256,128]{3,2,1,0:T(8,128)(2,1)}, u32[]{:S(2)}, u32[]{:S(2)}) collective-permute-start(bf16[2,4,256,128]{3,2,1,0:T(8,128)(2,1)} %get-tuple-element.86), channel_id=1, source_target_pairs={{0,1},{1,0},{2,3},{3,2},{4,5},{5,4},{6,7},{7,6},{8,9},{9,8},{10,11... | collective-permute-start | bytes 1572872 | tf_op jit(solution)/shard_map/ppermute | solution.py:680
  81.6 18.2 %collective-permute-start.13 = (bf16[2,4,256,128]{3,2,1,0:T(8,128)(2,1)}, bf16[2,4,256,128]{3,2,1,0:T(8,128)(2,1)}, u32[]{:S(2)}, u32[]{:S(2)}) collective-permute-start(bf16[2,4,256,128]{3,2,1,0:T(8,128)(2,1)} %get-tuple-element.87), channel_id=1, source_target_pairs={{0,4},{1,5},{2,6},{3,7},{4,0},{5,1},{6,2},{7,3},{8,12},{9,13},{10,... | collective-permute-start | bytes 1572872 | tf_op jit(solution)/shard_map/ppermute | solution.py:680
  94.9 31.8 %all-to-all-start.3 = ((bf16[32,64,128]{2,1,0:T(8,128)(2,1)}), bf16[32,64,128]{2,1,0:T(8,128)(2,1)S(1)}, u32[]{:S(2)}, u32[]{:S(2)}) async-start(bf16[32,64,128]{2,1,0:T(8,128)(2,1)} %get-tuple-element.98), calls=%async_computation.3 | async-start | bytes 1048576 | tf_op jit(solution)/shard_map/all_to_all | solution.py:803
  98.5 1.3 collective-permute-start.14
  101.3 15.3 %collective-permute-start.15 = (bf16[4,256,128]{2,1,0:T(8,128)(2,1)S(1)}, bf16[4,256,128]{2,1,0:T(8,128)(2,1)S(1)}, u32[]{:S(2)}, u32[]{:S(2)}) collective-permute-start(bf16[4,256,128]{2,1,0:T(8,128)(2,1)S(1)} %get-tuple-element.90), channel_id=1, source_target_pairs={{0,4},{1,5},{2,6},{3,7},{4,0},{5,1},{6,2},{7,3},{8,12},{9,13},{10,... | collective-permute-start | bytes 786440 | tf_op jit(solution)/shard_map/ppermute | solution.py:680
  103.1 13.5 %collective-permute-start.16 = (bf16[4,256,128]{2,1,0:T(8,128)(2,1)S(1)}, bf16[4,256,128]{2,1,0:T(8,128)(2,1)S(1)}, u32[]{:S(2)}, u32[]{:S(2)}) collective-permute-start(bf16[4,256,128]{2,1,0:T(8,128)(2,1)S(1)} %get-tuple-element.91), channel_id=1, source_target_pairs={{0,1},{1,0},{2,3},{3,2},{4,5},{5,4},{6,7},{7,6},{8,9},{9,8},{10,11... | collective-permute-start | bytes 786440 | tf_op jit(solution)/shard_map/ppermute | solution.py:680
  104.6 4.6 %collective-permute-start.17 = (bf16[160,128]{1,0:T(8,128)(2,1)S(1)}, bf16[160,128]{1,0:T(8,128)(2,1)S(1)}, u32[]{:S(2)}, u32[]{:S(2)}) collective-permute-start(bf16[160,128]{1,0:T(8,128)(2,1)S(1)} %get-tuple-element.92.refs_6_), channel_id=1, source_target_pairs={{0,8},{1,9},{2,10},{3,11},{4,12},{5,13},{6,14},{7,15},{8,0},{9,1},... | collective-permute-start | bytes 122888 | tf_op jit(solution)/shard_map/ppermute | solution.py:680
  106.1 10.5 %collective-permute-start.18 = (bf16[160,128]{1,0:T(8,128)(2,1)S(1)}, bf16[160,128]{1,0:T(8,128)(2,1)S(1)}, u32[]{:S(2)}, u32[]{:S(2)}) collective-permute-start(bf16[160,128]{1,0:T(8,128)(2,1)S(1)} %get-tuple-element.92.refs_6_), channel_id=1, source_target_pairs={{0,16},{1,17},{2,18},{3,19},{4,20},{5,21},{6,22},{7,23},{8,24},{9,... | collective-permute-start | bytes 122888 | tf_op jit(solution)/shard_map/ppermute | solution.py:680
  108.5 8.1 %collective-permute-start.19 = (bf16[160,128]{1,0:T(8,128)(2,1)S(1)}, bf16[160,128]{1,0:T(8,128)(2,1)S(1)}, u32[]{:S(2)}, u32[]{:S(2)}) collective-permute-start(bf16[160,128]{1,0:T(8,128)(2,1)S(1)} %get-tuple-element.92.refs_6_), channel_id=1, source_target_pairs={{0,24},{1,25},{2,26},{3,27},{4,28},{5,29},{6,30},{7,31},{8,16},{9,... | collective-permute-start | bytes 122888 | tf_op jit(solution)/shard_map/ppermute | solution.py:680
  118.7 5.2 %collective-permute-start.23 = (bf16[2,256,128]{2,1,0:T(8,128)(2,1)S(1)}, bf16[2,256,128]{2,1,0:T(8,128)(2,1)S(1)}, u32[]{:S(2)}, u32[]{:S(2)}) collective-permute-start(bf16[2,256,128]{2,1,0:T(8,128)(2,1)S(1)} %get-tuple-element.95), channel_id=1, source_target_pairs={{0,8},{1,9},{2,10},{3,11},{4,12},{5,13},{6,14},{7,15},{8,0},{9,1},... | collective-permute-start | bytes 393224 | tf_op jit(solution)/shard_map/ppermute | solution.py:680
  119.8 14.3 %collective-permute-start.20 = (bf16[4,160,128]{2,1,0:T(8,128)(2,1)S(1)}, bf16[4,160,128]{2,1,0:T(8,128)(2,1)S(1)}, u32[]{:S(2)}, u32[]{:S(2)}) collective-permute-start(bf16[4,160,128]{2,1,0:T(8,128)(2,1)S(1)} %get-tuple-element.94.refs_0_), channel_id=1, source_target_pairs={{0,1},{1,0},{2,3},{3,2},{4,5},{5,4},{6,7},{7,6},{8,9},{9,8},{10,11... | collective-permute-start | bytes 491528 | tf_op jit(solution)/shard_map/ppermute | solution.py:680
  121.3 12.9 %collective-permute-start.21 = (bf16[4,160,128]{2,1,0:T(8,128)(2,1)S(1)}, bf16[4,160,128]{2,1,0:T(8,128)(2,1)S(1)}, u32[]{:S(2)}, u32[]{:S(2)}) collective-permute-start(bf16[4,160,128]{2,1,0:T(8,128)(2,1)S(1)} %get-tuple-element.94.refs_0_), channel_id=1, source_target_pairs={{0,4},{1,5},{2,6},{3,7},{4,0},{5,1},{6,2},{7,3},{8,12},{9,13},{10,... | collective-permute-start | bytes 491528 | tf_op jit(solution)/shard_map/ppermute | solution.py:680
  122.8 11.4 %collective-permute-start.22 = (bf16[4,160,128]{2,1,0:T(8,128)(2,1)S(1)}, bf16[4,160,128]{2,1,0:T(8,128)(2,1)S(1)}, u32[]{:S(2)}, u32[]{:S(2)}) collective-permute-start(bf16[4,160,128]{2,1,0:T(8,128)(2,1)S(1)} %get-tuple-element.94.refs_0_), channel_id=1, source_target_pairs={{0,5},{1,4},{2,7},{3,6},{4,1},{5,0},{6,3},{7,2},{8,13},{9,12},{10,... | collective-permute-start | bytes 491528 | tf_op jit(solution)/shard_map/ppermute | solution.py:680
  123.3 10.8 %collective-permute-start.24 = (bf16[2,256,128]{2,1,0:T(8,128)(2,1)}, bf16[2,256,128]{2,1,0:T(8,128)(2,1)S(1)}, u32[]{:S(2)}, u32[]{:S(2)}) collective-permute-start(bf16[2,256,128]{2,1,0:T(8,128)(2,1)} %get-tuple-element.96), channel_id=1, source_target_pairs={{0,16},{1,17},{2,18},{3,19},{4,20},{5,21},{6,22},{7,23},{8,24},{9,... | collective-permute-start | bytes 393224 | tf_op jit(solution)/shard_map/ppermute | solution.py:680
  123.9 10.2 %collective-permute-start.25 = (bf16[2,256,128]{2,1,0:T(8,128)(2,1)}, bf16[2,256,128]{2,1,0:T(8,128)(2,1)S(1)}, u32[]{:S(2)}, u32[]{:S(2)}) collective-permute-start(bf16[2,256,128]{2,1,0:T(8,128)(2,1)} %get-tuple-element.97), channel_id=1, source_target_pairs={{0,24},{1,25},{2,26},{3,27},{4,28},{5,29},{6,30},{7,31},{8,16},{9,... | collective-permute-start | bytes 393224 | tf_op jit(solution)/shard_map/ppermute | solution.py:680
  126.7 9.0 %copy-start.3 = (f32[2,8,2,64,64]{4,3,2,1,0:T(8,128)S(1)}, f32[2,8,2,64,64]{4,3,2,1,0:T(8,128)}, u32[]{:S(2)}) copy-start(f32[2,8,2,64,64]{4,3,2,1,0:T(8,128)} %refs_13_.1) | copy-start | bytes 1572868
  126.7 9.0 %copy-start.4 = (f32[2,8,2,64,64]{4,3,2,1,0:T(8,128)S(1)}, f32[2,8,2,64,64]{4,3,2,1,0:T(8,128)}, u32[]{:S(2)}) copy-start(f32[2,8,2,64,64]{4,3,2,1,0:T(8,128)} %refs_14_.1) | copy-start | bytes 1572868
  126.7 9.0 %copy-start.5 = (f32[2,8,2,64,64]{4,3,2,1,0:T(8,128)S(1)}, f32[2,8,2,64,64]{4,3,2,1,0:T(8,128)}, u32[]{:S(2)}) copy-start(f32[2,8,2,64,64]{4,3,2,1,0:T(8,128)} %refs_15_.1) | copy-start | bytes 1572868
  126.7 9.0 %copy-start.8 = (f32[32,1024]{1,0:T(8,128)S(1)}, f32[32,1024]{1,0:T(8,128)}, u32[]{:S(2)}) copy-start(f32[32,1024]{1,0:T(8,128)} %refs_6_.1) | copy-start | bytes 393220
  126.7 9.0 %copy-start.9 = (f32[32,1024]{1,0:T(8,128)S(1)}, f32[32,1024]{1,0:T(8,128)}, u32[]{:S(2)}) copy-start(f32[32,1024]{1,0:T(8,128)} %refs_5_.3) | copy-start | bytes 393220
  126.7 9.0 %copy-start.11 = (f32[32,1024]{1,0:T(8,128)S(1)}, f32[32,1024]{1,0:T(8,128)}, u32[]{:S(2)}) copy-start(f32[32,1024]{1,0:T(8,128)} %refs_7_.2) | copy-start | bytes 393220
  126.7 9.0 %copy-start.12 = (f32[32,1024]{1,0:T(8,128)S(1)}, f32[32,1024]{1,0:T(8,128)}, u32[]{:S(2)}) copy-start(f32[32,1024]{1,0:T(8,128)} %refs_8_.1) | copy-start | bytes 393220
  126.8 9.0 %copy-start.13 = (f32[32,1024]{1,0:T(8,128)S(1)}, f32[32,1024]{1,0:T(8,128)}, u32[]{:S(2)}) copy-start(f32[32,1024]{1,0:T(8,128)} %refs_9_.2) | copy-start | bytes 393220
  126.8 9.0 %copy-start.14 = (f32[32,1024]{1,0:T(8,128)S(1)}, f32[32,1024]{1,0:T(8,128)}, u32[]{:S(2)}) copy-start(f32[32,1024]{1,0:T(8,128)} %refs_10_.2) | copy-start | bytes 393220
  126.8 9.0 %copy-start.15 = (f32[13,512]{1,0:T(8,128)S(1)}, f32[13,512]{1,0:T(8,128)}, u32[]{:S(2)}) copy-start(f32[13,512]{1,0:T(8,128)} %refs_17_.1) | copy-start | bytes 79876
  126.8 9.0 %copy-start.16 = (f32[13,512]{1,0:T(8,128)S(1)}, f32[13,512]{1,0:T(8,128)}, u32[]{:S(2)}) copy-start(f32[13,512]{1,0:T(8,128)} %refs_18_.1) | copy-start | bytes 79876
  134.3 1.5 %collective-permute-start.26 = (bf16[4,160,128]{2,1,0:T(8,128)(2,1)S(1)}, bf16[4,160,128]{2,1,0:T(8,128)(2,1)S(1)}, u32[]{:S(2)}, u32[]{:S(2)}) collective-permute-start(bf16[4,160,128]{2,1,0:T(8,128)(2,1)S(1)} %get-tuple-element.103.refs_11_), channel_id=1, source_target_pairs={{0,2},{1,3},{2,0},{3,1},{4,6},{5,7},{6,4},{7,5},{8,10},{9,11},{10,... | collective-permute-start | bytes 491528 | tf_op jit(solution)/shard_map/ppermute | solution.py:680
  (4 other events, 11.5 us)

commit v8 on v7

--- a/solution.py
+++ b/solution.py
@@ -161,9 +161,23 @@
     return parts[0] if modes == 1 else jnp.concatenate(parts, axis=1)
 
 
-def enter_kernel(groups, tokens_ref, table_ref, send_ref):
+def enter_kernel(groups, place_ref, tokens_ref, table_ref, *refs):
+    if len(refs) > 1:
+        ones_ref, mixer_ref, *refs, held, sems = refs
+        joined = held.shape[1]
+        blocks = pl.ds(place_ref[1] * joined, joined)
+        copies = [
+            pltpu.make_async_copy(mixer_ref.at[:, blocks], held, sems.at[0]),
+            pltpu.make_async_copy(ones_ref.at[place_ref[0]], refs[1], sems.at[1]),
+        ]
+        for copy in copies:
+            copy.start(priority=1)
     normal, _ = normalize(tokens_ref[...].astype(F32))
-    scatter_lanes(send_ref, along_w(table_ref, normal.astype(BF16), normal.shape[0]), groups)
+    scatter_lanes(refs[0], along_w(table_ref, normal.astype(BF16), normal.shape[0]), groups)
+    if len(refs) > 1:
+        for copy in copies:
+            copy.wait()
+        refs[2][...] = held[...].astype(BF16)
 
 
 def mix_kernel(
@@ -687,7 +701,26 @@
         weights = lax.all_gather(pair, "sp", axis=1, tiled=True)
         pieces, carried = [lax.all_gather(weights, "tp")], []
 
-    own_mixer = lax.dynamic_slice_in_dim(mixer_weights, group * joined, joined, 1).astype(BF16)
+    wide_f, wide_f_t = jnp.asarray(wide_f), jnp.asarray(wide_f.T)
+    wide_i, wide_i_t = jnp.asarray(wide_i), jnp.asarray(wide_i.T)
+    high, high_t = jnp.asarray(high), jnp.asarray(high.T)
+    wide_flops = 2 * MODES * 2 * local * width * SPAN
+    place = jnp.stack([me % per_group, group])
+    ones = jnp.asarray(np.swapaxes(ones.reshape(per_group, modes, -1), 1, 2))
+    part = (2, joined, 2, block, block)
+    cut = near and dict(
+        raw=[ones, mixer_weights], scratch=[pltpu.VMEM(part, F32), pltpu.SemaphoreType.DMA((2,))]
+    )
+    sent, *own = call(
+        functools.partial(enter_kernel, groups),
+        [(chunk, BF16)] + ([(ones.shape[1:], F32), (part, BF16)] if near else []),
+        Far(rows_all), Far(wide_f), scalars=[place], flops=wide_flops, **(cut or {}),
+    )
+    if near:
+        own_ones, own_mixer = own
+    else:
+        own_mixer = lax.dynamic_slice_in_dim(mixer_weights, group * joined, joined, 1).astype(BF16)
+        own_ones = lax.dynamic_index_in_dim(ones, me % per_group, 0, keepdims=False)
     eye = jnp.eye(joined, dtype=BF16)
     real = jnp.einsum("lbio,bc->lbico", own_mixer[:, :, 0], eye).reshape(2, lanes, lanes)
     imag = jnp.einsum("lbio,bc->lbico", own_mixer[:, :, 1], eye).reshape(2, lanes, lanes)
@@ -700,16 +733,7 @@
     own_bias = jnp.swapaxes(own_bias, 1, 2).reshape(2, 2 * lanes)
     own_gain = lax.dynamic_slice_in_dim(vectors[0:1], group * lanes, lanes, 1)
     own_shift = lax.dynamic_slice_in_dim(vectors[1:2], group * lanes, lanes, 1)
-    ones = jnp.asarray(np.swapaxes(ones.reshape(per_group, modes, -1), 1, 2))
-    own_ones = lax.dynamic_index_in_dim(ones, me % per_group, 0, keepdims=False)
-
-    wide_f, wide_f_t = jnp.asarray(wide_f), jnp.asarray(wide_f.T)
-    wide_i, wide_i_t = jnp.asarray(wide_i), jnp.asarray(wide_i.T)
-    high, high_t = jnp.asarray(high), jnp.asarray(high.T)
-    wide_flops = 2 * MODES * 2 * local * width * SPAN
-    (sent,) = call(
-        functools.partial(enter_kernel, groups), [(chunk, BF16)], Far(rows_all), Far(wide_f), flops=wide_flops
-    )
+
     got = exchange(sent)
     half_rows = items * MODES
     sent, hat, modal, inner, active, *carried = call(

time: 141 us -> 140 us (level)
  transfers between devices with their start and end apart: 31 -> 31, of which waited for: 12 -> 13; matrix products, arithmetic and copies ran while one was open for 3% -> 1% of each run, Pallas kernels for 17% -> 17%
where the time goes in v8:
time: 140 us
  starting transfers between devices  48.6 us (35%)
  Pallas kernels  47.5 us (34%)
  waiting for transfers between devices  39.2 us (28%)
  other arithmetic  1.61 us (1%)
    pallas_call x11, Pallas kernels, call(): pl.pallas_call(inner, out_shape=[(pltpu.HBM if f else pltpu.VMEM)(o.shape...  47.5 us
    ppermute x27, waiting for transfers between devices, permute(): return lax.ppermute(values, AXES, [(d, d ^ mask) for d in range(devices)])  34.9 us
    ppermute x27, starting transfers between devices, permute(): return lax.ppermute(values, AXES, [(d, d ^ mask) for d in range(devices)])  32.7 us
    all_to_all x4, starting transfers between devices, on_device(): got = exchange(sent)  15.9 us
    all_to_all x4, waiting for transfers between devices, on_device(): got = exchange(sent)  4.33 us
  transfers between devices with their start and end apart: 31, of which 13 were waited for; matrix products, arithmetic and copies ran while one was open for 1% of the time, Pallas kernels for 17%

profile of v8, /device:TPU:0, one launch (start us, length us, event | category | flops | bytes accessed | tf_op | source)
XLA Modules:
  0.0 139.7 jit_solution(4581798396806835707)
XLA Ops:
  0.6 1.0 convert_bitcast_fusion
  1.7 4.1 %collective-permute-start.2 = (bf16[2,32,1024]{2,1,0:T(8,128)(2,1)S(1)}, bf16[2,32,1024]{2,1,0:T(8,128)(2,1)S(1)}, u32[]{:S(2)}, u32[]{:S(2)}) collective-permute-start(bf16[2,32,1024]{2,1,0:T(8,128)(2,1)S(1)} %get-tuple-element.131), channel_id=1, source_target_pairs={{0,16},{1,17},{2,18},{3,19},{4,20},{5,21},{6,22},{7,23},{8,24},{9,... | collective-permute-start | bytes 393224 | tf_op jit(solution)/shard_map/ppermute | solution.py:694
  5.8 1.3 collective-permute-start.3
  7.4 3.6 %shard_map.324 = (bf16[32,64,128]{2,1,0:T(8,128)(2,1)}, f32[128,4]{1,0:T(8,128)S(1)}, bf16[2,2,2,64,64]{4,3,2,1,0:T(8,128)(2,1)S(1)}) custom-call(s32[2]{0:T(128)S(1)} %pad_add_fusion.refs_0_, bf16[1024,512]{1,0:T(8,128)(2,1)} %bitcast.39, bf16[256,512]{1,0:T(8,128)(2,1)} %constant.56.clone.refs_2_, f32[8,128,4]{2,1,0:T(8,128)} %constant.62.clone.refs_3_, ...), custom_call_target="tpu_custom_call" | custom-call | flops 268435456 | bytes 2443264 | tf_op jit(solution)/shard_map/pallas_call | solution.py:648
  11.0 5.2 %all-to-all-start = ((bf16[32,64,128]{2,1,0:T(8,128)(2,1)}), bf16[32,64,128]{2,1,0:T(8,128)(2,1)S(1)}, u32[]{:S(2)}, u32[]{:S(2)}) async-start(bf16[32,64,128]{2,1,0:T(8,128)(2,1)} %get-tuple-element.71), calls=%async_computation | async-start | bytes 1048576 | tf_op jit(solution)/shard_map/all_to_all | solution.py:737
  16.8 1.8 %collective-permute-start.4 = (bf16[2,2,32,1024]{3,2,1,0:T(8,128)(2,1)S(1)}, bf16[2,2,32,1024]{3,2,1,0:T(8,128)(2,1)S(1)}, u32[]{:S(2)}, u32[]{:S(2)}) collective-permute-start(bf16[2,2,32,1024]{3,2,1,0:T(8,128)(2,1)S(1)} %get-tuple-element.127), channel_id=1, source_target_pairs={{0,4},{1,5},{2,6},{3,7},{4,0},{5,1},{6,2},{7,3},{8,12},{9,13},{10,... | collective-permute-start | bytes 786440 | tf_op jit(solution)/shard_map/ppermute | solution.py:694
  18.7 1.5 %collective-permute-start.1 = (bf16[2,2,32,1024]{3,2,1,0:T(8,128)(2,1)S(1)}, bf16[2,2,32,1024]{3,2,1,0:T(8,128)(2,1)S(1)}, u32[]{:S(2)}, u32[]{:S(2)}) collective-permute-start(bf16[2,2,32,1024]{3,2,1,0:T(8,128)(2,1)S(1)} %get-tuple-element.129), channel_id=1, source_target_pairs={{0,1},{1,0},{2,3},{3,2},{4,5},{5,4},{6,7},{7,6},{8,9},{9,8},{10,11... | collective-permute-start | bytes 786440 | tf_op jit(solution)/shard_map/ppermute | solution.py:694
  20.6 9.4 %collective-permute-done.4 = bf16[2,2,32,1024]{3,2,1,0:T(8,128)(2,1)S(1)} collective-permute-done((bf16[2,2,32,1024]{3,2,1,0:T(8,128)(2,1)S(1)}, bf16[2,2,32,1024]{3,2,1,0:T(8,128)(2,1)S(1)}, u32[]{:S(2)}, u32[]{:S(2)}) %collective-permute-start.4) | collective-permute-done | bytes 262176 | tf_op jit(solution)/shard_map/ppermute | solution.py:694
  30.1 1.1 all-to-all-done.refs_0_
  31.2 2.3 %shard_map.325 = (bf16[32,64,128]{2,1,0:T(8,128)(2,1)}, f32[128,512]{1,0:T(8,128)}, bf16[256,256]{1,0:T(8,128)(2,1)}, f32[256,256]{1,0:T(8,128)}, bf16[256,256]{...) custom-call(bf16[32,64,128]{2,1,0:T(8,128)(2,1)S(1)} %all-to-all-don, ...), custom_call_target="tpu_custom_call", output_to_operand_aliasing={{5}: (8, {}), {6}: (9, {})} | custom-call | bytes 2364416 | tf_op jit(solution)/shard_map/pallas_call | solution.py:648
  33.6 1.9 %collective-permute-start.6 = (bf16[2,2,2,32,1024]{4,3,2,1,0:T(8,128)(2,1)S(1)}, bf16[2,2,2,32,1024]{4,3,2,1,0:T(8,128)(2,1)S(1)}, u32[]{:S(2)}, u32[]{:S(2)}) collective-permute-start(bf16[2,2,2,32,1024]{4,3,2,1,0:T(8,128)(2,1)S(1)} %get-tuple-element.76.refs_9_.refs_13_), channel_id=1, source_target_pairs={{0,1},{1,0},{2,3},{3,2},{4,5},{5,4},{6,7},{7,6},{8,9},{9,8},{10,11... | collective-permute-start | bytes 1572872 | tf_op jit(solution)/shard_map/ppermute | solution.py:694
  35.4 1.2 collective-permute-start.5
  36.6 3.5 %all-to-all-start.1 = ((bf16[32,64,128]{2,1,0:T(8,128)(2,1)}), bf16[32,64,128]{2,1,0:T(8,128)(2,1)}, u32[]{:S(2)}, u32[]{:S(2)}) async-start(bf16[32,64,128]{2,1,0:T(8,128)(2,1)} %get-tuple-element.74), calls=%async_computation.1 | async-start | bytes 1048576 | tf_op jit(solution)/shard_map/all_to_all | solution.py:754
  40.7 11.2 %collective-permute-done.6.refs_11_.refs_15_ = bf16[2,2,2,32,1024]{4,3,2,1,0:T(8,128)(2,1)S(1)} collective-permute-done((bf16[2,2,2,32,1024]{4,3,2,1,0:T(8,128)(2,1)S(1)}, bf16[2,2,2,32,1024]{4,3,2,1,0:T(8,128)(2,1)S(1)}, u32[]{:S(2)}, u32[]{:S(2)}) %collective-permute-start.6) | collective-permute-done | bytes 524320 | tf_op jit(solution)/shard_map/ppermute | solution.py:694
  51.8 0.4 collective-permute-start.10
  52.3 0.9 collective-permute-done.5.refs_10_.refs_14_
  53.2 1.7 %all-to-all-done.1.refs_1_ = bf16[32,64,128]{2,1,0:T(8,128)(2,1)} async-done(((bf16[32,64,128]{2,1,0:T(8,128)(2,1)}), bf16[32,64,128]{2,1,0:T(8,128)(2,1)}, u32[]{:S(2)}, u32[]{:S(2)}) %all-to-all-start.1) | async-done | bytes 524320 | tf_op jit(solution)/shard_map/all_to_all | solution.py:754
  55.3 0.7 copy-done.13
  56.0 17.4 %shard_map.326 = (bf16[1024,2048]{1,0:T(8,128)(2,1)}, f32[1024,512]{1,0:T(8,128)}, bf16[1024,512]{1,0:T(8,128)(2,1)}, bf16[32,64,128]{2,1,0:T(8,128)(2,1)}, f32[...) custom-call(s32[1]{0:T(128)} %bitcast.1.refs_0_, ...), custom_call_target="tpu_custom_call" | custom-call | flops 13421772800 | bytes 19449856 | tf_op jit(solution)/shard_map/pallas_call | solution.py:648
  73.5 0.8 collective-permute-start.11
  74.3 3.6 %all-to-all-start.2 = ((bf16[32,64,128]{2,1,0:T(8,128)(2,1)}), bf16[32,64,128]{2,1,0:T(8,128)(2,1)S(1)}, u32[]{:S(2)}, u32[]{:S(2)}) async-start(bf16[32,64,128]{2,1,0:T(8,128)(2,1)} %get-tuple-element.77), calls=%async_computation.2 | async-start | bytes 1048576 | tf_op jit(solution)/shard_map/all_to_all | solution.py:804
  77.9 0.5 collective-permute-done.11.refs_1_.refs_5_.refs_10_
  78.4 2.3 %shard_map.329 = (bf16[2,4,256,128]{3,2,1,0:T(8,128)(2,1)}, bf16[2,4,256,128]{3,2,1,0:T(8,128)(2,1)}) custom-call(bf16[2,2,2,4,256,128]{5,4,3,2,1,0:T(8,128)(2,1)S(1)} %get-tuple-element.90.refs_0_.refs_1_, bf16[2,2,2,4,256,128]{5,4,3,2,1,0:T(8,128)(2,1)} %collective-permute-done.11.refs_1_.refs_5_.refs_10_), custom_call_target="tpu_custom_call" | custom-call | tf_op jit(solution)/shard_map/pallas_call | solution.py:648
  80.8 1.3 collective-permute-start.12
  82.1 1.5 %collective-permute-start.13 = (bf16[2,4,256,128]{3,2,1,0:T(8,128)(2,1)}, bf16[2,4,256,128]{3,2,1,0:T(8,128)(2,1)}, u32[]{:S(2)}, u32[]{:S(2)}) collective-permute-start(bf16[2,4,256,128]{3,2,1,0:T(8,128)(2,1)} %get-tuple-element.93), channel_id=1, source_target_pairs={{0,4},{1,5},{2,6},{3,7},{4,0},{5,1},{6,2},{7,3},{8,12},{9,13},{10,... | collective-permute-start | bytes 1572872 | tf_op jit(solution)/shard_map/ppermute | solution.py:694
  83.6 7.8 %shard_map.327 = (bf16[1024,512]{1,0:T(8,128)(2,1)}, bf16[128,512]{1,0:T(8,128)(2,1)S(1)}, bf16[512,128]{1,0:T(8,128)(2,1)S(1)}, bf16[2,256,256]{2,1,0:T(8,128)(2,1)S(1)}) custom-call(s32[1]{0:T(128)} %bitcast.1.refs_0_, f32[1024,512]{1,0:T(8,128)} %get-tuple-element.78.refs_1_.refs_2_.refs_3_.refs_4_, ...), custom_call_target="tpu_custom_call" | custom-call | bytes 62914560 | tf_op jit(solution)/shard_map/pallas_call | solution.py:648
  91.4 1.5 %all-to-all-done.2.refs_1_ = bf16[32,64,128]{2,1,0:T(8,128)(2,1)S(1)} async-done(((bf16[32,64,128]{2,1,0:T(8,128)(2,1)}), bf16[32,64,128]{2,1,0:T(8,128)(2,1)S(1)}, u32[]{:S(2)}, u32[]{:S(2)}) %all-to-all-start.2) | async-done | bytes 524320 | tf_op jit(solution)/shard_map/all_to_all | solution.py:804
  92.9 2.6 %shard_map.328 = (bf16[32,64,128]{2,1,0:T(8,128)(2,1)}, bf16[160,128]{1,0:T(8,128)(2,1)S(1)}, bf16[160,128]{1,0:T(8,128)(2,1)S(1)}, bf16[1024,512]{1,0:T(8,128)(2,1)}) custom-call(s32[1]{0:T(128)} %bitcast.refs_0_, bf16[32,64,128]{2,1,0:T(8,128)(2,1)S(1)} %all-to-all-done.2.refs_1_, ...), custom_call_target="tpu_custom_call", output_to_operand_aliasing={{3}: (11, {})} | custom-call | bytes 62914560 | tf_op jit(solution)/shard_map/pallas_call | solution.py:648
  95.5 3.6 %all-to-all-start.3 = ((bf16[32,64,128]{2,1,0:T(8,128)(2,1)}), bf16[32,64,128]{2,1,0:T(8,128)(2,1)S(1)}, u32[]{:S(2)}, u32[]{:S(2)}) async-start(bf16[32,64,128]{2,1,0:T(8,128)(2,1)} %get-tuple-element.104), calls=%async_computation.3 | async-start | bytes 1048576 | tf_op jit(solution)/shard_map/all_to_all | solution.py:827
  99.4 1.0 collective-permute-done.14.refs_4_
  100.4 1.5 %shard_map.330 = (bf16[160,128]{1,0:T(8,128)(2,1)S(1)}, bf16[4,256,128]{2,1,0:T(8,128)(2,1)S(1)}, bf16[4,256,128]{2,1,0:T(8,128)(2,1)S(1)}) custom-call(bf16[2,2,2,4,256,128]{5,4,3,2,1,0:T(8,128)(2,1)S(1)} %get-tuple-element.90.refs_0_.refs_1_, bf16[2,4,256,128]{3,2,1,0:T(8,128)(2,1)} %collective-permute-done.12.refs_1_.refs_2_, ...), custom_call_target="tpu_custom_call" | custom-call | tf_op jit(solution)/shard_map/pallas_call | solution.py:648
  101.9 1.8 %collective-permute-start.15 = (bf16[4,256,128]{2,1,0:T(8,128)(2,1)S(1)}, bf16[4,256,128]{2,1,0:T(8,128)(2,1)S(1)}, u32[]{:S(2)}, u32[]{:S(2)}) collective-permute-start(bf16[4,256,128]{2,1,0:T(8,128)(2,1)S(1)} %get-tuple-element.96), channel_id=1, source_target_pairs={{0,4},{1,5},{2,6},{3,7},{4,0},{5,1},{6,2},{7,3},{8,12},{9,13},{10,... | collective-permute-start | bytes 786440 | tf_op jit(solution)/shard_map/ppermute | solution.py:694
  103.7 1.5 %collective-permute-start.16 = (bf16[4,256,128]{2,1,0:T(8,128)(2,1)S(1)}, bf16[4,256,128]{2,1,0:T(8,128)(2,1)S(1)}, u32[]{:S(2)}, u32[]{:S(2)}) collective-permute-start(bf16[4,256,128]{2,1,0:T(8,128)(2,1)S(1)} %get-tuple-element.97), channel_id=1, source_target_pairs={{0,1},{1,0},{2,3},{3,2},{4,5},{5,4},{6,7},{7,6},{8,9},{9,8},{10,11... | collective-permute-start | bytes 786440 | tf_op jit(solution)/shard_map/ppermute | solution.py:694
  105.2 1.5 %collective-permute-start.17 = (bf16[160,128]{1,0:T(8,128)(2,1)S(1)}, bf16[160,128]{1,0:T(8,128)(2,1)S(1)}, u32[]{:S(2)}, u32[]{:S(2)}) collective-permute-start(bf16[160,128]{1,0:T(8,128)(2,1)S(1)} %get-tuple-element.98.refs_6_), channel_id=1, source_target_pairs={{0,8},{1,9},{2,10},{3,11},{4,12},{5,13},{6,14},{7,15},{8,0},{9,1},... | collective-permute-start | bytes 122888 | tf_op jit(solution)/shard_map/ppermute | solution.py:694
  106.7 2.5 %collective-permute-start.18 = (bf16[160,128]{1,0:T(8,128)(2,1)S(1)}, bf16[160,128]{1,0:T(8,128)(2,1)S(1)}, u32[]{:S(2)}, u32[]{:S(2)}) collective-permute-start(bf16[160,128]{1,0:T(8,128)(2,1)S(1)} %get-tuple-element.98.refs_6_), channel_id=1, source_target_pairs={{0,16},{1,17},{2,18},{3,19},{4,20},{5,21},{6,22},{7,23},{8,24},{9,... | collective-permute-start | bytes 122888 | tf_op jit(solution)/shard_map/ppermute | solution.py:694
  109.1 0.5 collective-permute-start.19
  109.8 7.4 %collective-permute-done.18.refs_8_ = bf16[160,128]{1,0:T(8,128)(2,1)S(1)} collective-permute-done((bf16[160,128]{1,0:T(8,128)(2,1)S(1)}, bf16[160,128]{1,0:T(8,128)(2,1)S(1)}, u32[]{:S(2)}, u32[]{:S(2)}) %collective-permute-start.18) | collective-permute-done | bytes 40992 | tf_op jit(solution)/shard_map/ppermute | solution.py:694
  117.2 1.5 %shard_map.331 = (bf16[4,160,128]{2,1,0:T(8,128)(2,1)S(1)}, f32[2,256,128]{2,1,0:T(8,128)S(1)}, bf16[2,256,128]{2,1,0:T(8,128)(2,1)S(1)}, bf16[2,256,128]{2,1,0:T(8,128)(2,1)S(1)}, bf16[2,256,128]{2,1,0:T(8,128)(2,1)S(1)}) custom-call(s32[1]{0:T(128)} %bitcast.1.refs_0_, bf16[2,2,2,4,256,128]{5,4,3,2,1,0:T(8,128)(2,1)S(1)} %get-tuple-element.90.refs_0_.refs_1_, ...), custom_call_target="tpu_custom_call" | custom-call | tf_op jit(solution)/shard_map/pallas_call | solution.py:648
  118.7 1.1 collective-permute-start.23
  119.8 1.5 %collective-permute-start.20 = (bf16[4,160,128]{2,1,0:T(8,128)(2,1)S(1)}, bf16[4,160,128]{2,1,0:T(8,128)(2,1)S(1)}, u32[]{:S(2)}, u32[]{:S(2)}) collective-permute-start(bf16[4,160,128]{2,1,0:T(8,128)(2,1)S(1)} %get-tuple-element.100.refs_0_), channel_id=1, source_target_pairs={{0,1},{1,0},{2,3},{3,2},{4,5},{5,4},{6,7},{7,6},{8,9},{9,8},{10,11... | collective-permute-start | bytes 491528 | tf_op jit(solution)/shard_map/ppermute | solution.py:694
  121.3 1.5 %collective-permute-start.21 = (bf16[4,160,128]{2,1,0:T(8,128)(2,1)S(1)}, bf16[4,160,128]{2,1,0:T(8,128)(2,1)S(1)}, u32[]{:S(2)}, u32[]{:S(2)}) collective-permute-start(bf16[4,160,128]{2,1,0:T(8,128)(2,1)S(1)} %get-tuple-element.100.refs_0_), channel_id=1, source_target_pairs={{0,4},{1,5},{2,6},{3,7},{4,0},{5,1},{6,2},{7,3},{8,12},{9,13},{10,... | collective-permute-start | bytes 491528 | tf_op jit(solution)/shard_map/ppermute | solution.py:694
  122.7 0.5 collective-permute-start.22
  123.3 0.7 collective-permute-start.24
  123.9 2.7 %collective-permute-start.25 = (bf16[2,256,128]{2,1,0:T(8,128)(2,1)S(1)}, bf16[2,256,128]{2,1,0:T(8,128)(2,1)S(1)}, u32[]{:S(2)}, u32[]{:S(2)}) collective-permute-start(bf16[2,256,128]{2,1,0:T(8,128)(2,1)S(1)} %get-tuple-element.103), channel_id=1, source_target_pairs={{0,24},{1,25},{2,26},{3,27},{4,28},{5,29},{6,30},{7,31},{8,16},{9,... | collective-permute-start | bytes 393224 | tf_op jit(solution)/shard_map/ppermute | solution.py:694
  126.8 4.5 %shard_map.332.refs_7_ = bf16[1024,512]{1,0:T(8,128)(2,1)} custom-call(bf16[32,64,128]{2,1,0:T(8,128)(2,1)S(1)} %all-to-all-done.3.refs_0_, bf16[1024,512]{1,0:T(8,128)(2,1)} %bitcast.41, bf16[1024,512]{1,0:T(8,128)(2,1)} %get-tuple-element.105.refs_2_, f32[13,512]{1,0:T(8,128)S(1)} %copy-done.14, bf16[512,256]{1,0:T(8,128)(2,1)} %constant.57.clone.refs_4_), custom_call_target="tpu_custom_call" | custom-call | bytes 62914560 | tf_op jit(solution)/shard_map/pallas_call | solution.py:648
  131.3 2.6 %collective-permute-done.24.refs_5_ = bf16[2,256,128]{2,1,0:T(8,128)(2,1)S(1)} collective-permute-done((bf16[2,256,128]{2,1,0:T(8,128)(2,1)S(1)}, bf16[2,256,128]{2,1,0:T(8,128)(2,1)S(1)}, u32[]{:S(2)}, u32[]{:S(2)}) %collective-permute-start.24) | collective-permute-done | bytes 131104 | tf_op jit(solution)/shard_map/ppermute | solution.py:694
  134.1 1.4 collective-permute-done.26.refs_12_
  135.6 3.9 %shard_map.334 = (f32[32,1024]{1,0:T(8,128)}, f32[32,1024]{1,0:T(8,128)}, f32[32,1024]{1,0:T(8,128)}, f32[32,1024]{1,0:T(8,128)}, f32[32,1024]{1,0:T(8,128)}, /*...) custom-call(s32[1]{0:T(128)} %bitcast.refs_0_, ...), custom_call_target="tpu_custom_call", output_to_operand_aliasing={{14}: (19, {})} | custom-call | tf_op jit(solution)/shard_map/pallas_call | solution.py:648
  (96 shorter events, 3.0 us)
Async XLA Ops:
  1.7 15.0 %collective-permute-start.2 = (bf16[2,32,1024]{2,1,0:T(8,128)(2,1)S(1)}, bf16[2,32,1024]{2,1,0:T(8,128)(2,1)S(1)}, u32[]{:S(2)}, u32[]{:S(2)}) collective-permute-start(bf16[2,32,1024]{2,1,0:T(8,128)(2,1)S(1)} %get-tuple-element.131), channel_id=1, source_target_pairs={{0,16},{1,17},{2,18},{3,19},{4,20},{5,21},{6,22},{7,23},{8,24},{9,... | collective-permute-start | bytes 393224 | tf_op jit(solution)/shard_map/ppermute | solution.py:694
  5.8 11.0 %collective-permute-start.3 = (bf16[2,32,1024]{2,1,0:T(8,128)(2,1)S(1)}, bf16[2,32,1024]{2,1,0:T(8,128)(2,1)S(1)}, u32[]{:S(2)}, u32[]{:S(2)}) collective-permute-start(bf16[2,32,1024]{2,1,0:T(8,128)(2,1)S(1)} %get-tuple-element.131), channel_id=1, source_target_pairs={{0,24},{1,25},{2,26},{3,27},{4,28},{5,29},{6,30},{7,31},{8,16},{9,... | collective-permute-start | bytes 393224 | tf_op jit(solution)/shard_map/ppermute | solution.py:694
  7.1 11.5 %collective-permute-start = (bf16[2,32,1024]{2,1,0:T(8,128)(2,1)S(1)}, bf16[2,32,1024]{2,1,0:T(8,128)(2,1)S(1)}, u32[]{:S(2)}, u32[]{:S(2)}) collective-permute-start(bf16[2,32,1024]{2,1,0:T(8,128)(2,1)S(1)} %get-tuple-element.131), channel_id=1, source_target_pairs={{0,8},{1,9},{2,10},{3,11},{4,12},{5,13},{6,14},{7,15},{8,0},{9,1},... | collective-permute-start | bytes 393224 | tf_op jit(solution)/shard_map/ppermute | solution.py:694
  7.4 8.8 %copy-start.12 = (f32[13,512]{1,0:T(8,128)S(1)}, f32[13,512]{1,0:T(8,128)}, u32[]{:S(2)}) copy-start(f32[13,512]{1,0:T(8,128)} %refs_16_.1) | copy-start | bytes 79876
  11.0 20.2 %copy-start.10 = (f32[128,4]{1,0:T(8,128)}, f32[128,4]{1,0:T(8,128)S(1)}, u32[]{:S(2)}) copy-start(f32[128,4]{1,0:T(8,128)S(1)} %get-tuple-element.73.refs_7_.refs_5_) | copy-start | bytes 6148
  11.0 20.2 %all-to-all-start = ((bf16[32,64,128]{2,1,0:T(8,128)(2,1)}), bf16[32,64,128]{2,1,0:T(8,128)(2,1)S(1)}, u32[]{:S(2)}, u32[]{:S(2)}) async-start(bf16[32,64,128]{2,1,0:T(8,128)(2,1)} %get-tuple-element.71), calls=%async_computation | async-start | bytes 1048576 | tf_op jit(solution)/shard_map/all_to_all | solution.py:737
  16.8 14.5 %copy-start.6 = (bf16[128,512]{1,0:T(8,128)(2,1)S(1)}, bf16[128,512]{1,0:T(8,128)(2,1)}, u32[]{:S(2)}) copy-start(bf16[128,512]{1,0:T(8,128)(2,1)} %constant.60.clone.refs_1_.refs_9_) | copy-start | bytes 393220
  16.8 14.4 %copy-start.7 = (bf16[512,128]{1,0:T(8,128)(2,1)S(1)}, bf16[512,128]{1,0:T(8,128)(2,1)}, u32[]{:S(2)}) copy-start(bf16[512,128]{1,0:T(8,128)(2,1)} %constant.61.clone.refs_2_.refs_10_) | copy-start | bytes 393220
  16.8 13.2 %collective-permute-start.4 = (bf16[2,2,32,1024]{3,2,1,0:T(8,128)(2,1)S(1)}, bf16[2,2,32,1024]{3,2,1,0:T(8,128)(2,1)S(1)}, u32[]{:S(2)}, u32[]{:S(2)}) collective-permute-start(bf16[2,2,32,1024]{3,2,1,0:T(8,128)(2,1)S(1)} %get-tuple-element.127), channel_id=1, source_target_pairs={{0,4},{1,5},{2,6},{3,7},{4,0},{5,1},{6,2},{7,3},{8,12},{9,13},{10,... | collective-permute-start | bytes 786440 | tf_op jit(solution)/shard_map/ppermute | solution.py:694
  18.7 11.4 %collective-permute-start.1 = (bf16[2,2,32,1024]{3,2,1,0:T(8,128)(2,1)S(1)}, bf16[2,2,32,1024]{3,2,1,0:T(8,128)(2,1)S(1)}, u32[]{:S(2)}, u32[]{:S(2)}) collective-permute-start(bf16[2,2,32,1024]{3,2,1,0:T(8,128)(2,1)S(1)} %get-tuple-element.129), channel_id=1, source_target_pairs={{0,1},{1,0},{2,3},{3,2},{4,5},{5,4},{6,7},{7,6},{8,9},{9,8},{10,11... | collective-permute-start | bytes 786440 | tf_op jit(solution)/shard_map/ppermute | solution.py:694
  20.6 12.9 %copy-start.3 = (bf16[2,256,256]{2,1,0:T(8,128)(2,1)}, bf16[2,256,256]{2,1,0:T(8,128)(2,1)S(1)}, u32[]{:S(2)}) copy-start(bf16[2,256,256]{2,1,0:T(8,128)(2,1)S(1)} %maximum_maximum_fusion.refs_3_.refs_11_) | copy-start | bytes 786436
  33.5 21.7 %copy-start = (bf16[2,2,2,32,1024]{4,3,2,1,0:T(8,128)(2,1)}, bf16[2,2,2,32,1024]{4,3,2,1,0:T(8,128)(2,1)S(1)}, u32[]{:S(2)}) copy-start(bf16[2,2,2,32,1024]{4,3,2,1,0:T(8,128)(2,1)S(1)} %get-tuple-element.76.refs_9_.refs_13_) | copy-start | bytes 1572868
  33.5 21.7 %copy-start.1 = (bf16[2,2,2,32,1024]{4,3,2,1,0:T(8,128)(2,1)}, bf16[2,2,2,32,1024]{4,3,2,1,0:T(8,128)(2,1)S(1)}, u32[]{:S(2)}) copy-start(bf16[2,2,2,32,1024]{4,3,2,1,0:T(8,128)(2,1)S(1)} %get-tuple-element.75.refs_8_.refs_12_) | copy-start | bytes 1572868
  33.6 18.3 %collective-permute-start.6 = (bf16[2,2,2,32,1024]{4,3,2,1,0:T(8,128)(2,1)S(1)}, bf16[2,2,2,32,1024]{4,3,2,1,0:T(8,128)(2,1)S(1)}, u32[]{:S(2)}, u32[]{:S(2)}) collective-permute-start(bf16[2,2,2,32,1024]{4,3,2,1,0:T(8,128)(2,1)S(1)} %get-tuple-element.76.refs_9_.refs_13_), channel_id=1, source_target_pairs={{0,1},{1,0},{2,3},{3,2},{4,5},{5,4},{6,7},{7,6},{8,9},{9,8},{10,11... | collective-permute-start | bytes 1572872 | tf_op jit(solution)/shard_map/ppermute | solution.py:694
  35.4 17.7 %collective-permute-start.5 = (bf16[2,2,2,32,1024]{4,3,2,1,0:T(8,128)(2,1)S(1)}, bf16[2,2,2,32,1024]{4,3,2,1,0:T(8,128)(2,1)S(1)}, u32[]{:S(2)}, u32[]{:S(2)}) collective-permute-start(bf16[2,2,2,32,1024]{4,3,2,1,0:T(8,128)(2,1)S(1)} %get-tuple-element.75.refs_8_.refs_12_), channel_id=1, source_target_pairs={{0,4},{1,5},{2,6},{3,7},{4,0},{5,1},{6,2},{7,3},{8,12},{9,13},{10,... | collective-permute-start | bytes 1572872 | tf_op jit(solution)/shard_map/ppermute | solution.py:694
  36.6 18.3 %all-to-all-start.1 = ((bf16[32,64,128]{2,1,0:T(8,128)(2,1)}), bf16[32,64,128]{2,1,0:T(8,128)(2,1)}, u32[]{:S(2)}, u32[]{:S(2)}) async-start(bf16[32,64,128]{2,1,0:T(8,128)(2,1)} %get-tuple-element.74), calls=%async_computation.1 | async-start | bytes 1048576 | tf_op jit(solution)/shard_map/all_to_all | solution.py:754
  40.1 13.1 %collective-permute-start.7 = (bf16[2,2,2,32,1024]{4,3,2,1,0:T(8,128)(2,1)S(1)}, bf16[2,2,2,32,1024]{4,3,2,1,0:T(8,128)(2,1)S(1)}, u32[]{:S(2)}, u32[]{:S(2)}) collective-permute-start(bf16[2,2,2,32,1024]{4,3,2,1,0:T(8,128)(2,1)S(1)} %get-tuple-element.75.refs_8_.refs_12_), channel_id=1, source_target_pairs={{0,2},{1,3},{2,0},{3,1},{4,6},{5,7},{6,4},{7,5},{8,10},{9,11},{10,... | collective-permute-start | bytes 1572872 | tf_op jit(solution)/shard_map/ppermute | solution.py:694
  40.3 12.9 %collective-permute-start.8 = (bf16[2,2,2,32,1024]{4,3,2,1,0:T(8,128)(2,1)S(1)}, bf16[2,2,2,32,1024]{4,3,2,1,0:T(8,128)(2,1)S(1)}, u32[]{:S(2)}, u32[]{:S(2)}) collective-permute-start(bf16[2,2,2,32,1024]{4,3,2,1,0:T(8,128)(2,1)S(1)} %get-tuple-element.76.refs_9_.refs_13_), channel_id=1, source_target_pairs={{0,2},{1,3},{2,0},{3,1},{4,6},{5,7},{6,4},{7,5},{8,10},{9,11},{10,... | collective-permute-start | bytes 1572872 | tf_op jit(solution)/shard_map/ppermute | solution.py:694
  51.8 3.0 %collective-permute-start.10 = (bf16[2,2,2,32,1024]{4,3,2,1,0:T(8,128)(2,1)S(1)}, bf16[2,2,2,32,1024]{4,3,2,1,0:T(8,128)(2,1)}, u32[]{:S(2)}, u32[]{:S(2)}) collective-permute-start(bf16[2,2,2,32,1024]{4,3,2,1,0:T(8,128)(2,1)S(1)} %collective-permute-done.6.refs_11_.refs_15_), channel_id=1, source_target_pairs={{0,2},{1,3},{2,0},{3,1},{4,6},{5,7},{6,4},{7,5},{8,10},{9,11},{10,... | collective-permute-start | bytes 1572872 | tf_op jit(solution)/shard_map/ppermute | solution.py:694
  53.2 2.0 %collective-permute-start.9 = (bf16[2,2,2,32,1024]{4,3,2,1,0:T(8,128)(2,1)S(1)}, bf16[2,2,2,32,1024]{4,3,2,1,0:T(8,128)(2,1)}, u32[]{:S(2)}, u32[]{:S(2)}) collective-permute-start(bf16[2,2,2,32,1024]{4,3,2,1,0:T(8,128)(2,1)S(1)} %collective-permute-done.5.refs_10_.refs_14_), channel_id=1, source_target_pairs={{0,2},{1,3},{2,0},{3,1},{4,6},{5,7},{6,4},{7,5},{8,10},{9,11},{10,... | collective-permute-start | bytes 1572872 | tf_op jit(solution)/shard_map/ppermute | solution.py:694
  73.5 5.0 %collective-permute-start.11 = (bf16[2,2,2,4,256,128]{5,4,3,2,1,0:T(8,128)(2,1)}, bf16[2,2,2,4,256,128]{5,4,3,2,1,0:T(8,128)(2,1)}, u32[]{:S(2)}, u32[]{:S(2)}) collective-permute-start(bf16[2,2,2,4,256,128]{5,4,3,2,1,0:T(8,128)(2,1)} %get-tuple-element.91), channel_id=1, source_target_pairs={{0,2},{1,3},{2,0},{3,1},{4,6},{5,7},{6,4},{7,5},{8,10},{9,11},{10,... | collective-permute-start | bytes 6291464 | tf_op jit(solution)/shard_map/ppermute | solution.py:694
  74.3 18.6 %all-to-all-start.2 = ((bf16[32,64,128]{2,1,0:T(8,128)(2,1)}), bf16[32,64,128]{2,1,0:T(8,128)(2,1)S(1)}, u32[]{:S(2)}, u32[]{:S(2)}) async-start(bf16[32,64,128]{2,1,0:T(8,128)(2,1)} %get-tuple-element.77), calls=%async_computation.2 | async-start | bytes 1048576 | tf_op jit(solution)/shard_map/all_to_all | solution.py:804
  80.8 19.6 %collective-permute-start.12 = (bf16[2,4,256,128]{3,2,1,0:T(8,128)(2,1)}, bf16[2,4,256,128]{3,2,1,0:T(8,128)(2,1)}, u32[]{:S(2)}, u32[]{:S(2)}) collective-permute-start(bf16[2,4,256,128]{3,2,1,0:T(8,128)(2,1)} %get-tuple-element.92), channel_id=1, source_target_pairs={{0,1},{1,0},{2,3},{3,2},{4,5},{5,4},{6,7},{7,6},{8,9},{9,8},{10,11... | collective-permute-start | bytes 1572872 | tf_op jit(solution)/shard_map/ppermute | solution.py:694
  82.1 18.3 %collective-permute-start.13 = (bf16[2,4,256,128]{3,2,1,0:T(8,128)(2,1)}, bf16[2,4,256,128]{3,2,1,0:T(8,128)(2,1)}, u32[]{:S(2)}, u32[]{:S(2)}) collective-permute-start(bf16[2,4,256,128]{3,2,1,0:T(8,128)(2,1)} %get-tuple-element.93), channel_id=1, source_target_pairs={{0,4},{1,5},{2,6},{3,7},{4,0},{5,1},{6,2},{7,3},{8,12},{9,13},{10,... | collective-permute-start | bytes 1572872 | tf_op jit(solution)/shard_map/ppermute | solution.py:694
  83.6 9.3 %copy-start.11 = (f32[128,4]{1,0:T(8,128)S(1)}, f32[128,4]{1,0:T(8,128)}, u32[]{:S(2)}) copy-start(f32[128,4]{1,0:T(8,128)} %copy-done.10) | copy-start | bytes 6148
  95.5 31.2 %all-to-all-start.3 = ((bf16[32,64,128]{2,1,0:T(8,128)(2,1)}), bf16[32,64,128]{2,1,0:T(8,128)(2,1)S(1)}, u32[]{:S(2)}, u32[]{:S(2)}) async-start(bf16[32,64,128]{2,1,0:T(8,128)(2,1)} %get-tuple-element.104), calls=%async_computation.3 | async-start | bytes 1048576 | tf_op jit(solution)/shard_map/all_to_all | solution.py:827
  99.1 1.3 collective-permute-start.14
  101.9 15.3 %collective-permute-start.15 = (bf16[4,256,128]{2,1,0:T(8,128)(2,1)S(1)}, bf16[4,256,128]{2,1,0:T(8,128)(2,1)S(1)}, u32[]{:S(2)}, u32[]{:S(2)}) collective-permute-start(bf16[4,256,128]{2,1,0:T(8,128)(2,1)S(1)} %get-tuple-element.96), channel_id=1, source_target_pairs={{0,4},{1,5},{2,6},{3,7},{4,0},{5,1},{6,2},{7,3},{8,12},{9,13},{10,... | collective-permute-start | bytes 786440 | tf_op jit(solution)/shard_map/ppermute | solution.py:694
  103.7 13.5 %collective-permute-start.16 = (bf16[4,256,128]{2,1,0:T(8,128)(2,1)S(1)}, bf16[4,256,128]{2,1,0:T(8,128)(2,1)S(1)}, u32[]{:S(2)}, u32[]{:S(2)}) collective-permute-start(bf16[4,256,128]{2,1,0:T(8,128)(2,1)S(1)} %get-tuple-element.97), channel_id=1, source_target_pairs={{0,1},{1,0},{2,3},{3,2},{4,5},{5,4},{6,7},{7,6},{8,9},{9,8},{10,11... | collective-permute-start | bytes 786440 | tf_op jit(solution)/shard_map/ppermute | solution.py:694
  105.2 21.5 %copy-start.14 = (f32[13,512]{1,0:T(8,128)S(1)}, f32[13,512]{1,0:T(8,128)}, u32[]{:S(2)}) copy-start(f32[13,512]{1,0:T(8,128)} %refs_16_.1) | copy-start | bytes 79876
  105.2 4.6 %collective-permute-start.17 = (bf16[160,128]{1,0:T(8,128)(2,1)S(1)}, bf16[160,128]{1,0:T(8,128)(2,1)S(1)}, u32[]{:S(2)}, u32[]{:S(2)}) collective-permute-start(bf16[160,128]{1,0:T(8,128)(2,1)S(1)} %get-tuple-element.98.refs_6_), channel_id=1, source_target_pairs={{0,8},{1,9},{2,10},{3,11},{4,12},{5,13},{6,14},{7,15},{8,0},{9,1},... | collective-permute-start | bytes 122888 | tf_op jit(solution)/shard_map/ppermute | solution.py:694
  106.7 10.5 %collective-permute-start.18 = (bf16[160,128]{1,0:T(8,128)(2,1)S(1)}, bf16[160,128]{1,0:T(8,128)(2,1)S(1)}, u32[]{:S(2)}, u32[]{:S(2)}) collective-permute-start(bf16[160,128]{1,0:T(8,128)(2,1)S(1)} %get-tuple-element.98.refs_6_), channel_id=1, source_target_pairs={{0,16},{1,17},{2,18},{3,19},{4,20},{5,21},{6,22},{7,23},{8,24},{9,... | collective-permute-start | bytes 122888 | tf_op jit(solution)/shard_map/ppermute | solution.py:694
  109.1 8.1 %collective-permute-start.19 = (bf16[160,128]{1,0:T(8,128)(2,1)S(1)}, bf16[160,128]{1,0:T(8,128)(2,1)S(1)}, u32[]{:S(2)}, u32[]{:S(2)}) collective-permute-start(bf16[160,128]{1,0:T(8,128)(2,1)S(1)} %get-tuple-element.98.refs_6_), channel_id=1, source_target_pairs={{0,24},{1,25},{2,26},{3,27},{4,28},{5,29},{6,30},{7,31},{8,16},{9,... | collective-permute-start | bytes 122888 | tf_op jit(solution)/shard_map/ppermute | solution.py:694
  118.7 5.2 %collective-permute-start.23 = (bf16[2,256,128]{2,1,0:T(8,128)(2,1)S(1)}, bf16[2,256,128]{2,1,0:T(8,128)(2,1)S(1)}, u32[]{:S(2)}, u32[]{:S(2)}) collective-permute-start(bf16[2,256,128]{2,1,0:T(8,128)(2,1)S(1)} %get-tuple-element.101), channel_id=1, source_target_pairs={{0,8},{1,9},{2,10},{3,11},{4,12},{5,13},{6,14},{7,15},{8,0},{9,1},... | collective-permute-start | bytes 393224 | tf_op jit(solution)/shard_map/ppermute | solution.py:694
  119.8 14.1 %collective-permute-start.20 = (bf16[4,160,128]{2,1,0:T(8,128)(2,1)S(1)}, bf16[4,160,128]{2,1,0:T(8,128)(2,1)S(1)}, u32[]{:S(2)}, u32[]{:S(2)}) collective-permute-start(bf16[4,160,128]{2,1,0:T(8,128)(2,1)S(1)} %get-tuple-element.100.refs_0_), channel_id=1, source_target_pairs={{0,1},{1,0},{2,3},{3,2},{4,5},{5,4},{6,7},{7,6},{8,9},{9,8},{10,11... | collective-permute-start | bytes 491528 | tf_op jit(solution)/shard_map/ppermute | solution.py:694
  121.3 12.7 %collective-permute-start.21 = (bf16[4,160,128]{2,1,0:T(8,128)(2,1)S(1)}, bf16[4,160,128]{2,1,0:T(8,128)(2,1)S(1)}, u32[]{:S(2)}, u32[]{:S(2)}) collective-permute-start(bf16[4,160,128]{2,1,0:T(8,128)(2,1)S(1)} %get-tuple-element.100.refs_0_), channel_id=1, source_target_pairs={{0,4},{1,5},{2,6},{3,7},{4,0},{5,1},{6,2},{7,3},{8,12},{9,13},{10,... | collective-permute-start | bytes 491528 | tf_op jit(solution)/shard_map/ppermute | solution.py:694
  122.7 11.2 %collective-permute-start.22 = (bf16[4,160,128]{2,1,0:T(8,128)(2,1)S(1)}, bf16[4,160,128]{2,1,0:T(8,128)(2,1)S(1)}, u32[]{:S(2)}, u32[]{:S(2)}) collective-permute-start(bf16[4,160,128]{2,1,0:T(8,128)(2,1)S(1)} %get-tuple-element.100.refs_0_), channel_id=1, source_target_pairs={{0,5},{1,4},{2,7},{3,6},{4,1},{5,0},{6,3},{7,2},{8,13},{9,12},{10,... | collective-permute-start | bytes 491528 | tf_op jit(solution)/shard_map/ppermute | solution.py:694
  123.3 10.6 %collective-permute-start.24 = (bf16[2,256,128]{2,1,0:T(8,128)(2,1)S(1)}, bf16[2,256,128]{2,1,0:T(8,128)(2,1)S(1)}, u32[]{:S(2)}, u32[]{:S(2)}) collective-permute-start(bf16[2,256,128]{2,1,0:T(8,128)(2,1)S(1)} %get-tuple-element.102), channel_id=1, source_target_pairs={{0,16},{1,17},{2,18},{3,19},{4,20},{5,21},{6,22},{7,23},{8,24},{9,... | collective-permute-start | bytes 393224 | tf_op jit(solution)/shard_map/ppermute | solution.py:694
  123.9 10.0 %collective-permute-start.25 = (bf16[2,256,128]{2,1,0:T(8,128)(2,1)S(1)}, bf16[2,256,128]{2,1,0:T(8,128)(2,1)S(1)}, u32[]{:S(2)}, u32[]{:S(2)}) collective-permute-start(bf16[2,256,128]{2,1,0:T(8,128)(2,1)S(1)} %get-tuple-element.103), channel_id=1, source_target_pairs={{0,24},{1,25},{2,26},{3,27},{4,28},{5,29},{6,30},{7,31},{8,16},{9,... | collective-permute-start | bytes 393224 | tf_op jit(solution)/shard_map/ppermute | solution.py:694
  126.7 8.8 %copy-start.2 = (f32[2,8,2,64,64]{4,3,2,1,0:T(8,128)S(1)}, f32[2,8,2,64,64]{4,3,2,1,0:T(8,128)}, u32[]{:S(2)}) copy-start(f32[2,8,2,64,64]{4,3,2,1,0:T(8,128)} %refs_13_.1) | copy-start | bytes 1572868
  126.7 8.8 %copy-start.4 = (f32[2,8,2,64,64]{4,3,2,1,0:T(8,128)S(1)}, f32[2,8,2,64,64]{4,3,2,1,0:T(8,128)}, u32[]{:S(2)}) copy-start(f32[2,8,2,64,64]{4,3,2,1,0:T(8,128)} %refs_14_.1) | copy-start | bytes 1572868
  126.7 8.8 %copy-start.5 = (f32[2,8,2,64,64]{4,3,2,1,0:T(8,128)S(1)}, f32[2,8,2,64,64]{4,3,2,1,0:T(8,128)}, u32[]{:S(2)}) copy-start(f32[2,8,2,64,64]{4,3,2,1,0:T(8,128)} %refs_15_.1) | copy-start | bytes 1572868
  126.7 8.8 %copy-start.8 = (f32[32,1024]{1,0:T(8,128)S(1)}, f32[32,1024]{1,0:T(8,128)}, u32[]{:S(2)}) copy-start(f32[32,1024]{1,0:T(8,128)} %refs_6_.1) | copy-start | bytes 393220
  126.7 8.8 %copy-start.9 = (f32[32,1024]{1,0:T(8,128)S(1)}, f32[32,1024]{1,0:T(8,128)}, u32[]{:S(2)}) copy-start(f32[32,1024]{1,0:T(8,128)} %refs_5_.3) | copy-start | bytes 393220
  126.7 8.8 %copy-start.15 = (f32[32,1024]{1,0:T(8,128)S(1)}, f32[32,1024]{1,0:T(8,128)}, u32[]{:S(2)}) copy-start(f32[32,1024]{1,0:T(8,128)} %refs_7_.2) | copy-start | bytes 393220
  126.7 8.8 %copy-start.16 = (f32[32,1024]{1,0:T(8,128)S(1)}, f32[32,1024]{1,0:T(8,128)}, u32[]{:S(2)}) copy-start(f32[32,1024]{1,0:T(8,128)} %refs_8_.1) | copy-start | bytes 393220
  126.8 8.8 %copy-start.17 = (f32[32,1024]{1,0:T(8,128)S(1)}, f32[32,1024]{1,0:T(8,128)}, u32[]{:S(2)}) copy-start(f32[32,1024]{1,0:T(8,128)} %refs_9_.2) | copy-start | bytes 393220
  134.0 1.5 %collective-permute-start.26 = (bf16[4,160,128]{2,1,0:T(8,128)(2,1)S(1)}, bf16[4,160,128]{2,1,0:T(8,128)(2,1)S(1)}, u32[]{:S(2)}, u32[]{:S(2)}) collective-permute-start(bf16[4,160,128]{2,1,0:T(8,128)(2,1)S(1)} %get-tuple-element.109.refs_11_), channel_id=1, source_target_pairs={{0,2},{1,3},{2,0},{3,1},{4,6},{5,7},{6,4},{7,5},{8,10},{9,11},{10,... | collective-permute-start | bytes 491528 | tf_op jit(solution)/shard_map/ppermute | solution.py:694
  (8 other events, 36.6 us)
